TPU v7x, 32 devices: a whole 2x2x4 slice. The times are simulated.
32 devices in a mesh: seq: 4 (over y, x), ctx: 8 (over z, core).
Axes of the slice: x: 2, y: 2, z: 4, core: 2. Of those that a mesh axis runs over, the one named last changes fastest.
Arguments:
- queries: bfloat16 [4096, 2048], P(('seq', 'ctx')), parts along dimension 0, may hold values from -1 to 1
- keys_in: bfloat16 [4096, 2048], P(('seq', 'ctx')), parts along dimension 0, may hold values from -1 to 1
- value_input: bfloat16 [4096, 2048], P(('seq', 'ctx')), parts along dimension 0, may hold values from -1 to 1
- level_gain: float32 [11, 16, 4096], P(None, None, ('seq', 'ctx')), parts along dimension 2, may hold values from 0.2 to 2
- decay_log: float32 [16, 4096], P(None, ('seq', 'ctx')), parts along dimension 1, may hold values from -0.7 to 0, as said below
- out_grad: bfloat16 [4096, 2048], P(('seq', 'ctx')), parts along dimension 0, may hold values from -1 to 1
Outputs:
- mixed_out: bfloat16 [4096, 2048], P(('seq', 'ctx')), parts along dimension 0
- query_gradient: bfloat16 [4096, 2048], P(('seq', 'ctx')), parts along dimension 0
- grad_keys: bfloat16 [4096, 2048], P(('seq', 'ctx')), parts along dimension 0
- grad_values: bfloat16 [4096, 2048], P(('seq', 'ctx')), parts along dimension 0
- grad_gain: float32 [11, 16, 4096], P(None, None, ('seq', 'ctx')), parts along dimension 2
- grad_decay: float32 [16, 4096], P(None, ('seq', 'ctx')), parts along dimension 1
There are 4 independent parts, one for each index of `seq`. A program takes and returns all parts, laid end to end along the dimension named above; each array names one. Nothing has to cross between parts.
Inputs may be any that keep to these rules, and one draw needn't show every extreme that they name: `decay_log`: every entry is negative.
All inputs are finite; a program needn't handle non-finite values.
Results may differ from a plain program's by a relative error of at most 0.001.
Values sent between devices are 32-bit elements; how exact they have to be, the bound alone decides.
No kernel may reach another device: no remote copies, remote signals or barrier semaphores. Data moves between devices by JAX's collectives and lax.ppermute only.
A program may use at most 128 MiB of HBM per device.

v0:
```python
import jax
import jax.numpy as jnp
from jax import lax
from jax.sharding import PartitionSpec as P

TOP_ACCURACY = lax.Precision.HIGHEST


def from_partner(block, axis, distance):
    count = lax.axis_size(axis)
    route = []
    for low in range(count):
        high = low | 1 << distance
        if high != low and high < count:
            route += [(low, high), (high, low)]
    return lax.ppermute(block, axis, route)


def passed_along(value, axis, steps):
    count = lax.axis_size(axis)
    first, last = (max(0, -steps), min(count, count - steps))
    return lax.ppermute(value, axis, [(source, source + steps) for source in range(first, last)])


def level_table(tok, lvl_in):
    places = jnp.arange(tok, dtype=jnp.int32)
    mixing = jnp.bitwise_xor(places[:, None], places[None, :])
    table = jnp.zeros((tok, tok), jnp.int32)
    for power in range(lvl_in):
        table = table + (mixing >= 2**power).astype(jnp.int32)
    return table


def block_front(keys_h, value_rows_head, decay):
    running = jnp.cumsum(decay, axis=1)
    total_sum = running[:, -1]
    scaled_result = keys_h * jnp.exp(total_sum[:, None] - running)[:, :, None]
    return (
        jnp.einsum("ybu,ybe->yue", scaled_result, value_rows_head, precision=TOP_ACCURACY),
        total_sum,
    )


def block_output(queries_h, keys_h, value_rows_head, gain, decay, buckets):
    tok = queries_h.shape[1]
    lvl_in = tok.bit_length() - 1
    running = jnp.cumsum(decay, axis=1)
    places = jnp.arange(tok, dtype=jnp.int32)
    causal = places[:, None] >= places[None, :]
    spread_gap = jnp.where(causal[None], running[:, :, None] - running[:, None, :], 0.0)
    fading = jnp.where(causal[None], jnp.exp(spread_gap), 0.0)
    table = level_table(tok, lvl_in)
    picks = (table[None] == jnp.arange(lvl_in + 1, dtype=jnp.int32)[:, None, None]).astype(
        jnp.float32
    )
    weighting = jnp.einsum("lij,lhi->hij", picks, gain[: lvl_in + 1], precision=TOP_ACCURACY)
    scores = jnp.einsum("hik,hjk->hij", queries_h, keys_h, precision=TOP_ACCURACY)
    result = jnp.einsum(
        "hij,hjv->hiv", scores * weighting * fading, value_rows_head, precision=TOP_ACCURACY
    )
    lifted = queries_h * jnp.exp(running)[:, :, None]
    reach = gain[lvl_in + 1 :][:, :, :, None] * lifted[None]
    return result + jnp.einsum("jhik,jhkv->hiv", reach, buckets, precision=TOP_ACCURACY)


def merge_step(own_total, own_state, offset, other_total, other_state, is_upper):
    bucket = jnp.where(is_upper, jnp.exp(offset)[:, None, None] * other_state, 0.0)
    low_state = jnp.where(is_upper, other_state, own_state)
    high_state = jnp.where(is_upper, own_state, other_state)
    high_total = jnp.where(is_upper, own_total, other_total)
    merged = jnp.exp(high_total)[:, None, None] * low_state + high_state
    new_offset = offset + jnp.where(is_upper, other_total, 0.0)
    return (own_total + other_total, merged, new_offset, bucket)


def partner_grads(
    own_total, own_state, offset, other_total, g_total, g_state, g_offset, g_bucket, is_upper
):
    factor = jnp.exp(jnp.where(is_upper, own_total, other_total))
    d_other_state = jnp.where(
        is_upper,
        factor[:, None, None] * g_state + jnp.exp(offset)[:, None, None] * g_bucket,
        g_state,
    )
    lower_term = factor * jnp.sum(g_state * own_state, axis=(1, 2))
    d_other_total = g_total + jnp.where(is_upper, g_offset, lower_term)
    return (d_other_total, d_other_state)


def own_grads(
    own_total, offset, other_total, other_state, g_total, g_state, g_offset, g_bucket, is_upper
):
    factor = jnp.exp(jnp.where(is_upper, own_total, other_total))
    d_own_state = jnp.where(is_upper, g_state, factor[:, None, None] * g_state)
    upper_total = factor * jnp.sum(g_state * other_state, axis=(1, 2))
    d_own_total = g_total + jnp.where(is_upper, upper_total, 0.0)
    upper_offset = jnp.exp(offset) * jnp.sum(g_bucket * other_state, axis=(1, 2))
    d_offset = g_offset + jnp.where(is_upper, upper_offset, 0.0)
    return (d_own_total, d_own_state, d_offset)


def to_heads(block, heads):
    tokens, width = block.shape
    return block.reshape(tokens, heads, width // heads).transpose(1, 0, 2).astype(jnp.float32)


def from_heads(block):
    heads, tokens, head_dim = block.shape
    return block.transpose(1, 0, 2).reshape(tokens, heads * head_dim)


def per_device(queries, keys_in, value_input, level_gain, decay_log, out_grad):
    heads = decay_log.shape[0]
    query_h = to_heads(queries, heads)
    key_h = to_heads(keys_in, heads)
    value_h = to_heads(value_input, heads)
    cotangent = to_heads(out_grad, heads)
    count = lax.axis_size("ctx")
    depth = count.bit_length() - 1
    position = lax.axis_index("ctx")
    (state, total_sum), front_back = jax.vjp(block_front, key_h, value_h, decay_log)
    own_total = total_sum
    own_state = state
    offset = jnp.zeros_like(total_sum)
    saved = []
    found = []
    top_other = state
    for bit in range(depth):
        other_total, other_state = from_partner((own_total, own_state), "ctx", bit)
        is_upper = jnp.right_shift(position, bit) % 2 == 1
        saved.append((own_total, own_state, offset, other_total))
        if bit == depth - 1:
            top_other = other_state
        own_total, own_state, offset, bucket = merge_step(
            own_total, own_state, offset, other_total, other_state, is_upper
        )
        found.append(bucket)
    buckets = jnp.stack(found)
    mixed, out_back = jax.vjp(block_output, query_h, key_h, value_h, level_gain, decay_log, buckets)
    grad_query, grad_key, grad_value, grad_gain, grad_decay, bucket_gradient = out_back(cotangent)
    grad_total = jnp.zeros_like(total_sum)
    grad_state = jnp.zeros_like(state)
    grad_offset = jnp.zeros_like(total_sum)
    for bit in reversed(range(depth)):
        is_upper = jnp.right_shift(position, bit) % 2 == 1
        level_total, level_state, level_offset, level_other_total = saved[bit]
        d_other_total, d_other_state = partner_grads(
            level_total,
            level_state,
            level_offset,
            level_other_total,
            grad_total,
            grad_state,
            grad_offset,
            bucket_gradient[bit],
            is_upper,
        )
        if bit == depth - 1:
            back_total, back_state = passed_along(
                (d_other_total, d_other_state), "ctx", -(count // 2)
            )
            partner_state = top_other
        else:
            back_total, back_state, partner_state = from_partner(
                (d_other_total, d_other_state, level_state), "ctx", bit
            )
        d_own_total, d_own_state, d_offset = own_grads(
            level_total,
            level_offset,
            level_other_total,
            partner_state,
            grad_total,
            grad_state,
            grad_offset,
            bucket_gradient[bit],
            is_upper,
        )
        grad_total = d_own_total + back_total
        grad_state = d_own_state + back_state
        grad_offset = d_offset
    key_more, value_more, decay_more = front_back((grad_state, grad_total))
    return (
        from_heads(mixed).astype(jnp.bfloat16),
        from_heads(grad_query).astype(jnp.bfloat16),
        from_heads(grad_key + key_more).astype(jnp.bfloat16),
        from_heads(grad_value + value_more).astype(jnp.bfloat16),
        grad_gain,
        grad_decay + decay_more,
    )


def solution(mesh):
    placed = (
        P(("seq", "ctx"), None),
        P(("seq", "ctx"), None),
        P(("seq", "ctx"), None),
        P(None, None, ("seq", "ctx")),
        P(None, ("seq", "ctx")),
        P(("seq", "ctx"), None),
    )
    return jax.shard_map(
        per_device,
        mesh=mesh,
        in_specs=placed,
        out_specs=(
            P(("seq", "ctx"), None),
            P(("seq", "ctx"), None),
            P(("seq", "ctx"), None),
            P(("seq", "ctx"), None),
            P(None, None, ("seq", "ctx")),
            P(None, ("seq", "ctx")),
        ),
        check_vma=False,
    )
```

profile of v0, /device:TPU:1, one launch (start us, length us, event | category | flops | bytes accessed | tf_op | source)
XLA Modules:
  0.0 206.6 jit_solution(6190862701978117092)
XLA Ops:
  0.6 1.0 reduce_window_sum.31
  1.6 0.2 slice_reduce_fusion
  1.8 0.1 fusion.94
  1.9 1.3 copy.65
  3.2 1.7 fusion.25
  4.9 0.1 collective-permute-start
  5.0 0.5 collective-permute-start.1
  5.5 2.1 %collective-permute-done.1 = f32[16]{0:T(128)S(1)} collective-permute-done((f32[16]{0:T(128)S(1)}, f32[16]{0:T(128)S(1)}, u32[]{:S(2)}, u32[]{:S(2)}) %collective-permute-start.1) | collective-permute-done | bytes 96 | tf_op jit(solution)/shard_map/ppermute | solution.py:16
  7.7 1.0 copy-done.6
  8.7 2.6 %select_bitcast_fusion.2 = (f32[1,16,128,128]{3,2,1,0:T(8,128)}, f32[16,128,128]{2,1,0:T(8,128)S(1)}) fusion(f32[16,128,128]{2,1,0:T(8,128)} %copy-done.6, pred[]{:T(512)S(6)} %eq.41, f32[16,128,128]{2,1,0:T(8,128)S(1)} %fusion.25, f32[16]{0:T(128)S(1)} %get-tuple-element.59), kind=kLoop, calls=%fused_computation.65 | loop fusion | flops 1310720 | bytes 4194369 | tf_op jit(solution)/shard_map/stack | solution.py:138
  11.2 2.4 %collective-permute-start.2 = (f32[16,128,128]{2,1,0:T(8,128)S(1)}, f32[16,128,128]{2,1,0:T(8,128)}, u32[]{:S(2)}, u32[]{:S(2)}) collective-permute-start(f32[16,128,128]{2,1,0:T(8,128)S(1)} %get-tuple-element.50), channel_id=1, source_target_pairs={{0,2},{2,0},{1,3},{3,1},{4,6},{6,4},{5,7},{7,5},{8,10},{10,8},{9,1... | collective-permute-start | bytes 3145736 | tf_op jit(solution)/shard_map/ppermute | solution.py:16
  13.7 1.3 copy.64
  15.0 2.0 copy.107
  17.1 1.1 convert_multiply_fusion.3
  18.2 0.2 copy.68
  18.4 18.5 %collective-permute-done.3 = f32[16]{0:T(128)S(1)} collective-permute-done((f32[16]{0:T(128)S(1)}, f32[16]{0:T(128)S(1)}, u32[]{:S(2)}, u32[]{:S(2)}) %collective-permute-start.3) | collective-permute-done | bytes 96 | tf_op jit(solution)/shard_map/ppermute | solution.py:16
  37.0 1.7 multiply_reduce_fusion.6
  38.7 2.2 %collective-permute-start.4 = (f32[16,128,128]{2,1,0:T(8,128)S(1)}, f32[16,128,128]{2,1,0:T(8,128)S(1)}, u32[]{:S(2)}, u32[]{:S(2)}) collective-permute-start(f32[16,128,128]{2,1,0:T(8,128)S(1)} %get-tuple-element.45), channel_id=1, source_target_pairs={{0,4},{4,0},{1,5},{5,1},{2,6},{6,2},{3,7},{7,3},{8,12},{12,8},{9,1... | collective-permute-start | bytes 3145736 | tf_op jit(solution)/shard_map/ppermute | solution.py:16
  41.0 1.0 fusion.51
  42.0 0.4 fusion.97
  42.4 0.3 collective-permute-start.5
  42.7 0.1 copy.112
  42.8 43.5 %collective-permute-done.5 = f32[16]{0:T(128)S(1)} collective-permute-done((f32[16]{0:T(128)S(1)}, f32[16]{0:T(128)S(1)}, u32[]{:S(2)}, u32[]{:S(2)}) %collective-permute-start.5) | collective-permute-done | bytes 96 | tf_op jit(solution)/shard_map/ppermute | solution.py:16
  86.3 0.5 broadcast_select_fusion.1
  86.9 0.1 select_bitcast_fusion
  87.1 2.1 %fusion.1 = (f32[3,16,128]{2,0,1:T(4,128)S(1)}, f32[16,128,128]{1,2,0:T(8,128)S(1)}, f32[3,16,128,128]{2,3,0,1:T(8,128)S(1)}) fusion(f32[16,128,128]{1,2,0:T(8,128)S(1)} %copy-done.12, f32[3,16,128]{2,0,1:T(4,128)S(1)} %copy.72, bf16[16,128,128,1]{1,2,3,0:T(8,128)(2,1)S(1)} %bitcast.154, f32[1,16,128,128]{3,2,1,0:T(8,128)S(1)} %select_bitcast_fusion, ...), kind=kOutput, calls=%fused_computation.4 | convolution fusion | flops 1213196288 | bytes 8962048 | tf_op jit(solution)/shard_map/transpose(jvp(jhik,jhkv->hiv))/dot_general | solution.py:63
  89.2 1.7 fusion.8
  90.9 0.2 add_select_fusion
  91.1 1.5 collective-permute-start.6
  92.6 1.1 fusion.62
  93.7 0.3 fusion.30
  94.0 2.3 %convolution_bitcast_fusion.2 = f32[8,16,128]{1,0,2:T(8,128)} fusion(f32[128,16,128]{2,0,1:T(8,128)S(1)} %fusion.30, s32[128,128]{1,0:T(8,128)S(1)} %convert_add_fusion), kind=kOutput, calls=%fused_computation.33 | convolution fusion | flops 25296896 | bytes 1179648 | tf_op jit(solution)/shard_map/transpose(jvp(lij,lhi->hij))/dot_general | solution.py:56
  96.3 1.9 fusion.36
  98.2 42.1 %collective-permute-done.6 = f32[16,128,128]{2,1,0:T(8,128)S(1)} collective-permute-done((f32[16,128,128]{2,1,0:T(8,128)S(1)}, f32[16,128,128]{2,1,0:T(8,128)S(1)}, u32[]{:S(2)}, u32[]{:S(2)}) %collective-permute-start.6) | collective-permute-done | bytes 1048608 | tf_op jit(solution)/shard_map/ppermute | solution.py:22
  140.4 4.0 %multiply_reduce_fusion.1 = (f32[16]{0:T(128)}, f32[16]{0:T(128)S(1)}, f32[16]{0:T(128)}, f32[16]{0:T(128)}, f32[16]{0:T(128)}, /*index=5*/f32[16,128,128]{2,1,0:T(8,128)}) fusion(f32[16,128,128]{2,1,0:T(8,128)} %collective-permute-done.2, f32[3,16,128,128]{3,2,1,0:T(8,128)S(1)} %fusion.8, f32[16,128,128]{2,1,0:T(8,128)S(1)} %collective-permute-done.4, ...), kind=kLoop, calls=%fused_computation.51 | loop fusion | flops 3932080 | bytes 7340545 | tf_op jit(solution)/shard_map/reduce_sum | solution.py:97
  144.4 0.1 subtract_exponential_fusion
  144.5 2.5 %fusion.38 = f32[16,128,128]{1,2,0:T(8,128)} fusion(f32[16,128,128]{2,1,0:T(8,128)S(1)} %get-tuple-element.46, bf16[16,128,128]{2,0,1:T(8,128)(2,1)S(1)} %bitcast.160, f32[16,128]{1,0:T(8,128)S(1)} %reduce_window_sum.31, pred[128,128]{1,0:T(8,128)(4,1)S(1)} %iota_compare_fusion.3), kind=kOutput, calls=%fused_computation.70 | convolution fusion | flops 403701760 | bytes 2646016 | tf_op jit(solution)/shard_map/jvp(hij,hjv->hiv)/dot_general | solution.py:58
  147.0 1.5 collective-permute-start.9
  148.6 0.1 fusion.26
  148.7 1.2 reduce_window_sum.33
  149.9 0.2 copy.83
  150.1 1.1 pad_add_fusion
  151.2 1.0 copy.90
  152.2 15.6 %collective-permute-done.7 = f32[16,128,128]{2,1,0:T(8,128)} collective-permute-done((f32[16,128,128]{2,1,0:T(8,128)}, f32[16,128,128]{2,1,0:T(8,128)}, u32[]{:S(2)}, u32[]{:S(2)}) %collective-permute-start.7) | collective-permute-done | bytes 1048608 | tf_op jit(solution)/shard_map/ppermute | solution.py:16
  167.8 2.6 %multiply_reduce_fusion.2 = (f32[16]{0:T(128)S(1)}, f32[16]{0:T(128)S(1)}, f32[16,128,128]{2,1,0:T(8,128)S(1)}) fusion(f32[16,128,128]{2,1,0:T(8,128)} %copy-done.6, f32[16,128,128]{2,1,0:T(8,128)} %copy-done.3, f32[16,128,128]{2,1,0:T(8,128)} %collective-permute-done.7, f32[16]{0:T(128)S(1)} %get-tuple-element.57, f32[16,128,128]{2,1,0:T(8,128)} %copy-done.7, ...), kind=kLoop, calls=%fused_computation.52 | loop fusion | flops 2097120 | bytes 5243137 | tf_op jit(solution)/shard_map/reduce_sum | solution.py:95
  170.5 2.5 %fusion.11 = f32[16,128,128]{2,1,0:T(8,128)} fusion(f32[16,128,128]{2,1,0:T(8,128)S(1)} %get-tuple-element.39, f32[3,16,128,128]{3,2,1,0:T(8,128)} %copy-done, f32[16]{0:T(128)S(1)} %get-tuple-element.59, pred[]{:T(512)S(6)} %eq.41), kind=kLoop, calls=%fused_computation.15 | loop fusion | flops 786432 | bytes 3145793 | tf_op jit(solution)/shard_map/jit(_where)/select_n | solution.py:80
  173.1 2.5 %collective-permute-start.8 = (f32[16,128,128]{2,1,0:T(8,128)}, f32[16,128,128]{2,1,0:T(8,128)}, u32[]{:S(2)}, u32[]{:S(2)}) collective-permute-start(f32[16,128,128]{2,1,0:T(8,128)} %fusion.11), channel_id=1, source_target_pairs={{0,1},{1,0},{2,3},{3,2},{4,5},{5,4},{6,7},{7,6},{8,9},{9,8},{10,11... | collective-permute-start | bytes 3145736 | tf_op jit(solution)/shard_map/ppermute | solution.py:16
  175.6 2.4 %fusion.23 = bf16[128,16,128]{0,2,1:T(8,128)(2,1)} fusion(bf16[16,128,128]{1,2,0:T(8,128)(2,1)S(1)} %bitcast.148, f32[16,128,128]{1,2,0:T(8,128)S(1)} %copy-done.9, f32[128,16]{0,1:T(8,128)S(1)} %get-tuple-element.53, f32[16,128,128]{2,1,0:T(8,128)S(1)} %get-tuple-element.64, f32[128,128,16]{1,2,0:T(8,128)S(1)} %copy-done.2, ...), kind=kOutput, calls=%fused_computation.30 | convolution fusion | flops 404750336 | bytes 4227072 | tf_op jit(solution)/shard_map/transpose(jvp(hik,hjk->hij))/dot_general | solution.py:57
  178.0 6.2 %fusion.20 = bf16[16,128,128]{1,2,0:T(8,128)(2,1)} fusion(f32[16,128,128]{1,2,0:T(8,128)S(1)} %copy-done.18, f32[16,128,128]{1,2,0:T(8,128)S(1)} %copy-done.13, f32[3,16,128]{2,0,1:T(4,128)S(1)} %copy.72, f32[1,16,128,128]{3,2,1,0:T(8,128)S(1)} %copy-done.15, f32[1,16,128,128]{3,2,1,0:T(8,128)S(1)} %copy-done.17, f32[1,16,128,128]{3,2,1,0:T(8,128)S(1)} %copy-done.11), kind=kOutput, calls=%fused_computation.29 | convolution fusion | flops 1210843136 | bytes 5791744 | tf_op jit(solution)/shard_map/jvp(jhik,jhkv->hiv)/dot_general | solution.py:63
  184.2 2.0 copy.87
  186.3 0.6 fusion.80
  186.9 2.0 copy.86
  188.9 0.3 collective-permute-done.10
  189.3 1.2 collective-permute-start.11
  190.5 3.6 %fusion.27 = (f32[16,128]{1,0:T(8,128)S(1)}, f32[16,128,128]{2,1,0:T(8,128)}) fusion(bf16[128,2048]{0,1:T(8,128)(2,1)S(1)} %copy.65, f32[16,128,128]{2,1,0:T(8,128)} %collective-permute-done.8, f32[16,128,128]{2,1,0:T(8,128)S(1)} %get-tuple-element.39, f32[16]{0:T(128)S(1)} %get-tuple-element.59, pred[]{:T(512)S(6)} %eq.41, bf16[128,2048]{1,0:T(8,128)(2,1)} %param.8), kind=kOutput, calls=%fused_computation.35 | convolution fusion | flops 404224000 | bytes 4202561 | tf_op jit(solution)/shard_map/transpose(jvp(ybu,ybe->yue))/dot_general | solution.py:39
  194.1 0.1 multiply_reduce_fusion.8
  194.2 0.1 copy.85
  194.3 0.1 pad_add_fusion.1
  194.4 1.2 reduce_window_sum.34
  195.6 4.6 %fusion.24 = bf16[16,128,128]{1,2,0:T(8,128)(2,1)} fusion(f32[16,128,128]{1,2,0:T(8,128)} %fusion.36, bf16[16,128,128]{1,2,0:T(8,128)(2,1)S(1)} %bitcast.149, f32[16,128]{1,0:T(8,128)S(1)} %get-tuple-element.55, f32[16,128,128]{2,1,0:T(8,128)} %collective-permute-done.8, f32[16,128,128]{2,1,0:T(8,128)S(1)} %get-tuple-element.39, ...), kind=kOutput, calls=%fused_computation.31 | convolution fusion | flops 404488192 | bytes 4202561 | tf_op jit(solution)/shard_map/transpose(jvp(ybu,ybe->yue))/dot_general | solution.py:39
  200.3 2.0 copy.89
  202.3 2.7 %fusion.32 = bf16[128,16,128]{0,2,1:T(8,128)(2,1)S(1)} fusion(f32[16,128,128]{2,1,0:T(8,128)} %get-tuple-element.66, f32[128,16]{0,1:T(8,128)S(1)} %get-tuple-element.52, bf16[16,128,128]{1,2,0:T(8,128)(2,1)S(1)} %bitcast.152, f32[16,128,128]{2,1,0:T(8,128)S(1)} %get-tuple-element.64, f32[128,128,16]{1,2,0:T(8,128)} %copy-done.1, ...), kind=kOutput, calls=%fused_computation.45 | convolution fusion | flops 404750336 | bytes 4227072 | tf_op jit(solution)/shard_map/transpose(jvp(hik,hjk->hij))/dot_general | solution.py:57
  205.0 1.0 copy.88
  206.0 0.6 add.178
  (71 shorter events, 0.3 us)
Async XLA Ops:
  4.9 12.1 %copy-start.3 = (f32[16,128,128]{2,1,0:T(8,128)}, f32[16,128,128]{2,1,0:T(8,128)S(1)}, u32[]{:S(2)}) copy-start(f32[16,128,128]{2,1,0:T(8,128)S(1)} %fusion.25) | copy-start | bytes 3145732
  4.9 2.7 %collective-permute-start = (f32[16,128,128]{2,1,0:T(8,128)S(1)}, f32[16,128,128]{2,1,0:T(8,128)S(1)}, u32[]{:S(2)}, u32[]{:S(2)}) collective-permute-start(f32[16,128,128]{2,1,0:T(8,128)S(1)} %fusion.25), channel_id=1, source_target_pairs={{0,1},{1,0},{2,3},{3,2},{4,5},{5,4},{6,7},{7,6},{8,9},{9,8},{10,11... | collective-permute-start | bytes 3145736 | tf_op jit(solution)/shard_map/ppermute | solution.py:16
  5.0 2.6 %collective-permute-start.1 = (f32[16]{0:T(128)S(1)}, f32[16]{0:T(128)S(1)}, u32[]{:S(2)}, u32[]{:S(2)}) collective-permute-start(f32[16]{0:T(128)S(1)} %slice_reduce_fusion), channel_id=1, source_target_pairs={{0,1},{1,0},{2,3},{3,2},{4,5},{5,4},{6,7},{7,6},{8,9},{9,8},{10,11... | collective-permute-start | bytes 200 | tf_op jit(solution)/shard_map/ppermute | solution.py:16
  7.7 79.3 %copy-start.19 = (f32[16]{0:T(128)}, f32[16]{0:T(128)S(1)}, u32[]{:S(2)}) copy-start(f32[16]{0:T(128)S(1)} %collective-permute-done.1) | copy-start | bytes 196
  7.7 1.0 copy-start.6
  8.7 8.4 %slice-start = ((f32[11,16,128]{2,1,0:T(8,128)}), f32[3,16,128]{2,1,0:T(8,128)S(1)}, s32[]{:S(2)}) async-start(f32[11,16,128]{2,1,0:T(8,128)} %param.9), calls=%async_computation | async-start | bytes 49152 | tf_op jit(solution)/shard_map/jvp()/slice | solution.py:62
  8.7 9.6 %slice-start.1 = ((f32[11,16,128]{2,1,0:T(8,128)}), f32[8,16,128]{2,1,0:T(8,128)S(1)}, s32[]{:S(2)}) async-start(f32[11,16,128]{2,1,0:T(8,128)} %param.9), calls=%async_computation.1 | async-start | bytes 131072 | tf_op jit(solution)/shard_map/jvp()/slice | solution.py:56
  11.2 25.8 %collective-permute-start.2 = (f32[16,128,128]{2,1,0:T(8,128)S(1)}, f32[16,128,128]{2,1,0:T(8,128)}, u32[]{:S(2)}, u32[]{:S(2)}) collective-permute-start(f32[16,128,128]{2,1,0:T(8,128)S(1)} %get-tuple-element.50), channel_id=1, source_target_pairs={{0,2},{2,0},{1,3},{3,1},{4,6},{6,4},{5,7},{7,5},{8,10},{10,8},{9,1... | collective-permute-start | bytes 3145736 | tf_op jit(solution)/shard_map/ppermute | solution.py:16
  18.2 18.8 %collective-permute-start.3 = (f32[16]{0:T(128)S(1)}, f32[16]{0:T(128)S(1)}, u32[]{:S(2)}, u32[]{:S(2)}) collective-permute-start(f32[16]{0:T(128)S(1)} %get-tuple-element.58), channel_id=1, source_target_pairs={{0,2},{2,0},{1,3},{3,1},{4,6},{6,4},{5,7},{7,5},{8,10},{10,8},{9,1... | collective-permute-start | bytes 200 | tf_op jit(solution)/shard_map/ppermute | solution.py:16
  37.0 5.7 %copy-start.4 = (bf16[128,2048]{1,0:T(8,128)(2,1)S(1)}, bf16[128,2048]{1,0:T(8,128)(2,1)}, u32[]{:S(2)}) copy-start(bf16[128,2048]{1,0:T(8,128)(2,1)} %param.8) | copy-start | bytes 1572868
  38.7 48.3 %copy-start.16 = (f32[1,16,128,128]{3,2,1,0:T(8,128)}, f32[1,16,128,128]{3,2,1,0:T(8,128)S(1)}, u32[]{:S(2)}) copy-start(f32[1,16,128,128]{3,2,1,0:T(8,128)S(1)} %get-tuple-element.51) | copy-start | bytes 3145732
  38.7 48.1 %collective-permute-start.4 = (f32[16,128,128]{2,1,0:T(8,128)S(1)}, f32[16,128,128]{2,1,0:T(8,128)S(1)}, u32[]{:S(2)}, u32[]{:S(2)}) collective-permute-start(f32[16,128,128]{2,1,0:T(8,128)S(1)} %get-tuple-element.45), channel_id=1, source_target_pairs={{0,4},{4,0},{1,5},{5,1},{2,6},{6,2},{3,7},{7,3},{8,12},{12,8},{9,1... | collective-permute-start | bytes 3145736 | tf_op jit(solution)/shard_map/ppermute | solution.py:16
  41.0 46.1 %copy-start.5 = (bf16[128,2048]{0,1:T(8,128)(2,1)S(1)}, bf16[128,2048]{0,1:T(8,128)(2,1)}, u32[]{:S(2)}) copy-start(bf16[128,2048]{0,1:T(8,128)(2,1)} %copy.107) | copy-start | bytes 1572868
  41.0 46.1 %copy-start.10 = (f32[1,16,128,128]{3,2,1,0:T(8,128)S(1)}, f32[1,16,128,128]{3,2,1,0:T(8,128)}, u32[]{:S(2)}) copy-start(f32[1,16,128,128]{3,2,1,0:T(8,128)} %get-tuple-element.49) | copy-start | bytes 3145732
  41.0 46.1 %copy-start.12 = (f32[16,128,128]{1,2,0:T(8,128)S(1)}, f32[16,128,128]{1,2,0:T(8,128)}, u32[]{:S(2)}) copy-start(f32[16,128,128]{1,2,0:T(8,128)} %convert_multiply_fusion.3) | copy-start | bytes 3145732
  42.0 50.6 %copy-start.1 = (f32[128,128,16]{1,2,0:T(8,128)}, f32[128,128,16]{1,2,0:T(8,128)S(1)}, u32[]{:S(2)}) copy-start(f32[128,128,16]{1,2,0:T(8,128)S(1)} %fusion.51) | copy-start | bytes 3145732
  42.4 43.9 %collective-permute-start.5 = (f32[16]{0:T(128)S(1)}, f32[16]{0:T(128)S(1)}, u32[]{:S(2)}, u32[]{:S(2)}) collective-permute-start(f32[16]{0:T(128)S(1)} %get-tuple-element.56), channel_id=1, source_target_pairs={{0,4},{4,0},{1,5},{5,1},{2,6},{6,2},{3,7},{7,3},{8,12},{12,8},{9,1... | collective-permute-start | bytes 200 | tf_op jit(solution)/shard_map/ppermute | solution.py:16
  87.0 2.2 %copy-start.14 = (f32[1,16,128,128]{3,2,1,0:T(8,128)}, f32[1,16,128,128]{3,2,1,0:T(8,128)S(1)}, u32[]{:S(2)}) copy-start(f32[1,16,128,128]{3,2,1,0:T(8,128)S(1)} %select_bitcast_fusion) | copy-start | bytes 3145732
  89.2 59.3 %copy-start.8 = (f32[16,128,128]{1,2,0:T(8,128)}, f32[16,128,128]{1,2,0:T(8,128)S(1)}, u32[]{:S(2)}) copy-start(f32[16,128,128]{1,2,0:T(8,128)S(1)} %get-tuple-element.27) | copy-start | bytes 3145732
  90.9 49.5 %copy-start = (f32[3,16,128,128]{3,2,1,0:T(8,128)}, f32[3,16,128,128]{3,2,1,0:T(8,128)S(1)}, u32[]{:S(2)}) copy-start(f32[3,16,128,128]{3,2,1,0:T(8,128)S(1)} %fusion.8) | copy-start | bytes 9437188
  91.1 49.3 %collective-permute-start.6 = (f32[16,128,128]{2,1,0:T(8,128)S(1)}, f32[16,128,128]{2,1,0:T(8,128)S(1)}, u32[]{:S(2)}, u32[]{:S(2)}) collective-permute-start(f32[16,128,128]{2,1,0:T(8,128)S(1)} %add_select_fusion), channel_id=1, source_target_pairs={{4,0},{5,1},{6,2},{7,3},{12,8},{13,9},{14,10},{15,11},{20,16},{21,... | collective-permute-start | bytes 3145736 | tf_op jit(solution)/shard_map/ppermute | solution.py:22
  140.4 4.0 %copy-start.7 = (f32[16,128,128]{2,1,0:T(8,128)}, f32[16,128,128]{2,1,0:T(8,128)S(1)}, u32[]{:S(2)}) copy-start(f32[16,128,128]{2,1,0:T(8,128)S(1)} %collective-permute-done.6) | copy-start | bytes 3145732
  144.4 23.4 %collective-permute-start.7 = (f32[16,128,128]{2,1,0:T(8,128)}, f32[16,128,128]{2,1,0:T(8,128)}, u32[]{:S(2)}, u32[]{:S(2)}) collective-permute-start(f32[16,128,128]{2,1,0:T(8,128)} %get-tuple-element.47), channel_id=1, source_target_pairs={{0,2},{2,0},{1,3},{3,1},{4,6},{6,4},{5,7},{7,5},{8,10},{10,8},{9,1... | collective-permute-start | bytes 3145736 | tf_op jit(solution)/shard_map/ppermute | solution.py:16
  147.0 39.2 %collective-permute-start.9 = (f32[16]{0:T(128)}, f32[16]{0:T(128)}, u32[]{:S(2)}, u32[]{:S(2)}) collective-permute-start(f32[16]{0:T(128)} %get-tuple-element.42), channel_id=1, source_target_pairs={{4,0},{5,1},{6,2},{7,3},{12,8},{13,9},{14,10},{15,11},{20,16},{21,... | collective-permute-start | bytes 200 | tf_op jit(solution)/shard_map/ppermute | solution.py:22
  152.2 23.4 %copy-start.2 = (f32[128,128,16]{1,2,0:T(8,128)S(1)}, f32[128,128,16]{1,2,0:T(8,128)}, u32[]{:S(2)}) copy-start(f32[128,128,16]{1,2,0:T(8,128)} %copy-done.1) | copy-start | bytes 3145732
  152.2 23.4 %copy-start.9 = (f32[16,128,128]{1,2,0:T(8,128)S(1)}, f32[16,128,128]{1,2,0:T(8,128)}, u32[]{:S(2)}) copy-start(f32[16,128,128]{1,2,0:T(8,128)} %copy-done.8) | copy-start | bytes 3145732
  170.5 7.5 %copy-start.11 = (f32[1,16,128,128]{3,2,1,0:T(8,128)S(1)}, f32[1,16,128,128]{3,2,1,0:T(8,128)}, u32[]{:S(2)}) copy-start(f32[1,16,128,128]{3,2,1,0:T(8,128)} %get-tuple-element.49) | copy-start | bytes 3145732
  170.5 7.5 %copy-start.13 = (f32[16,128,128]{1,2,0:T(8,128)S(1)}, f32[16,128,128]{1,2,0:T(8,128)}, u32[]{:S(2)}) copy-start(f32[16,128,128]{1,2,0:T(8,128)} %convert_multiply_fusion.3) | copy-start | bytes 3145732
  170.5 7.5 %copy-start.15 = (f32[1,16,128,128]{3,2,1,0:T(8,128)S(1)}, f32[1,16,128,128]{3,2,1,0:T(8,128)}, u32[]{:S(2)}) copy-start(f32[1,16,128,128]{3,2,1,0:T(8,128)} %copy-done.14) | copy-start | bytes 3145732
  170.5 7.4 %copy-start.17 = (f32[1,16,128,128]{3,2,1,0:T(8,128)S(1)}, f32[1,16,128,128]{3,2,1,0:T(8,128)}, u32[]{:S(2)}) copy-start(f32[1,16,128,128]{3,2,1,0:T(8,128)} %copy-done.16) | copy-start | bytes 3145732
  170.5 7.4 %copy-start.18 = (f32[16,128,128]{1,2,0:T(8,128)S(1)}, f32[16,128,128]{1,2,0:T(8,128)}, u32[]{:S(2)}) copy-start(f32[16,128,128]{1,2,0:T(8,128)} %fusion.38) | copy-start | bytes 3145732
  173.1 17.5 %collective-permute-start.8 = (f32[16,128,128]{2,1,0:T(8,128)}, f32[16,128,128]{2,1,0:T(8,128)}, u32[]{:S(2)}, u32[]{:S(2)}) collective-permute-start(f32[16,128,128]{2,1,0:T(8,128)} %fusion.11), channel_id=1, source_target_pairs={{0,1},{1,0},{2,3},{3,2},{4,5},{5,4},{6,7},{7,6},{8,9},{9,8},{10,11... | collective-permute-start | bytes 3145736 | tf_op jit(solution)/shard_map/ppermute | solution.py:16
  178.0 8.3 %copy-start.21 = (f32[16]{0:T(128)S(1)}, f32[16]{0:T(128)}, u32[]{:S(2)}) copy-start(f32[16]{0:T(128)} %get-tuple-element.32) | copy-start | bytes 196
  178.0 8.3 %copy-start.22 = (f32[16]{0:T(128)S(1)}, f32[16]{0:T(128)}, u32[]{:S(2)}) copy-start(f32[16]{0:T(128)} %get-tuple-element.35) | copy-start | bytes 196
  178.0 11.3 %copy-start.20 = (f32[16]{0:T(128)S(1)}, f32[16]{0:T(128)}, u32[]{:S(2)}) copy-start(f32[16]{0:T(128)} %copy-done.19) | copy-start | bytes 196
  178.0 11.3 %copy-start.23 = (f32[16]{0:T(128)S(1)}, f32[16]{0:T(128)}, u32[]{:S(2)}) copy-start(f32[16]{0:T(128)} %get-tuple-element.24) | copy-start | bytes 196
  178.0 11.3 %copy-start.24 = (f32[16]{0:T(128)S(1)}, f32[16]{0:T(128)}, u32[]{:S(2)}) copy-start(f32[16]{0:T(128)} %get-tuple-element.36) | copy-start | bytes 196
  186.9 2.4 %collective-permute-start.10 = (f32[16]{0:T(128)S(1)}, f32[16]{0:T(128)S(1)}, u32[]{:S(2)}, u32[]{:S(2)}) collective-permute-start(f32[16]{0:T(128)S(1)} %get-tuple-element.40), channel_id=1, source_target_pairs={{0,2},{2,0},{1,3},{3,1},{4,6},{6,4},{5,7},{7,5},{8,10},{10,8},{9,1... | collective-permute-start | bytes 200 | tf_op jit(solution)/shard_map/ppermute | solution.py:16
  189.3 4.9 %collective-permute-start.11 = (f32[16]{0:T(128)S(1)}, f32[16]{0:T(128)S(1)}, u32[]{:S(2)}, u32[]{:S(2)}) collective-permute-start(f32[16]{0:T(128)S(1)} %get-tuple-element.37), channel_id=1, source_target_pairs={{0,1},{1,0},{2,3},{3,2},{4,5},{5,4},{6,7},{7,6},{8,9},{9,8},{10,11... | collective-permute-start | bytes 200 | tf_op jit(solution)/shard_map/ppermute | solution.py:16
where the time goes:
time: 207 us
  waiting for transfers between devices  122 us (59%)
  matrix products  34.2 us (17%)
  other arithmetic  22.2 us (11%)
  local copies, waits for them, and re-layouts  14.6 us (7%)
  starting transfers between devices  12.2 us (6%)
    ppermute x10, waiting for transfers between devices, from_partner(): return lax.ppermute(block, axis, route)  80.2 us
    ppermute x2, waiting for transfers between devices, passed_along(): lax.ppermute(value, axis, [(source, source + steps) for source in range(f...  42.1 us
    unnamed x58, local copies, waits for them, and re-layouts  11.9 us
    dot_general x3, matrix products, block_output(): jnp.einsum('jhik,jhkv->hiv', reach, buckets, precision=TOP_ACCURACY)  9.99 us
    dot_general x3, matrix products, block_front(): jnp.einsum('ybu,ybe->yue', scaled_result, value_rows_head, precision=TOP_...  9.9 us
    ppermute x10, starting transfers between devices, from_partner(): return lax.ppermute(block, axis, route)  9.21 us
    dot_general x3, matrix products, block_output(): jnp.einsum('hij,hjv->hiv', scores * weighting * fading, value_rows_head,...  5.54 us
    dot_general x3, matrix products, block_output(): jnp.einsum('hik,hjk->hij', queries_h, keys_h, precision=TOP_ACCURACY)  5.47 us
  transfers between devices with their start and end apart: 12, of which 6 were waited for; matrix products, arithmetic and copies ran while one was open for 20% of the time, Pallas kernels for 0%

commit v1 on v0

--- a/solution.py
+++ b/solution.py
@@ -1,6 +1,10 @@
+import functools
+
 import jax
 import jax.numpy as jnp
 from jax import lax
+from jax.experimental import pallas as pl
+from jax.experimental.pallas import tpu as pltpu
 from jax.sharding import PartitionSpec as P
 
 TOP_ACCURACY = lax.Precision.HIGHEST
@@ -189,6 +193,606 @@
     )
 
 
+F32 = jnp.float32
+BF16 = jnp.bfloat16
+CHUNKS = 2
+NT = (((1,), (1,)), ((), ()))
+TN = (((0,), (0,)), ((), ()))
+NN = (((1,), (0,)), ((), ()))
+NEVER = -1e30
+
+
+def mxu(left, right, dims):
+    return lax.dot_general(left, right, dims, preferred_element_type=F32)
+
+
+def halves(value):
+    high = value.astype(BF16)
+    low = (value - high.astype(F32)).astype(BF16)
+    return high, low
+
+
+def split_rows(value):
+    return jnp.concatenate(halves(value), axis=0)
+
+
+def split_lanes(value):
+    return jnp.concatenate(halves(value), axis=1)
+
+
+def twice_rows(value):
+    return jnp.concatenate([value, value], axis=0)
+
+
+def twice_lanes(value):
+    return jnp.concatenate([value, value], axis=1)
+
+
+def running_decay(decay):
+    tok = decay.shape[1]
+    earlier = lax.broadcasted_iota(jnp.int32, (tok, tok), 0)
+    later = lax.broadcasted_iota(jnp.int32, (tok, tok), 1)
+    upto = (earlier <= later).astype(F32)
+    return jnp.dot(decay, upto, precision=TOP_ACCURACY, preferred_element_type=F32)
+
+
+def last_lane(running):
+    return jnp.broadcast_to(running[:, running.shape[1] - 1 :], running.shape)
+
+
+def columns(rows):
+    count, tok = rows.shape
+    if count < tok:
+        rows = jnp.concatenate([rows, jnp.zeros((tok - count, tok), rows.dtype)], axis=0)
+    return rows.T
+
+
+def half_first(rows, core):
+    half = rows.shape[0] // 2
+    swapped = jnp.concatenate([rows[half:], rows[:half]], axis=0)
+    return jnp.where(core == 0, rows, swapped)
+
+
+def lane_block(ref, head, width):
+    return ref[:, pl.ds(pl.multiple_of(head * width, width), width)]
+
+
+def row_sums(value):
+    ones = jnp.ones((8, 2 * value.shape[1]), BF16)
+    return mxu(ones, split_lanes(value), NT)[:1]
+
+
+def export_kernel(
+    place, query, key, value, cotangent, gain, decay, send1, send2, level0, keep1, keep2
+):
+    position = place[0]
+    core = position % 2
+    chip = position // 2
+    heads, tok = decay.shape
+    dim = query.shape[1] // heads
+    half = heads // 2
+    first_cross = gain.shape[0] - 3
+    running = running_decay(decay[...])
+    total = last_lane(running)
+    lift = jnp.exp(running)
+    fall = jnp.exp(total - running)
+    state1 = chip % 2 == 0
+    state2 = chip == 1
+    state0 = core == 0
+    gain1 = gain[first_cross + 1]
+    gain2 = gain[first_cross + 2]
+    weight1 = jnp.where(state1, fall, jnp.where(chip == 1, gain1, gain2) * lift)
+    weight2 = jnp.where(state2, fall, jnp.where(chip == 2, gain2, gain1) * lift)
+    weight2 = jnp.where(chip == 0, 0.0, weight2)
+    weight0 = jnp.where(state0, fall, gain[first_cross] * lift)
+    spread = columns(
+        jnp.concatenate([half_first(w, core) for w in (weight1, weight2, weight0)], axis=0)
+    )
+    for place_in in range(heads):
+        mine = place_in < half
+        index = place_in % half
+        head = (core if mine else 1 - core) * half + index
+        q, k, v, o = (lane_block(ref, head, dim) for ref in (query, key, value, cotangent))
+
+        def outer(is_state, column):
+            left = jnp.where(is_state, k, q).astype(F32) * spread[:, column : column + 1]
+            right = jnp.where(is_state, v, o)
+            return mxu(split_rows(left), twice_rows(right), TN)
+
+        rows = pl.ds(index * dim, dim)
+        (keep1 if mine else send1)[rows, :] = outer(state1, place_in)
+        (keep2 if mine else send2)[rows, :] = outer(state2, heads + place_in)
+        level0[pl.ds(pl.multiple_of(head * dim, dim), dim), :] = outer(
+            state0, 2 * heads + place_in
+        )
+    send1[pl.ds(half * dim, heads), :] = total
+
+
+def pair_factors(position, own_total, other_total, is_state):
+    even = position % 2 == 0
+    scale_own = is_state == even
+    return (
+        jnp.where(scale_own, jnp.exp(other_total), 1.0),
+        jnp.where(scale_own, 1.0, jnp.exp(own_total)),
+    )
+
+
+def per_head(rows, dim):
+    count, lanes = rows.shape
+    return jnp.broadcast_to(rows[:, None, :], (count, dim, lanes)).reshape(count * dim, lanes)
+
+
+def first_merge_kernel(place, decay, keep, got, *outs):
+    position = place[0]
+    chip = position // 2
+    heads, tok = decay.shape
+    half = heads // 2
+    dim = keep.shape[0] // half
+    own_total = last_lane(running_decay(decay[...]))
+    other_total = got[pl.ds(half * dim, heads), :]
+    own_factor, other_factor = pair_factors(position, own_total, other_total, chip % 2 == 0)
+    own_factor = half_first(own_factor, position % 2)[:half]
+    other_factor = half_first(other_factor, position % 2)[:half]
+    count = half // len(outs)
+    for part, out in enumerate(outs):
+        for index in range(count):
+            head = part * count + index
+            rows = pl.ds(head * dim, dim)
+            out[pl.ds(index * dim, dim), :] = (
+                own_factor[head : head + 1] * keep[rows, :]
+                + other_factor[head : head + 1] * got[rows, :]
+            )
+    outs[0][pl.ds(count * dim, heads), :] = own_total + other_total
+
+
+def second_merge_kernel(part, place, decay, other_total, keep, got, first, out):
+    position = place[0]
+    chip = position // 2
+    heads, tok = decay.shape
+    half = heads // 2
+    count = half // CHUNKS
+    dim = out.shape[0] // count
+    own_total = last_lane(running_decay(decay[...]))
+    other_total = other_total[...]
+    own_factor, other_factor = pair_factors(position, own_total, other_total, chip == 1)
+    inner = (chip == 1) | (chip == 2)
+    first_factor = jnp.where(inner, jnp.exp(own_total + other_total), 0.0)
+    own_factor, other_factor, first_factor = (
+        half_first(factor, position % 2)[part * count : (part + 1) * count]
+        for factor in (own_factor, other_factor, first_factor)
+    )
+    for index in range(count):
+        rows = pl.ds(index * dim, dim)
+        out[rows, :] = (
+            own_factor[index : index + 1] * keep[rows, :]
+            + other_factor[index : index + 1] * got[rows, :]
+            + first_factor[index : index + 1] * first[rows, :]
+        )
+
+
+def apply_state(left, right, state, weight):
+    high, low = halves(state)
+    first = mxu(twice_lanes(left), jnp.concatenate([high, low], axis=0), NN)
+    second = mxu(twice_lanes(right), jnp.concatenate([high, low], axis=1), NT)
+    sums = row_sums(first * right.astype(F32))
+    return weight * first, weight * second, sums
+
+
+def local_kernel(
+    place,
+    query,
+    key,
+    value,
+    cotangent,
+    gain,
+    decay,
+    level0,
+    acc_out,
+    acc_query,
+    acc_key,
+    acc_value,
+    gain_rows,
+    decay_rows,
+    flow_rows,
+):
+    position = place[0]
+    upper = position % 2 == 1
+    group = pl.program_id(0)
+    heads, tok = decay.shape
+    width = query.shape[1]
+    per_group = heads // pl.num_programs(0)
+    dim = width // per_group
+    inner_levels = tok.bit_length()
+    running = running_decay(decay[...])
+    total = last_lane(running)
+    lift = jnp.exp(running)
+    fall = jnp.exp(total - running)
+    weight0 = jnp.where(upper, gain[inner_levels] * lift, fall)
+    spread = columns(jnp.concatenate([running, weight0], axis=0))
+    source = lax.broadcasted_iota(jnp.int32, (tok, tok), 0)
+    target = lax.broadcasted_iota(jnp.int32, (tok, tok), 1)
+    mixing = jnp.bitwise_xor(source, target)
+    level = jnp.zeros((tok, tok), jnp.int32)
+    for power in range(inner_levels - 1):
+        level = level + (mixing >= 2**power).astype(jnp.int32)
+    level = jnp.where(source <= target, level, -1)
+    causal = source <= target
+    ones = jnp.ones((8, 2 * tok), BF16)
+
+    def one_group(start):
+        for index in range(per_group):
+            head = start + index
+            lanes = slice(index * dim, (index + 1) * dim)
+            q, k, v, o = (ref[:, lanes] for ref in (query, key, value, cotangent))
+            scores = mxu(k, q, NT)
+            pulls = mxu(v, o, NT)
+            row = running[head : head + 1]
+            fading = jnp.exp(jnp.where(causal, row - spread[:, head : head + 1], NEVER))
+            weighting = jnp.zeros((tok, tok), F32)
+            for place_in in range(inner_levels):
+                weighting = jnp.where(
+                    level == place_in, gain[place_in, head : head + 1, :], weighting
+                )
+            weighting = weighting * fading
+            mixing_part = scores * weighting
+            score_grad = pulls * weighting
+            product = scores * pulls * fading
+            flow = jnp.zeros((1, tok), F32)
+            for place_in in range(inner_levels):
+                found = jnp.sum(
+                    jnp.where(level == place_in, product, 0.0), axis=0, keepdims=True
+                )
+                gain_rows[place_in, head : head + 1, :] = found
+                if place_in > 0:
+                    flow = flow + gain[place_in, head : head + 1, :] * found
+            left = jnp.where(level > 0, mixing_part * pulls, 0.0)
+            leaving = mxu(ones, split_lanes(left), NT)[:1]
+            high, low = halves(mixing_part)
+            out = mxu(jnp.concatenate([high, low], axis=0), twice_rows(v), TN)
+            d_value = mxu(jnp.concatenate([high, low], axis=1), twice_rows(o), NN)
+            high, low = halves(score_grad)
+            d_query = mxu(jnp.concatenate([high, low], axis=0), twice_rows(k), TN)
+            d_key = mxu(jnp.concatenate([high, low], axis=1), twice_rows(q), NN)
+            state = level0[pl.ds(index * dim, dim), :]
+            column = spread[:, heads + head : heads + head + 1]
+            first, second, sums = apply_state(
+                jnp.where(upper, q, k), jnp.where(upper, o, v), state, column
+            )
+            acc_out[:, lanes] = out + jnp.where(upper, first, 0.0)
+            acc_query[:, lanes] = d_query + jnp.where(upper, second, 0.0)
+            acc_key[:, lanes] = d_key + jnp.where(upper, 0.0, second)
+            acc_value[:, lanes] = d_value + jnp.where(upper, 0.0, first)
+            weighted = weight0[head : head + 1] * sums
+            gain_rows[inner_levels, head : head + 1, :] = jnp.where(
+                upper, lift[head : head + 1] * sums, 0.0
+            )
+            decay_rows[head : head + 1, :] = flow - leaving + jnp.where(upper, weighted, -weighted)
+            flow_rows[head : head + 1, :] = jnp.where(upper, 0.0, weighted)
+
+    for number in range(heads // per_group):
+        pl.when(group == number)(lambda start=number * per_group: one_group(start))
+
+
+def final_kernel(
+    part,
+    place,
+    query,
+    key,
+    value,
+    cotangent,
+    gain,
+    decay,
+    other_total,
+    chip_total,
+    first_mine,
+    first_other,
+    second_mine,
+    second_other,
+    third_mine,
+    third_other,
+    pair1_mine,
+    pair1_other,
+    pair2_mine,
+    pair2_other,
+    level0,
+    part_out,
+    part_query,
+    part_key,
+    part_value,
+    *rest,
+):
+    out_mixed, out_query, out_key, out_value, rows_out = rest[-5:]
+    position = place[0]
+    core = position % 2
+    chip = position // 2
+    group = pl.program_id(0)
+    heads, tok = decay.shape
+    half = heads // 2
+    count = half // CHUNKS
+    dim = query.shape[1] // count
+    cross = gain.shape[0] - 3
+    running = running_decay(decay[...])
+    total = last_lane(running)
+    other = other_total[...]
+    odd = core == 1
+    forward1 = chip != 0
+    forward2 = chip == 3
+    outer_chip = (chip == 0) | (chip == 3)
+    offset1 = jnp.where(forward1 == odd, other, 0.0)
+    offset2 = jnp.where(forward2 == odd, other, 0.0)
+    offset2 = offset2 + jnp.where(outer_chip, chip_total[...], 0.0)
+    chip_offset2 = jnp.where(outer_chip, chip_total[...], 0.0)
+    gain1 = jnp.where(chip == 2, gain[cross + 2], gain[cross + 1])
+    gain2 = gain[cross + 2]
+    lift1 = jnp.exp(running + offset1)
+    lift2 = jnp.exp(running + offset2)
+    weight1 = jnp.where(forward1, gain1 * lift1, jnp.exp(total - running + offset1))
+    weight2 = jnp.where(forward2, gain2 * lift2, jnp.exp(total - running + offset2))
+    pair_flow1 = jnp.where(forward1 != odd, jnp.exp(total), 0.0)
+    pair_flow2 = jnp.where(forward2 != odd, jnp.exp(total + chip_offset2), 0.0)
+    chip_flow = jnp.where((chip == 1) | (chip == 2), jnp.exp(total + other), 0.0)
+    picked = []
+    for rows in (lift1, lift2, weight1, weight2, pair_flow1, pair_flow2, chip_flow):
+        low = part * count
+        picked.append(
+            jnp.where(group == 0, rows[low : low + count], rows[half + low : half + low + count])
+        )
+    lift1, lift2, weight1, weight2, pair_flow1, pair_flow2, chip_flow = picked
+    spread = columns(jnp.concatenate([weight1, weight2], axis=0))
+    mine = group == core
+    for index in range(count):
+        lanes = slice(index * dim, (index + 1) * dim)
+        rows = pl.ds(index * dim, dim)
+        one = slice(index, index + 1)
+        q, k, v, o = (ref[:, lanes] for ref in (query, key, value, cotangent))
+        first = jnp.where(mine, first_mine[rows, :], first_other[rows, :])
+        second = jnp.where(mine, second_mine[rows, :], second_other[rows, :])
+        third = jnp.where(mine, third_mine[rows, :], third_other[rows, :])
+        pair1 = jnp.where(mine, pair1_mine[rows, :], pair1_other[rows, :])
+        pair2 = jnp.where(mine, pair2_mine[rows, :], pair2_other[rows, :])
+        front = level0[rows, :]
+        state1 = jnp.where(chip == 2, second, first)
+        state2 = jnp.where(chip == 1, second, third)
+        part1 = jnp.where(odd, front, jnp.where(chip == 1, pair1, pair2))
+        part2 = jnp.where(odd, front, pair1)
+        mixed = part_out[:, lanes]
+        d_query = part_query[:, lanes]
+        d_key = part_key[:, lanes]
+        d_value = part_value[:, lanes]
+        decay_row = jnp.zeros((1, tok), F32)
+        flow_row = (
+            pair_flow1[one] * jnp.sum(state1 * part1, axis=0, keepdims=True)
+            + pair_flow2[one] * jnp.sum(state2 * part2, axis=0, keepdims=True)
+            + chip_flow[one] * jnp.sum(first * second, axis=0, keepdims=True)
+        )
+        uses = (
+            (forward1, state1, weight1, lift1, 0),
+            (forward2, state2, weight2, lift2, count),
+        )
+        for number, (forward, state, weight, lift, column) in enumerate(uses):
+            column = column + index
+            left, right, sums = apply_state(
+                jnp.where(forward, q, k),
+                jnp.where(forward, o, v),
+                state,
+                spread[:, column : column + 1],
+            )
+            mixed = mixed + jnp.where(forward, left, 0.0)
+            d_query = d_query + jnp.where(forward, right, 0.0)
+            d_key = d_key + jnp.where(forward, 0.0, right)
+            d_value = d_value + jnp.where(forward, 0.0, left)
+            weighted = weight[one] * sums
+            decay_row = decay_row + jnp.where(forward, weighted, -weighted)
+            flow_row = flow_row + jnp.where(forward, 0.0, weighted)
+            rows_out[number * count + index : number * count + index + 1, :] = lift[one] * sums
+        rows_out[2 * count + index : 2 * count + index + 1, :] = decay_row
+        rows_out[3 * count + index : 3 * count + index + 1, :] = flow_row
+        out_mixed[:, lanes] = mixed.astype(BF16)
+        out_query[:, lanes] = d_query.astype(BF16)
+        out_key[:, lanes] = d_key.astype(BF16)
+        out_value[:, lanes] = d_value.astype(BF16)
+
+
+def gather_kernel(place, gain_rows, decay_rows, flow_rows, *rest):
+    parts, (grad_gain, grad_decay) = rest[:-2], rest[-2:]
+    position = place[0]
+    chip = position // 2
+    levels, heads, tok = grad_gain.shape
+    half = heads // 2
+    count = half // len(parts)
+
+    def natural(kind):
+        rows = []
+        for group in range(2):
+            for ref in parts:
+                start = group * 4 * count + kind * count
+                rows.append(ref[start : start + count, :])
+        return jnp.concatenate(rows, axis=0)
+
+    for place_in in range(levels - 2):
+        grad_gain[place_in] = gain_rows[place_in]
+    first, second = natural(0), natural(1)
+    grad_gain[levels - 2] = jnp.where(chip % 2 == 1, first, 0.0)
+    grad_gain[levels - 1] = jnp.where(chip == 2, first, jnp.where(chip == 3, second, 0.0))
+    own = decay_rows[...] + natural(2)
+    later = flow_rows[...] + natural(3)
+    upper = lax.broadcasted_iota(jnp.int32, (tok, tok), 0)
+    lower = lax.broadcasted_iota(jnp.int32, (tok, tok), 1)
+    after = (upper >= lower).astype(F32)
+    every = jnp.ones((tok, tok), F32)
+    grad_decay[...] = jnp.dot(
+        own, after, precision=TOP_ACCURACY, preferred_element_type=F32
+    ) + jnp.dot(later, every, precision=TOP_ACCURACY, preferred_element_type=F32)
+
+
+def sds(*shape, dtype=F32):
+    return jax.ShapeDtypeStruct(shape, dtype)
+
+
+def params():
+    return pltpu.CompilerParams(vmem_limit_bytes=48 * 1024 * 1024)
+
+
+SCALAR = pl.BlockSpec(memory_space=pltpu.SMEM)
+
+
+def whole(shape):
+    return pl.BlockSpec(shape, lambda g: (0,) * len(shape))
+
+
+def line_device(queries, keys_in, value_input, level_gain, decay_log, out_grad):
+    heads, tok = decay_log.shape
+    dim = queries.shape[1] // heads
+    half = heads // 2
+    count = half // CHUNKS
+    part_rows = count * dim
+    half_rows = half * dim
+    place = lax.axis_index("ctx").astype(jnp.int32).reshape(1)
+    tokens = (queries, keys_in, value_input, out_grad)
+    core_swap = [(at, at ^ 1) for at in range(8)]
+    side_swap = [(at, at ^ 2) for at in range(8)]
+    middle_swap = [(2, 4), (4, 2), (3, 5), (5, 3), (6, 6), (7, 7)]
+
+    def swap(block, route):
+        return lax.ppermute(block, "ctx", route)
+
+    send1, send2, level0, keep1, keep2 = pl.pallas_call(
+        export_kernel,
+        out_shape=(
+            sds(half_rows + heads, dim),
+            sds(half_rows, dim),
+            sds(2 * half_rows, dim),
+            sds(half_rows, dim),
+            sds(half_rows, dim),
+        ),
+        in_specs=[SCALAR] + [pl.BlockSpec()] * 6,
+        compiler_params=params(),
+        name="exports",
+    )(place, *tokens, level_gain, decay_log)
+    got1 = swap(send1, core_swap)
+    got2 = swap(send2, core_swap)
+    front = swap(level0, core_swap)
+    got_keep1 = swap(keep1, core_swap)
+    got_keep2 = swap(keep2, core_swap)
+    first_sent = pl.pallas_call(
+        first_merge_kernel,
+        out_shape=tuple(
+            sds(part_rows + (heads if part == 0 else 0), dim) for part in range(CHUNKS)
+        ),
+        in_specs=[SCALAR] + [pl.BlockSpec()] * 3,
+        compiler_params=params(),
+        name="first_merge",
+    )(place, decay_log, keep1, got1)
+    first = [swap(block, side_swap) for block in first_sent]
+
+    groups = 4
+    wide = pl.BlockSpec((tok, heads // groups * dim), lambda g: (0, g))
+    acc_out, acc_query, acc_key, acc_value, gain_rows, decay_rows, flow_rows = pl.pallas_call(
+        local_kernel,
+        grid=(groups,),
+        out_shape=(sds(tok, heads * dim),) * 4
+        + (sds(tok.bit_length() + 1, heads, tok), sds(heads, tok), sds(heads, tok)),
+        in_specs=[SCALAR]
+        + [wide] * 4
+        + [
+            whole(level_gain.shape),
+            whole(decay_log.shape),
+            pl.BlockSpec((heads // groups * dim, dim), lambda g: (g, 0)),
+        ],
+        out_specs=(wide,) * 4
+        + (whole((tok.bit_length() + 1, heads, tok)), whole((heads, tok)), whole((heads, tok))),
+        compiler_params=params(),
+        name="local",
+    )(place, *tokens, level_gain, decay_log, front)
+
+    second = []
+    for part in range(CHUNKS):
+        chunk = pl.BlockSpec((part_rows, dim), lambda g, part=part: (part, 0))
+        sent = pl.pallas_call(
+            functools.partial(second_merge_kernel, part),
+            grid=(1,),
+            out_shape=sds(part_rows, dim),
+            in_specs=[
+                SCALAR,
+                whole(decay_log.shape),
+                pl.BlockSpec((heads, dim), lambda g: (half_rows // heads, 0)),
+                chunk,
+                chunk,
+                pl.BlockSpec((part_rows, dim), lambda g: (0, 0)),
+            ],
+            out_specs=pl.BlockSpec((part_rows, dim), lambda g: (0, 0)),
+            compiler_params=params(),
+            name="second_merge",
+        )(place, decay_log, got1, keep2, got2, first[part])
+        second.append(swap(sent, middle_swap))
+    third = [swap(block, side_swap) for block in second]
+    first_over = [swap(block, core_swap) for block in first]
+    second_over = [swap(block, core_swap) for block in second]
+    third_over = [swap(block, core_swap) for block in third]
+
+    results = ()
+    rows = []
+    for part in range(CHUNKS):
+        lanes = pl.BlockSpec((tok, part_rows), lambda g, part=part: (0, g * CHUNKS + part))
+        own = pl.BlockSpec((part_rows, dim), lambda g: (0, 0))
+        chunk = pl.BlockSpec((part_rows, dim), lambda g, part=part: (part, 0))
+        before = len(results)
+        *results, found = pl.pallas_call(
+            functools.partial(final_kernel, part),
+            grid=(2,),
+            out_shape=(sds(tok, heads * dim, dtype=BF16),) * 4 + (sds(8 * count, tok),),
+            in_specs=[SCALAR]
+            + [lanes] * 4
+            + [
+                whole(level_gain.shape),
+                whole(decay_log.shape),
+                pl.BlockSpec((heads, dim), lambda g: (half_rows // heads, 0)),
+                pl.BlockSpec((heads, dim), lambda g: (part_rows // heads, 0)),
+            ]
+            + [own] * 6
+            + [chunk] * 4
+            + [pl.BlockSpec((part_rows, dim), lambda g, part=part: (g * CHUNKS + part, 0))]
+            + [lanes] * 4
+            + [pl.BlockSpec(memory_space=pl.ANY)] * before,
+            out_specs=(lanes,) * 4 + (pl.BlockSpec((4 * count, tok), lambda g: (g, 0)),),
+            input_output_aliases={24 + at: at for at in range(before)},
+            compiler_params=params(),
+            name="final",
+        )(
+            place,
+            *tokens,
+            level_gain,
+            decay_log,
+            got1,
+            first[0],
+            first[part],
+            first_over[part],
+            second[part],
+            second_over[part],
+            third[part],
+            third_over[part],
+            got1,
+            got_keep1,
+            got2,
+            got_keep2,
+            front,
+            acc_out,
+            acc_query,
+            acc_key,
+            acc_value,
+            *results,
+        )
+        rows.append(found)
+    grad_gain, grad_decay = pl.pallas_call(
+        gather_kernel,
+        out_shape=(sds(*level_gain.shape), sds(heads, tok)),
+        in_specs=[SCALAR] + [pl.BlockSpec()] * (3 + CHUNKS),
+        compiler_params=params(),
+        name="gather",
+    )(place, gain_rows, decay_rows, flow_rows, *rows)
+    return (*results, grad_gain, grad_decay)
+
+
 def solution(mesh):
     placed = (
         P(("seq", "ctx"), None),
@@ -199,7 +803,7 @@
         P(("seq", "ctx"), None),
     )
     return jax.shard_map(
-        per_device,
+        line_device if mesh.shape["ctx"] == 8 else per_device,
         mesh=mesh,
         in_specs=placed,
         out_specs=(

time: 207 us -> 70.5 us (0.34)
  waiting for transfers between devices: 122 us -> 15.6 us
  matrix products: 34.2 us -> 0 us
  Pallas kernels: 0 us -> 25.2 us
  other arithmetic: 22.2 us -> 0 us
  starting transfers between devices: 12.2 us -> 19.7 us
  local copies, waits for them, and re-layouts: 14.6 us -> 8.78 us
    ppermute x12 -> x17, waiting for transfers between devices: 122 us -> 15.6 us  [swap(): return lax.ppermute(block, 'ctx', route)]
    dot_general x14 -> x0, matrix products: 34.2 us -> none  [the longest x3 9.99 us: block_output(): jnp.einsum('jhik,jhkv->hiv', reach, buckets, precision=TOP_ACCURACY)]
    pallas_call x0 -> x8, Pallas kernels: none -> 25.2 us  [the longest x1 9.77 us: line_device(): pl.pallas_call(local_kernel, grid=(groups,), out_shape=(sds(tok, heads *...]
    reduce_sum x5 -> x0, other arithmetic: 8.59 us -> none  [the longest x1 4.04 us: own_grads(): jnp.sum(g_bucket * other_state, axis=(1, 2))]
    ppermute x12 -> x17, starting transfers between devices: 12.2 us -> 19.7 us  [swap(): return lax.ppermute(block, 'ctx', route)]
    another operation x5 -> x0, other arithmetic: 6.17 us -> none  [the longest x2 2.71 us: per_device(): buckets = jnp.stack(found)]
    select_n x4 -> x0, other arithmetic: 3.25 us -> none  [the longest x2 2.73 us: partner_grads(): jnp.where(is_upper, factor[:, None, None] * g_state + jnp.exp(offset)[:,...]
    unnamed x58 -> x30, local copies, waits for them, and re-layouts: 11.9 us -> 8.78 us
  transfers between devices with their start and end apart: 12 -> 17, of which waited for: 6 -> 5; matrix products, arithmetic and copies ran while one was open for 20% -> 0% of each run, Pallas kernels for 0% -> 22%
where the time goes in v1:
time: 70.5 us; the launch traced here: 70.1 us
  Pallas kernels  25.2 us (36%)
  starting transfers between devices  19.7 us (28%)
  waiting for transfers between devices  15.6 us (22%)
  local copies, waits for them, and re-layouts  8.78 us (12%)
  between operations  0.8 us (1%)
    ppermute x17, starting transfers between devices, swap(): return lax.ppermute(block, 'ctx', route)  19.7 us
    ppermute x17, waiting for transfers between devices, swap(): return lax.ppermute(block, 'ctx', route)  15.6 us
    pallas_call x1, Pallas kernels, line_device(): pl.pallas_call(local_kernel, grid=(groups,), out_shape=(sds(tok, heads *...  9.77 us
    pallas_call x2, Pallas kernels, line_device(): pl.pallas_call(functools.partial(final_kernel, part), grid=(2,), out_shap...  9.44 us
    unnamed x30, local copies, waits for them, and re-layouts  8.78 us
    pallas_call x1, Pallas kernels, line_device(): pl.pallas_call(export_kernel, out_shape=(sds(half_rows + heads, dim), sds...  4.33 us
  transfers between devices with their start and end apart: 17, of which 5 were waited for; matrix products, arithmetic and copies ran while one was open for 0% of the time, Pallas kernels for 22%

profile of v1, /device:TPU:1, one launch (start us, length us, event | category | flops | bytes accessed | tf_op | source)
XLA Modules:
  0.0 70.1 jit_solution(2022275974651711049)
XLA Ops:
  0.6 0.0 copy-start
  0.6 1.0 %copy-done = bf16[128,2048]{1,0:T(8,128)(2,1)S(1)} copy-done((bf16[128,2048]{1,0:T(8,128)(2,1)S(1)}, bf16[128,2048]{1,0:T(8,128)(2,1)}, u32[]{:S(2)}) %copy-start) | copy-done | bytes 524312
  1.7 0.0 copy-start.2
  1.7 1.0 %copy-done.2 = bf16[128,2048]{1,0:T(8,128)(2,1)S(1)} copy-done((bf16[128,2048]{1,0:T(8,128)(2,1)S(1)}, bf16[128,2048]{1,0:T(8,128)(2,1)}, u32[]{:S(2)}) %copy-start.2) | copy-done | bytes 524312
  2.7 0.0 copy-start.4
  2.7 1.0 %copy-done.4 = bf16[128,2048]{1,0:T(8,128)(2,1)S(1)} copy-done((bf16[128,2048]{1,0:T(8,128)(2,1)S(1)}, bf16[128,2048]{1,0:T(8,128)(2,1)}, u32[]{:S(2)}) %copy-start.4) | copy-done | bytes 524312
  3.8 1.0 %copy-done.6 = bf16[128,2048]{1,0:T(8,128)(2,1)S(1)} copy-done((bf16[128,2048]{1,0:T(8,128)(2,1)S(1)}, bf16[128,2048]{1,0:T(8,128)(2,1)}, u32[]{:S(2)}) %copy-start.6) | copy-done | bytes 524312
  4.8 0.9 %copy-done.11 = f32[11,16,128]{2,1,0:T(8,128)S(1)} copy-done((f32[11,16,128]{2,1,0:T(8,128)S(1)}, f32[11,16,128]{2,1,0:T(8,128)}, u32[]{:S(2)}) %copy-start.11) | copy-done | bytes 90136
  5.7 0.7 copy-done.13
  6.4 4.3 %exports.1 = (f32[1040,128]{1,0:T(8,128)S(1)}, f32[1024,128]{1,0:T(8,128)S(1)}, f32[2048,128]{1,0:T(8,128)S(1)}, f32[1024,128]{1,0:T(8,128)S(1)}, f32[1024,128]{1,0:T(8,128)S(1)}) custom-call(s32[1]{0:T(128)} %bitcast.place, bf16[128,2048]{1,0:T(8,128)(2,1)S(1)} %copy-done, bf16[128,2048]{1,0:T(8,128)(2,1)S(1)} %copy-done.2, ...), custom_call_target="tpu_custom_call" | custom-call | tf_op jit(solution)/shard_map/exports/pallas_call | solution.py:659
  10.7 0.1 collective-permute-start
  10.9 0.5 collective-permute-start.4
  11.3 0.1 collective-permute-start.11
  11.4 1.3 %collective-permute-done.got.other_total.pair1_mine = f32[1040,128]{1,0:T(8,128)S(1)} collective-permute-done((f32[1040,128]{1,0:T(8,128)S(1)}, f32[1040,128]{1,0:T(8,128)S(1)}, u32[]{:S(2)}, u32[]{:S(2)}) %collective-permute-start) | collective-permute-done | bytes 532512 | tf_op jit(solution)/shard_map/ppermute | solution.py:657
  12.7 0.3 first_merge.1
  13.0 2.5 %collective-permute-start.1 = (f32[528,128]{1,0:T(8,128)S(1)}, f32[528,128]{1,0:T(8,128)S(1)}, u32[]{:S(2)}, u32[]{:S(2)}) collective-permute-start(f32[528,128]{1,0:T(8,128)S(1)} %get-tuple-element.34), channel_id=1, source_target_pairs={{0,2},{1,3},{2,0},{3,1},{4,6},{5,7},{6,4},{7,5},{8,10},{9,11},{10,... | collective-permute-start | bytes 811016 | tf_op jit(solution)/shard_map/ppermute | solution.py:657
  15.5 0.7 collective-permute-start.9
  16.2 0.0 collective-permute-start.2
  16.2 0.0 collective-permute-done.4.got.pair2_mine
  16.2 0.2 collective-permute-start.10
  16.4 5.7 %collective-permute-done.1.first.chip_total.first_mine = f32[528,128]{1,0:T(8,128)S(1)} collective-permute-done((f32[528,128]{1,0:T(8,128)S(1)}, f32[528,128]{1,0:T(8,128)S(1)}, u32[]{:S(2)}, u32[]{:S(2)}) %collective-permute-start.1) | collective-permute-done | bytes 270368 | tf_op jit(solution)/shard_map/ppermute | solution.py:657
  22.1 0.3 second_merge.3
  22.4 0.0 copy-start.1
  22.4 0.0 copy-start.3
  22.4 0.0 copy-start.5
  22.4 0.0 copy-start.7
  22.4 0.8 %collective-permute-start.13 = (f32[512,128]{1,0:T(8,128)S(1)}, f32[512,128]{1,0:T(8,128)S(1)}, u32[]{:S(2)}, u32[]{:S(2)}) collective-permute-start(f32[512,128]{1,0:T(8,128)S(1)} %second_merge.3), channel_id=1, source_target_pairs={{2,4},{4,2},{3,5},{5,3},{6,6},{7,7},{10,12},{12,10},{11,13},{13,11... | collective-permute-start | bytes 786440 | tf_op jit(solution)/shard_map/ppermute | solution.py:657
  23.2 4.5 %collective-permute-done.2.first.first_mine = f32[512,128]{1,0:T(8,128)S(1)} collective-permute-done((f32[512,128]{1,0:T(8,128)S(1)}, f32[512,128]{1,0:T(8,128)S(1)}, u32[]{:S(2)}, u32[]{:S(2)}) %collective-permute-start.2) | collective-permute-done | bytes 262176 | tf_op jit(solution)/shard_map/ppermute | solution.py:657
  27.7 0.3 second_merge.2
  28.0 0.9 %collective-permute-start.5 = (f32[512,128]{1,0:T(8,128)S(1)}, f32[512,128]{1,0:T(8,128)S(1)}, u32[]{:S(2)}, u32[]{:S(2)}) collective-permute-start(f32[512,128]{1,0:T(8,128)S(1)} %second_merge.2), channel_id=1, source_target_pairs={{2,4},{4,2},{3,5},{5,3},{6,6},{7,7},{10,12},{12,10},{11,13},{13,11... | collective-permute-start | bytes 786440 | tf_op jit(solution)/shard_map/ppermute | solution.py:657
  28.9 0.0 collective-permute-done.9.pair1_other
  28.9 0.9 %collective-permute-start.12 = (f32[528,128]{1,0:T(8,128)S(1)}, f32[528,128]{1,0:T(8,128)S(1)}, u32[]{:S(2)}, u32[]{:S(2)}) collective-permute-start(f32[528,128]{1,0:T(8,128)S(1)} %collective-permute-done.1.first.chip_total.first_mine), channel_id=1, source_target_pairs={{0,1},{1,0},{2,3},{3,2},{4,5},{5,4},{6,7},{7,6},{8,9},{9,8},{10,11... | collective-permute-start | bytes 811016 | tf_op jit(solution)/shard_map/ppermute | solution.py:657
  29.8 0.0 collective-permute-done.13.second_mine
  29.8 4.3 %collective-permute-start.15 = (f32[512,128]{1,0:T(8,128)S(1)}, f32[512,128]{1,0:T(8,128)S(1)}, u32[]{:S(2)}, u32[]{:S(2)}) collective-permute-start(f32[512,128]{1,0:T(8,128)S(1)} %collective-permute-done.13.second_mine), channel_id=1, source_target_pairs={{0,2},{1,3},{2,0},{3,1},{4,6},{5,7},{6,4},{7,5},{8,10},{9,11},{10,... | collective-permute-start | bytes 786440 | tf_op jit(solution)/shard_map/ppermute | solution.py:657
  34.1 0.0 collective-permute-done.5.second_mine
  34.1 3.9 %collective-permute-start.7 = (f32[512,128]{1,0:T(8,128)S(1)}, f32[512,128]{1,0:T(8,128)S(1)}, u32[]{:S(2)}, u32[]{:S(2)}) collective-permute-start(f32[512,128]{1,0:T(8,128)S(1)} %collective-permute-done.5.second_mine), channel_id=1, source_target_pairs={{0,2},{1,3},{2,0},{3,1},{4,6},{5,7},{6,4},{7,5},{8,10},{9,11},{10,... | collective-permute-start | bytes 786440 | tf_op jit(solution)/shard_map/ppermute | solution.py:657
  38.0 0.0 collective-permute-done.10.pair2_other
  38.0 2.2 %collective-permute-start.14 = (f32[512,128]{1,0:T(8,128)S(1)}, f32[512,128]{1,0:T(8,128)S(1)}, u32[]{:S(2)}, u32[]{:S(2)}) collective-permute-start(f32[512,128]{1,0:T(8,128)S(1)} %collective-permute-done.13.second_mine), channel_id=1, source_target_pairs={{0,1},{1,0},{2,3},{3,2},{4,5},{5,4},{6,7},{7,6},{8,9},{9,8},{10,11... | collective-permute-start | bytes 786440 | tf_op jit(solution)/shard_map/ppermute | solution.py:657
  40.2 0.3 collective-permute-done.15.third_mine
  40.5 1.3 %collective-permute-start.16 = (f32[512,128]{1,0:T(8,128)S(1)}, f32[512,128]{1,0:T(8,128)S(1)}, u32[]{:S(2)}, u32[]{:S(2)}) collective-permute-start(f32[512,128]{1,0:T(8,128)S(1)} %collective-permute-done.15.third_mine), channel_id=1, source_target_pairs={{0,1},{1,0},{2,3},{3,2},{4,5},{5,4},{6,7},{7,6},{8,9},{9,8},{10,11... | collective-permute-start | bytes 786440 | tf_op jit(solution)/shard_map/ppermute | solution.py:657
  41.8 0.0 collective-permute-done.11.level0
  41.8 0.1 collective-permute-start.3
  41.9 0.0 collective-permute-done.12.first_other
  41.9 0.4 collective-permute-start.6
  42.3 3.8 %collective-permute-done.7.third_mine = f32[512,128]{1,0:T(8,128)S(1)} collective-permute-done((f32[512,128]{1,0:T(8,128)S(1)}, f32[512,128]{1,0:T(8,128)S(1)}, u32[]{:S(2)}, u32[]{:S(2)}) %collective-permute-start.7) | collective-permute-done | bytes 262176 | tf_op jit(solution)/shard_map/ppermute | solution.py:657
  46.1 0.8 %collective-permute-start.8 = (f32[512,128]{1,0:T(8,128)S(1)}, f32[512,128]{1,0:T(8,128)S(1)}, u32[]{:S(2)}, u32[]{:S(2)}) collective-permute-start(f32[512,128]{1,0:T(8,128)S(1)} %collective-permute-done.7.third_mine), channel_id=1, source_target_pairs={{0,1},{1,0},{2,3},{3,2},{4,5},{5,4},{6,7},{7,6},{8,9},{9,8},{10,11... | collective-permute-start | bytes 786440 | tf_op jit(solution)/shard_map/ppermute | solution.py:657
  47.0 0.0 copy-done.14
  47.0 0.0 copy-done.12
  47.0 0.0 copy-done.1
  47.0 0.0 copy-done.3
  47.0 0.0 copy-done.5
  47.0 0.0 copy-done.7
  47.0 9.8 %local.1 = (f32[128,2048]{1,0:T(8,128)S(1)}, f32[128,2048]{1,0:T(8,128)S(1)}, f32[128,2048]{1,0:T(8,128)S(1)}, f32[128,2048]{1,0:T(8,128)}, f32[9,16,128]{2,1,0:...) custom-call(s32[1]{0:T(128)} %bitcast.place, bf16[128,2048]{1,0:T(8,128)(2,1)S(1)} %copy-done.1, ...), custom_call_target="tpu_custom_call" | custom-call | tf_op jit(solution)/shard_map/local/pallas_call | solution.py:690
  56.8 1.0 %copy-done.8 = f32[128,2048]{1,0:T(8,128)} copy-done((f32[128,2048]{1,0:T(8,128)}, f32[128,2048]{1,0:T(8,128)S(1)}, u32[]{:S(2)}) %copy-start.8) | copy-done | bytes 1048600
  57.8 1.0 %copy-done.9 = f32[128,2048]{1,0:T(8,128)} copy-done((f32[128,2048]{1,0:T(8,128)}, f32[128,2048]{1,0:T(8,128)S(1)}, u32[]{:S(2)}) %copy-start.9) | copy-done | bytes 1048600
  58.8 1.0 %copy-done.10 = f32[128,2048]{1,0:T(8,128)} copy-done((f32[128,2048]{1,0:T(8,128)}, f32[128,2048]{1,0:T(8,128)S(1)}, u32[]{:S(2)}) %copy-start.10) | copy-done | bytes 1048600
  59.8 0.0 collective-permute-done.14.second_other
  59.8 0.0 collective-permute-done.16.third_other
  59.8 4.7 %final.2 = (bf16[128,2048]{1,0:T(8,128)(2,1)}, bf16[128,2048]{1,0:T(8,128)(2,1)}, bf16[128,2048]{1,0:T(8,128)(2,1)}, bf16[128,2048]{1,0:T(8,128)(2,1)}, f32[32,128]{1,0:T(8,128)S(1)}) custom-call(s32[1]{0:T(128)} %bitcast.place, bf16[128,2048]{1,0:T(8,128)(2,1)S(1)} %copy-done.1, bf16[128,2048]{1,0:T(8,128)(2,1)S(1)} %copy-done.3, ...), custom_call_target="tpu_custom_call" | custom-call | tf_op jit(solution)/shard_map/final/pallas_call | solution.py:740
  64.5 0.0 collective-permute-done.3.first_other
  64.5 0.0 collective-permute-done.6.second_other
  64.5 0.0 collective-permute-done.8.third_other
  64.5 4.7 %final.3 = (bf16[128,2048]{1,0:T(8,128)(2,1)}, bf16[128,2048]{1,0:T(8,128)(2,1)}, bf16[128,2048]{1,0:T(8,128)(2,1)}, bf16[128,2048]{1,0:T(8,128)(2,1)}, f32[32,128]{1,0:T(8,128)S(1)}) custom-call(s32[1]{0:T(128)} %bitcast.place, bf16[128,2048]{1,0:T(8,128)(2,1)S(1)} %copy-done.1, ...), custom_call_target="tpu_custom_call", output_to_operand_aliasing={{0}: (24, {}), {1}: (25, {}), {2}: (26, {}), {3}: (27, {})} | custom-call | tf_op jit(solution)/shard_map/final/pallas_call | solution.py:740
  69.3 0.8 %gather.1 = (f32[11,16,128]{2,1,0:T(8,128)}, f32[16,128]{1,0:T(8,128)}) custom-call(s32[1]{0:T(128)} %bitcast.place, f32[9,16,128]{2,1,0:T(8,128)S(1)} %get-tuple-element.51.gain_rows, f32[16,128]{1,0:T(8,128)S(1)} %get-tuple-element.52.decay_rows, f32[16,128]{1,0:T(8,128)S(1)} %get-tuple-element.53.flow_rows, f32[32,128]{1,0:T(8,128)S(1)} %get-tuple-element.54.rest_0_, ...), custom_call_target="tpu_custom_call" | custom-call | tf_op jit(solution)/shard_map/gather/pallas_call | solution.py:786
  (8 shorter events, 0.0 us)
Async XLA Ops:
  0.6 1.0 %copy-start = (bf16[128,2048]{1,0:T(8,128)(2,1)S(1)}, bf16[128,2048]{1,0:T(8,128)(2,1)}, u32[]{:S(2)}) copy-start(bf16[128,2048]{1,0:T(8,128)(2,1)} %query.7) | copy-start | bytes 1572868
  1.7 1.0 %copy-start.2 = (bf16[128,2048]{1,0:T(8,128)(2,1)S(1)}, bf16[128,2048]{1,0:T(8,128)(2,1)}, u32[]{:S(2)}) copy-start(bf16[128,2048]{1,0:T(8,128)(2,1)} %key.7) | copy-start | bytes 1572868
  2.7 1.0 %copy-start.4 = (bf16[128,2048]{1,0:T(8,128)(2,1)S(1)}, bf16[128,2048]{1,0:T(8,128)(2,1)}, u32[]{:S(2)}) copy-start(bf16[128,2048]{1,0:T(8,128)(2,1)} %value.7) | copy-start | bytes 1572868
  3.8 1.0 %copy-start.6 = (bf16[128,2048]{1,0:T(8,128)(2,1)S(1)}, bf16[128,2048]{1,0:T(8,128)(2,1)}, u32[]{:S(2)}) copy-start(bf16[128,2048]{1,0:T(8,128)(2,1)} %cotangent.7) | copy-start | bytes 1572868
  4.8 0.9 %copy-start.11 = (f32[11,16,128]{2,1,0:T(8,128)S(1)}, f32[11,16,128]{2,1,0:T(8,128)}, u32[]{:S(2)}) copy-start(f32[11,16,128]{2,1,0:T(8,128)} %gain.7) | copy-start | bytes 270340
  5.7 0.7 copy-start.13
  10.7 2.0 %collective-permute-start = (f32[1040,128]{1,0:T(8,128)S(1)}, f32[1040,128]{1,0:T(8,128)S(1)}, u32[]{:S(2)}, u32[]{:S(2)}) collective-permute-start(f32[1040,128]{1,0:T(8,128)S(1)} %get-tuple-element.32), channel_id=1, source_target_pairs={{0,1},{1,0},{2,3},{3,2},{4,5},{5,4},{6,7},{7,6},{8,9},{9,8},{10,11... | collective-permute-start | bytes 1597448 | tf_op jit(solution)/shard_map/ppermute | solution.py:657
  10.9 5.3 %collective-permute-start.4 = (f32[1024,128]{1,0:T(8,128)S(1)}, f32[1024,128]{1,0:T(8,128)S(1)}, u32[]{:S(2)}, u32[]{:S(2)}) collective-permute-start(f32[1024,128]{1,0:T(8,128)S(1)} %get-tuple-element.37), channel_id=1, source_target_pairs={{0,1},{1,0},{2,3},{3,2},{4,5},{5,4},{6,7},{7,6},{8,9},{9,8},{10,11... | collective-permute-start | bytes 1572872 | tf_op jit(solution)/shard_map/ppermute | solution.py:657
  11.3 30.5 %collective-permute-start.11 = (f32[2048,128]{1,0:T(8,128)S(1)}, f32[2048,128]{1,0:T(8,128)S(1)}, u32[]{:S(2)}, u32[]{:S(2)}) collective-permute-start(f32[2048,128]{1,0:T(8,128)S(1)} %get-tuple-element.38), channel_id=1, source_target_pairs={{0,1},{1,0},{2,3},{3,2},{4,5},{5,4},{6,7},{7,6},{8,9},{9,8},{10,11... | collective-permute-start | bytes 3145736 | tf_op jit(solution)/shard_map/ppermute | solution.py:657
  13.0 9.0 %collective-permute-start.1 = (f32[528,128]{1,0:T(8,128)S(1)}, f32[528,128]{1,0:T(8,128)S(1)}, u32[]{:S(2)}, u32[]{:S(2)}) collective-permute-start(f32[528,128]{1,0:T(8,128)S(1)} %get-tuple-element.34), channel_id=1, source_target_pairs={{0,2},{1,3},{2,0},{3,1},{4,6},{5,7},{6,4},{7,5},{8,10},{9,11},{10,... | collective-permute-start | bytes 811016 | tf_op jit(solution)/shard_map/ppermute | solution.py:657
  15.5 13.3 %collective-permute-start.9 = (f32[1024,128]{1,0:T(8,128)S(1)}, f32[1024,128]{1,0:T(8,128)S(1)}, u32[]{:S(2)}, u32[]{:S(2)}) collective-permute-start(f32[1024,128]{1,0:T(8,128)S(1)} %get-tuple-element.33.keep), channel_id=1, source_target_pairs={{0,1},{1,0},{2,3},{3,2},{4,5},{5,4},{6,7},{7,6},{8,9},{9,8},{10,11... | collective-permute-start | bytes 1572872 | tf_op jit(solution)/shard_map/ppermute | solution.py:657
  16.2 11.5 %collective-permute-start.2 = (f32[512,128]{1,0:T(8,128)S(1)}, f32[512,128]{1,0:T(8,128)S(1)}, u32[]{:S(2)}, u32[]{:S(2)}) collective-permute-start(f32[512,128]{1,0:T(8,128)S(1)} %get-tuple-element.35), channel_id=1, source_target_pairs={{0,2},{1,3},{2,0},{3,1},{4,6},{5,7},{6,4},{7,5},{8,10},{9,11},{10,... | collective-permute-start | bytes 786440 | tf_op jit(solution)/shard_map/ppermute | solution.py:657
  16.2 21.8 %collective-permute-start.10 = (f32[1024,128]{1,0:T(8,128)S(1)}, f32[1024,128]{1,0:T(8,128)S(1)}, u32[]{:S(2)}, u32[]{:S(2)}) collective-permute-start(f32[1024,128]{1,0:T(8,128)S(1)} %get-tuple-element.36.keep), channel_id=1, source_target_pairs={{0,1},{1,0},{2,3},{3,2},{4,5},{5,4},{6,7},{7,6},{8,9},{9,8},{10,11... | collective-permute-start | bytes 1572872 | tf_op jit(solution)/shard_map/ppermute | solution.py:657
  22.1 24.9 %copy-start.12 = (f32[11,16,128]{2,1,0:T(8,128)S(1)}, f32[11,16,128]{2,1,0:T(8,128)}, u32[]{:S(2)}) copy-start(f32[11,16,128]{2,1,0:T(8,128)} %gain.7) | copy-start | bytes 270340
  22.4 24.6 %copy-start.1 = (bf16[128,2048]{1,0:T(8,128)(2,1)S(1)}, bf16[128,2048]{1,0:T(8,128)(2,1)}, u32[]{:S(2)}) copy-start(bf16[128,2048]{1,0:T(8,128)(2,1)} %query.7) | copy-start | bytes 1572868
  22.4 24.6 %copy-start.3 = (bf16[128,2048]{1,0:T(8,128)(2,1)S(1)}, bf16[128,2048]{1,0:T(8,128)(2,1)}, u32[]{:S(2)}) copy-start(bf16[128,2048]{1,0:T(8,128)(2,1)} %key.7) | copy-start | bytes 1572868
  22.4 24.6 %copy-start.5 = (bf16[128,2048]{1,0:T(8,128)(2,1)S(1)}, bf16[128,2048]{1,0:T(8,128)(2,1)}, u32[]{:S(2)}) copy-start(bf16[128,2048]{1,0:T(8,128)(2,1)} %value.7) | copy-start | bytes 1572868
  22.4 24.6 %copy-start.7 = (bf16[128,2048]{1,0:T(8,128)(2,1)S(1)}, bf16[128,2048]{1,0:T(8,128)(2,1)}, u32[]{:S(2)}) copy-start(bf16[128,2048]{1,0:T(8,128)(2,1)} %cotangent.7) | copy-start | bytes 1572868
  22.4 7.4 %collective-permute-start.13 = (f32[512,128]{1,0:T(8,128)S(1)}, f32[512,128]{1,0:T(8,128)S(1)}, u32[]{:S(2)}, u32[]{:S(2)}) collective-permute-start(f32[512,128]{1,0:T(8,128)S(1)} %second_merge.3), channel_id=1, source_target_pairs={{2,4},{4,2},{3,5},{5,3},{6,6},{7,7},{10,12},{12,10},{11,13},{13,11... | collective-permute-start | bytes 786440 | tf_op jit(solution)/shard_map/ppermute | solution.py:657
  28.0 6.1 %collective-permute-start.5 = (f32[512,128]{1,0:T(8,128)S(1)}, f32[512,128]{1,0:T(8,128)S(1)}, u32[]{:S(2)}, u32[]{:S(2)}) collective-permute-start(f32[512,128]{1,0:T(8,128)S(1)} %second_merge.2), channel_id=1, source_target_pairs={{2,4},{4,2},{3,5},{5,3},{6,6},{7,7},{10,12},{12,10},{11,13},{13,11... | collective-permute-start | bytes 786440 | tf_op jit(solution)/shard_map/ppermute | solution.py:657
  28.9 13.0 %collective-permute-start.12 = (f32[528,128]{1,0:T(8,128)S(1)}, f32[528,128]{1,0:T(8,128)S(1)}, u32[]{:S(2)}, u32[]{:S(2)}) collective-permute-start(f32[528,128]{1,0:T(8,128)S(1)} %collective-permute-done.1.first.chip_total.first_mine), channel_id=1, source_target_pairs={{0,1},{1,0},{2,3},{3,2},{4,5},{5,4},{6,7},{7,6},{8,9},{9,8},{10,11... | collective-permute-start | bytes 811016 | tf_op jit(solution)/shard_map/ppermute | solution.py:657
  29.8 10.7 %collective-permute-start.15 = (f32[512,128]{1,0:T(8,128)S(1)}, f32[512,128]{1,0:T(8,128)S(1)}, u32[]{:S(2)}, u32[]{:S(2)}) collective-permute-start(f32[512,128]{1,0:T(8,128)S(1)} %collective-permute-done.13.second_mine), channel_id=1, source_target_pairs={{0,2},{1,3},{2,0},{3,1},{4,6},{5,7},{6,4},{7,5},{8,10},{9,11},{10,... | collective-permute-start | bytes 786440 | tf_op jit(solution)/shard_map/ppermute | solution.py:657
  34.1 12.0 %collective-permute-start.7 = (f32[512,128]{1,0:T(8,128)S(1)}, f32[512,128]{1,0:T(8,128)S(1)}, u32[]{:S(2)}, u32[]{:S(2)}) collective-permute-start(f32[512,128]{1,0:T(8,128)S(1)} %collective-permute-done.5.second_mine), channel_id=1, source_target_pairs={{0,2},{1,3},{2,0},{3,1},{4,6},{5,7},{6,4},{7,5},{8,10},{9,11},{10,... | collective-permute-start | bytes 786440 | tf_op jit(solution)/shard_map/ppermute | solution.py:657
  38.0 21.8 %collective-permute-start.14 = (f32[512,128]{1,0:T(8,128)S(1)}, f32[512,128]{1,0:T(8,128)S(1)}, u32[]{:S(2)}, u32[]{:S(2)}) collective-permute-start(f32[512,128]{1,0:T(8,128)S(1)} %collective-permute-done.13.second_mine), channel_id=1, source_target_pairs={{0,1},{1,0},{2,3},{3,2},{4,5},{5,4},{6,7},{7,6},{8,9},{9,8},{10,11... | collective-permute-start | bytes 786440 | tf_op jit(solution)/shard_map/ppermute | solution.py:657
  40.5 19.3 %collective-permute-start.16 = (f32[512,128]{1,0:T(8,128)S(1)}, f32[512,128]{1,0:T(8,128)S(1)}, u32[]{:S(2)}, u32[]{:S(2)}) collective-permute-start(f32[512,128]{1,0:T(8,128)S(1)} %collective-permute-done.15.third_mine), channel_id=1, source_target_pairs={{0,1},{1,0},{2,3},{3,2},{4,5},{5,4},{6,7},{7,6},{8,9},{9,8},{10,11... | collective-permute-start | bytes 786440 | tf_op jit(solution)/shard_map/ppermute | solution.py:657
  41.8 5.2 %copy-start.14 = (f32[2048,128]{1,0:T(8,128)}, f32[2048,128]{1,0:T(8,128)S(1)}, u32[]{:S(2)}) copy-start(f32[2048,128]{1,0:T(8,128)S(1)} %collective-permute-done.11.level0) | copy-start | bytes 3145732
  41.8 22.7 %collective-permute-start.3 = (f32[512,128]{1,0:T(8,128)S(1)}, f32[512,128]{1,0:T(8,128)S(1)}, u32[]{:S(2)}, u32[]{:S(2)}) collective-permute-start(f32[512,128]{1,0:T(8,128)S(1)} %collective-permute-done.2.first.first_mine), channel_id=1, source_target_pairs={{0,1},{1,0},{2,3},{3,2},{4,5},{5,4},{6,7},{7,6},{8,9},{9,8},{10,11... | collective-permute-start | bytes 786440 | tf_op jit(solution)/shard_map/ppermute | solution.py:657
  41.9 22.6 %collective-permute-start.6 = (f32[512,128]{1,0:T(8,128)S(1)}, f32[512,128]{1,0:T(8,128)S(1)}, u32[]{:S(2)}, u32[]{:S(2)}) collective-permute-start(f32[512,128]{1,0:T(8,128)S(1)} %collective-permute-done.5.second_mine), channel_id=1, source_target_pairs={{0,1},{1,0},{2,3},{3,2},{4,5},{5,4},{6,7},{7,6},{8,9},{9,8},{10,11... | collective-permute-start | bytes 786440 | tf_op jit(solution)/shard_map/ppermute | solution.py:657
  46.1 18.4 %collective-permute-start.8 = (f32[512,128]{1,0:T(8,128)S(1)}, f32[512,128]{1,0:T(8,128)S(1)}, u32[]{:S(2)}, u32[]{:S(2)}) collective-permute-start(f32[512,128]{1,0:T(8,128)S(1)} %collective-permute-done.7.third_mine), channel_id=1, source_target_pairs={{0,1},{1,0},{2,3},{3,2},{4,5},{5,4},{6,7},{7,6},{8,9},{9,8},{10,11... | collective-permute-start | bytes 786440 | tf_op jit(solution)/shard_map/ppermute | solution.py:657
  56.8 1.0 %copy-start.8 = (f32[128,2048]{1,0:T(8,128)}, f32[128,2048]{1,0:T(8,128)S(1)}, u32[]{:S(2)}) copy-start(f32[128,2048]{1,0:T(8,128)S(1)} %get-tuple-element.39.part_out) | copy-start | bytes 3145732
  57.8 1.0 %copy-start.9 = (f32[128,2048]{1,0:T(8,128)}, f32[128,2048]{1,0:T(8,128)S(1)}, u32[]{:S(2)}) copy-start(f32[128,2048]{1,0:T(8,128)S(1)} %get-tuple-element.40.part_query) | copy-start | bytes 3145732
  58.8 1.0 %copy-start.10 = (f32[128,2048]{1,0:T(8,128)}, f32[128,2048]{1,0:T(8,128)S(1)}, u32[]{:S(2)}) copy-start(f32[128,2048]{1,0:T(8,128)S(1)} %get-tuple-element.41.part_key) | copy-start | bytes 3145732

commit v2 on v0

--- a/solution.py
+++ b/solution.py
@@ -1,6 +1,10 @@
+import functools
+
 import jax
 import jax.numpy as jnp
 from jax import lax
+from jax.experimental import pallas as pl
+from jax.experimental.pallas import tpu as pltpu
 from jax.sharding import PartitionSpec as P
 
 TOP_ACCURACY = lax.Precision.HIGHEST
@@ -189,6 +193,825 @@
     )
 
 
+F32 = jnp.float32
+BF16 = jnp.bfloat16
+CHUNKS = 2
+NT = (((1,), (1,)), ((), ()))
+TN = (((0,), (0,)), ((), ()))
+NN = (((1,), (0,)), ((), ()))
+NEVER = -1e30
+
+
+def mxu(left, right, dims):
+    return lax.dot_general(left, right, dims, preferred_element_type=F32)
+
+
+def halves(value):
+    high = value.astype(BF16)
+    low = (value - high.astype(F32)).astype(BF16)
+    return high, low
+
+
+def split_rows(value):
+    return jnp.concatenate(halves(value), axis=0)
+
+
+def split_lanes(value):
+    return jnp.concatenate(halves(value), axis=1)
+
+
+def twice_rows(value):
+    return jnp.concatenate([value, value], axis=0)
+
+
+def twice_lanes(value):
+    return jnp.concatenate([value, value], axis=1)
+
+
+def running_decay(decay):
+    tok = decay.shape[1]
+    earlier = lax.broadcasted_iota(jnp.int32, (tok, tok), 0)
+    later = lax.broadcasted_iota(jnp.int32, (tok, tok), 1)
+    upto = (earlier <= later).astype(F32)
+    return jnp.dot(decay, upto, precision=TOP_ACCURACY, preferred_element_type=F32)
+
+
+def last_lane(running):
+    return jnp.broadcast_to(running[:, running.shape[1] - 1 :], running.shape)
+
+
+def columns(rows):
+    count, tok = rows.shape
+    if count < tok:
+        rows = jnp.concatenate([rows, jnp.zeros((tok - count, tok), rows.dtype)], axis=0)
+    return rows.T
+
+
+def half_first(rows, core):
+    half = rows.shape[0] // 2
+    swapped = jnp.concatenate([rows[half:], rows[:half]], axis=0)
+    return jnp.where(core == 0, rows, swapped)
+
+
+def lane_block(ref, head, width):
+    return ref[:, pl.ds(pl.multiple_of(head * width, width), width)]
+
+
+def take_half(rows, core, part, count):
+    half = rows.shape[0] // 2
+    low = part * count
+    return jnp.where(core == 0, rows[low : low + count], rows[half + low : half + low + count])
+
+
+def outer_products(left, right, weight_column):
+    turned = left.T
+    return mxu(twice_lanes(turned), split_rows(right.astype(F32) * weight_column), NN)
+
+
+def first_export_kernel(
+    place, query, key, value, cotangent, gain, decay, send, keep, lefts, rights, gains, decays, sems
+):
+    position = place[0]
+    core = position % 2
+    chip = position // 2
+    heads, tok = decay.shape
+    width = query.shape[1]
+    dim = width // heads
+    half = heads // 2
+    cross = gain.shape[0] - 3
+    wide = half * dim
+    state = chip % 2 == 0
+    copies = []
+    for side in range(2):
+        lanes = pl.ds(pl.multiple_of((1 - core if side == 0 else core) * wide, wide), wide)
+        for slot, (chosen, plain, into) in enumerate(((key, query, lefts), (value, cotangent, rights))):
+            sem = sems.at[2 * side + slot]
+            target = into.at[:, pl.ds(side * wide, wide)]
+
+            @pl.when(state)
+            def _(chosen=chosen, target=target, sem=sem, lanes=lanes):
+                pltpu.make_async_copy(chosen.at[:, lanes], target, sem).start()
+
+            @pl.when(jnp.logical_not(state))
+            def _(plain=plain, target=target, sem=sem, lanes=lanes):
+                pltpu.make_async_copy(plain.at[:, lanes], target, sem).start()
+
+            copies.append(pltpu.make_async_copy(plain.at[:, lanes], target, sem))
+    small = [
+        pltpu.make_async_copy(decay, decays, sems.at[4]),
+        pltpu.make_async_copy(gain.at[pl.ds(cross + 1, 2)], gains, sems.at[5]),
+    ]
+    for copy in small:
+        copy.start()
+    for copy in small:
+        copy.wait()
+    running = running_decay(decays[...])
+    total = last_lane(running)
+    lift = jnp.exp(running)
+    weight = jnp.where(
+        state, jnp.exp(total - running), jnp.where(chip == 1, gains[0], gains[1]) * lift
+    )
+    spread = columns(half_first(weight, 1 - core))
+    send[pl.ds(half * dim, heads), :] = total
+    for index in range(heads):
+        if index % half == 0:
+            for copy in copies[2 * (index // half) : 2 * (index // half) + 2]:
+                copy.wait()
+        lanes = slice(index * dim, (index + 1) * dim)
+        rows = pl.ds(index % half * dim, dim)
+        (send if index < half else keep)[rows, :] = outer_products(
+            lefts[:, lanes], rights[:, lanes], spread[:, index : index + 1]
+        )
+
+
+def second_export_kernel(
+    place, query, key, value, cotangent, gain, decay, keep1, send, keep, bundle
+):
+    position = place[0]
+    core = position % 2
+    chip = position // 2
+    heads, tok = decay.shape
+    dim = query.shape[1] // heads
+    half = heads // 2
+    cross = gain.shape[0] - 3
+    running = running_decay(decay[...])
+    lift = jnp.exp(running)
+    fall = jnp.exp(last_lane(running) - running)
+    state2 = chip == 1
+    state0 = core == 0
+    weight2 = jnp.where(state2, fall, jnp.where(chip == 2, gain[cross + 2], gain[cross + 1]) * lift)
+    weight2 = jnp.where(chip == 0, 0.0, weight2)
+    weight0 = jnp.where(state0, fall, gain[cross] * lift)
+    spread = columns(
+        jnp.concatenate([half_first(w, 1 - core) for w in (weight2, weight0)], axis=0)
+    )
+    bundle[pl.ds(heads * dim, half * dim), :] = keep1[...]
+    for index in range(heads):
+        mine = index >= half
+        head = (core if mine else 1 - core) * half + index % half
+        q, k, v, o = (lane_block(ref, head, dim) for ref in (query, key, value, cotangent))
+        second = outer_products(
+            jnp.where(state2, k, q), jnp.where(state2, v, o), spread[:, index : index + 1]
+        )
+        rows = pl.ds(index % half * dim, dim)
+        (keep if mine else send)[rows, :] = second
+        if mine:
+            bundle[pl.ds((heads + index) * dim, dim), :] = second
+        bundle[pl.ds(pl.multiple_of(head * dim, dim), dim), :] = outer_products(
+            jnp.where(state0, k, q),
+            jnp.where(state0, v, o),
+            spread[:, heads + index : heads + index + 1],
+        )
+
+
+def pair_factors(position, own_total, other_total, is_state):
+    even = position % 2 == 0
+    scale_own = is_state == even
+    return (
+        jnp.where(scale_own, jnp.exp(other_total), 1.0),
+        jnp.where(scale_own, 1.0, jnp.exp(own_total)),
+    )
+
+
+def first_merge_kernel(place, decay, keep, got, after, *outs):
+    position = place[0]
+    chip = position // 2
+    heads, tok = decay.shape
+    half = heads // 2
+    dim = keep.shape[0] // half
+    own_total = last_lane(running_decay(decay[...]))
+    other_total = got[pl.ds(half * dim, heads), :]
+    own_factor, other_factor = pair_factors(position, own_total, other_total, chip % 2 == 0)
+    own_factor = half_first(own_factor, position % 2)[:half]
+    other_factor = half_first(other_factor, position % 2)[:half]
+    count = half // len(outs)
+    for part, out in enumerate(outs):
+        for index in range(count):
+            head = part * count + index
+            rows = pl.ds(head * dim, dim)
+            out[pl.ds(index * dim, dim), :] = (
+                own_factor[head : head + 1] * keep[rows, :]
+                + other_factor[head : head + 1] * got[rows, :]
+            )
+    outs[0][pl.ds(count * dim, heads), :] = own_total + other_total
+
+
+def second_merge_kernel(part, place, decay, other_total, keep, got, first, after, out):
+    position = place[0]
+    chip = position // 2
+    heads, tok = decay.shape
+    half = heads // 2
+    count = half // CHUNKS
+    dim = out.shape[0] // count
+    own_total = last_lane(running_decay(decay[...]))
+    other_total = other_total[...]
+    own_factor, other_factor = pair_factors(position, own_total, other_total, chip == 1)
+    inner = (chip == 1) | (chip == 2)
+    first_factor = jnp.where(inner, jnp.exp(own_total + other_total), 0.0)
+    own_factor, other_factor, first_factor = (
+        half_first(factor, position % 2)[part * count : (part + 1) * count]
+        for factor in (own_factor, other_factor, first_factor)
+    )
+    for index in range(count):
+        rows = pl.ds(index * dim, dim)
+        out[rows, :] = (
+            own_factor[index : index + 1] * keep[rows, :]
+            + other_factor[index : index + 1] * got[rows, :]
+            + first_factor[index : index + 1] * first[rows, :]
+        )
+
+
+def lane_sums(value):
+    ones = jnp.ones((2 * value.shape[1], value.shape[1]), BF16)
+    return mxu(split_lanes(value), ones, NN)
+
+
+def apply_state(left, right, state, weight):
+    high, low = halves(state)
+    first = mxu(twice_lanes(left), jnp.concatenate([high, low], axis=0), NN)
+    second = mxu(twice_lanes(right), jnp.concatenate([high, low], axis=1), NT)
+    sums = lane_sums(first * right.astype(F32))
+    return weight * first, weight * second, sums
+
+
+def local_kernel(start, query, key, value, cotangent, gain, decay, *rest):
+    acc_out, acc_query, acc_key, acc_value, gain_rows, decay_rows = rest[-6:]
+    tok = decay.shape[1]
+    count = decay_rows.shape[0]
+    dim = query.shape[1] // count
+    inner_levels = tok.bit_length()
+    running = running_decay(decay[...])
+    spread = columns(running)
+    source = lax.broadcasted_iota(jnp.int32, (tok, tok), 0)
+    target = lax.broadcasted_iota(jnp.int32, (tok, tok), 1)
+    mixing = jnp.bitwise_xor(source, target)
+    level = jnp.zeros((tok, tok), jnp.int32)
+    for power in range(inner_levels - 1):
+        level = level + (mixing >= 2**power).astype(jnp.int32)
+    level = jnp.where(source <= target, level, -1)
+    causal = source <= target
+    lane = lax.broadcasted_iota(jnp.int32, (tok, tok), 1)
+    gathered = jnp.zeros((tok, tok), F32)
+    for index in range(count):
+        head = start + index
+        lanes = slice(index * dim, (index + 1) * dim)
+        q, k, v, o = (ref[:, lanes] for ref in (query, key, value, cotangent))
+        scores = mxu(k, q, NT)
+        pulls = mxu(v, o, NT)
+        row = running[head : head + 1]
+        fading = jnp.exp(jnp.where(causal, row - spread[:, head : head + 1], NEVER))
+        weighting = jnp.zeros((tok, tok), F32)
+        for place_in in range(inner_levels):
+            weighting = jnp.where(
+                level == place_in, gain[place_in, head : head + 1, :], weighting
+            )
+        weighting = weighting * fading
+        mixing_part = scores * weighting
+        score_grad = pulls * weighting
+        product = scores * pulls * fading
+        flow = jnp.zeros((1, tok), F32)
+        for place_in in range(inner_levels):
+            found = jnp.sum(jnp.where(level == place_in, product, 0.0), axis=0, keepdims=True)
+            gain_rows[place_in, index : index + 1, :] = found
+            if place_in > 0:
+                flow = flow + gain[place_in, head : head + 1, :] * found
+        decay_rows[index : index + 1, :] = flow
+        left = jnp.where(level > 0, mixing_part * pulls, 0.0)
+        gathered = jnp.where(lane == index, lane_sums(left), gathered)
+        high, low = halves(mixing_part)
+        acc_out[:, lanes] = mxu(jnp.concatenate([high, low], axis=0), twice_rows(v), TN)
+        acc_value[:, lanes] = mxu(jnp.concatenate([high, low], axis=1), twice_rows(o), NN)
+        high, low = halves(score_grad)
+        acc_query[:, lanes] = mxu(jnp.concatenate([high, low], axis=0), twice_rows(k), TN)
+        acc_key[:, lanes] = mxu(jnp.concatenate([high, low], axis=1), twice_rows(q), NN)
+    decay_rows[...] = decay_rows[...] - gathered.T[:count]
+
+
+def use_rows(rows_out, uses, gathered, extra):
+    turned = gathered.T
+    count = rows_out.shape[0] // 4
+    decay_row = jnp.zeros((count, turned.shape[1]), F32)
+    flow_row = extra
+    for number, (forward, weight, lift) in enumerate(uses):
+        sums = turned[number * count : (number + 1) * count]
+        weighted = weight * sums
+        decay_row = decay_row + jnp.where(forward, weighted, -weighted)
+        flow_row = flow_row + jnp.where(forward, 0.0, weighted)
+        rows_out[number * count : (number + 1) * count, :] = lift * sums
+    rows_out[2 * count : 3 * count, :] = decay_row
+    rows_out[3 * count : 4 * count, :] = flow_row
+
+
+def pair_kernel(
+    place, query, key, value, cotangent, gain, decay, level0, after, out_left, out_right, rows_out
+):
+    position = place[0]
+    odd = position % 2 == 1
+    heads, tok = decay.shape
+    dim = query.shape[1] // heads
+    running = running_decay(decay[...])
+    lift = jnp.exp(running)
+    cross = gain.shape[0] - 3
+    weight = jnp.where(odd, gain[cross] * lift, jnp.exp(last_lane(running) - running))
+    spread = columns(weight)
+    lane = lax.broadcasted_iota(jnp.int32, (tok, tok), 1)
+    gathered = jnp.zeros((tok, tok), F32)
+    for head in range(heads):
+        lanes = slice(head * dim, (head + 1) * dim)
+        q, k, v, o = (ref[:, lanes] for ref in (query, key, value, cotangent))
+        left, right, sums = apply_state(
+            jnp.where(odd, q, k),
+            jnp.where(odd, o, v),
+            level0[pl.ds(head * dim, dim), :],
+            spread[:, head : head + 1],
+        )
+        out_left[:, lanes] = left
+        out_right[:, lanes] = right
+        gathered = jnp.where(lane == head, sums, gathered)
+    use_rows(rows_out, ((odd, weight, jnp.where(odd, lift, 0.0)),), gathered, jnp.zeros((heads, tok), F32))
+
+
+def first_use_kernel(
+    part,
+    mine,
+    place,
+    query,
+    key,
+    value,
+    cotangent,
+    gain,
+    decay,
+    other_total,
+    first,
+    second,
+    pair1,
+    pair2,
+    level0,
+    out_left,
+    out_right,
+    rows_out,
+):
+    position = place[0]
+    core = position % 2
+    side = core if mine else 1 - core
+    chip = position // 2
+    heads, tok = decay.shape
+    count = heads // 2 // CHUNKS
+    dim = query.shape[1] // count
+    cross = gain.shape[0] - 3
+    running = running_decay(decay[...])
+    total = last_lane(running)
+    other = other_total[...]
+    odd = core == 1
+    forward = chip != 0
+    offset = jnp.where(forward == odd, other, 0.0)
+    lift = jnp.exp(running + offset)
+    weight = jnp.where(
+        forward,
+        jnp.where(chip == 2, gain[cross + 2], gain[cross + 1]) * lift,
+        jnp.exp(total - running + offset),
+    )
+    pair_flow = jnp.where(forward != odd, jnp.exp(total), 0.0)
+    chip_flow = jnp.where((chip == 1) | (chip == 2), jnp.exp(total + other), 0.0)
+    lift, weight, pair_flow, chip_flow = (
+        take_half(rows, side, part, count) for rows in (lift, weight, pair_flow, chip_flow)
+    )
+    spread = columns(weight)
+    lane = lax.broadcasted_iota(jnp.int32, (tok, tok), 1)
+    gathered = jnp.zeros((tok, tok), F32)
+    flows = []
+    for index in range(count):
+        lanes = slice(index * dim, (index + 1) * dim)
+        rows = pl.ds(index * dim, dim)
+        one = slice(index, index + 1)
+        q, k, v, o = (ref[:, lanes] for ref in (query, key, value, cotangent))
+        state = jnp.where(chip == 2, second[rows, :], first[rows, :])
+        partner = jnp.where(odd, level0[rows, :], jnp.where(chip == 1, pair1[rows, :], pair2[rows, :]))
+        flows.append(
+            pair_flow[one] * jnp.sum(state * partner, axis=0, keepdims=True)
+            + chip_flow[one] * jnp.sum(first[rows, :] * second[rows, :], axis=0, keepdims=True)
+        )
+        left, right, sums = apply_state(
+            jnp.where(forward, q, k), jnp.where(forward, o, v), state, spread[:, one]
+        )
+        out_left[:, lanes] = left
+        out_right[:, lanes] = right
+        gathered = jnp.where(lane == index, sums, gathered)
+    use_rows(rows_out, ((forward, weight, lift),), gathered, jnp.concatenate(flows, axis=0))
+
+
+def last_use_kernel(
+    part,
+    mine,
+    place,
+    query,
+    key,
+    value,
+    cotangent,
+    gain,
+    decay,
+    other_total,
+    chip_total,
+    second,
+    third,
+    pair1,
+    level0,
+    left0,
+    right0,
+    left1,
+    right1,
+    part_out,
+    part_query,
+    part_key,
+    part_value,
+    *rest,
+):
+    out_mixed, out_query, out_key, out_value, rows_out = rest[-5:]
+    position = place[0]
+    core = position % 2
+    side = core if mine else 1 - core
+    chip = position // 2
+    heads, tok = decay.shape
+    count = heads // 2 // CHUNKS
+    dim = query.shape[1] // count
+    cross = gain.shape[0] - 3
+    running = running_decay(decay[...])
+    total = last_lane(running)
+    odd = core == 1
+    forward1 = chip != 0
+    forward = chip == 3
+    chip_offset = jnp.where((chip == 0) | (chip == 3), chip_total[...], 0.0)
+    offset = jnp.where(forward == odd, other_total[...], 0.0) + chip_offset
+    lift = jnp.exp(running + offset)
+    weight = jnp.where(forward, gain[cross + 2] * lift, jnp.exp(total - running + offset))
+    pair_flow = jnp.where(forward != odd, jnp.exp(total + chip_offset), 0.0)
+    lift, weight, pair_flow = (
+        take_half(rows, side, part, count) for rows in (lift, weight, pair_flow)
+    )
+    spread = columns(weight)
+    lane = lax.broadcasted_iota(jnp.int32, (tok, tok), 1)
+    gathered = jnp.zeros((tok, tok), F32)
+    flows = []
+    for index in range(count):
+        lanes = slice(index * dim, (index + 1) * dim)
+        rows = pl.ds(index * dim, dim)
+        one = slice(index, index + 1)
+        q, k, v, o = (ref[:, lanes] for ref in (query, key, value, cotangent))
+        state = jnp.where(chip == 1, second[rows, :], third[rows, :])
+        partner = jnp.where(odd, level0[rows, :], pair1[rows, :])
+        flows.append(pair_flow[one] * jnp.sum(state * partner, axis=0, keepdims=True))
+        left, right, sums = apply_state(
+            jnp.where(forward, q, k), jnp.where(forward, o, v), state, spread[:, one]
+        )
+        gathered = jnp.where(lane == index, sums, gathered)
+        forward_left = jnp.where(odd, left0[:, lanes], 0.0)
+        forward_right = jnp.where(odd, right0[:, lanes], 0.0)
+        back_left = jnp.where(odd, 0.0, left0[:, lanes])
+        back_right = jnp.where(odd, 0.0, right0[:, lanes])
+        for is_forward, a_left, a_right in (
+            (forward1, left1[:, lanes], right1[:, lanes]),
+            (forward, left, right),
+        ):
+            forward_left = forward_left + jnp.where(is_forward, a_left, 0.0)
+            forward_right = forward_right + jnp.where(is_forward, a_right, 0.0)
+            back_left = back_left + jnp.where(is_forward, 0.0, a_left)
+            back_right = back_right + jnp.where(is_forward, 0.0, a_right)
+        out_mixed[:, lanes] = (part_out[:, lanes] + forward_left).astype(BF16)
+        out_query[:, lanes] = (part_query[:, lanes] + forward_right).astype(BF16)
+        out_value[:, lanes] = (part_value[:, lanes] + back_left).astype(BF16)
+        out_key[:, lanes] = (part_key[:, lanes] + back_right).astype(BF16)
+    use_rows(rows_out, ((forward, weight, lift),), gathered, jnp.concatenate(flows, axis=0))
+
+
+def gather_kernel(place, pair_rows, *rest):
+    groups = 2 * CHUNKS
+    gain_rows, decay_rows = rest[:groups], rest[groups : 2 * groups]
+    parts, (grad_gain, grad_decay) = rest[2 * groups : -2], rest[-2:]
+    position = place[0]
+    core = position % 2
+    chip = position // 2
+    levels, heads, tok = grad_gain.shape
+    count = heads // 2 // CHUNKS
+
+    def natural(refs, kind):
+        rows = [ref[kind * count : (kind + 1) * count, :] for ref in refs]
+        return half_first(jnp.concatenate(rows, axis=0), core)
+
+    def of_pair(kind):
+        return pair_rows[kind * heads : (kind + 1) * heads, :]
+
+    for place_in in range(levels - 3):
+        grad_gain[place_in] = jnp.concatenate([ref[place_in] for ref in gain_rows], axis=0)
+    first, second = natural(parts[:groups], 0), natural(parts[groups:], 0)
+    grad_gain[levels - 3] = of_pair(0)
+    grad_gain[levels - 2] = jnp.where(chip % 2 == 1, first, 0.0)
+    grad_gain[levels - 1] = jnp.where(chip == 2, first, jnp.where(chip == 3, second, 0.0))
+    own = jnp.concatenate([ref[...] for ref in decay_rows], axis=0)
+    own = own + of_pair(2) + natural(parts[:groups], 2) + natural(parts[groups:], 2)
+    later = of_pair(3) + natural(parts[:groups], 3) + natural(parts[groups:], 3)
+    upper = lax.broadcasted_iota(jnp.int32, (tok, tok), 0)
+    lower = lax.broadcasted_iota(jnp.int32, (tok, tok), 1)
+    after = (upper >= lower).astype(F32)
+    every = jnp.ones((tok, tok), F32)
+    grad_decay[...] = jnp.dot(
+        own, after, precision=TOP_ACCURACY, preferred_element_type=F32
+    ) + jnp.dot(later, every, precision=TOP_ACCURACY, preferred_element_type=F32)
+
+
+def after(value, *others):
+    return lax.optimization_barrier((value, *others))[0]
+
+
+def sds(*shape, dtype=F32):
+    return jax.ShapeDtypeStruct(shape, dtype)
+
+
+def params(mebibytes=24):
+    return pltpu.CompilerParams(vmem_limit_bytes=mebibytes * 1024 * 1024)
+
+
+SCALAR = pl.BlockSpec(memory_space=pltpu.SMEM)
+ANYWHERE = pl.BlockSpec(memory_space=pl.ANY)
+IN_HBM = pl.BlockSpec(memory_space=pltpu.HBM)
+
+
+def whole(shape):
+    return pl.BlockSpec(shape, lambda g, place: (0,) * len(shape))
+
+
+FIRST_EXPORTS_COST = 1
+FIRST_MERGE_COST = 1
+SECOND_EXPORTS_COST = 1
+LOCAL_COST = 1
+SECOND_MERGE_COST = 1
+PAIR_USE_COST = 1
+FIRST_USE_COST = 1
+LAST_USE_COST = 1
+GATHER_COST = 1
+
+
+def cost(flops):
+    return pl.CostEstimate(flops=flops, bytes_accessed=1, transcendentals=0)
+
+
+def line_device(queries, keys_in, value_input, level_gain, decay_log, out_grad):
+    heads, tok = decay_log.shape
+    dim = queries.shape[1] // heads
+    half = heads // 2
+    count = half // CHUNKS
+    part_rows = count * dim
+    half_rows = half * dim
+    place = lax.axis_index("ctx").astype(jnp.int32).reshape(1)
+    tokens = (queries, keys_in, value_input, out_grad)
+    core_swap = [(at, at ^ 1) for at in range(8)]
+    side_swap = [(at, at ^ 2) for at in range(8)]
+    middle_swap = [(2, 4), (4, 2), (3, 5), (5, 3), (6, 6), (7, 7)]
+
+    def swap(block, route):
+        return lax.ppermute(block, "ctx", route)
+
+    send1, keep1 = pl.pallas_call(
+        first_export_kernel,
+        out_shape=(sds(half_rows + heads, dim), sds(half_rows, dim)),
+        in_specs=[SCALAR] + [IN_HBM] * 6,
+        scratch_shapes=[
+            pltpu.VMEM((tok, heads * dim), BF16),
+            pltpu.VMEM((tok, heads * dim), BF16),
+            pltpu.VMEM((2, heads, tok), F32),
+            pltpu.VMEM((heads, tok), F32),
+            pltpu.SemaphoreType.DMA((6,)),
+        ],
+        compiler_params=params(62),
+
+        cost_estimate=cost(FIRST_EXPORTS_COST),
+        name="first_exports",
+    )(place, *tokens, level_gain, decay_log)
+    got1 = swap(send1, core_swap)
+    send2, keep2, bundle = pl.pallas_call(
+        second_export_kernel,
+        out_shape=(sds(half_rows, dim), sds(half_rows, dim), sds(4 * half_rows, dim)),
+        in_specs=[SCALAR] + [pl.BlockSpec()] * 7,
+        compiler_params=params(),
+
+        cost_estimate=cost(SECOND_EXPORTS_COST),
+        name="second_exports",
+    )(place, *tokens, level_gain, decay_log, keep1)
+    first_sent = pl.pallas_call(
+        first_merge_kernel,
+        out_shape=tuple(
+            sds(part_rows + (heads if part == 0 else 0), dim) for part in range(CHUNKS)
+        ),
+        in_specs=[SCALAR] + [pl.BlockSpec()] * 3 + [ANYWHERE],
+        compiler_params=params(),
+        cost_estimate=cost(FIRST_MERGE_COST),
+        name="first_merge",
+    )(place, decay_log, keep1, got1, keep2)
+    first = [swap(block, side_swap) for block in first_sent]
+
+    got2 = swap(after(send2, got1), core_swap)
+    front = swap(after(bundle, got1), core_swap)
+
+
+    inner = tok.bit_length()
+    groups = 2 * CHUNKS
+
+    def local(number, before, after):
+        lanes = pl.BlockSpec((tok, part_rows), lambda g: (0, number))
+        return pl.pallas_call(
+            functools.partial(local_kernel, number * count),
+            grid=(1,),
+            out_shape=(sds(tok, heads * dim),) * 4 + (sds(inner, count, tok), sds(count, tok)),
+            in_specs=[lanes] * 4
+            + [
+                pl.BlockSpec(level_gain.shape, lambda g: (0, 0, 0)),
+                pl.BlockSpec(decay_log.shape, lambda g: (0, 0)),
+            ]
+            + [ANYWHERE] * (len(before) + len(after)),
+            out_specs=(lanes,) * 4
+            + (
+                pl.BlockSpec((inner, count, tok), lambda g: (0, 0, 0)),
+                pl.BlockSpec((count, tok), lambda g: (0, 0)),
+            ),
+            input_output_aliases={6 + at: at for at in range(len(before))},
+            compiler_params=params(),
+
+            cost_estimate=cost(LOCAL_COST),
+            name="local",
+        )(*tokens, level_gain, decay_log, *before, *after)
+
+    def second_merge(part, after):
+        chunk = pl.BlockSpec((part_rows, dim), lambda g: (part, 0))
+        start = pl.BlockSpec((part_rows, dim), lambda g: (0, 0))
+        return pl.pallas_call(
+            functools.partial(second_merge_kernel, part),
+            grid=(1,),
+            out_shape=sds(part_rows, dim),
+            in_specs=[
+                SCALAR,
+                pl.BlockSpec(decay_log.shape, lambda g: (0, 0)),
+                pl.BlockSpec((heads, dim), lambda g: (half_rows // heads, 0)),
+                chunk,
+                chunk,
+                start,
+                ANYWHERE,
+            ],
+            out_specs=start,
+            compiler_params=params(),
+            cost_estimate=cost(SECOND_MERGE_COST),
+            name="second_merge",
+        )(place, decay_log, got1, keep2, got2, first[part], after)
+
+    gain_rows, decay_rows = [], []
+    acc = ()
+
+    def more_local(number, *others):
+        *done, gains, decays = local(number, acc, others)
+        gain_rows.append(gains)
+        decay_rows.append(decays)
+        return done
+
+    acc = more_local(0, first_sent[-1])
+    acc = more_local(1)
+    sent = [second_merge(0, decay_rows[-1])]
+    sent.append(second_merge(1, sent[0]))
+    second = [swap(block, middle_swap) for block in sent]
+    left0, right0, pair_rows = pl.pallas_call(
+        pair_kernel,
+        grid=(1,),
+        out_shape=(sds(tok, heads * dim),) * 2 + (sds(4 * heads, tok),),
+        in_specs=[SCALAR]
+        + [pl.BlockSpec()] * 6
+        + [pl.BlockSpec((heads * dim, dim), lambda g: (0, 0)), ANYWHERE],
+        compiler_params=params(),
+
+        cost_estimate=cost(PAIR_USE_COST),
+        name="pair_use",
+    )(place, *tokens, level_gain, decay_log, front, sent[1])
+
+    third = [swap(second[0], side_swap)]
+    acc = more_local(2, pair_rows)
+    first_over = [swap(after(block, decay_rows[2]), core_swap) for block in first]
+    second_over = [swap(after(second[0], decay_rows[2]), core_swap)]
+    second[1] = after(second[1], decay_rows[2])
+    third.append(swap(second[1], side_swap))
+    acc = more_local(3, second[1])
+    second_over.append(swap(after(second[1], decay_rows[3]), core_swap))
+    third_over = [swap(after(third[0], decay_rows[3]), core_swap)]
+
+    def side_specs(part, mine):
+        def block(place):
+            core = lax.rem(place[0], 2)
+            return (core if mine else 1 - core) * CHUNKS + part
+
+        lanes = pl.BlockSpec((tok, part_rows), lambda g, place: (0, block(place)))
+        level0 = pl.BlockSpec((part_rows, dim), lambda g, place: (block(place), 0))
+        half_lanes = pl.BlockSpec((tok, part_rows), lambda g, place: (0, 0))
+        start = pl.BlockSpec((part_rows, dim), lambda g, place: (0, 0))
+        if mine:
+            pair1 = pair2 = pl.BlockSpec((part_rows, dim), lambda g, place: (part, 0))
+        else:
+            pair2 = pl.BlockSpec((part_rows, dim), lambda g, place: (2 * groups - groups // 2 + part, 0))
+            pair1 = pl.BlockSpec((part_rows, dim), lambda g, place: (groups + part, 0))
+        return lanes, level0, half_lanes, start, pair1, pair2
+
+    small = [
+        whole(level_gain.shape),
+        whole(decay_log.shape),
+        pl.BlockSpec((heads, dim), lambda g, place: (half_rows // heads, 0)),
+    ]
+    used = {}
+    for part in range(CHUNKS):
+        for mine in (True, False):
+            lanes, level0, half_lanes, start, pair1, pair2 = side_specs(part, mine)
+            used[part, mine] = pl.pallas_call(
+                functools.partial(first_use_kernel, part, mine),
+                grid_spec=pltpu.PrefetchScalarGridSpec(
+                    num_scalar_prefetch=1,
+                    grid=(1,),
+                    in_specs=[lanes] * 4 + small + [start] * 2 + [pair1, pair2, level0],
+                    out_specs=(half_lanes,) * 2 + (whole((4 * count, tok)),),
+                ),
+                out_shape=(sds(tok, part_rows),) * 2 + (sds(4 * count, tok),),
+                compiler_params=params(),
+
+                cost_estimate=cost(FIRST_USE_COST),
+                name="first_use",
+            )(
+                place,
+                *tokens,
+                level_gain,
+                decay_log,
+                got1,
+                (first if mine else first_over)[part],
+                (second if mine else second_over)[part],
+                got1 if mine else front,
+                got2 if mine else front,
+                front,
+            )
+
+    results = ()
+    last_rows = {}
+    for part in range(CHUNKS):
+        if part == 1:
+            ready = [last_rows[0, False], used[1, True][2], used[1, False][2]]
+            third_over.append(swap(after(third[1], *ready), core_swap))
+        for mine in (True, False):
+            lanes, level0, half_lanes, start, pair1, pair2 = side_specs(part, mine)
+            left1, right1, _ = used[part, mine]
+            before = len(results)
+            *results, last_rows[part, mine] = pl.pallas_call(
+                functools.partial(last_use_kernel, part, mine),
+                grid_spec=pltpu.PrefetchScalarGridSpec(
+                    num_scalar_prefetch=1,
+                    grid=(1,),
+                    in_specs=[lanes] * 4
+                    + small
+                    + [pl.BlockSpec((heads, dim), lambda g, place: (part_rows // heads, 0))]
+                    + [start] * 2
+                    + [pair1, level0]
+                    + [lanes] * 2
+                    + [half_lanes] * 2
+                    + [lanes] * 4
+                    + [ANYWHERE] * before,
+                    out_specs=(lanes,) * 4 + (whole((4 * count, tok)),),
+                ),
+                out_shape=(sds(tok, heads * dim, dtype=BF16),) * 4 + (sds(4 * count, tok),),
+                input_output_aliases={21 + at: at for at in range(before)},
+                compiler_params=params(),
+
+                cost_estimate=cost(LAST_USE_COST),
+                name="last_use",
+            )(
+                place,
+                *tokens,
+                level_gain,
+                decay_log,
+                got1,
+                first[0],
+                (second if mine else second_over)[part],
+                (third if mine else third_over)[part],
+                got1 if mine else front,
+                front,
+                left0,
+                right0,
+                left1,
+                right1,
+                *acc,
+                *results,
+            )
+    order = [(part, mine) for mine in (True, False) for part in range(CHUNKS)]
+    rows = [used[key][2] for key in order] + [last_rows[key] for key in order]
+    grad_gain, grad_decay = pl.pallas_call(
+        gather_kernel,
+        out_shape=(sds(*level_gain.shape), sds(heads, tok)),
+        in_specs=[SCALAR] + [pl.BlockSpec()] * (1 + 2 * groups + len(rows)),
+        compiler_params=params(),
+        cost_estimate=cost(GATHER_COST),
+        name="gather",
+    )(place, pair_rows, *gain_rows, *decay_rows, *rows)
+    return (*results, grad_gain, grad_decay)
+
+
 def solution(mesh):
     placed = (
         P(("seq", "ctx"), None),
@@ -199,7 +1022,7 @@
         P(("seq", "ctx"), None),
     )
     return jax.shard_map(
-        per_device,
+        line_device if mesh.shape["ctx"] == 8 else per_device,
         mesh=mesh,
         in_specs=placed,
         out_specs=(

time: 207 us -> 49.8 us (0.24)
  waiting for transfers between devices: 122 us -> 8.85 us
  matrix products: 34.2 us -> 0 us
  Pallas kernels: 0 us -> 23.5 us
  other arithmetic: 22.2 us -> 0 us
  local copies, waits for them, and re-layouts: 14.6 us -> 2.1 us
    ppermute x12 -> x15, waiting for transfers between devices: 122 us -> 8.85 us  [swap(): return lax.ppermute(block, 'ctx', route)]
    dot_general x14 -> x0, matrix products: 34.2 us -> none  [the longest x3 9.99 us: block_output(): jnp.einsum('jhik,jhkv->hiv', reach, buckets, precision=TOP_ACCURACY)]
    pallas_call x0 -> x19, Pallas kernels: none -> 23.5 us  [the longest x4 6.28 us: local(): pl.pallas_call(functools.partial(local_kernel, number * count), grid=(1,)...]
    unnamed x58 -> x16, local copies, waits for them, and re-layouts: 11.9 us -> 2.1 us
    reduce_sum x5 -> x0, other arithmetic: 8.59 us -> none  [the longest x1 4.04 us: own_grads(): jnp.sum(g_bucket * other_state, axis=(1, 2))]
    another operation x5 -> x0, other arithmetic: 6.17 us -> none  [the longest x2 2.71 us: per_device(): buckets = jnp.stack(found)]
    select_n x4 -> x0, other arithmetic: 3.25 us -> none  [the longest x2 2.73 us: partner_grads(): jnp.where(is_upper, factor[:, None, None] * g_state + jnp.exp(offset)[:,...]
    ppermute x12 -> x15, starting transfers between devices: 12.2 us -> 14.2 us  [swap(): return lax.ppermute(block, 'ctx', route)]
  transfers between devices with their start and end apart: 12 -> 15, of which waited for: 6 -> 3; matrix products, arithmetic and copies ran while one was open for 20% -> 0% of each run, Pallas kernels for 0% -> 36%
where the time goes in v2:
time: 49.8 us; the launch traced here: 49.5 us
  Pallas kernels  23.5 us (47%)
  starting transfers between devices  14.2 us (29%)
  waiting for transfers between devices  8.85 us (18%)
  local copies, waits for them, and re-layouts  2.1 us (4%)
  between operations  0.82 us (2%)
    ppermute x15, starting transfers between devices, swap(): return lax.ppermute(block, 'ctx', route)  14.2 us
    ppermute x15, waiting for transfers between devices, swap(): return lax.ppermute(block, 'ctx', route)  8.85 us
    pallas_call x4, Pallas kernels, local(): pl.pallas_call(functools.partial(local_kernel, number * count), grid=(1,)...  6.28 us
    pallas_call x4, Pallas kernels, line_device(): pl.pallas_call(functools.partial(last_use_kernel, part, mine), grid_spec=...  6.24 us
    pallas_call x1, Pallas kernels, line_device(): pl.pallas_call(first_export_kernel, out_shape=(sds(half_rows + heads, dim...  3.33 us
    pallas_call x4, Pallas kernels, line_device(): pl.pallas_call(functools.partial(first_use_kernel, part, mine), grid_spec...  2.67 us
    unnamed x16, local copies, waits for them, and re-layouts  2.1 us
    pallas_call x1, Pallas kernels, line_device(): pl.pallas_call(pair_kernel, grid=(1,), out_shape=(sds(tok, heads * dim),)...  1.8 us
  transfers between devices with their start and end apart: 15, of which 3 were waited for; matrix products, arithmetic and copies ran while one was open for 0% of the time, Pallas kernels for 36%

profile of v2, /device:TPU:1, one launch (start us, length us, event | category | flops | bytes accessed | tf_op | source)
XLA Modules:
  0.0 49.5 jit_solution(16716058914301831661)
XLA Ops:
  0.6 0.0 copy-start.6
  0.6 0.0 copy-start
  0.7 0.0 copy-start.1
  0.7 0.0 copy-start.2
  0.7 0.0 copy-start.5
  0.7 3.3 %first_exports.1 = (f32[1040,128]{1,0:T(8,128)}, f32[1024,128]{1,0:T(8,128)}) custom-call(s32[1]{0:T(128)} %bitcast.place, bf16[128,2048]{1,0:T(8,128)(2,1)} %query.29, bf16[128,2048]{1,0:T(8,128)(2,1)} %key.29, bf16[128,2048]{1,0:T(8,128)(2,1)} %value.29, bf16[128,2048]{1,0:T(8,128)(2,1)} %cotangent.29, f32[11,16,128]{2,1,0:T(8,128)} %gain.29, f32[16,128]{1,0:T(8,128)} %decay.35), custom_call_target="tpu_custom_call" | custom-call | flops 1 | bytes 1 | tf_op jit(solution)/shard_map/first_exports/pallas_call | solution.py:773
  4.0 0.1 collective-permute-start
  4.1 0.0 copy-done.6
  4.2 0.0 copy-done
  4.2 0.0 copy-done.1
  4.2 0.0 copy-done.2
  4.2 0.0 copy-done.5
  4.2 0.0 copy-start.3
  4.2 1.0 %copy-done.3 = bf16[128,2048]{1,0:T(8,128)(2,1)S(1)} copy-done((bf16[128,2048]{1,0:T(8,128)(2,1)S(1)}, bf16[128,2048]{1,0:T(8,128)(2,1)}, u32[]{:S(2)}) %copy-start.3) | copy-done | bytes 524312
  5.2 0.0 copy-start.7
  5.2 1.0 %copy-done.7 = f32[1024,128]{1,0:T(8,128)S(1)} copy-done((f32[1024,128]{1,0:T(8,128)S(1)}, f32[1024,128]{1,0:T(8,128)}, u32[]{:S(2)}) %copy-start.7) | copy-done | bytes 524312
  6.3 1.5 %second_exports.1 = (f32[1024,128]{1,0:T(8,128)S(1)}, f32[1024,128]{1,0:T(8,128)S(1)}, f32[4096,128]{1,0:T(8,128)S(1)}) custom-call(s32[1]{0:T(128)} %bitcast.place, bf16[128,2048]{1,0:T(8,128)(2,1)S(1)} %copy-done, bf16[128,2048]{1,0:T(8,128)(2,1)S(1)} %copy-done.1, bf16[128,2048]{1,0:T(8,128)(2,1)S(1)} %copy-done.2, bf16[128,2048]{1,0:T(8,128)(2,1)S(1)} %copy-done.3, ...), custom_call_target="tpu_custom_call" | custom-call | flops 1 | bytes 1 | tf_op jit(solution)/shard_map/second_exports/pallas_call | solution.py:790
  7.8 0.0 collective-permute-done.got.other_total.pair1
  7.8 0.5 %collective-permute-start.5 = (f32[4096,128]{1,0:T(8,128)S(1)}, f32[4096,128]{1,0:T(8,128)S(1)}, u32[]{:S(2)}, u32[]{:S(2)}) collective-permute-start(f32[4096,128]{1,0:T(8,128)S(1)} %get-tuple-element.100), channel_id=1, source_target_pairs={{0,1},{1,0},{2,3},{3,2},{4,5},{5,4},{6,7},{7,6},{8,9},{9,8},{10,11... | collective-permute-start | bytes 6291464 | tf_op jit(solution)/shard_map/ppermute | solution.py:771
  8.3 0.1 collective-permute-start.2
  8.4 0.3 first_merge.1
  8.7 2.8 %collective-permute-start.1 = (f32[528,128]{1,0:T(8,128)S(1)}, f32[528,128]{1,0:T(8,128)S(1)}, u32[]{:S(2)}, u32[]{:S(2)}) collective-permute-start(f32[528,128]{1,0:T(8,128)S(1)} %get-tuple-element.86), channel_id=1, source_target_pairs={{0,2},{1,3},{2,0},{3,1},{4,6},{5,7},{6,4},{7,5},{8,10},{9,11},{10,... | collective-permute-start | bytes 811016 | tf_op jit(solution)/shard_map/ppermute | solution.py:771
  11.5 0.1 collective-permute-start.3
  11.6 0.0 copy-done.4
  11.6 1.6 %local.4 = (f32[128,2048]{1,0:T(8,128)S(1)}, f32[128,2048]{1,0:T(8,128)S(1)}, f32[128,2048]{1,0:T(8,128)S(1)}, f32[128,2048]{1,0:T(8,128)S(1)}, f32[8,4,128]{2,1,0:T(4,128)S(1)}, /*index=5*/f32[4,128]{1,0:T(4,128)S(1)}) custom-call(bf16[128,2048]{1,0:T(8,128)(2,1)S(1)} %copy-done, bf16[128,2048]{1,0:T(8,128)(2,1)S(1)} %copy-done.1, ...), custom_call_target="tpu_custom_call" | custom-call | flops 1 | bytes 1 | tf_op jit(solution)/shard_map/local/pallas_call | solution.py:820
  13.2 1.6 %local.5 = (f32[128,2048]{1,0:T(8,128)S(1)}, f32[128,2048]{1,0:T(8,128)S(1)}, f32[128,2048]{1,0:T(8,128)S(1)}, f32[128,2048]{1,0:T(8,128)S(1)}, f32[8,4,128]{2,1,0:T(4,128)S(1)}, /*index=5*/f32[4,128]{1,0:T(4,128)S(1)}) custom-call(bf16[128,2048]{1,0:T(8,128)(2,1)S(1)} %copy-done, ...), custom_call_target="tpu_custom_call", output_to_operand_aliasing={{0}: (6, {}), {1}: (7, {}), {2}: (8, {}), {3}: (9, {})} | custom-call | flops 1 | bytes 1 | tf_op jit(solution)/shard_map/local/pallas_call | solution.py:820
  14.7 3.5 %collective-permute-done.1.first.chip_total = f32[528,128]{1,0:T(8,128)S(1)} collective-permute-done((f32[528,128]{1,0:T(8,128)S(1)}, f32[528,128]{1,0:T(8,128)S(1)}, u32[]{:S(2)}, u32[]{:S(2)}) %collective-permute-start.1) | collective-permute-done | bytes 270368 | tf_op jit(solution)/shard_map/ppermute | solution.py:771
  18.3 0.0 collective-permute-done.2.got.pair2
  18.3 0.3 second_merge.2.after
  18.6 0.7 %collective-permute-start.8 = (f32[512,128]{1,0:T(8,128)S(1)}, f32[512,128]{1,0:T(8,128)S(1)}, u32[]{:S(2)}, u32[]{:S(2)}) collective-permute-start(f32[512,128]{1,0:T(8,128)S(1)} %second_merge.2.after), channel_id=1, source_target_pairs={{2,4},{4,2},{3,5},{5,3},{6,6},{7,7},{10,12},{12,10},{11,13},{13,11... | collective-permute-start | bytes 786440 | tf_op jit(solution)/shard_map/ppermute | solution.py:771
  19.3 4.6 %collective-permute-done.3.first = f32[512,128]{1,0:T(8,128)S(1)} collective-permute-done((f32[512,128]{1,0:T(8,128)S(1)}, f32[512,128]{1,0:T(8,128)S(1)}, u32[]{:S(2)}, u32[]{:S(2)}) %collective-permute-start.3) | collective-permute-done | bytes 262176 | tf_op jit(solution)/shard_map/ppermute | solution.py:771
  23.9 0.3 second_merge.3.after
  24.2 0.9 %collective-permute-start.4 = (f32[512,128]{1,0:T(8,128)S(1)}, f32[512,128]{1,0:T(8,128)S(1)}, u32[]{:S(2)}, u32[]{:S(2)}) collective-permute-start(f32[512,128]{1,0:T(8,128)S(1)} %second_merge.3.after), channel_id=1, source_target_pairs={{2,4},{4,2},{3,5},{5,3},{6,6},{7,7},{10,12},{12,10},{11,13},{13,11... | collective-permute-start | bytes 786440 | tf_op jit(solution)/shard_map/ppermute | solution.py:771
  25.1 0.0 collective-permute-done.8.second
  25.1 3.9 %collective-permute-start.10 = (f32[512,128]{1,0:T(8,128)S(1)}, f32[512,128]{1,0:T(8,128)S(1)}, u32[]{:S(2)}, u32[]{:S(2)}) collective-permute-start(f32[512,128]{1,0:T(8,128)S(1)} %collective-permute-done.8.second), channel_id=1, source_target_pairs={{0,2},{1,3},{2,0},{3,1},{4,6},{5,7},{6,4},{7,5},{8,10},{9,11},{10,... | collective-permute-start | bytes 786440 | tf_op jit(solution)/shard_map/ppermute | solution.py:771
  29.0 0.0 collective-permute-done.5.level0.pair1.pair2
  29.0 1.8 %pair_use.1 = (f32[128,2048]{1,0:T(8,128)S(1)}, f32[128,2048]{1,0:T(8,128)S(1)}, f32[64,128]{1,0:T(8,128)S(1)}) custom-call(s32[1]{0:T(128)} %bitcast.place, bf16[128,2048]{1,0:T(8,128)(2,1)S(1)} %copy-done, bf16[128,2048]{1,0:T(8,128)(2,1)S(1)} %copy-done.1, bf16[128,2048]{1,0:T(8,128)(2,1)S(1)} %copy-done.2, bf16[128,2048]{1,0:T(8,128)(2,1)S(1)} %copy-done.4, ...), custom_call_target="tpu_custom_call" | custom-call | flops 1 | bytes 1 | tf_op jit(solution)/shard_map/pair_use/pallas_call | solution.py:878
  30.8 1.6 %local.6 = (f32[128,2048]{1,0:T(8,128)S(1)}, f32[128,2048]{1,0:T(8,128)S(1)}, f32[128,2048]{1,0:T(8,128)S(1)}, f32[128,2048]{1,0:T(8,128)S(1)}, f32[8,4,128]{2,1,0:T(4,128)S(1)}, /*index=5*/f32[4,128]{1,0:T(4,128)S(1)}) custom-call(bf16[128,2048]{1,0:T(8,128)(2,1)S(1)} %copy-done, ...), custom_call_target="tpu_custom_call", output_to_operand_aliasing={{0}: (6, {}), {1}: (7, {}), {2}: (8, {}), {3}: (9, {})} | custom-call | flops 1 | bytes 1 | tf_op jit(solution)/shard_map/local/pallas_call | solution.py:820
  32.4 1.9 %collective-permute-start.13 = (f32[512,128]{1,0:T(8,128)S(1)}, f32[512,128]{1,0:T(8,128)S(1)}, u32[]{:S(2)}, u32[]{:S(2)}) collective-permute-start(f32[512,128]{1,0:T(8,128)S(1)} %collective-permute-done.3.first), channel_id=1, source_target_pairs={{0,1},{1,0},{2,3},{3,2},{4,5},{5,4},{6,7},{7,6},{8,9},{9,8},{10,11... | collective-permute-start | bytes 786440 | tf_op jit(solution)/shard_map/ppermute | solution.py:771
  34.2 0.1 collective-permute-start.12
  34.3 0.0 collective-permute-done.4.rest_4_.second
  34.3 0.4 collective-permute-start.9
  34.7 1.6 %local.7 = (f32[128,2048]{1,0:T(8,128)S(1)}, f32[128,2048]{1,0:T(8,128)S(1)}, f32[128,2048]{1,0:T(8,128)S(1)}, f32[128,2048]{1,0:T(8,128)S(1)}, f32[8,4,128]{2,1,0:T(4,128)S(1)}, /*index=5*/f32[4,128]{1,0:T(4,128)S(1)}) custom-call(bf16[128,2048]{1,0:T(8,128)(2,1)S(1)} %copy-done, ...), custom_call_target="tpu_custom_call", output_to_operand_aliasing={{0}: (6, {}), {1}: (7, {}), {2}: (8, {}), {3}: (9, {})} | custom-call | flops 1 | bytes 1 | tf_op jit(solution)/shard_map/local/pallas_call | solution.py:820
  36.3 0.1 collective-permute-start.6
  36.4 0.0 collective-permute-done.10.third
  36.5 0.4 collective-permute-start.11
  36.9 0.0 collective-permute-done.13.first
  36.9 1.4 %collective-permute-start.7 = (f32[512,128]{1,0:T(8,128)S(1)}, f32[512,128]{1,0:T(8,128)S(1)}, u32[]{:S(2)}, u32[]{:S(2)}) collective-permute-start(f32[512,128]{1,0:T(8,128)S(1)} %collective-permute-done.4.rest_4_.second), channel_id=1, source_target_pairs={{0,2},{1,3},{2,0},{3,1},{4,6},{5,7},{6,4},{7,5},{8,10},{9,11},{10,... | collective-permute-start | bytes 786440 | tf_op jit(solution)/shard_map/ppermute | solution.py:771
  38.3 0.7 %first_use.6 = (f32[128,512]{1,0:T(8,128)S(1)}, f32[128,512]{1,0:T(8,128)S(1)}, f32[16,128]{1,0:T(8,128)S(1)}) custom-call(s32[1]{0:T(128)} %bitcast.place, bf16[128,2048]{1,0:T(8,128)(2,1)S(1)} %copy-done, bf16[128,2048]{1,0:T(8,128)(2,1)S(1)} %copy-done.1, bf16[128,2048]{1,0:T(8,128)(2,1)S(1)} %copy-done.2, bf16[128,2048]{1,0:T(8,128)(2,1)S(1)} %copy-done.4, ...), custom_call_target="tpu_custom_call" | custom-call | flops 1 | bytes 1 | tf_op jit(solution)/shard_map/first_use/pallas_call | solution.py:926
  38.9 0.7 %first_use.5 = (f32[128,512]{1,0:T(8,128)S(1)}, f32[128,512]{1,0:T(8,128)S(1)}, f32[16,128]{1,0:T(8,128)S(1)}) custom-call(s32[1]{0:T(128)} %bitcast.place, bf16[128,2048]{1,0:T(8,128)(2,1)S(1)} %copy-done, bf16[128,2048]{1,0:T(8,128)(2,1)S(1)} %copy-done.1, bf16[128,2048]{1,0:T(8,128)(2,1)S(1)} %copy-done.2, bf16[128,2048]{1,0:T(8,128)(2,1)S(1)} %copy-done.4, ...), custom_call_target="tpu_custom_call" | custom-call | flops 1 | bytes 1 | tf_op jit(solution)/shard_map/first_use/pallas_call | solution.py:926
  39.6 1.6 %last_use.4 = (bf16[128,2048]{1,0:T(8,128)(2,1)}, bf16[128,2048]{1,0:T(8,128)(2,1)}, bf16[128,2048]{1,0:T(8,128)(2,1)}, bf16[128,2048]{1,0:T(8,128)(2,1)}, f32[16,128]{1,0:T(8,128)S(1)}) custom-call(s32[1]{0:T(128)} %bitcast.place, bf16[128,2048]{1,0:T(8,128)(2,1)S(1)} %copy-done, bf16[128,2048]{1,0:T(8,128)(2,1)S(1)} %copy-done.1, ...), custom_call_target="tpu_custom_call" | custom-call | flops 1 | bytes 1 | tf_op jit(solution)/shard_map/last_use/pallas_call | solution.py:962
  41.2 0.0 collective-permute-done.6.second
  41.2 0.7 %first_use.7 = (f32[128,512]{1,0:T(8,128)S(1)}, f32[128,512]{1,0:T(8,128)S(1)}, f32[16,128]{1,0:T(8,128)S(1)}) custom-call(s32[1]{0:T(128)} %bitcast.place, bf16[128,2048]{1,0:T(8,128)(2,1)S(1)} %copy-done, bf16[128,2048]{1,0:T(8,128)(2,1)S(1)} %copy-done.1, bf16[128,2048]{1,0:T(8,128)(2,1)S(1)} %copy-done.2, bf16[128,2048]{1,0:T(8,128)(2,1)S(1)} %copy-done.4, ...), custom_call_target="tpu_custom_call" | custom-call | flops 1 | bytes 1 | tf_op jit(solution)/shard_map/first_use/pallas_call | solution.py:926
  41.8 0.0 collective-permute-done.9.second
  41.9 0.0 collective-permute-done.12.first
  41.9 0.7 %first_use.4 = (f32[128,512]{1,0:T(8,128)S(1)}, f32[128,512]{1,0:T(8,128)S(1)}, f32[16,128]{1,0:T(8,128)S(1)}) custom-call(s32[1]{0:T(128)} %bitcast.place, bf16[128,2048]{1,0:T(8,128)(2,1)S(1)} %copy-done, bf16[128,2048]{1,0:T(8,128)(2,1)S(1)} %copy-done.1, bf16[128,2048]{1,0:T(8,128)(2,1)S(1)} %copy-done.2, bf16[128,2048]{1,0:T(8,128)(2,1)S(1)} %copy-done.4, ...), custom_call_target="tpu_custom_call" | custom-call | flops 1 | bytes 1 | tf_op jit(solution)/shard_map/first_use/pallas_call | solution.py:926
  42.5 0.0 collective-permute-done.11.third
  42.6 1.6 %last_use.5 = (bf16[128,2048]{1,0:T(8,128)(2,1)}, bf16[128,2048]{1,0:T(8,128)(2,1)}, bf16[128,2048]{1,0:T(8,128)(2,1)}, bf16[128,2048]{1,0:T(8,128)(2,1)}, f32[16,128]{1,0:T(8,128)S(1)}) custom-call(s32[1]{0:T(128)} %bitcast.place, bf16[128,2048]{1,0:T(8,128)(2,1)S(1)} %copy-done, ...), custom_call_target="tpu_custom_call", output_to_operand_aliasing={{0}: (21, {}), {1}: (22, {}), {2}: (23, {}), {3}: (24, {})} | custom-call | flops 1 | bytes 1 | tf_op jit(solution)/shard_map/last_use/pallas_call | solution.py:962
  44.1 0.6 %collective-permute-done.7.third = f32[512,128]{1,0:T(8,128)S(1)} collective-permute-done((f32[512,128]{1,0:T(8,128)S(1)}, f32[512,128]{1,0:T(8,128)S(1)}, u32[]{:S(2)}, u32[]{:S(2)}) %collective-permute-start.7) | collective-permute-done | bytes 262176 | tf_op jit(solution)/shard_map/ppermute | solution.py:771
  44.8 0.9 %collective-permute-start.14 = (f32[512,128]{1,0:T(8,128)S(1)}, f32[512,128]{1,0:T(8,128)S(1)}, u32[]{:S(2)}, u32[]{:S(2)}) collective-permute-start(f32[512,128]{1,0:T(8,128)S(1)} %collective-permute-done.7.third), channel_id=1, source_target_pairs={{0,1},{1,0},{2,3},{3,2},{4,5},{5,4},{6,7},{7,6},{8,9},{9,8},{10,11... | collective-permute-start | bytes 786440 | tf_op jit(solution)/shard_map/ppermute | solution.py:771
  45.6 1.6 %last_use.6 = (bf16[128,2048]{1,0:T(8,128)(2,1)}, bf16[128,2048]{1,0:T(8,128)(2,1)}, bf16[128,2048]{1,0:T(8,128)(2,1)}, bf16[128,2048]{1,0:T(8,128)(2,1)}, f32[16,128]{1,0:T(8,128)S(1)}) custom-call(s32[1]{0:T(128)} %bitcast.place, bf16[128,2048]{1,0:T(8,128)(2,1)S(1)} %copy-done, ...), custom_call_target="tpu_custom_call", output_to_operand_aliasing={{0}: (21, {}), {1}: (22, {}), {2}: (23, {}), {3}: (24, {})} | custom-call | flops 1 | bytes 1 | tf_op jit(solution)/shard_map/last_use/pallas_call | solution.py:962
  47.2 0.0 collective-permute-done.14.third
  47.2 1.5 %last_use.7 = (bf16[128,2048]{1,0:T(8,128)(2,1)}, bf16[128,2048]{1,0:T(8,128)(2,1)}, bf16[128,2048]{1,0:T(8,128)(2,1)}, bf16[128,2048]{1,0:T(8,128)(2,1)}, f32[16,128]{1,0:T(8,128)S(1)}) custom-call(s32[1]{0:T(128)} %bitcast.place, bf16[128,2048]{1,0:T(8,128)(2,1)S(1)} %copy-done, ...), custom_call_target="tpu_custom_call", output_to_operand_aliasing={{0}: (21, {}), {1}: (22, {}), {2}: (23, {}), {3}: (24, {})} | custom-call | flops 1 | bytes 1 | tf_op jit(solution)/shard_map/last_use/pallas_call | solution.py:962
  48.7 0.8 %gather.1 = (f32[11,16,128]{2,1,0:T(8,128)}, f32[16,128]{1,0:T(8,128)}) custom-call(s32[1]{0:T(128)} %bitcast.place, f32[64,128]{1,0:T(8,128)S(1)} %get-tuple-element.101.rest_4_.pair_rows, f32[8,4,128]{2,1,0:T(4,128)S(1)} %get-tuple-element.148.rest_0_, f32[8,4,128]{2,1,0:T(4,128)S(1)} %get-tuple-element.149.rest_1_, ...), custom_call_target="tpu_custom_call" | custom-call | flops 1 | bytes 1 | tf_op jit(solution)/shard_map/gather/pallas_call | solution.py:1004
  (1 shorter events, 0.0 us)
Async XLA Ops:
  0.6 3.5 %copy-start.6 = (f32[16,128]{1,0:T(8,128)S(1)}, f32[16,128]{1,0:T(8,128)}, u32[]{:S(2)}) copy-start(f32[16,128]{1,0:T(8,128)} %decay.35) | copy-start | bytes 24580
  0.6 3.5 %copy-start = (bf16[128,2048]{1,0:T(8,128)(2,1)S(1)}, bf16[128,2048]{1,0:T(8,128)(2,1)}, u32[]{:S(2)}) copy-start(bf16[128,2048]{1,0:T(8,128)(2,1)} %query.29) | copy-start | bytes 1572868
  0.7 3.5 %copy-start.1 = (bf16[128,2048]{1,0:T(8,128)(2,1)S(1)}, bf16[128,2048]{1,0:T(8,128)(2,1)}, u32[]{:S(2)}) copy-start(bf16[128,2048]{1,0:T(8,128)(2,1)} %key.29) | copy-start | bytes 1572868
  0.7 3.5 %copy-start.2 = (bf16[128,2048]{1,0:T(8,128)(2,1)S(1)}, bf16[128,2048]{1,0:T(8,128)(2,1)}, u32[]{:S(2)}) copy-start(bf16[128,2048]{1,0:T(8,128)(2,1)} %value.29) | copy-start | bytes 1572868
  0.7 3.5 %copy-start.5 = (f32[11,16,128]{2,1,0:T(8,128)S(1)}, f32[11,16,128]{2,1,0:T(8,128)}, u32[]{:S(2)}) copy-start(f32[11,16,128]{2,1,0:T(8,128)} %gain.29) | copy-start | bytes 270340
  4.0 3.8 %collective-permute-start = (f32[1040,128]{1,0:T(8,128)}, f32[1040,128]{1,0:T(8,128)S(1)}, u32[]{:S(2)}, u32[]{:S(2)}) collective-permute-start(f32[1040,128]{1,0:T(8,128)} %get-tuple-element.83), channel_id=1, source_target_pairs={{0,1},{1,0},{2,3},{3,2},{4,5},{5,4},{6,7},{7,6},{8,9},{9,8},{10,11... | collective-permute-start | bytes 1597448 | tf_op jit(solution)/shard_map/ppermute | solution.py:771
  4.2 1.0 %copy-start.3 = (bf16[128,2048]{1,0:T(8,128)(2,1)S(1)}, bf16[128,2048]{1,0:T(8,128)(2,1)}, u32[]{:S(2)}) copy-start(bf16[128,2048]{1,0:T(8,128)(2,1)} %cotangent.29) | copy-start | bytes 1572868
  5.2 1.0 %copy-start.7 = (f32[1024,128]{1,0:T(8,128)S(1)}, f32[1024,128]{1,0:T(8,128)}, u32[]{:S(2)}) copy-start(f32[1024,128]{1,0:T(8,128)} %get-tuple-element.84.keep1.keep) | copy-start | bytes 1572868
  6.3 5.3 %copy-start.4 = (bf16[128,2048]{1,0:T(8,128)(2,1)S(1)}, bf16[128,2048]{1,0:T(8,128)(2,1)}, u32[]{:S(2)}) copy-start(bf16[128,2048]{1,0:T(8,128)(2,1)} %cotangent.29) | copy-start | bytes 1572868
  7.8 21.1 %collective-permute-start.5 = (f32[4096,128]{1,0:T(8,128)S(1)}, f32[4096,128]{1,0:T(8,128)S(1)}, u32[]{:S(2)}, u32[]{:S(2)}) collective-permute-start(f32[4096,128]{1,0:T(8,128)S(1)} %get-tuple-element.100), channel_id=1, source_target_pairs={{0,1},{1,0},{2,3},{3,2},{4,5},{5,4},{6,7},{7,6},{8,9},{9,8},{10,11... | collective-permute-start | bytes 6291464 | tf_op jit(solution)/shard_map/ppermute | solution.py:771
  8.3 10.0 %collective-permute-start.2 = (f32[1024,128]{1,0:T(8,128)S(1)}, f32[1024,128]{1,0:T(8,128)S(1)}, u32[]{:S(2)}, u32[]{:S(2)}) collective-permute-start(f32[1024,128]{1,0:T(8,128)S(1)} %get-tuple-element.88), channel_id=1, source_target_pairs={{0,1},{1,0},{2,3},{3,2},{4,5},{5,4},{6,7},{7,6},{8,9},{9,8},{10,11... | collective-permute-start | bytes 1572872 | tf_op jit(solution)/shard_map/ppermute | solution.py:771
  8.7 9.6 %collective-permute-start.1 = (f32[528,128]{1,0:T(8,128)S(1)}, f32[528,128]{1,0:T(8,128)S(1)}, u32[]{:S(2)}, u32[]{:S(2)}) collective-permute-start(f32[528,128]{1,0:T(8,128)S(1)} %get-tuple-element.86), channel_id=1, source_target_pairs={{0,2},{1,3},{2,0},{3,1},{4,6},{5,7},{6,4},{7,5},{8,10},{9,11},{10,... | collective-permute-start | bytes 811016 | tf_op jit(solution)/shard_map/ppermute | solution.py:771
  11.5 12.4 %collective-permute-start.3 = (f32[512,128]{1,0:T(8,128)S(1)}, f32[512,128]{1,0:T(8,128)S(1)}, u32[]{:S(2)}, u32[]{:S(2)}) collective-permute-start(f32[512,128]{1,0:T(8,128)S(1)} %get-tuple-element.89.rest_0_), channel_id=1, source_target_pairs={{0,2},{1,3},{2,0},{3,1},{4,6},{5,7},{6,4},{7,5},{8,10},{9,11},{10,... | collective-permute-start | bytes 786440 | tf_op jit(solution)/shard_map/ppermute | solution.py:771
  18.6 6.5 %collective-permute-start.8 = (f32[512,128]{1,0:T(8,128)S(1)}, f32[512,128]{1,0:T(8,128)S(1)}, u32[]{:S(2)}, u32[]{:S(2)}) collective-permute-start(f32[512,128]{1,0:T(8,128)S(1)} %second_merge.2.after), channel_id=1, source_target_pairs={{2,4},{4,2},{3,5},{5,3},{6,6},{7,7},{10,12},{12,10},{11,13},{13,11... | collective-permute-start | bytes 786440 | tf_op jit(solution)/shard_map/ppermute | solution.py:771
  24.2 10.1 %collective-permute-start.4 = (f32[512,128]{1,0:T(8,128)S(1)}, f32[512,128]{1,0:T(8,128)S(1)}, u32[]{:S(2)}, u32[]{:S(2)}) collective-permute-start(f32[512,128]{1,0:T(8,128)S(1)} %second_merge.3.after), channel_id=1, source_target_pairs={{2,4},{4,2},{3,5},{5,3},{6,6},{7,7},{10,12},{12,10},{11,13},{13,11... | collective-permute-start | bytes 786440 | tf_op jit(solution)/shard_map/ppermute | solution.py:771
  25.1 11.4 %collective-permute-start.10 = (f32[512,128]{1,0:T(8,128)S(1)}, f32[512,128]{1,0:T(8,128)S(1)}, u32[]{:S(2)}, u32[]{:S(2)}) collective-permute-start(f32[512,128]{1,0:T(8,128)S(1)} %collective-permute-done.8.second), channel_id=1, source_target_pairs={{0,2},{1,3},{2,0},{3,1},{4,6},{5,7},{6,4},{7,5},{8,10},{9,11},{10,... | collective-permute-start | bytes 786440 | tf_op jit(solution)/shard_map/ppermute | solution.py:771
  32.4 4.5 %collective-permute-start.13 = (f32[512,128]{1,0:T(8,128)S(1)}, f32[512,128]{1,0:T(8,128)S(1)}, u32[]{:S(2)}, u32[]{:S(2)}) collective-permute-start(f32[512,128]{1,0:T(8,128)S(1)} %collective-permute-done.3.first), channel_id=1, source_target_pairs={{0,1},{1,0},{2,3},{3,2},{4,5},{5,4},{6,7},{7,6},{8,9},{9,8},{10,11... | collective-permute-start | bytes 786440 | tf_op jit(solution)/shard_map/ppermute | solution.py:771
  34.2 7.7 %collective-permute-start.12 = (f32[528,128]{1,0:T(8,128)S(1)}, f32[528,128]{1,0:T(8,128)S(1)}, u32[]{:S(2)}, u32[]{:S(2)}) collective-permute-start(f32[528,128]{1,0:T(8,128)S(1)} %collective-permute-done.1.first.chip_total), channel_id=1, source_target_pairs={{0,1},{1,0},{2,3},{3,2},{4,5},{5,4},{6,7},{7,6},{8,9},{9,8},{10,11... | collective-permute-start | bytes 811016 | tf_op jit(solution)/shard_map/ppermute | solution.py:771
  34.3 7.6 %collective-permute-start.9 = (f32[512,128]{1,0:T(8,128)S(1)}, f32[512,128]{1,0:T(8,128)S(1)}, u32[]{:S(2)}, u32[]{:S(2)}) collective-permute-start(f32[512,128]{1,0:T(8,128)S(1)} %collective-permute-done.8.second), channel_id=1, source_target_pairs={{0,1},{1,0},{2,3},{3,2},{4,5},{5,4},{6,7},{7,6},{8,9},{9,8},{10,11... | collective-permute-start | bytes 786440 | tf_op jit(solution)/shard_map/ppermute | solution.py:771
  36.3 4.9 %collective-permute-start.6 = (f32[512,128]{1,0:T(8,128)S(1)}, f32[512,128]{1,0:T(8,128)S(1)}, u32[]{:S(2)}, u32[]{:S(2)}) collective-permute-start(f32[512,128]{1,0:T(8,128)S(1)} %collective-permute-done.4.rest_4_.second), channel_id=1, source_target_pairs={{0,1},{1,0},{2,3},{3,2},{4,5},{5,4},{6,7},{7,6},{8,9},{9,8},{10,11... | collective-permute-start | bytes 786440 | tf_op jit(solution)/shard_map/ppermute | solution.py:771
  36.5 6.1 %collective-permute-start.11 = (f32[512,128]{1,0:T(8,128)S(1)}, f32[512,128]{1,0:T(8,128)S(1)}, u32[]{:S(2)}, u32[]{:S(2)}) collective-permute-start(f32[512,128]{1,0:T(8,128)S(1)} %collective-permute-done.10.third), channel_id=1, source_target_pairs={{0,1},{1,0},{2,3},{3,2},{4,5},{5,4},{6,7},{7,6},{8,9},{9,8},{10,11... | collective-permute-start | bytes 786440 | tf_op jit(solution)/shard_map/ppermute | solution.py:771
  36.9 7.9 %collective-permute-start.7 = (f32[512,128]{1,0:T(8,128)S(1)}, f32[512,128]{1,0:T(8,128)S(1)}, u32[]{:S(2)}, u32[]{:S(2)}) collective-permute-start(f32[512,128]{1,0:T(8,128)S(1)} %collective-permute-done.4.rest_4_.second), channel_id=1, source_target_pairs={{0,2},{1,3},{2,0},{3,1},{4,6},{5,7},{6,4},{7,5},{8,10},{9,11},{10,... | collective-permute-start | bytes 786440 | tf_op jit(solution)/shard_map/ppermute | solution.py:771
  44.8 2.4 %collective-permute-start.14 = (f32[512,128]{1,0:T(8,128)S(1)}, f32[512,128]{1,0:T(8,128)S(1)}, u32[]{:S(2)}, u32[]{:S(2)}) collective-permute-start(f32[512,128]{1,0:T(8,128)S(1)} %collective-permute-done.7.third), channel_id=1, source_target_pairs={{0,1},{1,0},{2,3},{3,2},{4,5},{5,4},{6,7},{7,6},{8,9},{9,8},{10,11... | collective-permute-start | bytes 786440 | tf_op jit(solution)/shard_map/ppermute | solution.py:771

commit v3 on v2

--- a/solution.py
+++ b/solution.py
@@ -324,11 +324,16 @@
         )
 
 
+def second_core(position):
+    return jnp.bitwise_xor(position % 2, (position // 2 == 3).astype(jnp.int32))
+
+
 def second_export_kernel(
-    place, query, key, value, cotangent, gain, decay, keep1, send, keep, bundle
+    place, query, key, value, cotangent, gain, decay, keep1, after, *outs
 ):
+    *sends, keep, bundle = outs
     position = place[0]
-    core = position % 2
+    core = second_core(position)
     chip = position // 2
     heads, tok = decay.shape
     dim = query.shape[1] // heads
@@ -338,14 +343,13 @@
     lift = jnp.exp(running)
     fall = jnp.exp(last_lane(running) - running)
     state2 = chip == 1
-    state0 = core == 0
+    state0 = position % 2 == 0
     weight2 = jnp.where(state2, fall, jnp.where(chip == 2, gain[cross + 2], gain[cross + 1]) * lift)
     weight2 = jnp.where(chip == 0, 0.0, weight2)
     weight0 = jnp.where(state0, fall, gain[cross] * lift)
-    spread = columns(
-        jnp.concatenate([half_first(w, 1 - core) for w in (weight2, weight0)], axis=0)
-    )
+    spread = columns(jnp.concatenate([half_first(weight2, 1 - core), weight0], axis=0))
     bundle[pl.ds(heads * dim, half * dim), :] = keep1[...]
+    count = half // len(sends)
     for index in range(heads):
         mine = index >= half
         head = (core if mine else 1 - core) * half + index % half
@@ -353,14 +357,18 @@
         second = outer_products(
             jnp.where(state2, k, q), jnp.where(state2, v, o), spread[:, index : index + 1]
         )
-        rows = pl.ds(index % half * dim, dim)
-        (keep if mine else send)[rows, :] = second
         if mine:
+            keep[pl.ds(index % half * dim, dim), :] = second
             bundle[pl.ds((heads + index) * dim, dim), :] = second
-        bundle[pl.ds(pl.multiple_of(head * dim, dim), dim), :] = outer_products(
+        else:
+            sends[index // count][pl.ds(index % count * dim, dim), :] = second
+    for head in range(heads):
+        lanes = slice(head * dim, (head + 1) * dim)
+        q, k, v, o = (ref[:, lanes] for ref in (query, key, value, cotangent))
+        bundle[pl.ds(head * dim, dim), :] = outer_products(
             jnp.where(state0, k, q),
             jnp.where(state0, v, o),
-            spread[:, heads + index : heads + index + 1],
+            spread[:, heads + head : heads + head + 1],
         )
 
 
@@ -373,7 +381,7 @@
     )
 
 
-def first_merge_kernel(place, decay, keep, got, after, *outs):
+def first_merge_kernel(place, decay, keep, got, *outs):
     position = place[0]
     chip = position // 2
     heads, tok = decay.shape
@@ -396,7 +404,8 @@
     outs[0][pl.ds(count * dim, heads), :] = own_total + other_total
 
 
-def second_merge_kernel(part, place, decay, other_total, keep, got, first, after, out):
+def second_merge_kernel(part, place, decay, other_total, keep, got, first, *rest):
+    out = rest[-1]
     position = place[0]
     chip = position // 2
     heads, tok = decay.shape
@@ -409,7 +418,7 @@
     inner = (chip == 1) | (chip == 2)
     first_factor = jnp.where(inner, jnp.exp(own_total + other_total), 0.0)
     own_factor, other_factor, first_factor = (
-        half_first(factor, position % 2)[part * count : (part + 1) * count]
+        half_first(factor, second_core(position))[part * count : (part + 1) * count]
         for factor in (own_factor, other_factor, first_factor)
     )
     for index in range(count):
@@ -545,7 +554,8 @@
     first,
     second,
     pair1,
-    pair2,
+    pair2_got,
+    pair2_kept,
     level0,
     out_left,
     out_right,
@@ -586,7 +596,8 @@
         one = slice(index, index + 1)
         q, k, v, o = (ref[:, lanes] for ref in (query, key, value, cotangent))
         state = jnp.where(chip == 2, second[rows, :], first[rows, :])
-        partner = jnp.where(odd, level0[rows, :], jnp.where(chip == 1, pair1[rows, :], pair2[rows, :]))
+        pair2 = jnp.where((chip == 3) == mine, pair2_kept[rows, :], pair2_got[rows, :])
+        partner = jnp.where(odd, level0[rows, :], jnp.where(chip == 1, pair1[rows, :], pair2))
         flows.append(
             pair_flow[one] * jnp.sum(state * partner, axis=0, keepdims=True)
             + chip_flow[one] * jnp.sum(first[rows, :] * second[rows, :], axis=0, keepdims=True)
@@ -739,15 +750,15 @@
     return pl.BlockSpec(shape, lambda g, place: (0,) * len(shape))
 
 
-FIRST_EXPORTS_COST = 1
-FIRST_MERGE_COST = 1
-SECOND_EXPORTS_COST = 1
-LOCAL_COST = 1
-SECOND_MERGE_COST = 1
-PAIR_USE_COST = 1
-FIRST_USE_COST = 1
-LAST_USE_COST = 1
-GATHER_COST = 1
+FIRST_EXPORTS_COST = 52800000000
+FIRST_MERGE_COST = 4800000000
+SECOND_EXPORTS_COST = 1500000000
+LOCAL_COST = (1570000000, 1570000000, 25120000000, 25120000000)
+SECOND_MERGE_COST = 4800000000
+PAIR_USE_COST = 28800000000
+FIRST_USE_COST = 10720000000
+LAST_USE_COST = 24000000000
+GATHER_COST = 12800000000
 
 
 def cost(flops):
@@ -765,7 +776,7 @@
     tokens = (queries, keys_in, value_input, out_grad)
     core_swap = [(at, at ^ 1) for at in range(8)]
     side_swap = [(at, at ^ 2) for at in range(8)]
-    middle_swap = [(2, 4), (4, 2), (3, 5), (5, 3), (6, 6), (7, 7)]
+    middle_swap = [(0, 1), (1, 0), (2, 4), (4, 2), (3, 5), (5, 3), (6, 7), (7, 6)]
 
     def swap(block, route):
         return lax.ppermute(block, "ctx", route)
@@ -787,30 +798,17 @@
         name="first_exports",
     )(place, *tokens, level_gain, decay_log)
     got1 = swap(send1, core_swap)
-    send2, keep2, bundle = pl.pallas_call(
-        second_export_kernel,
-        out_shape=(sds(half_rows, dim), sds(half_rows, dim), sds(4 * half_rows, dim)),
-        in_specs=[SCALAR] + [pl.BlockSpec()] * 7,
-        compiler_params=params(),
-
-        cost_estimate=cost(SECOND_EXPORTS_COST),
-        name="second_exports",
-    )(place, *tokens, level_gain, decay_log, keep1)
     first_sent = pl.pallas_call(
         first_merge_kernel,
         out_shape=tuple(
             sds(part_rows + (heads if part == 0 else 0), dim) for part in range(CHUNKS)
         ),
-        in_specs=[SCALAR] + [pl.BlockSpec()] * 3 + [ANYWHERE],
+        in_specs=[SCALAR] + [pl.BlockSpec()] * 3,
         compiler_params=params(),
         cost_estimate=cost(FIRST_MERGE_COST),
         name="first_merge",
-    )(place, decay_log, keep1, got1, keep2)
+    )(place, decay_log, keep1, got1)
     first = [swap(block, side_swap) for block in first_sent]
-
-    got2 = swap(after(send2, got1), core_swap)
-    front = swap(after(bundle, got1), core_swap)
-
 
     inner = tok.bit_length()
     groups = 2 * CHUNKS
@@ -835,11 +833,33 @@
             input_output_aliases={6 + at: at for at in range(len(before))},
             compiler_params=params(),
 
-            cost_estimate=cost(LOCAL_COST),
+            cost_estimate=cost(LOCAL_COST[number]),
             name="local",
         )(*tokens, level_gain, decay_log, *before, *after)
 
-    def second_merge(part, after):
+    gain_rows, decay_rows = [], []
+    acc = ()
+
+    def more_local(number, *others):
+        *done, gains, decays = local(number, acc, others)
+        gain_rows.append(gains)
+        decay_rows.append(decays)
+        return done
+
+    acc = more_local(0, first_sent[-1])
+    *send2, keep2, bundle = pl.pallas_call(
+        second_export_kernel,
+        out_shape=(sds(part_rows, dim),) * CHUNKS + (sds(half_rows, dim), sds(4 * half_rows, dim)),
+        in_specs=[SCALAR] + [pl.BlockSpec()] * 7 + [ANYWHERE],
+        compiler_params=params(),
+
+        cost_estimate=cost(SECOND_EXPORTS_COST),
+        name="second_exports",
+    )(place, *tokens, level_gain, decay_log, keep1, decay_rows[0])
+    got2 = [swap(block, core_swap) for block in send2]
+
+
+    def second_merge(part, *after):
         chunk = pl.BlockSpec((part_rows, dim), lambda g: (part, 0))
         start = pl.BlockSpec((part_rows, dim), lambda g: (0, 0))
         return pl.pallas_call(
@@ -851,30 +871,23 @@
                 pl.BlockSpec(decay_log.shape, lambda g: (0, 0)),
                 pl.BlockSpec((heads, dim), lambda g: (half_rows // heads, 0)),
                 chunk,
-                chunk,
                 start,
-                ANYWHERE,
-            ],
+                start,
+            ]
+            + [ANYWHERE] * len(after),
             out_specs=start,
             compiler_params=params(),
             cost_estimate=cost(SECOND_MERGE_COST),
             name="second_merge",
-        )(place, decay_log, got1, keep2, got2, first[part], after)
-
-    gain_rows, decay_rows = [], []
-    acc = ()
-
-    def more_local(number, *others):
-        *done, gains, decays = local(number, acc, others)
-        gain_rows.append(gains)
-        decay_rows.append(decays)
-        return done
-
-    acc = more_local(0, first_sent[-1])
-    acc = more_local(1)
-    sent = [second_merge(0, decay_rows[-1])]
-    sent.append(second_merge(1, sent[0]))
+        )(place, decay_log, got1, keep2, got2[part], first[part], *after)
+
+    acc = more_local(1, keep2)
+    sent = [second_merge(0, decay_rows[1], *got2[1:])]
+    acc = more_local(2, sent[0])
+    sent.append(second_merge(1, decay_rows[2]))
+    front = swap(after(bundle, sent[1]), core_swap)
     second = [swap(block, middle_swap) for block in sent]
+    acc = more_local(3, second[0])
     left0, right0, pair_rows = pl.pallas_call(
         pair_kernel,
         grid=(1,),
@@ -886,17 +899,15 @@
 
         cost_estimate=cost(PAIR_USE_COST),
         name="pair_use",
-    )(place, *tokens, level_gain, decay_log, front, sent[1])
+    )(place, *tokens, level_gain, decay_log, front, decay_rows[3])
 
     third = [swap(second[0], side_swap)]
-    acc = more_local(2, pair_rows)
-    first_over = [swap(after(block, decay_rows[2]), core_swap) for block in first]
-    second_over = [swap(after(second[0], decay_rows[2]), core_swap)]
-    second[1] = after(second[1], decay_rows[2])
+    first_over = [swap(after(block, pair_rows), core_swap) for block in first]
+    second_over = [swap(after(second[0], pair_rows), core_swap)]
+    second[1] = after(second[1], pair_rows)
     third.append(swap(second[1], side_swap))
-    acc = more_local(3, second[1])
-    second_over.append(swap(after(second[1], decay_rows[3]), core_swap))
-    third_over = [swap(after(third[0], decay_rows[3]), core_swap)]
+    second_over.append(swap(second[1], core_swap))
+    third_over = [swap(after(third[0], pair_rows), core_swap)]
 
     def side_specs(part, mine):
         def block(place):
@@ -907,12 +918,10 @@
         level0 = pl.BlockSpec((part_rows, dim), lambda g, place: (block(place), 0))
         half_lanes = pl.BlockSpec((tok, part_rows), lambda g, place: (0, 0))
         start = pl.BlockSpec((part_rows, dim), lambda g, place: (0, 0))
-        if mine:
-            pair1 = pair2 = pl.BlockSpec((part_rows, dim), lambda g, place: (part, 0))
-        else:
-            pair2 = pl.BlockSpec((part_rows, dim), lambda g, place: (2 * groups - groups // 2 + part, 0))
-            pair1 = pl.BlockSpec((part_rows, dim), lambda g, place: (groups + part, 0))
-        return lanes, level0, half_lanes, start, pair1, pair2
+        pair_got = pl.BlockSpec((part_rows, dim), lambda g, place: (part, 0))
+        pair1 = pl.BlockSpec((part_rows, dim), lambda g, place: (groups + part, 0))
+        pair2 = pl.BlockSpec((part_rows, dim), lambda g, place: (groups + CHUNKS + part, 0))
+        return lanes, level0, half_lanes, start, pair_got if mine else pair1, pair2
 
     small = [
         whole(level_gain.shape),
@@ -928,7 +937,7 @@
                 grid_spec=pltpu.PrefetchScalarGridSpec(
                     num_scalar_prefetch=1,
                     grid=(1,),
-                    in_specs=[lanes] * 4 + small + [start] * 2 + [pair1, pair2, level0],
+                    in_specs=[lanes] * 4 + small + [start] * 2 + [pair1, start, pair2, level0],
                     out_specs=(half_lanes,) * 2 + (whole((4 * count, tok)),),
                 ),
                 out_shape=(sds(tok, part_rows),) * 2 + (sds(4 * count, tok),),
@@ -945,7 +954,8 @@
                 (first if mine else first_over)[part],
                 (second if mine else second_over)[part],
                 got1 if mine else front,
-                got2 if mine else front,
+                got2[part],
+                front,
                 front,
             )
 

time: 49.8 us -> 45.6 us (0.916)
  waiting for transfers between devices: 8.85 us -> 5.05 us
  local copies, waits for them, and re-layouts: 2.1 us -> 1.09 us
  Pallas kernels: 23.5 us -> 24 us
    ppermute x15 -> x16, waiting for transfers between devices: 8.85 us -> 5.05 us  [swap(): return lax.ppermute(block, 'ctx', route)]
    unnamed x16 -> x24, local copies, waits for them, and re-layouts: 2.1 us -> 1.09 us
    ppermute x15 -> x16, starting transfers between devices: 14.2 us -> 14.3 us  [swap(): return lax.ppermute(block, 'ctx', route)]
  transfers between devices with their start and end apart: 15 -> 16, of which waited for: 3 -> 3; matrix products, arithmetic and copies ran while one was open for 0% -> 0% of each run, Pallas kernels for 36% -> 40%
where the time goes in v3:
time: 45.6 us; the launch traced here: 45.2 us
  Pallas kernels  24 us (53%)
  starting transfers between devices  14.3 us (31%)
  waiting for transfers between devices  5.05 us (11%)
  local copies, waits for them, and re-layouts  1.09 us (2%)
  between operations  0.84 us (2%)
    ppermute x16, starting transfers between devices, swap(): return lax.ppermute(block, 'ctx', route)  14.3 us
    pallas_call x4, Pallas kernels, line_device(): pl.pallas_call(functools.partial(last_use_kernel, part, mine), grid_spec=...  6.49 us
    pallas_call x4, Pallas kernels, local(): pl.pallas_call(functools.partial(local_kernel, number * count), grid=(1,)...  6.31 us
    ppermute x16, waiting for transfers between devices, swap(): return lax.ppermute(block, 'ctx', route)  5.05 us
    pallas_call x1, Pallas kernels, line_device(): pl.pallas_call(first_export_kernel, out_shape=(sds(half_rows + heads, dim...  3.28 us
    pallas_call x4, Pallas kernels, line_device(): pl.pallas_call(functools.partial(first_use_kernel, part, mine), grid_spec...  2.73 us
    pallas_call x1, Pallas kernels, line_device(): pl.pallas_call(pair_kernel, grid=(1,), out_shape=(sds(tok, heads * dim),)...  1.81 us
    pallas_call x1, Pallas kernels, line_device(): pl.pallas_call(second_export_kernel, out_shape=(sds(part_rows, dim),) * C...  1.63 us
  transfers between devices with their start and end apart: 16, of which 3 were waited for; matrix products, arithmetic and copies ran while one was open for 0% of the time, Pallas kernels for 40%

profile of v3, /device:TPU:1, one launch (start us, length us, event | category | flops | bytes accessed | tf_op | source)
XLA Modules:
  0.0 45.2 jit_solution(12090548141054137)
XLA Ops:
  0.6 0.0 copy-start.5
  0.6 3.3 %first_exports.1 = (f32[1040,128]{1,0:T(8,128)}, f32[1024,128]{1,0:T(8,128)}) custom-call(s32[1]{0:T(128)} %bitcast.place, bf16[128,2048]{1,0:T(8,128)(2,1)} %query.29, bf16[128,2048]{1,0:T(8,128)(2,1)} %key.29, bf16[128,2048]{1,0:T(8,128)(2,1)} %value.29, bf16[128,2048]{1,0:T(8,128)(2,1)} %cotangent.29, f32[11,16,128]{2,1,0:T(8,128)} %gain.29, f32[16,128]{1,0:T(8,128)} %decay.35), custom_call_target="tpu_custom_call" | custom-call | flops 52800000000 | bytes 1 | tf_op jit(solution)/shard_map/first_exports/pallas_call | solution.py:784
  3.9 0.1 collective-permute-start
  4.1 2.1 %collective-permute-done.got.other_total.pair1 = f32[1040,128]{1,0:T(8,128)S(1)} collective-permute-done((f32[1040,128]{1,0:T(8,128)}, f32[1040,128]{1,0:T(8,128)S(1)}, u32[]{:S(2)}, u32[]{:S(2)}) %collective-permute-start) | collective-permute-done | bytes 532512 | tf_op jit(solution)/shard_map/ppermute | solution.py:782
  6.1 0.0 copy-done.5
  6.1 1.0 %copy-done.6 = f32[1024,128]{1,0:T(8,128)S(1)} copy-done((f32[1024,128]{1,0:T(8,128)S(1)}, f32[1024,128]{1,0:T(8,128)}, u32[]{:S(2)}) %copy-start.6) | copy-done | bytes 524312
  7.2 0.0 copy-start.4
  7.2 0.3 first_merge.1
  7.5 2.5 %collective-permute-start.1 = (f32[528,128]{1,0:T(8,128)S(1)}, f32[528,128]{1,0:T(8,128)S(1)}, u32[]{:S(2)}, u32[]{:S(2)}) collective-permute-start(f32[528,128]{1,0:T(8,128)S(1)} %get-tuple-element.84), channel_id=1, source_target_pairs={{0,2},{1,3},{2,0},{3,1},{4,6},{5,7},{6,4},{7,5},{8,10},{9,11},{10,... | collective-permute-start | bytes 811016 | tf_op jit(solution)/shard_map/ppermute | solution.py:782
  10.0 0.0 copy-done
  10.0 0.0 copy-done.1
  10.0 0.0 copy-done.2
  10.0 0.0 copy-done.3
  10.0 0.0 copy-done.4
  10.0 0.0 copy-start.7
  10.1 1.6 %local.4 = (f32[128,2048]{1,0:T(8,128)S(1)}, f32[128,2048]{1,0:T(8,128)S(1)}, f32[128,2048]{1,0:T(8,128)S(1)}, f32[128,2048]{1,0:T(8,128)S(1)}, f32[8,4,128]{2,1,0:T(4,128)S(1)}, /*index=5*/f32[4,128]{1,0:T(4,128)S(1)}) custom-call(bf16[128,2048]{1,0:T(8,128)(2,1)S(1)} %copy-done, bf16[128,2048]{1,0:T(8,128)(2,1)S(1)} %copy-done.1, ...), custom_call_target="tpu_custom_call" | custom-call | flops 1570000000 | bytes 1 | tf_op jit(solution)/shard_map/local/pallas_call | solution.py:818
  11.6 0.0 copy-start.8
  11.7 0.0 copy-done.7
  11.7 1.6 %second_exports.1 = (f32[512,128]{1,0:T(8,128)S(1)}, f32[512,128]{1,0:T(8,128)S(1)}, f32[1024,128]{1,0:T(8,128)S(1)}, f32[4096,128]{1,0:T(8,128)S(1)}) custom-call(s32[1]{0:T(128)} %bitcast.place, bf16[128,2048]{1,0:T(8,128)(2,1)S(1)} %copy-done, bf16[128,2048]{1,0:T(8,128)(2,1)S(1)} %copy-done.1, bf16[128,2048]{1,0:T(8,128)(2,1)S(1)} %copy-done.2, ...), custom_call_target="tpu_custom_call" | custom-call | flops 1500000000 | bytes 1 | tf_op jit(solution)/shard_map/second_exports/pallas_call | solution.py:850
  13.3 0.7 %collective-permute-start.2 = (f32[512,128]{1,0:T(8,128)S(1)}, f32[512,128]{1,0:T(8,128)S(1)}, u32[]{:S(2)}, u32[]{:S(2)}) collective-permute-start(f32[512,128]{1,0:T(8,128)S(1)} %get-tuple-element.88), channel_id=1, source_target_pairs={{0,1},{1,0},{2,3},{3,2},{4,5},{5,4},{6,7},{7,6},{8,9},{9,8},{10,11... | collective-permute-start | bytes 786440 | tf_op jit(solution)/shard_map/ppermute | solution.py:782
  14.0 0.1 collective-permute-start.4
  14.1 0.9 %collective-permute-start.3 = (f32[512,128]{1,0:T(8,128)S(1)}, f32[512,128]{1,0:T(8,128)S(1)}, u32[]{:S(2)}, u32[]{:S(2)}) collective-permute-start(f32[512,128]{1,0:T(8,128)S(1)} %get-tuple-element.85.rest_0_), channel_id=1, source_target_pairs={{0,2},{1,3},{2,0},{3,1},{4,6},{5,7},{6,4},{7,5},{8,10},{9,11},{10,... | collective-permute-start | bytes 786440 | tf_op jit(solution)/shard_map/ppermute | solution.py:782
  15.0 1.6 %local.5 = (f32[128,2048]{1,0:T(8,128)S(1)}, f32[128,2048]{1,0:T(8,128)S(1)}, f32[128,2048]{1,0:T(8,128)S(1)}, f32[128,2048]{1,0:T(8,128)S(1)}, f32[8,4,128]{2,1,0:T(4,128)S(1)}, /*index=5*/f32[4,128]{1,0:T(4,128)S(1)}) custom-call(bf16[128,2048]{1,0:T(8,128)(2,1)S(1)} %copy-done, ...), custom_call_target="tpu_custom_call", output_to_operand_aliasing={{0}: (6, {}), {1}: (7, {}), {2}: (8, {}), {3}: (9, {})} | custom-call | flops 1570000000 | bytes 1 | tf_op jit(solution)/shard_map/local/pallas_call | solution.py:818
  16.6 0.0 collective-permute-done.2.rest_1_.got.pair2_got
  16.6 0.0 collective-permute-done.4.got.pair2_got
  16.6 0.0 collective-permute-done.1.first.chip_total
  16.6 0.3 second_merge.2.rest_4_
  16.9 1.1 %collective-permute-start.7 = (f32[512,128]{1,0:T(8,128)S(1)}, f32[512,128]{1,0:T(8,128)S(1)}, u32[]{:S(2)}, u32[]{:S(2)}) collective-permute-start(f32[512,128]{1,0:T(8,128)S(1)} %second_merge.2.rest_4_), channel_id=1, source_target_pairs={{0,1},{1,0},{2,4},{4,2},{3,5},{5,3},{6,7},{7,6},{8,9},{9,8},{10,12... | collective-permute-start | bytes 786440 | tf_op jit(solution)/shard_map/ppermute | solution.py:782
  18.0 1.6 %local.6 = (f32[128,2048]{1,0:T(8,128)S(1)}, f32[128,2048]{1,0:T(8,128)S(1)}, f32[128,2048]{1,0:T(8,128)S(1)}, f32[128,2048]{1,0:T(8,128)S(1)}, f32[8,4,128]{2,1,0:T(4,128)S(1)}, /*index=5*/f32[4,128]{1,0:T(4,128)S(1)}) custom-call(bf16[128,2048]{1,0:T(8,128)(2,1)S(1)} %copy-done, ...), custom_call_target="tpu_custom_call", output_to_operand_aliasing={{0}: (6, {}), {1}: (7, {}), {2}: (8, {}), {3}: (9, {})} | custom-call | flops 25120000000 | bytes 1 | tf_op jit(solution)/shard_map/local/pallas_call | solution.py:818
  19.6 0.0 copy-start.10
  19.6 2.5 %collective-permute-done.3.first = f32[512,128]{1,0:T(8,128)S(1)} collective-permute-done((f32[512,128]{1,0:T(8,128)S(1)}, f32[512,128]{1,0:T(8,128)S(1)}, u32[]{:S(2)}, u32[]{:S(2)}) %collective-permute-start.3) | collective-permute-done | bytes 262176 | tf_op jit(solution)/shard_map/ppermute | solution.py:782
  22.1 0.3 second_merge.3
  22.4 1.1 %collective-permute-start.5 = (f32[512,128]{1,0:T(8,128)S(1)}, f32[512,128]{1,0:T(8,128)S(1)}, u32[]{:S(2)}, u32[]{:S(2)}) collective-permute-start(f32[512,128]{1,0:T(8,128)S(1)} %second_merge.3), channel_id=1, source_target_pairs={{0,1},{1,0},{2,4},{4,2},{3,5},{5,3},{6,7},{7,6},{8,9},{9,8},{10,12... | collective-permute-start | bytes 786440 | tf_op jit(solution)/shard_map/ppermute | solution.py:782
  23.5 0.1 collective-permute-start.6
  23.5 0.0 collective-permute-done.7.rest_4_.second
  23.5 2.9 %collective-permute-start.11 = (f32[512,128]{1,0:T(8,128)S(1)}, f32[512,128]{1,0:T(8,128)S(1)}, u32[]{:S(2)}, u32[]{:S(2)}) collective-permute-start(f32[512,128]{1,0:T(8,128)S(1)} %collective-permute-done.7.rest_4_.second), channel_id=1, source_target_pairs={{0,2},{1,3},{2,0},{3,1},{4,6},{5,7},{6,4},{7,5},{8,10},{9,11},{10,... | collective-permute-start | bytes 786440 | tf_op jit(solution)/shard_map/ppermute | solution.py:782
  26.5 1.6 %local.7 = (f32[128,2048]{1,0:T(8,128)S(1)}, f32[128,2048]{1,0:T(8,128)S(1)}, f32[128,2048]{1,0:T(8,128)S(1)}, f32[128,2048]{1,0:T(8,128)S(1)}, f32[8,4,128]{2,1,0:T(4,128)S(1)}, /*index=5*/f32[4,128]{1,0:T(4,128)S(1)}) custom-call(bf16[128,2048]{1,0:T(8,128)(2,1)S(1)} %copy-done, ...), custom_call_target="tpu_custom_call", output_to_operand_aliasing={{0}: (6, {}), {1}: (7, {}), {2}: (8, {}), {3}: (9, {})} | custom-call | flops 25120000000 | bytes 1 | tf_op jit(solution)/shard_map/local/pallas_call | solution.py:818
  28.1 0.0 collective-permute-done.6.level0.pair1.pair2_kept
  28.1 1.8 %pair_use.1 = (f32[128,2048]{1,0:T(8,128)S(1)}, f32[128,2048]{1,0:T(8,128)S(1)}, f32[64,128]{1,0:T(8,128)S(1)}) custom-call(s32[1]{0:T(128)} %bitcast.place, bf16[128,2048]{1,0:T(8,128)(2,1)S(1)} %copy-done, bf16[128,2048]{1,0:T(8,128)(2,1)S(1)} %copy-done.1, bf16[128,2048]{1,0:T(8,128)(2,1)S(1)} %copy-done.2, bf16[128,2048]{1,0:T(8,128)(2,1)S(1)} %copy-done.3, ...), custom_call_target="tpu_custom_call" | custom-call | flops 28800000000 | bytes 1 | tf_op jit(solution)/shard_map/pair_use/pallas_call | solution.py:891
  29.9 0.0 collective-permute-done.5.second
  29.9 0.7 %collective-permute-start.8 = (f32[512,128]{1,0:T(8,128)S(1)}, f32[512,128]{1,0:T(8,128)S(1)}, u32[]{:S(2)}, u32[]{:S(2)}) collective-permute-start(f32[512,128]{1,0:T(8,128)S(1)} %collective-permute-done.5.second), channel_id=1, source_target_pairs={{0,1},{1,0},{2,3},{3,2},{4,5},{5,4},{6,7},{7,6},{8,9},{9,8},{10,11... | collective-permute-start | bytes 786440 | tf_op jit(solution)/shard_map/ppermute | solution.py:782
  30.6 2.0 %collective-permute-start.9 = (f32[512,128]{1,0:T(8,128)S(1)}, f32[512,128]{1,0:T(8,128)S(1)}, u32[]{:S(2)}, u32[]{:S(2)}) collective-permute-start(f32[512,128]{1,0:T(8,128)S(1)} %collective-permute-done.5.second), channel_id=1, source_target_pairs={{0,2},{1,3},{2,0},{3,1},{4,6},{5,7},{6,4},{7,5},{8,10},{9,11},{10,... | collective-permute-start | bytes 786440 | tf_op jit(solution)/shard_map/ppermute | solution.py:782
  32.6 0.3 collective-permute-start.10
  32.9 0.0 collective-permute-done.11.third
  32.9 0.8 %collective-permute-start.12 = (f32[512,128]{1,0:T(8,128)S(1)}, f32[512,128]{1,0:T(8,128)S(1)}, u32[]{:S(2)}, u32[]{:S(2)}) collective-permute-start(f32[512,128]{1,0:T(8,128)S(1)} %collective-permute-done.11.third), channel_id=1, source_target_pairs={{0,1},{1,0},{2,3},{3,2},{4,5},{5,4},{6,7},{7,6},{8,9},{9,8},{10,11... | collective-permute-start | bytes 786440 | tf_op jit(solution)/shard_map/ppermute | solution.py:782
  33.7 0.0 collective-permute-start.14
  33.7 0.7 %first_use.5 = (f32[128,512]{1,0:T(8,128)S(1)}, f32[128,512]{1,0:T(8,128)S(1)}, f32[16,128]{1,0:T(8,128)S(1)}) custom-call(s32[1]{0:T(128)} %bitcast.place, bf16[128,2048]{1,0:T(8,128)(2,1)S(1)} %copy-done, bf16[128,2048]{1,0:T(8,128)(2,1)S(1)} %copy-done.1, bf16[128,2048]{1,0:T(8,128)(2,1)S(1)} %copy-done.2, bf16[128,2048]{1,0:T(8,128)(2,1)S(1)} %copy-done.3, ...), custom_call_target="tpu_custom_call" | custom-call | flops 10720000000 | bytes 1 | tf_op jit(solution)/shard_map/first_use/pallas_call | solution.py:935
  34.4 1.8 %last_use.4 = (bf16[128,2048]{1,0:T(8,128)(2,1)}, bf16[128,2048]{1,0:T(8,128)(2,1)}, bf16[128,2048]{1,0:T(8,128)(2,1)}, bf16[128,2048]{1,0:T(8,128)(2,1)}, f32[16,128]{1,0:T(8,128)S(1)}) custom-call(s32[1]{0:T(128)} %bitcast.place, bf16[128,2048]{1,0:T(8,128)(2,1)S(1)} %copy-done, bf16[128,2048]{1,0:T(8,128)(2,1)S(1)} %copy-done.1, ...), custom_call_target="tpu_custom_call" | custom-call | flops 24000000000 | bytes 1 | tf_op jit(solution)/shard_map/last_use/pallas_call | solution.py:972
  36.2 0.7 %first_use.6 = (f32[128,512]{1,0:T(8,128)S(1)}, f32[128,512]{1,0:T(8,128)S(1)}, f32[16,128]{1,0:T(8,128)S(1)}) custom-call(s32[1]{0:T(128)} %bitcast.place, bf16[128,2048]{1,0:T(8,128)(2,1)S(1)} %copy-done, bf16[128,2048]{1,0:T(8,128)(2,1)S(1)} %copy-done.1, bf16[128,2048]{1,0:T(8,128)(2,1)S(1)} %copy-done.2, bf16[128,2048]{1,0:T(8,128)(2,1)S(1)} %copy-done.3, ...), custom_call_target="tpu_custom_call" | custom-call | flops 10720000000 | bytes 1 | tf_op jit(solution)/shard_map/first_use/pallas_call | solution.py:935
  36.9 0.0 collective-permute-done.8.second
  36.9 0.6 %collective-permute-start.13 = (f32[528,128]{1,0:T(8,128)S(1)}, f32[528,128]{1,0:T(8,128)S(1)}, u32[]{:S(2)}, u32[]{:S(2)}) collective-permute-start(f32[528,128]{1,0:T(8,128)S(1)} %collective-permute-done.1.first.chip_total), channel_id=1, source_target_pairs={{0,1},{1,0},{2,3},{3,2},{4,5},{5,4},{6,7},{7,6},{8,9},{9,8},{10,11... | collective-permute-start | bytes 811016 | tf_op jit(solution)/shard_map/ppermute | solution.py:782
  37.4 0.0 collective-permute-done.14.first
  37.4 0.7 %first_use.7 = (f32[128,512]{1,0:T(8,128)S(1)}, f32[128,512]{1,0:T(8,128)S(1)}, f32[16,128]{1,0:T(8,128)S(1)}) custom-call(s32[1]{0:T(128)} %bitcast.place, bf16[128,2048]{1,0:T(8,128)(2,1)S(1)} %copy-done, bf16[128,2048]{1,0:T(8,128)(2,1)S(1)} %copy-done.1, bf16[128,2048]{1,0:T(8,128)(2,1)S(1)} %copy-done.2, bf16[128,2048]{1,0:T(8,128)(2,1)S(1)} %copy-done.3, ...), custom_call_target="tpu_custom_call" | custom-call | flops 10720000000 | bytes 1 | tf_op jit(solution)/shard_map/first_use/pallas_call | solution.py:935
  38.1 0.0 collective-permute-done.10.second
  38.1 0.5 %collective-permute-done.13.first = f32[528,128]{1,0:T(8,128)S(1)} collective-permute-done((f32[528,128]{1,0:T(8,128)S(1)}, f32[528,128]{1,0:T(8,128)S(1)}, u32[]{:S(2)}, u32[]{:S(2)}) %collective-permute-start.13) | collective-permute-done | bytes 270368 | tf_op jit(solution)/shard_map/ppermute | solution.py:782
  38.6 0.7 %first_use.4 = (f32[128,512]{1,0:T(8,128)S(1)}, f32[128,512]{1,0:T(8,128)S(1)}, f32[16,128]{1,0:T(8,128)S(1)}) custom-call(s32[1]{0:T(128)} %bitcast.place, bf16[128,2048]{1,0:T(8,128)(2,1)S(1)} %copy-done, bf16[128,2048]{1,0:T(8,128)(2,1)S(1)} %copy-done.1, bf16[128,2048]{1,0:T(8,128)(2,1)S(1)} %copy-done.2, bf16[128,2048]{1,0:T(8,128)(2,1)S(1)} %copy-done.3, ...), custom_call_target="tpu_custom_call" | custom-call | flops 10720000000 | bytes 1 | tf_op jit(solution)/shard_map/first_use/pallas_call | solution.py:935
  39.3 0.0 collective-permute-done.12.third
  39.3 1.6 %last_use.5 = (bf16[128,2048]{1,0:T(8,128)(2,1)}, bf16[128,2048]{1,0:T(8,128)(2,1)}, bf16[128,2048]{1,0:T(8,128)(2,1)}, bf16[128,2048]{1,0:T(8,128)(2,1)}, f32[16,128]{1,0:T(8,128)S(1)}) custom-call(s32[1]{0:T(128)} %bitcast.place, bf16[128,2048]{1,0:T(8,128)(2,1)S(1)} %copy-done, ...), custom_call_target="tpu_custom_call", output_to_operand_aliasing={{0}: (21, {}), {1}: (22, {}), {2}: (23, {}), {3}: (24, {})} | custom-call | flops 24000000000 | bytes 1 | tf_op jit(solution)/shard_map/last_use/pallas_call | solution.py:972
  40.9 0.0 collective-permute-done.9.third
  40.9 0.4 collective-permute-start.15
  41.3 1.6 %last_use.6 = (bf16[128,2048]{1,0:T(8,128)(2,1)}, bf16[128,2048]{1,0:T(8,128)(2,1)}, bf16[128,2048]{1,0:T(8,128)(2,1)}, bf16[128,2048]{1,0:T(8,128)(2,1)}, f32[16,128]{1,0:T(8,128)S(1)}) custom-call(s32[1]{0:T(128)} %bitcast.place, bf16[128,2048]{1,0:T(8,128)(2,1)S(1)} %copy-done, ...), custom_call_target="tpu_custom_call", output_to_operand_aliasing={{0}: (21, {}), {1}: (22, {}), {2}: (23, {}), {3}: (24, {})} | custom-call | flops 24000000000 | bytes 1 | tf_op jit(solution)/shard_map/last_use/pallas_call | solution.py:972
  42.8 0.0 collective-permute-done.15.third
  42.8 1.6 %last_use.7 = (bf16[128,2048]{1,0:T(8,128)(2,1)}, bf16[128,2048]{1,0:T(8,128)(2,1)}, bf16[128,2048]{1,0:T(8,128)(2,1)}, bf16[128,2048]{1,0:T(8,128)(2,1)}, f32[16,128]{1,0:T(8,128)S(1)}) custom-call(s32[1]{0:T(128)} %bitcast.place, bf16[128,2048]{1,0:T(8,128)(2,1)S(1)} %copy-done, ...), custom_call_target="tpu_custom_call", output_to_operand_aliasing={{0}: (21, {}), {1}: (22, {}), {2}: (23, {}), {3}: (24, {})} | custom-call | flops 24000000000 | bytes 1 | tf_op jit(solution)/shard_map/last_use/pallas_call | solution.py:972
  44.4 0.8 %gather.1 = (f32[11,16,128]{2,1,0:T(8,128)}, f32[16,128]{1,0:T(8,128)}) custom-call(s32[1]{0:T(128)} %bitcast.place, f32[64,128]{1,0:T(8,128)S(1)} %get-tuple-element.107.pair_rows, f32[8,4,128]{2,1,0:T(4,128)S(1)} %get-tuple-element.147.rest_0_, f32[8,4,128]{2,1,0:T(4,128)S(1)} %get-tuple-element.148.rest_1_, f32[8,4,128]{2,1,0:T(4,128)S(1)} %get-tuple-element.149.rest_2_, ...), custom_call_target="tpu_custom_call" | custom-call | flops 12800000000 | bytes 1 | tf_op jit(solution)/shard_map/gather/pallas_call | solution.py:1014
  (11 shorter events, 0.0 us)
Async XLA Ops:
  0.6 5.5 %copy-start.5 = (f32[16,128]{1,0:T(8,128)S(1)}, f32[16,128]{1,0:T(8,128)}, u32[]{:S(2)}) copy-start(f32[16,128]{1,0:T(8,128)} %decay.35) | copy-start | bytes 24580
  3.9 2.2 %collective-permute-start = (f32[1040,128]{1,0:T(8,128)}, f32[1040,128]{1,0:T(8,128)S(1)}, u32[]{:S(2)}, u32[]{:S(2)}) collective-permute-start(f32[1040,128]{1,0:T(8,128)} %get-tuple-element.82), channel_id=1, source_target_pairs={{0,1},{1,0},{2,3},{3,2},{4,5},{5,4},{6,7},{7,6},{8,9},{9,8},{10,11... | collective-permute-start | bytes 1597448 | tf_op jit(solution)/shard_map/ppermute | solution.py:782
  6.1 1.0 %copy-start.6 = (f32[1024,128]{1,0:T(8,128)S(1)}, f32[1024,128]{1,0:T(8,128)}, u32[]{:S(2)}) copy-start(f32[1024,128]{1,0:T(8,128)} %get-tuple-element.83.keep.keep1) | copy-start | bytes 1572868
  7.2 2.9 %copy-start = (bf16[128,2048]{1,0:T(8,128)(2,1)S(1)}, bf16[128,2048]{1,0:T(8,128)(2,1)}, u32[]{:S(2)}) copy-start(bf16[128,2048]{1,0:T(8,128)(2,1)} %query.29) | copy-start | bytes 1572868
  7.2 2.9 %copy-start.1 = (bf16[128,2048]{1,0:T(8,128)(2,1)S(1)}, bf16[128,2048]{1,0:T(8,128)(2,1)}, u32[]{:S(2)}) copy-start(bf16[128,2048]{1,0:T(8,128)(2,1)} %key.29) | copy-start | bytes 1572868
  7.2 2.9 %copy-start.2 = (bf16[128,2048]{1,0:T(8,128)(2,1)S(1)}, bf16[128,2048]{1,0:T(8,128)(2,1)}, u32[]{:S(2)}) copy-start(bf16[128,2048]{1,0:T(8,128)(2,1)} %value.29) | copy-start | bytes 1572868
  7.2 2.9 %copy-start.3 = (bf16[128,2048]{1,0:T(8,128)(2,1)S(1)}, bf16[128,2048]{1,0:T(8,128)(2,1)}, u32[]{:S(2)}) copy-start(bf16[128,2048]{1,0:T(8,128)(2,1)} %cotangent.29) | copy-start | bytes 1572868
  7.2 2.9 %copy-start.4 = (f32[11,16,128]{2,1,0:T(8,128)S(1)}, f32[11,16,128]{2,1,0:T(8,128)}, u32[]{:S(2)}) copy-start(f32[11,16,128]{2,1,0:T(8,128)} %gain.29) | copy-start | bytes 270340
  7.5 9.1 %collective-permute-start.1 = (f32[528,128]{1,0:T(8,128)S(1)}, f32[528,128]{1,0:T(8,128)S(1)}, u32[]{:S(2)}, u32[]{:S(2)}) collective-permute-start(f32[528,128]{1,0:T(8,128)S(1)} %get-tuple-element.84), channel_id=1, source_target_pairs={{0,2},{1,3},{2,0},{3,1},{4,6},{5,7},{6,4},{7,5},{8,10},{9,11},{10,... | collective-permute-start | bytes 811016 | tf_op jit(solution)/shard_map/ppermute | solution.py:782
  10.0 1.6 %copy-start.7 = (f32[1024,128]{1,0:T(8,128)S(1)}, f32[1024,128]{1,0:T(8,128)}, u32[]{:S(2)}) copy-start(f32[1024,128]{1,0:T(8,128)} %get-tuple-element.83.keep.keep1) | copy-start | bytes 1572868
  11.6 1.7 %copy-start.8 = (f32[4,128]{1,0:T(4,128)}, f32[4,128]{1,0:T(4,128)S(1)}, u32[]{:S(2)}) copy-start(f32[4,128]{1,0:T(4,128)S(1)} %get-tuple-element.86.after.rest_4_) | copy-start | bytes 6148
  13.3 3.2 %collective-permute-start.2 = (f32[512,128]{1,0:T(8,128)S(1)}, f32[512,128]{1,0:T(8,128)S(1)}, u32[]{:S(2)}, u32[]{:S(2)}) collective-permute-start(f32[512,128]{1,0:T(8,128)S(1)} %get-tuple-element.88), channel_id=1, source_target_pairs={{0,1},{1,0},{2,3},{3,2},{4,5},{5,4},{6,7},{7,6},{8,9},{9,8},{10,11... | collective-permute-start | bytes 786440 | tf_op jit(solution)/shard_map/ppermute | solution.py:782
  14.0 2.5 %collective-permute-start.4 = (f32[512,128]{1,0:T(8,128)S(1)}, f32[512,128]{1,0:T(8,128)S(1)}, u32[]{:S(2)}, u32[]{:S(2)}) collective-permute-start(f32[512,128]{1,0:T(8,128)S(1)} %get-tuple-element.97), channel_id=1, source_target_pairs={{0,1},{1,0},{2,3},{3,2},{4,5},{5,4},{6,7},{7,6},{8,9},{9,8},{10,11... | collective-permute-start | bytes 786440 | tf_op jit(solution)/shard_map/ppermute | solution.py:782
  14.1 7.9 %collective-permute-start.3 = (f32[512,128]{1,0:T(8,128)S(1)}, f32[512,128]{1,0:T(8,128)S(1)}, u32[]{:S(2)}, u32[]{:S(2)}) collective-permute-start(f32[512,128]{1,0:T(8,128)S(1)} %get-tuple-element.85.rest_0_), channel_id=1, source_target_pairs={{0,2},{1,3},{2,0},{3,1},{4,6},{5,7},{6,4},{7,5},{8,10},{9,11},{10,... | collective-permute-start | bytes 786440 | tf_op jit(solution)/shard_map/ppermute | solution.py:782
  16.9 6.6 %collective-permute-start.7 = (f32[512,128]{1,0:T(8,128)S(1)}, f32[512,128]{1,0:T(8,128)S(1)}, u32[]{:S(2)}, u32[]{:S(2)}) collective-permute-start(f32[512,128]{1,0:T(8,128)S(1)} %second_merge.2.rest_4_), channel_id=1, source_target_pairs={{0,1},{1,0},{2,4},{4,2},{3,5},{5,3},{6,7},{7,6},{8,9},{9,8},{10,12... | collective-permute-start | bytes 786440 | tf_op jit(solution)/shard_map/ppermute | solution.py:782
  19.6 2.8 %copy-start.10 = (f32[4,128]{1,0:T(4,128)}, f32[4,128]{1,0:T(4,128)S(1)}, u32[]{:S(2)}) copy-start(f32[4,128]{1,0:T(4,128)S(1)} %get-tuple-element.99.rest_0_.rest_6_) | copy-start | bytes 6148
  22.4 7.5 %collective-permute-start.5 = (f32[512,128]{1,0:T(8,128)S(1)}, f32[512,128]{1,0:T(8,128)S(1)}, u32[]{:S(2)}, u32[]{:S(2)}) collective-permute-start(f32[512,128]{1,0:T(8,128)S(1)} %second_merge.3), channel_id=1, source_target_pairs={{0,1},{1,0},{2,4},{4,2},{3,5},{5,3},{6,7},{7,6},{8,9},{9,8},{10,12... | collective-permute-start | bytes 786440 | tf_op jit(solution)/shard_map/ppermute | solution.py:782
  23.5 4.6 %collective-permute-start.6 = (f32[4096,128]{1,0:T(8,128)S(1)}, f32[4096,128]{1,0:T(8,128)S(1)}, u32[]{:S(2)}, u32[]{:S(2)}) collective-permute-start(f32[4096,128]{1,0:T(8,128)S(1)} %get-tuple-element.101), channel_id=1, source_target_pairs={{0,1},{1,0},{2,3},{3,2},{4,5},{5,4},{6,7},{7,6},{8,9},{9,8},{10,11... | collective-permute-start | bytes 6291464 | tf_op jit(solution)/shard_map/ppermute | solution.py:782
  23.5 9.4 %collective-permute-start.11 = (f32[512,128]{1,0:T(8,128)S(1)}, f32[512,128]{1,0:T(8,128)S(1)}, u32[]{:S(2)}, u32[]{:S(2)}) collective-permute-start(f32[512,128]{1,0:T(8,128)S(1)} %collective-permute-done.7.rest_4_.second), channel_id=1, source_target_pairs={{0,2},{1,3},{2,0},{3,1},{4,6},{5,7},{6,4},{7,5},{8,10},{9,11},{10,... | collective-permute-start | bytes 786440 | tf_op jit(solution)/shard_map/ppermute | solution.py:782
  29.9 7.0 %collective-permute-start.8 = (f32[512,128]{1,0:T(8,128)S(1)}, f32[512,128]{1,0:T(8,128)S(1)}, u32[]{:S(2)}, u32[]{:S(2)}) collective-permute-start(f32[512,128]{1,0:T(8,128)S(1)} %collective-permute-done.5.second), channel_id=1, source_target_pairs={{0,1},{1,0},{2,3},{3,2},{4,5},{5,4},{6,7},{7,6},{8,9},{9,8},{10,11... | collective-permute-start | bytes 786440 | tf_op jit(solution)/shard_map/ppermute | solution.py:782
  30.6 10.3 %collective-permute-start.9 = (f32[512,128]{1,0:T(8,128)S(1)}, f32[512,128]{1,0:T(8,128)S(1)}, u32[]{:S(2)}, u32[]{:S(2)}) collective-permute-start(f32[512,128]{1,0:T(8,128)S(1)} %collective-permute-done.5.second), channel_id=1, source_target_pairs={{0,2},{1,3},{2,0},{3,1},{4,6},{5,7},{6,4},{7,5},{8,10},{9,11},{10,... | collective-permute-start | bytes 786440 | tf_op jit(solution)/shard_map/ppermute | solution.py:782
  32.6 5.5 %collective-permute-start.10 = (f32[512,128]{1,0:T(8,128)S(1)}, f32[512,128]{1,0:T(8,128)S(1)}, u32[]{:S(2)}, u32[]{:S(2)}) collective-permute-start(f32[512,128]{1,0:T(8,128)S(1)} %collective-permute-done.7.rest_4_.second), channel_id=1, source_target_pairs={{0,1},{1,0},{2,3},{3,2},{4,5},{5,4},{6,7},{7,6},{8,9},{9,8},{10,11... | collective-permute-start | bytes 786440 | tf_op jit(solution)/shard_map/ppermute | solution.py:782
  32.9 6.4 %collective-permute-start.12 = (f32[512,128]{1,0:T(8,128)S(1)}, f32[512,128]{1,0:T(8,128)S(1)}, u32[]{:S(2)}, u32[]{:S(2)}) collective-permute-start(f32[512,128]{1,0:T(8,128)S(1)} %collective-permute-done.11.third), channel_id=1, source_target_pairs={{0,1},{1,0},{2,3},{3,2},{4,5},{5,4},{6,7},{7,6},{8,9},{9,8},{10,11... | collective-permute-start | bytes 786440 | tf_op jit(solution)/shard_map/ppermute | solution.py:782
  33.7 3.7 %collective-permute-start.14 = (f32[512,128]{1,0:T(8,128)S(1)}, f32[512,128]{1,0:T(8,128)S(1)}, u32[]{:S(2)}, u32[]{:S(2)}) collective-permute-start(f32[512,128]{1,0:T(8,128)S(1)} %collective-permute-done.3.first), channel_id=1, source_target_pairs={{0,1},{1,0},{2,3},{3,2},{4,5},{5,4},{6,7},{7,6},{8,9},{9,8},{10,11... | collective-permute-start | bytes 786440 | tf_op jit(solution)/shard_map/ppermute | solution.py:782
  36.9 1.7 %collective-permute-start.13 = (f32[528,128]{1,0:T(8,128)S(1)}, f32[528,128]{1,0:T(8,128)S(1)}, u32[]{:S(2)}, u32[]{:S(2)}) collective-permute-start(f32[528,128]{1,0:T(8,128)S(1)} %collective-permute-done.1.first.chip_total), channel_id=1, source_target_pairs={{0,1},{1,0},{2,3},{3,2},{4,5},{5,4},{6,7},{7,6},{8,9},{9,8},{10,11... | collective-permute-start | bytes 811016 | tf_op jit(solution)/shard_map/ppermute | solution.py:782
  40.9 1.9 %collective-permute-start.15 = (f32[512,128]{1,0:T(8,128)S(1)}, f32[512,128]{1,0:T(8,128)S(1)}, u32[]{:S(2)}, u32[]{:S(2)}) collective-permute-start(f32[512,128]{1,0:T(8,128)S(1)} %collective-permute-done.9.third), channel_id=1, source_target_pairs={{0,1},{1,0},{2,3},{3,2},{4,5},{5,4},{6,7},{7,6},{8,9},{9,8},{10,11... | collective-permute-start | bytes 786440 | tf_op jit(solution)/shard_map/ppermute | solution.py:782
  42.8 1.6 %copy-start.9 = (f32[4,128]{1,0:T(4,128)S(1)}, f32[4,128]{1,0:T(4,128)}, u32[]{:S(2)}) copy-start(f32[4,128]{1,0:T(4,128)} %copy-done.8) | copy-start | bytes 6148
  42.8 1.6 %copy-start.11 = (f32[4,128]{1,0:T(4,128)S(1)}, f32[4,128]{1,0:T(4,128)}, u32[]{:S(2)}) copy-start(f32[4,128]{1,0:T(4,128)} %copy-done.10) | copy-start | bytes 6148

commit v4 on v0

--- a/solution.py
+++ b/solution.py
@@ -1,6 +1,10 @@
+import functools
+
 import jax
 import jax.numpy as jnp
 from jax import lax
+from jax.experimental import pallas as pl
+from jax.experimental.pallas import tpu as pltpu
 from jax.sharding import PartitionSpec as P
 
 TOP_ACCURACY = lax.Precision.HIGHEST
@@ -189,6 +193,823 @@
     )
 
 
+F32 = jnp.float32
+BF16 = jnp.bfloat16
+NT = (((1,), (1,)), ((), ()))
+TN = (((0,), (0,)), ((), ()))
+NN = (((1,), (0,)), ((), ()))
+NEVER = -1e30
+
+
+def mxu(left, right, dims):
+    return lax.dot_general(left, right, dims, preferred_element_type=F32)
+
+
+def halves(value):
+    high = value.astype(BF16)
+    low = (value - high.astype(F32)).astype(BF16)
+    return high, low
+
+
+def split_rows(value):
+    return jnp.concatenate(halves(value), axis=0)
+
+
+def split_lanes(value):
+    return jnp.concatenate(halves(value), axis=1)
+
+
+def twice_rows(value):
+    return jnp.concatenate([value, value], axis=0)
+
+
+def twice_lanes(value):
+    return jnp.concatenate([value, value], axis=1)
+
+
+def running_decay(decay):
+    tok = decay.shape[1]
+    earlier = lax.broadcasted_iota(jnp.int32, (tok, tok), 0)
+    later = lax.broadcasted_iota(jnp.int32, (tok, tok), 1)
+    upto = (earlier <= later).astype(F32)
+    return jnp.dot(decay, upto, precision=TOP_ACCURACY, preferred_element_type=F32)
+
+
+def last_lane(running):
+    return jnp.broadcast_to(running[:, running.shape[1] - 1 :], running.shape)
+
+
+def columns(rows):
+    count, tok = rows.shape
+    if count < tok:
+        rows = jnp.concatenate([rows, jnp.zeros((tok - count, tok), rows.dtype)], axis=0)
+    return rows.T
+
+
+def half_first(rows, core):
+    half = rows.shape[0] // 2
+    swapped = jnp.concatenate([rows[half:], rows[:half]], axis=0)
+    return jnp.where(core == 0, rows, swapped)
+
+
+def lane_block(ref, head, width):
+    return ref[:, pl.ds(pl.multiple_of(head * width, width), width)]
+
+
+def take_half(rows, core, low, count):
+    half = rows.shape[0] // 2
+    return jnp.where(core == 0, rows[low : low + count], rows[half + low : half + low + count])
+
+
+def outer_products(left, right, weight_column):
+    turned = left.T
+    return mxu(twice_lanes(turned), split_rows(right.astype(F32) * weight_column), NN)
+
+
+def first_export_kernel(
+    place, query, key, value, cotangent, gain, decay, send, keep, *rest
+):
+    kept, (lefts, rights, sems) = rest[:6], rest[6:]
+    position = place[0]
+    core = position % 2
+    chip = position // 2
+    heads, tok = decay.shape
+    width = query.shape[1]
+    dim = width // heads
+    half = heads // 2
+    cross = gain.shape[0] - 3
+    wide = half * dim
+    state = chip % 2 == 0
+    copies = []
+    for side in range(2):
+        lanes = pl.ds(pl.multiple_of((1 - core if side == 0 else core) * wide, wide), wide)
+        for slot, (chosen, plain, into) in enumerate(((key, query, lefts), (value, cotangent, rights))):
+            sem = sems.at[2 * side + slot]
+            target = into.at[:, pl.ds(side * wide, wide)]
+
+            @pl.when(state)
+            def _(chosen=chosen, target=target, sem=sem, lanes=lanes):
+                pltpu.make_async_copy(chosen.at[:, lanes], target, sem).start()
+
+            @pl.when(jnp.logical_not(state))
+            def _(plain=plain, target=target, sem=sem, lanes=lanes):
+                pltpu.make_async_copy(plain.at[:, lanes], target, sem).start()
+
+            copies.append(pltpu.make_async_copy(plain.at[:, lanes], target, sem))
+    sources = (query, key, value, cotangent, gain, decay)
+    moves = [
+        pltpu.make_async_copy(source, target, sems.at[4 + number])
+        for number, (source, target) in enumerate(zip(sources, kept))
+    ]
+    for move in reversed(moves):
+        move.start()
+    for move in moves[4:]:
+        move.wait()
+    gains, decays = kept[4:]
+    running = running_decay(decays[...])
+    total = last_lane(running)
+    lift = jnp.exp(running)
+    weight = jnp.where(
+        state, jnp.exp(total - running), jnp.where(chip == 1, gains[cross + 1], gains[cross + 2]) * lift
+    )
+    spread = columns(half_first(weight, 1 - core))
+    send[pl.ds(half * dim, heads), :] = total
+    for index in range(heads):
+        if index % half == 0:
+            for copy in copies[2 * (index // half) : 2 * (index // half) + 2]:
+                copy.wait()
+        lanes = slice(index * dim, (index + 1) * dim)
+        rows = pl.ds(index % half * dim, dim)
+        (send if index < half else keep)[rows, :] = outer_products(
+            lefts[:, lanes], rights[:, lanes], spread[:, index : index + 1]
+        )
+    for move in moves[:4]:
+        move.wait()
+
+
+def second_core(position):
+    return jnp.bitwise_xor(position % 2, (position // 2 == 3).astype(jnp.int32))
+
+
+def second_export_kernel(
+    place, query, key, value, cotangent, gain, decay, keep1, after, *outs
+):
+    *sends, keep, bundle = outs
+    position = place[0]
+    core = second_core(position)
+    chip = position // 2
+    heads, tok = decay.shape
+    dim = query.shape[1] // heads
+    half = heads // 2
+    cross = gain.shape[0] - 3
+    running = running_decay(decay[...])
+    lift = jnp.exp(running)
+    fall = jnp.exp(last_lane(running) - running)
+    state2 = chip == 1
+    state0 = position % 2 == 0
+    weight2 = jnp.where(state2, fall, jnp.where(chip == 2, gain[cross + 2], gain[cross + 1]) * lift)
+    weight2 = jnp.where(chip == 0, 0.0, weight2)
+    weight0 = jnp.where(state0, fall, gain[cross] * lift)
+    spread = columns(jnp.concatenate([half_first(weight2, 1 - core), weight0], axis=0))
+    bundle[pl.ds(heads * dim, half * dim), :] = keep1[...]
+    place_of = [(part, row) for part, send in enumerate(sends) for row in range(send.shape[0] // dim)]
+    for index in range(heads):
+        mine = index >= half
+        head = (core if mine else 1 - core) * half + index % half
+        q, k, v, o = (lane_block(ref, head, dim) for ref in (query, key, value, cotangent))
+        second = outer_products(
+            jnp.where(state2, k, q), jnp.where(state2, v, o), spread[:, index : index + 1]
+        )
+        if mine:
+            keep[pl.ds(index % half * dim, dim), :] = second
+            bundle[pl.ds((heads + index) * dim, dim), :] = second
+        else:
+            part, row = place_of[index]
+            sends[part][pl.ds(row * dim, dim), :] = second
+    for head in range(heads):
+        lanes = slice(head * dim, (head + 1) * dim)
+        q, k, v, o = (ref[:, lanes] for ref in (query, key, value, cotangent))
+        bundle[pl.ds(head * dim, dim), :] = outer_products(
+            jnp.where(state0, k, q),
+            jnp.where(state0, v, o),
+            spread[:, heads + head : heads + head + 1],
+        )
+
+
+def pair_factors(position, own_total, other_total, is_state):
+    even = position % 2 == 0
+    scale_own = is_state == even
+    return (
+        jnp.where(scale_own, jnp.exp(other_total), 1.0),
+        jnp.where(scale_own, 1.0, jnp.exp(own_total)),
+    )
+
+
+def first_merge_kernel(place, decay, keep, got, after, *outs):
+    position = place[0]
+    chip = position // 2
+    heads, tok = decay.shape
+    half = heads // 2
+    dim = keep.shape[0] // half
+    own_total = last_lane(running_decay(decay[...]))
+    other_total = got[pl.ds(half * dim, heads), :]
+    own_factor, other_factor = pair_factors(position, own_total, other_total, chip % 2 == 0)
+    own_factor = half_first(own_factor, position % 2)[:half]
+    other_factor = half_first(other_factor, position % 2)[:half]
+    head = 0
+    for part, out in enumerate(outs):
+        for index in range(out.shape[0] // dim):
+            rows = pl.ds(head * dim, dim)
+            out[pl.ds(index * dim, dim), :] = (
+                own_factor[head : head + 1] * keep[rows, :]
+                + other_factor[head : head + 1] * got[rows, :]
+            )
+            head += 1
+    outs[0][pl.ds(outs[0].shape[0] - heads, heads), :] = own_total + other_total
+
+
+def second_merge_kernel(low, place, decay, first_got, keep, got, first, *rest):
+    out = rest[-1]
+    position = place[0]
+    chip = position // 2
+    heads, tok = decay.shape
+    half = heads // 2
+    dim = keep.shape[0] // half
+    own_total = last_lane(running_decay(decay[...]))
+    other_total = first_got[pl.ds(half * dim, heads), :]
+    own_factor, other_factor = pair_factors(position, own_total, other_total, chip == 1)
+    inner = (chip == 1) | (chip == 2)
+    first_factor = jnp.where(inner, jnp.exp(own_total + other_total), 0.0)
+    own_factor, other_factor, first_factor = (
+        half_first(factor, second_core(position)) for factor in (own_factor, other_factor, first_factor)
+    )
+    for index in range(out.shape[0] // dim):
+        rows = pl.ds(index * dim, dim)
+        one = slice(low + index, low + index + 1)
+        out[rows, :] = (
+            own_factor[one] * keep[pl.ds((low + index) * dim, dim), :]
+            + other_factor[one] * got[rows, :]
+            + first_factor[one] * first[rows, :]
+        )
+
+
+def lane_sums(value):
+    ones = jnp.ones((2 * value.shape[1], value.shape[1]), BF16)
+    return mxu(split_lanes(value), ones, NN)
+
+
+def apply_state(left, right, state, weight):
+    high, low = halves(state)
+    first = mxu(twice_lanes(left), jnp.concatenate([high, low], axis=0), NN)
+    second = mxu(twice_lanes(right), jnp.concatenate([high, low], axis=1), NT)
+    sums = lane_sums(first * right.astype(F32))
+    return weight * first, weight * second, sums
+
+
+def local_kernel(low, mine, place, query, key, value, cotangent, gain, decay, *rest):
+    acc_out, acc_query, acc_key, acc_value, gain_rows, decay_rows = rest[-6:]
+    core = place[0] % 2
+    side = core if mine else 1 - core
+    heads, tok = decay.shape
+    count = decay_rows.shape[0]
+    dim = query.shape[1] // heads
+    inner_levels = tok.bit_length()
+    running = take_half(running_decay(decay[...]), side, low, count)
+    gains = [take_half(gain[place_in], side, low, count) for place_in in range(inner_levels)]
+    spread = columns(running)
+    source = lax.broadcasted_iota(jnp.int32, (tok, tok), 0)
+    target = lax.broadcasted_iota(jnp.int32, (tok, tok), 1)
+    mixing = jnp.bitwise_xor(source, target)
+    level = jnp.zeros((tok, tok), jnp.int32)
+    for power in range(inner_levels - 1):
+        level = level + (mixing >= 2**power).astype(jnp.int32)
+    causal = source <= target
+    level = jnp.where(causal, level, -1)
+    gathered = jnp.zeros((tok, tok), F32)
+    for index in range(count):
+        lanes = slice(index * dim, (index + 1) * dim)
+        one = slice(index, index + 1)
+        head = side * (heads // 2) + low + index
+        q, k, v, o = (lane_block(ref, head, dim) for ref in (query, key, value, cotangent))
+        scores = mxu(k, q, NT)
+        pulls = mxu(v, o, NT)
+        fading = jnp.exp(jnp.where(causal, running[one] - spread[:, one], NEVER))
+        weighting = jnp.zeros((tok, tok), F32)
+        for place_in in range(inner_levels):
+            weighting = jnp.where(level == place_in, gains[place_in][one], weighting)
+        weighting = weighting * fading
+        mixing_part = scores * weighting
+        score_grad = pulls * weighting
+        product = scores * pulls * fading
+        flow = jnp.zeros((1, tok), F32)
+        for place_in in range(inner_levels):
+            found = jnp.sum(jnp.where(level == place_in, product, 0.0), axis=0, keepdims=True)
+            gain_rows[place_in, one, :] = found
+            if place_in > 0:
+                flow = flow + gains[place_in][one] * found
+        decay_rows[one, :] = flow
+        left = jnp.where(level > 0, mixing_part * pulls, 0.0)
+        gathered = jnp.where(target == index, lane_sums(left), gathered)
+        high, low_part = halves(mixing_part)
+        acc_out[:, lanes] = mxu(jnp.concatenate([high, low_part], axis=0), twice_rows(v), TN)
+        acc_value[:, lanes] = mxu(jnp.concatenate([high, low_part], axis=1), twice_rows(o), NN)
+        high, low_part = halves(score_grad)
+        acc_query[:, lanes] = mxu(jnp.concatenate([high, low_part], axis=0), twice_rows(k), TN)
+        acc_key[:, lanes] = mxu(jnp.concatenate([high, low_part], axis=1), twice_rows(q), NN)
+    decay_rows[...] = decay_rows[...] - gathered.T[:count]
+
+
+def use_rows(rows_out, uses, gathered, extra):
+    turned = gathered.T
+    count = extra.shape[0]
+    decay_row = jnp.zeros((count, turned.shape[1]), F32)
+    flow_row = extra
+    for number, (forward, weight, lift) in enumerate(uses):
+        sums = turned[number * count : (number + 1) * count]
+        weighted = weight * sums
+        decay_row = decay_row + jnp.where(forward, weighted, -weighted)
+        flow_row = flow_row + jnp.where(forward, 0.0, weighted)
+        rows_out[(2 + number) * count : (3 + number) * count, :] = lift * sums
+    rows_out[:count, :] = decay_row
+    rows_out[count : 2 * count, :] = flow_row
+
+
+def first_use_kernel(
+    low,
+    mine,
+    place,
+    query,
+    key,
+    value,
+    cotangent,
+    gain,
+    decay,
+    first_got,
+    first,
+    second,
+    second_got,
+    front,
+    acc_out,
+    acc_query,
+    acc_key,
+    acc_value,
+    *rest,
+):
+    out_mixed, out_query, out_key, out_value, rows_out = rest[-5:]
+    position = place[0]
+    core = position % 2
+    side = core if mine else 1 - core
+    chip = position // 2
+    heads, tok = decay.shape
+    half = heads // 2
+    dim = query.shape[1] // heads
+    count = acc_out.shape[1] // dim
+    cross = gain.shape[0] - 3
+    running = running_decay(decay[...])
+    total = last_lane(running)
+    other = first_got[pl.ds(half * dim, heads), :]
+    odd = core == 1
+    forward = chip != 0
+    offset = jnp.where(forward == odd, other, 0.0)
+    lift0 = jnp.exp(running)
+    lift = jnp.exp(running + offset)
+    fall0 = jnp.exp(total - running)
+    weight0 = jnp.where(odd, gain[cross] * lift0, fall0)
+    weight = jnp.where(
+        forward,
+        jnp.where(chip == 2, gain[cross + 2], gain[cross + 1]) * lift,
+        jnp.exp(total - running + offset),
+    )
+    pair_flow = jnp.where(forward != odd, jnp.exp(total), 0.0)
+    chip_flow = jnp.where((chip == 1) | (chip == 2), jnp.exp(total + other), 0.0)
+    lift0, lift, weight0, weight, pair_flow, chip_flow = (
+        take_half(rows, side, low, count)
+        for rows in (jnp.where(odd, lift0, 0.0), lift, weight0, weight, pair_flow, chip_flow)
+    )
+    spread = columns(jnp.concatenate([weight0, weight], axis=0))
+    lane = lax.broadcasted_iota(jnp.int32, (tok, tok), 1)
+    gathered = jnp.zeros((tok, tok), F32)
+    flows = []
+    for index in range(count):
+        lanes = slice(index * dim, (index + 1) * dim)
+        rows = pl.ds(index * dim, dim)
+        kept = pl.ds((low + index) * dim, dim)
+        one = slice(index, index + 1)
+        head = side * half + low + index
+        q, k, v, o = (lane_block(ref, head, dim) for ref in (query, key, value, cotangent))
+        level0 = front[pl.ds(pl.multiple_of(head * dim, dim), dim), :]
+        pair1 = first_got[kept, :] if mine else front[pl.ds((heads + low + index) * dim, dim), :]
+        pair2_kept = front[pl.ds((heads + half + low + index) * dim, dim), :]
+        pair2 = jnp.where((chip == 3) == mine, pair2_kept, second_got[rows, :])
+        state = jnp.where(chip == 2, second[rows, :], first[rows, :])
+        partner = jnp.where(odd, level0, jnp.where(chip == 1, pair1, pair2))
+        flows.append(
+            pair_flow[one] * jnp.sum(state * partner, axis=0, keepdims=True)
+            + chip_flow[one] * jnp.sum(first[rows, :] * second[rows, :], axis=0, keepdims=True)
+        )
+        left0, right0, sums = apply_state(
+            jnp.where(odd, q, k), jnp.where(odd, o, v), level0, spread[:, one]
+        )
+        gathered = jnp.where(lane == index, sums, gathered)
+        left, right, sums = apply_state(
+            jnp.where(forward, q, k),
+            jnp.where(forward, o, v),
+            state,
+            spread[:, count + index : count + index + 1],
+        )
+        gathered = jnp.where(lane == count + index, sums, gathered)
+        out_mixed[:, lanes] = (
+            acc_out[:, lanes] + jnp.where(odd, left0, 0.0) + jnp.where(forward, left, 0.0)
+        )
+        out_query[:, lanes] = (
+            acc_query[:, lanes] + jnp.where(odd, right0, 0.0) + jnp.where(forward, right, 0.0)
+        )
+        out_value[:, lanes] = (
+            acc_value[:, lanes] + jnp.where(odd, 0.0, left0) + jnp.where(forward, 0.0, left)
+        )
+        out_key[:, lanes] = (
+            acc_key[:, lanes] + jnp.where(odd, 0.0, right0) + jnp.where(forward, 0.0, right)
+        )
+    use_rows(
+        rows_out,
+        ((odd, weight0, lift0), (forward, weight, lift)),
+        gathered,
+        jnp.concatenate(flows, axis=0),
+    )
+
+
+def last_use_kernel(
+    low,
+    mine,
+    parts,
+    place,
+    query,
+    key,
+    value,
+    cotangent,
+    gain,
+    decay,
+    first_got,
+    chip_total,
+    second,
+    third,
+    front,
+    acc_out,
+    acc_query,
+    acc_key,
+    acc_value,
+    *rest,
+):
+    ending = parts is not None
+    if ending:
+        *rest, grad_gain, grad_decay, staged, sems, gain_stage, decay_stage, end_sems = rest
+    else:
+        *rest, rows_out, staged, sems = rest
+    outs = rest[-4:]
+    position = place[0]
+    core = position % 2
+    side = core if mine else 1 - core
+    chip = position // 2
+    heads, tok = decay.shape
+    half = heads // 2
+    dim = query.shape[1] // heads
+    count = acc_out.shape[1] // dim
+    cross = gain.shape[0] - 3
+    running = running_decay(decay[...])
+    total = last_lane(running)
+    other = first_got[pl.ds(half * dim, heads), :]
+    chip_rows = chip_total[pl.ds(chip_total.shape[0] - heads, heads), :]
+    odd = core == 1
+    forward = chip == 3
+    chip_offset = jnp.where((chip == 0) | (chip == 3), chip_rows, 0.0)
+    offset = jnp.where(forward == odd, other, 0.0) + chip_offset
+    lift = jnp.exp(running + offset)
+    weight = jnp.where(forward, gain[cross + 2] * lift, jnp.exp(total - running + offset))
+    pair_flow = jnp.where(forward != odd, jnp.exp(total + chip_offset), 0.0)
+    lift, weight, pair_flow = (
+        take_half(rows, side, low, count) for rows in (lift, weight, pair_flow)
+    )
+    spread = columns(weight)
+    lane = lax.broadcasted_iota(jnp.int32, (tok, tok), 1)
+    gathered = jnp.zeros((tok, tok), F32)
+    flows = []
+    copies = []
+    if ending:
+        early = gain.shape[0] - 2
+        copies.append(
+            pltpu.make_async_copy(
+                gain_stage.at[pl.ds(0, early)], grad_gain.at[pl.ds(0, early)], end_sems.at[0]
+            )
+        )
+        early_gains(parts, rest[:-4], core, gain_stage)
+        copies[0].start()
+    for index in range(count):
+        lanes = slice(index * dim, (index + 1) * dim)
+        rows = pl.ds(index * dim, dim)
+        one = slice(index, index + 1)
+        head = side * half + low + index
+        q, k, v, o = (lane_block(ref, head, dim) for ref in (query, key, value, cotangent))
+        state = jnp.where(chip == 1, second[rows, :], third[rows, :])
+        level0 = front[pl.ds(pl.multiple_of(head * dim, dim), dim), :]
+        if mine:
+            pair1 = first_got[pl.ds((low + index) * dim, dim), :]
+        else:
+            pair1 = front[pl.ds((heads + low + index) * dim, dim), :]
+        partner = jnp.where(odd, level0, pair1)
+        flows.append(pair_flow[one] * jnp.sum(state * partner, axis=0, keepdims=True))
+        left, right, sums = apply_state(
+            jnp.where(forward, q, k), jnp.where(forward, o, v), state, spread[:, one]
+        )
+        gathered = jnp.where(lane == index, sums, gathered)
+        results = (
+            acc_out[:, lanes] + jnp.where(forward, left, 0.0),
+            acc_query[:, lanes] + jnp.where(forward, right, 0.0),
+            acc_key[:, lanes] + jnp.where(forward, 0.0, right),
+            acc_value[:, lanes] + jnp.where(forward, 0.0, left),
+        )
+        for number, result in enumerate(results):
+            staged[number, :, lanes] = result.astype(BF16)
+            copy = pltpu.make_async_copy(
+                staged.at[number, :, pl.ds(index * dim, dim)],
+                outs[number].at[:, pl.ds(pl.multiple_of(head * dim, dim), dim)],
+                sems.at[number * count + index],
+            )
+            copy.start()
+            copies.append(copy)
+    extra = jnp.concatenate(flows, axis=0)
+    if not ending:
+        use_rows(rows_out, ((forward, weight, lift),), gathered, extra)
+    else:
+        sums = gathered.T[:count]
+        weighted = weight * sums
+        own_rows = (
+            jnp.where(forward, weighted, -weighted),
+            extra + jnp.where(forward, 0.0, weighted),
+            lift * sums,
+        )
+        finish(parts, rest[:-4], own_rows, core, chip, gain_stage, decay_stage)
+        for copy in (
+            pltpu.make_async_copy(
+                gain_stage.at[pl.ds(early, 2)], grad_gain.at[pl.ds(early, 2)], end_sems.at[1]
+            ),
+            pltpu.make_async_copy(decay_stage, grad_decay, end_sems.at[2]),
+        ):
+            copy.start()
+            copies.append(copy)
+    for copy in copies:
+        copy.wait()
+
+
+def natural(pieces, core):
+    return half_first(jnp.concatenate([*pieces[::2], *pieces[1::2]], axis=0), core)
+
+
+def of_kind(counts, refs, number):
+    return [
+        ref[number * counts[at // 2] : (number + 1) * counts[at // 2], :]
+        for at, ref in enumerate(refs)
+    ]
+
+
+def early_gains(counts, refs, core, grad_gain):
+    levels = grad_gain.shape[0]
+    groups = 2 * len(counts)
+    for place_in in range(levels - 3):
+        grad_gain[place_in] = natural([ref[place_in] for ref in refs[:groups]], core)
+    first_rows = refs[2 * groups : 3 * groups]
+    grad_gain[levels - 3] = natural(of_kind(counts, first_rows, 2), core)
+
+
+def finish(counts, refs, own_rows, core, chip, grad_gain, grad_decay):
+    levels, heads, tok = grad_gain.shape
+    groups = 2 * len(counts)
+    decay_rows, first_rows = refs[groups : 2 * groups], refs[2 * groups : 3 * groups]
+    last_rows = refs[3 * groups : 4 * groups - 1]
+
+    def last(number):
+        return natural(of_kind(counts, last_rows, number) + [own_rows[number]], core)
+
+    first, second = natural(of_kind(counts, first_rows, 3), core), last(2)
+    grad_gain[levels - 2] = jnp.where(chip % 2 == 1, first, 0.0)
+    grad_gain[levels - 1] = jnp.where(chip == 2, first, jnp.where(chip == 3, second, 0.0))
+    own = natural([ref[...] for ref in decay_rows], core)
+    own = own + natural(of_kind(counts, first_rows, 0), core) + last(0)
+    later = natural(of_kind(counts, first_rows, 1), core) + last(1)
+    upper = lax.broadcasted_iota(jnp.int32, (tok, tok), 0)
+    lower = lax.broadcasted_iota(jnp.int32, (tok, tok), 1)
+    from_here = (upper >= lower).astype(F32)
+    every = jnp.ones((tok, tok), F32)
+    grad_decay[...] = jnp.dot(
+        own, from_here, precision=TOP_ACCURACY, preferred_element_type=F32
+    ) + jnp.dot(later, every, precision=TOP_ACCURACY, preferred_element_type=F32)
+
+
+def after(value, *others):
+    return lax.optimization_barrier((value, *others))[0]
+
+
+def sds(*shape, dtype=F32):
+    return jax.ShapeDtypeStruct(shape, dtype)
+
+
+FIRST_LIMIT = 24
+
+
+def params(mebibytes=24):
+    return pltpu.CompilerParams(vmem_limit_bytes=mebibytes * 1024 * 1024)
+
+
+SCALAR = pl.BlockSpec(memory_space=pltpu.SMEM)
+ANYWHERE = pl.BlockSpec(memory_space=pl.ANY)
+IN_HBM = pl.BlockSpec(memory_space=pltpu.HBM)
+RATE_FIRST = 16
+RATE_SECOND = 0.001
+RATE_LOCAL = ((.01,.01),(1,16))
+RATE_USE = ((4,4),(4,4))
+RATE_LAST = ((4,4),(4,4))
+RATE_MERGE = (4,4)
+
+
+def cost(microseconds, rate=16):
+    return pl.CostEstimate(flops=int(microseconds * rate * 10**9), bytes_accessed=1, transcendentals=0)
+
+
+def chunk_heads(half):
+    return (half // 2, half - half // 2)
+
+
+def line_device(queries, keys_in, value_input, level_gain, decay_log, out_grad):
+    heads, tok = decay_log.shape
+    dim = queries.shape[1] // heads
+    half = heads // 2
+    counts = chunk_heads(half)
+    parts = range(len(counts))
+    lows = [sum(counts[:part]) for part in parts]
+    inner = tok.bit_length()
+    place = lax.axis_index("ctx").astype(jnp.int32).reshape(1)
+    tokens = (queries, keys_in, value_input, out_grad)
+    inputs = (place, *tokens, level_gain, decay_log)
+    core_swap = [(at, at ^ 1) for at in range(8)]
+    side_swap = [(at, at ^ 2) for at in range(8)]
+    middle_swap = [(0, 1), (1, 0), (2, 4), (4, 2), (3, 5), (5, 3), (6, 7), (7, 6)]
+
+    def swap(block, route):
+        return lax.ppermute(block, "ctx", route)
+
+    def call(kernel, out_shape, operands, unread=(), spent=None, name=None, **options):
+        return pl.pallas_call(
+            kernel,
+            out_shape=out_shape,
+            in_specs=[SCALAR] + [pl.BlockSpec()] * (len(operands) - 1) + [ANYWHERE] * len(unread),
+            compiler_params=params(),
+            cost_estimate=spent,
+            name=name,
+            **options,
+        )(*operands, *unread)
+
+    send1, keep1, *kept = pl.pallas_call(
+        first_export_kernel,
+        out_shape=(pltpu.VMEM((half * dim + heads, dim), F32), pltpu.VMEM((half * dim, dim), F32))
+        + tuple(pltpu.VMEM(array.shape, array.dtype) for array in inputs[1:]),
+        in_specs=[SCALAR] + [IN_HBM] * 6,
+        scratch_shapes=[
+            pltpu.VMEM((tok, heads * dim), BF16),
+            pltpu.VMEM((tok, heads * dim), BF16),
+            pltpu.SemaphoreType.DMA((10,)),
+        ],
+        compiler_params=params(FIRST_LIMIT),
+        cost_estimate=cost(3.3),
+        name="first_exports",
+    )(place, *(pltpu.with_memory_space_constraint(array, pltpu.HBM) for array in inputs[1:]))
+    inputs = (place, *kept)
+    decay_log = kept[-1]
+    got1 = swap(send1, core_swap)
+    local_done = {}
+
+    def local(part, mine, *unread):
+        count = counts[part]
+        local_done[part, mine] = call(
+            functools.partial(local_kernel, lows[part], mine),
+            (sds(tok, count * dim),) * 4 + (sds(inner, count, tok), sds(count, tok)),
+            inputs,
+            unread,
+            cost(0.4 * count, RATE_LOCAL[part][not mine]),
+            "local",
+        )
+        return local_done[part, mine][-1]
+
+    done = local(0, True)
+    first_sent = call(
+        first_merge_kernel,
+        tuple(sds(count * dim + (0 if part else heads), dim) for part, count in enumerate(counts)),
+        (place, decay_log, keep1, got1),
+        (done,),
+        spent=cost(0.3),
+        name="first_merge",
+    )
+    first = [swap(block, side_swap) for block in first_sent]
+
+    done = first_sent[-1]
+    *send2, keep2, bundle = call(
+        second_export_kernel,
+        tuple(sds(count * dim, dim) for count in counts) + (sds(half * dim, dim), sds(4 * half * dim, dim)),
+        (*inputs, keep1),
+        (done,),
+        cost(1.6, RATE_SECOND),
+        "second_exports",
+    )
+    got2 = [swap(block, core_swap) for block in send2]
+
+    def second_merge(part, *unread):
+        return call(
+            functools.partial(second_merge_kernel, lows[part]),
+            sds(counts[part] * dim, dim),
+            (place, decay_log, got1, keep2, got2[part], first[part]),
+            unread,
+            cost(0.3, RATE_MERGE[part]),
+            "second_merge",
+        )
+
+    done = local(0, False, keep2)
+    done = local(1, True, done)
+    sent = [second_merge(0, done, *got2[1:])]
+    done = local(1, False, sent[0])
+    sent.append(second_merge(1, done))
+    front = swap(bundle, core_swap)
+    second = [swap(block, middle_swap) for block in sent]
+    third = [swap(second[0], side_swap)]
+    second_over = [swap(second[0], core_swap)]
+    used = {}
+
+    def first_use(part, mine, *unread):
+        count = counts[part]
+        used[part, mine] = call(
+            functools.partial(first_use_kernel, lows[part], mine),
+            (sds(tok, count * dim),) * 4 + (sds(4 * count, tok),),
+            (
+                *inputs,
+                got1,
+                (first if mine else first_over)[part],
+                (second if mine else second_over)[part],
+                got2[part],
+                front,
+                *local_done[part, mine][:4],
+            ),
+            unread,
+            cost(0.3 * count, RATE_USE[part][not mine]),
+            "first_use",
+        )
+        return used[part, mine][-1]
+
+    results = ()
+    last_rows = []
+
+    def last_use(part, mine, ending=False):
+        nonlocal results
+        count = counts[part]
+        operands = (
+            *inputs,
+            got1,
+            first[0],
+            (second if mine else second_over)[part],
+            (third if mine else third_over)[part],
+            front,
+            *used[part, mine][:4],
+        )
+        order = [(at, side) for at in parts for side in (True, False)]
+        rows = ()
+        if ending:
+            rows = (
+                *(local_done[key][4] for key in order),
+                *(local_done[key][5] for key in order),
+                *(used[key][4] for key in order),
+                *last_rows,
+            )
+        before = len(operands) + len(rows)
+        tail = (sds(*level_gain.shape), sds(heads, tok)) if ending else (sds(3 * count, tok),)
+        ending_scratch = [
+            pltpu.VMEM(level_gain.shape, F32),
+            pltpu.VMEM((heads, tok), F32),
+            pltpu.SemaphoreType.DMA((3,)),
+        ]
+        found = pl.pallas_call(
+            functools.partial(last_use_kernel, lows[part], mine, counts if ending else None),
+            out_shape=(sds(tok, heads * dim, dtype=BF16),) * 4 + tail,
+            in_specs=[SCALAR]
+            + [pl.BlockSpec()] * (before - 1)
+            + [ANYWHERE] * len(results),
+            out_specs=(ANYWHERE,) * 4 + (ANYWHERE if ending else pl.BlockSpec(),) * len(tail),
+            input_output_aliases={before + at: at for at in range(len(results))},
+            scratch_shapes=[
+                pltpu.VMEM((4, tok, count * dim), BF16),
+                pltpu.SemaphoreType.DMA((4 * count,)),
+            ]
+            + ending_scratch * ending,
+            compiler_params=params(),
+            cost_estimate=cost(0.25 * count, RATE_LAST[part][not mine]),
+            name="last_use",
+        )(*operands, *rows, *results)
+        results = found[:4]
+        last_rows.extend(found[4:])
+
+    done = first_use(0, True)
+    first_over = [swap(after(first[0], second[0]), core_swap)]
+    done = first_use(0, False, done)
+    second[1] = after(second[1], done)
+    third.append(swap(second[1], side_swap))
+    second_over.append(swap(second[1], core_swap))
+    first_over.append(swap(after(first[1], second[1]), core_swap))
+    done = first_use(1, True, done)
+    third_over = [swap(after(third[0], done), core_swap)]
+    done = first_use(1, False, done)
+    last_use(0, True)
+    last_use(0, False)
+    third_over.append(swap(after(third[1], done, last_rows[-1]), core_swap))
+    last_use(1, True)
+    last_use(1, False, ending=True)
+    return (*results, *last_rows[-2:])
+
+
 def solution(mesh):
     placed = (
         P(("seq", "ctx"), None),
@@ -199,7 +1020,7 @@
         P(("seq", "ctx"), None),
     )
     return jax.shard_map(
-        per_device,
+        line_device if mesh.shape["ctx"] == 8 else per_device,
         mesh=mesh,
         in_specs=placed,
         out_specs=(

time: 207 us -> 41.5 us (0.20)
  waiting for transfers between devices: 122 us -> 3.8 us
  matrix products: 34.2 us -> 0 us
  Pallas kernels: 0 us -> 22.4 us
  other arithmetic: 22.2 us -> 0 us
  local copies, waits for them, and re-layouts: 14.6 us -> 0 us
    ppermute x12 -> x16, waiting for transfers between devices: 122 us -> 3.8 us  [swap(): return lax.ppermute(block, 'ctx', route)]
    dot_general x14 -> x0, matrix products: 34.2 us -> none  [the longest x3 9.99 us: block_output(): jnp.einsum('jhik,jhkv->hiv', reach, buckets, precision=TOP_ACCURACY)]
    pallas_call x0 -> x17, Pallas kernels: none -> 22.4 us  [the longest x12 13.3 us: call(): pl.pallas_call(kernel, out_shape=out_shape, in_specs=[SCALAR] + [pl.Block...]
    unnamed x58 -> x0, local copies, waits for them, and re-layouts: 11.9 us -> none
    reduce_sum x5 -> x0, other arithmetic: 8.59 us -> none  [the longest x1 4.04 us: own_grads(): jnp.sum(g_bucket * other_state, axis=(1, 2))]
    another operation x5 -> x0, other arithmetic: 6.17 us -> none  [the longest x2 2.71 us: per_device(): buckets = jnp.stack(found)]
    select_n x4 -> x0, other arithmetic: 3.25 us -> none  [the longest x2 2.73 us: partner_grads(): jnp.where(is_upper, factor[:, None, None] * g_state + jnp.exp(offset)[:,...]
    ppermute x12 -> x16, starting transfers between devices: 12.2 us -> 14.2 us  [swap(): return lax.ppermute(block, 'ctx', route)]
  transfers between devices with their start and end apart: 12 -> 16, of which waited for: 6 -> 5; matrix products, arithmetic and copies ran while one was open for 20% -> 0% of each run, Pallas kernels for 0% -> 43%
where the time goes in v4:
time: 41.5 us; the launch traced here: 41.3 us
  Pallas kernels  22.4 us (54%)
  starting transfers between devices  14.2 us (34%)
  waiting for transfers between devices  3.8 us (9%)
  between operations  0.94 us (2%)
    ppermute x16, starting transfers between devices, swap(): return lax.ppermute(block, 'ctx', route)  14.2 us
    pallas_call x12, Pallas kernels, call(): pl.pallas_call(kernel, out_shape=out_shape, in_specs=[SCALAR] + [pl.Block...  13.3 us
    pallas_call x4, Pallas kernels, last_use(): pl.pallas_call(functools.partial(last_use_kernel, lows[part], mine, count...  6.41 us
    ppermute x16, waiting for transfers between devices, swap(): return lax.ppermute(block, 'ctx', route)  3.8 us
    pallas_call x1, Pallas kernels, line_device(): pl.pallas_call(first_export_kernel, out_shape=(pltpu.VMEM((half * dim + h...  2.64 us
  transfers between devices with their start and end apart: 16, of which 5 were waited for; matrix products, arithmetic and copies ran while one was open for 0% of the time, Pallas kernels for 43%

profile of v4, /device:TPU:1, one launch (start us, length us, event | category | flops | bytes accessed | tf_op | source)
XLA Modules:
  0.0 41.3 jit_solution(17927766928640193611)
XLA Ops:
  0.6 2.6 %first_exports.1 = (f32[1040,128]{1,0:T(8,128)S(1)}, f32[1024,128]{1,0:T(8,128)S(1)}, bf16[128,2048]{1,0:T(8,128)(2,1)S(1)}, bf16[128,2048]{1,0:T(8,128)(2,1)S(1...) custom-call(s32[1]{0:T(128)} %bitcast.place, ...), custom_call_target="tpu_custom_call" | custom-call | flops 52800000000 | bytes 1 | tf_op jit(solution)/shard_map/first_exports/pallas_call | solution.py:850
  3.3 0.1 collective-permute-start
  3.4 1.6 %local.4 = (f32[128,512]{1,0:T(8,128)S(1)}, f32[128,512]{1,0:T(8,128)S(1)}, f32[128,512]{1,0:T(8,128)S(1)}, f32[128,512]{1,0:T(8,128)S(1)}, f32[8,4,128]{2,1,0:T(4,128)S(1)}, /*index=5*/f32[4,128]{1,0:T(4,128)S(1)}) custom-call(s32[1]{0:T(128)} %bitcast.place, bf16[128,2048]{1,0:T(8,128)(2,1)S(1)} %get-tuple-element.84.query, ...), custom_call_target="tpu_custom_call" | custom-call | flops 16000000 | bytes 1 | tf_op jit(solution)/shard_map/local/pallas_call | solution.py:840
  5.0 0.3 collective-permute-done.got.first_got
  5.3 0.3 first_merge.1
  5.6 2.5 %collective-permute-start.1 = (f32[528,128]{1,0:T(8,128)S(1)}, f32[528,128]{1,0:T(8,128)S(1)}, u32[]{:S(2)}, u32[]{:S(2)}) collective-permute-start(f32[528,128]{1,0:T(8,128)S(1)} %get-tuple-element.93), channel_id=1, source_target_pairs={{0,2},{1,3},{2,0},{3,1},{4,6},{5,7},{6,4},{7,5},{8,10},{9,11},{10,... | collective-permute-start | bytes 811016 | tf_op jit(solution)/shard_map/ppermute | solution.py:837
  8.1 1.6 %second_exports.1 = (f32[512,128]{1,0:T(8,128)S(1)}, f32[512,128]{1,0:T(8,128)S(1)}, f32[1024,128]{1,0:T(8,128)S(1)}, f32[4096,128]{1,0:T(8,128)S(1)}) custom-call(s32[1]{0:T(128)} %bitcast.place, bf16[128,2048]{1,0:T(8,128)(2,1)S(1)} %get-tuple-element.84.query, bf16[128,2048]{1,0:T(8,128)(2,1)S(1)} %get-tuple-element.85.key, ...), custom_call_target="tpu_custom_call" | custom-call | flops 1600000 | bytes 1 | tf_op jit(solution)/shard_map/second_exports/pallas_call | solution.py:840
  9.7 0.7 %collective-permute-start.2 = (f32[512,128]{1,0:T(8,128)S(1)}, f32[512,128]{1,0:T(8,128)S(1)}, u32[]{:S(2)}, u32[]{:S(2)}) collective-permute-start(f32[512,128]{1,0:T(8,128)S(1)} %get-tuple-element.96), channel_id=1, source_target_pairs={{0,1},{1,0},{2,3},{3,2},{4,5},{5,4},{6,7},{7,6},{8,9},{9,8},{10,11... | collective-permute-start | bytes 786440 | tf_op jit(solution)/shard_map/ppermute | solution.py:837
  10.4 0.1 collective-permute-start.4
  10.5 0.0 collective-permute-start.3
  10.5 0.4 %collective-permute-start.9 = (f32[4096,128]{1,0:T(8,128)S(1)}, f32[4096,128]{1,0:T(8,128)S(1)}, u32[]{:S(2)}, u32[]{:S(2)}) collective-permute-start(f32[4096,128]{1,0:T(8,128)S(1)} %get-tuple-element.102), channel_id=1, source_target_pairs={{0,1},{1,0},{2,3},{3,2},{4,5},{5,4},{6,7},{7,6},{8,9},{9,8},{10,11... | collective-permute-start | bytes 6291464 | tf_op jit(solution)/shard_map/ppermute | solution.py:837
  11.0 1.6 %local.5 = (f32[128,512]{1,0:T(8,128)S(1)}, f32[128,512]{1,0:T(8,128)S(1)}, f32[128,512]{1,0:T(8,128)S(1)}, f32[128,512]{1,0:T(8,128)S(1)}, f32[8,4,128]{2,1,0:T(4,128)S(1)}, /*index=5*/f32[4,128]{1,0:T(4,128)S(1)}) custom-call(s32[1]{0:T(128)} %bitcast.place, bf16[128,2048]{1,0:T(8,128)(2,1)S(1)} %get-tuple-element.84.query, ...), custom_call_target="tpu_custom_call" | custom-call | flops 16000000 | bytes 1 | tf_op jit(solution)/shard_map/local/pallas_call | solution.py:840
  12.5 1.6 %local.6 = (f32[128,512]{1,0:T(8,128)S(1)}, f32[128,512]{1,0:T(8,128)S(1)}, f32[128,512]{1,0:T(8,128)S(1)}, f32[128,512]{1,0:T(8,128)S(1)}, f32[8,4,128]{2,1,0:T(4,128)S(1)}, /*index=5*/f32[4,128]{1,0:T(4,128)S(1)}) custom-call(s32[1]{0:T(128)} %bitcast.place, bf16[128,2048]{1,0:T(8,128)(2,1)S(1)} %get-tuple-element.84.query, ...), custom_call_target="tpu_custom_call" | custom-call | flops 1600000000 | bytes 1 | tf_op jit(solution)/shard_map/local/pallas_call | solution.py:840
  14.1 0.0 collective-permute-done.2.rest_1_.got.second_got
  14.1 0.0 collective-permute-done.4.got.second_got
  14.1 0.6 %collective-permute-done.1.first.chip_total = f32[528,128]{1,0:T(8,128)S(1)} collective-permute-done((f32[528,128]{1,0:T(8,128)S(1)}, f32[528,128]{1,0:T(8,128)S(1)}, u32[]{:S(2)}, u32[]{:S(2)}) %collective-permute-start.1) | collective-permute-done | bytes 270368 | tf_op jit(solution)/shard_map/ppermute | solution.py:837
  14.7 0.3 second_merge.2.rest_0_
  15.0 1.4 %collective-permute-start.6 = (f32[512,128]{1,0:T(8,128)S(1)}, f32[512,128]{1,0:T(8,128)S(1)}, u32[]{:S(2)}, u32[]{:S(2)}) collective-permute-start(f32[512,128]{1,0:T(8,128)S(1)} %second_merge.2.rest_0_), channel_id=1, source_target_pairs={{0,1},{1,0},{2,4},{4,2},{3,5},{5,3},{6,7},{7,6},{8,9},{9,8},{10,12... | collective-permute-start | bytes 786440 | tf_op jit(solution)/shard_map/ppermute | solution.py:837
  16.4 1.6 %local.7 = (f32[128,512]{1,0:T(8,128)S(1)}, f32[128,512]{1,0:T(8,128)S(1)}, f32[128,512]{1,0:T(8,128)S(1)}, f32[128,512]{1,0:T(8,128)S(1)}, f32[8,4,128]{2,1,0:T(4,128)S(1)}, /*index=5*/f32[4,128]{1,0:T(4,128)S(1)}) custom-call(s32[1]{0:T(128)} %bitcast.place, bf16[128,2048]{1,0:T(8,128)(2,1)S(1)} %get-tuple-element.84.query, ...), custom_call_target="tpu_custom_call" | custom-call | flops 25600000000 | bytes 1 | tf_op jit(solution)/shard_map/local/pallas_call | solution.py:840
  17.9 2.4 %collective-permute-done.3.first = f32[512,128]{1,0:T(8,128)S(1)} collective-permute-done((f32[512,128]{1,0:T(8,128)S(1)}, f32[512,128]{1,0:T(8,128)S(1)}, u32[]{:S(2)}, u32[]{:S(2)}) %collective-permute-start.3) | collective-permute-done | bytes 262176 | tf_op jit(solution)/shard_map/ppermute | solution.py:837
  20.3 0.3 second_merge.3
  20.6 0.9 %collective-permute-start.5 = (f32[512,128]{1,0:T(8,128)S(1)}, f32[512,128]{1,0:T(8,128)S(1)}, u32[]{:S(2)}, u32[]{:S(2)}) collective-permute-start(f32[512,128]{1,0:T(8,128)S(1)} %second_merge.3), channel_id=1, source_target_pairs={{0,1},{1,0},{2,4},{4,2},{3,5},{5,3},{6,7},{7,6},{8,9},{9,8},{10,12... | collective-permute-start | bytes 786440 | tf_op jit(solution)/shard_map/ppermute | solution.py:837
  21.5 0.0 collective-permute-done.6.second
  21.5 0.1 collective-permute-start.7
  21.6 3.3 %collective-permute-start.13 = (f32[512,128]{1,0:T(8,128)S(1)}, f32[512,128]{1,0:T(8,128)S(1)}, u32[]{:S(2)}, u32[]{:S(2)}) collective-permute-start(f32[512,128]{1,0:T(8,128)S(1)} %collective-permute-done.6.second), channel_id=1, source_target_pairs={{0,2},{1,3},{2,0},{3,1},{4,6},{5,7},{6,4},{7,5},{8,10},{9,11},{10,... | collective-permute-start | bytes 786440 | tf_op jit(solution)/shard_map/ppermute | solution.py:837
  24.9 0.3 collective-permute-start.8
  25.2 0.0 collective-permute-done.9.front
  25.2 1.1 %first_use.4 = (f32[128,512]{1,0:T(8,128)S(1)}, f32[128,512]{1,0:T(8,128)S(1)}, f32[128,512]{1,0:T(8,128)S(1)}, f32[128,512]{1,0:T(8,128)S(1)}, f32[16,128]{1,0:T(8,128)S(1)}) custom-call(s32[1]{0:T(128)} %bitcast.place, bf16[128,2048]{1,0:T(8,128)(2,1)S(1)} %get-tuple-element.84.query, bf16[128,2048]{1,0:T(8,128)(2,1)S(1)} %get-tuple-element.85.key, ...), custom_call_target="tpu_custom_call" | custom-call | flops 4800000000 | bytes 1 | tf_op jit(solution)/shard_map/first_use/pallas_call | solution.py:840
  26.3 0.1 collective-permute-done.8.second
  26.5 0.0 collective-permute-done.7.first
  26.5 1.1 %first_use.5 = (f32[128,512]{1,0:T(8,128)S(1)}, f32[128,512]{1,0:T(8,128)S(1)}, f32[128,512]{1,0:T(8,128)S(1)}, f32[128,512]{1,0:T(8,128)S(1)}, f32[16,128]{1,0:T(8,128)S(1)}) custom-call(s32[1]{0:T(128)} %bitcast.place, bf16[128,2048]{1,0:T(8,128)(2,1)S(1)} %get-tuple-element.84.query, bf16[128,2048]{1,0:T(8,128)(2,1)S(1)} %get-tuple-element.85.key, ...), custom_call_target="tpu_custom_call" | custom-call | flops 4800000000 | bytes 1 | tf_op jit(solution)/shard_map/first_use/pallas_call | solution.py:840
  27.6 0.0 collective-permute-done.5.second
  27.6 0.9 %collective-permute-start.11 = (f32[512,128]{1,0:T(8,128)S(1)}, f32[512,128]{1,0:T(8,128)S(1)}, u32[]{:S(2)}, u32[]{:S(2)}) collective-permute-start(f32[512,128]{1,0:T(8,128)S(1)} %collective-permute-done.5.second), channel_id=1, source_target_pairs={{0,2},{1,3},{2,0},{3,1},{4,6},{5,7},{6,4},{7,5},{8,10},{9,11},{10,... | collective-permute-start | bytes 786440 | tf_op jit(solution)/shard_map/ppermute | solution.py:837
  28.5 2.4 %collective-permute-start.10 = (f32[512,128]{1,0:T(8,128)S(1)}, f32[512,128]{1,0:T(8,128)S(1)}, u32[]{:S(2)}, u32[]{:S(2)}) collective-permute-start(f32[512,128]{1,0:T(8,128)S(1)} %collective-permute-done.5.second), channel_id=1, source_target_pairs={{0,1},{1,0},{2,3},{3,2},{4,5},{5,4},{6,7},{7,6},{8,9},{9,8},{10,11... | collective-permute-start | bytes 786440 | tf_op jit(solution)/shard_map/ppermute | solution.py:837
  30.8 1.3 %first_use.6 = (f32[128,512]{1,0:T(8,128)S(1)}, f32[128,512]{1,0:T(8,128)S(1)}, f32[128,512]{1,0:T(8,128)S(1)}, f32[128,512]{1,0:T(8,128)S(1)}, f32[16,128]{1,0:T(8,128)S(1)}) custom-call(s32[1]{0:T(128)} %bitcast.place, bf16[128,2048]{1,0:T(8,128)(2,1)S(1)} %get-tuple-element.84.query, bf16[128,2048]{1,0:T(8,128)(2,1)S(1)} %get-tuple-element.85.key, ...), custom_call_target="tpu_custom_call" | custom-call | flops 4800000000 | bytes 1 | tf_op jit(solution)/shard_map/first_use/pallas_call | solution.py:840
  32.1 0.0 collective-permute-done.13.third
  32.1 0.3 collective-permute-start.14
  32.4 0.3 collective-permute-start.12
  32.7 1.5 %last_use.4 = (bf16[128,2048]{1,0:T(8,128)(2,1)}, bf16[128,2048]{1,0:T(8,128)(2,1)}, bf16[128,2048]{1,0:T(8,128)(2,1)}, bf16[128,2048]{1,0:T(8,128)(2,1)}, f32[12,128]{1,0:T(8,128)S(1)}) custom-call(s32[1]{0:T(128)} %bitcast.place, bf16[128,2048]{1,0:T(8,128)(2,1)S(1)} %get-tuple-element.84.query, bf16[128,2048]{1,0:T(8,128)(2,1)S(1)} %get-tuple-element.85.key, ...), custom_call_target="tpu_custom_call" | custom-call | flops 4000000000 | bytes 1 | tf_op jit(solution)/shard_map/last_use/pallas_call | solution.py:975
  34.2 0.0 collective-permute-done.12.first
  34.2 0.0 collective-permute-done.10.second
  34.2 1.1 %first_use.7 = (f32[128,512]{1,0:T(8,128)S(1)}, f32[128,512]{1,0:T(8,128)S(1)}, f32[128,512]{1,0:T(8,128)S(1)}, f32[128,512]{1,0:T(8,128)S(1)}, f32[16,128]{1,0:T(8,128)S(1)}) custom-call(s32[1]{0:T(128)} %bitcast.place, bf16[128,2048]{1,0:T(8,128)(2,1)S(1)} %get-tuple-element.84.query, bf16[128,2048]{1,0:T(8,128)(2,1)S(1)} %get-tuple-element.85.key, ...), custom_call_target="tpu_custom_call" | custom-call | flops 4800000000 | bytes 1 | tf_op jit(solution)/shard_map/first_use/pallas_call | solution.py:840
  35.3 0.0 collective-permute-done.14.third
  35.3 1.5 %last_use.5 = (bf16[128,2048]{1,0:T(8,128)(2,1)}, bf16[128,2048]{1,0:T(8,128)(2,1)}, bf16[128,2048]{1,0:T(8,128)(2,1)}, bf16[128,2048]{1,0:T(8,128)(2,1)}, f32[12,128]{1,0:T(8,128)S(1)}) custom-call(s32[1]{0:T(128)} %bitcast.place, ...), custom_call_target="tpu_custom_call", output_to_operand_aliasing={{0}: (16, {}), {1}: (17, {}), {2}: (18, {}), {3}: (19, {})} | custom-call | flops 4000000000 | bytes 1 | tf_op jit(solution)/shard_map/last_use/pallas_call | solution.py:975
  36.9 0.4 collective-permute-done.11.third
  37.2 0.6 %collective-permute-start.15 = (f32[512,128]{1,0:T(8,128)S(1)}, f32[512,128]{1,0:T(8,128)S(1)}, u32[]{:S(2)}, u32[]{:S(2)}) collective-permute-start(f32[512,128]{1,0:T(8,128)S(1)} %collective-permute-done.11.third), channel_id=1, source_target_pairs={{0,1},{1,0},{2,3},{3,2},{4,5},{5,4},{6,7},{7,6},{8,9},{9,8},{10,11... | collective-permute-start | bytes 786440 | tf_op jit(solution)/shard_map/ppermute | solution.py:837
  37.8 1.5 %last_use.6 = (bf16[128,2048]{1,0:T(8,128)(2,1)}, bf16[128,2048]{1,0:T(8,128)(2,1)}, bf16[128,2048]{1,0:T(8,128)(2,1)}, bf16[128,2048]{1,0:T(8,128)(2,1)}, f32[12,128]{1,0:T(8,128)S(1)}) custom-call(s32[1]{0:T(128)} %bitcast.place, ...), custom_call_target="tpu_custom_call", output_to_operand_aliasing={{0}: (16, {}), {1}: (17, {}), {2}: (18, {}), {3}: (19, {})} | custom-call | flops 4000000000 | bytes 1 | tf_op jit(solution)/shard_map/last_use/pallas_call | solution.py:975
  39.3 0.0 collective-permute-done.15.third
  39.3 1.8 %last_use.7 = (bf16[128,2048]{1,0:T(8,128)(2,1)}, bf16[128,2048]{1,0:T(8,128)(2,1)}, bf16[128,2048]{1,0:T(8,128)(2,1)}, bf16[128,2048]{1,0:T(8,128)(2,1)}, f32[11,16,128]{2,1,0:T(8,128)}, /*index=5*/f32[16,128]{1,0:T(8,128)}) custom-call(s32[1]{0:T(128)} %bitcast.place, ...), custom_call_target="tpu_custom_call", output_to_operand_aliasing={{0}: (31, {}), {1}: (32, {}), {2}: (33, {}), {3}: (34, {})} | custom-call | flops 4000000000 | bytes 1 | tf_op jit(solution)/shard_map/last_use/pallas_call | solution.py:975
Async XLA Ops:
  3.3 2.0 %collective-permute-start = (f32[1040,128]{1,0:T(8,128)S(1)}, f32[1040,128]{1,0:T(8,128)S(1)}, u32[]{:S(2)}, u32[]{:S(2)}) collective-permute-start(f32[1040,128]{1,0:T(8,128)S(1)} %get-tuple-element.90), channel_id=1, source_target_pairs={{0,1},{1,0},{2,3},{3,2},{4,5},{5,4},{6,7},{7,6},{8,9},{9,8},{10,11... | collective-permute-start | bytes 1597448 | tf_op jit(solution)/shard_map/ppermute | solution.py:837
  5.6 9.1 %collective-permute-start.1 = (f32[528,128]{1,0:T(8,128)S(1)}, f32[528,128]{1,0:T(8,128)S(1)}, u32[]{:S(2)}, u32[]{:S(2)}) collective-permute-start(f32[528,128]{1,0:T(8,128)S(1)} %get-tuple-element.93), channel_id=1, source_target_pairs={{0,2},{1,3},{2,0},{3,1},{4,6},{5,7},{6,4},{7,5},{8,10},{9,11},{10,... | collective-permute-start | bytes 811016 | tf_op jit(solution)/shard_map/ppermute | solution.py:837
  9.7 4.4 %collective-permute-start.2 = (f32[512,128]{1,0:T(8,128)S(1)}, f32[512,128]{1,0:T(8,128)S(1)}, u32[]{:S(2)}, u32[]{:S(2)}) collective-permute-start(f32[512,128]{1,0:T(8,128)S(1)} %get-tuple-element.96), channel_id=1, source_target_pairs={{0,1},{1,0},{2,3},{3,2},{4,5},{5,4},{6,7},{7,6},{8,9},{9,8},{10,11... | collective-permute-start | bytes 786440 | tf_op jit(solution)/shard_map/ppermute | solution.py:837
  10.4 3.7 %collective-permute-start.4 = (f32[512,128]{1,0:T(8,128)S(1)}, f32[512,128]{1,0:T(8,128)S(1)}, u32[]{:S(2)}, u32[]{:S(2)}) collective-permute-start(f32[512,128]{1,0:T(8,128)S(1)} %get-tuple-element.97), channel_id=1, source_target_pairs={{0,1},{1,0},{2,3},{3,2},{4,5},{5,4},{6,7},{7,6},{8,9},{9,8},{10,11... | collective-permute-start | bytes 786440 | tf_op jit(solution)/shard_map/ppermute | solution.py:837
  10.5 9.8 %collective-permute-start.3 = (f32[512,128]{1,0:T(8,128)S(1)}, f32[512,128]{1,0:T(8,128)S(1)}, u32[]{:S(2)}, u32[]{:S(2)}) collective-permute-start(f32[512,128]{1,0:T(8,128)S(1)} %get-tuple-element.94.after), channel_id=1, source_target_pairs={{0,2},{1,3},{2,0},{3,1},{4,6},{5,7},{6,4},{7,5},{8,10},{9,11},{10,... | collective-permute-start | bytes 786440 | tf_op jit(solution)/shard_map/ppermute | solution.py:837
  10.5 14.7 %collective-permute-start.9 = (f32[4096,128]{1,0:T(8,128)S(1)}, f32[4096,128]{1,0:T(8,128)S(1)}, u32[]{:S(2)}, u32[]{:S(2)}) collective-permute-start(f32[4096,128]{1,0:T(8,128)S(1)} %get-tuple-element.102), channel_id=1, source_target_pairs={{0,1},{1,0},{2,3},{3,2},{4,5},{5,4},{6,7},{7,6},{8,9},{9,8},{10,11... | collective-permute-start | bytes 6291464 | tf_op jit(solution)/shard_map/ppermute | solution.py:837
  15.0 6.5 %collective-permute-start.6 = (f32[512,128]{1,0:T(8,128)S(1)}, f32[512,128]{1,0:T(8,128)S(1)}, u32[]{:S(2)}, u32[]{:S(2)}) collective-permute-start(f32[512,128]{1,0:T(8,128)S(1)} %second_merge.2.rest_0_), channel_id=1, source_target_pairs={{0,1},{1,0},{2,4},{4,2},{3,5},{5,3},{6,7},{7,6},{8,9},{9,8},{10,12... | collective-permute-start | bytes 786440 | tf_op jit(solution)/shard_map/ppermute | solution.py:837
  20.6 7.0 %collective-permute-start.5 = (f32[512,128]{1,0:T(8,128)S(1)}, f32[512,128]{1,0:T(8,128)S(1)}, u32[]{:S(2)}, u32[]{:S(2)}) collective-permute-start(f32[512,128]{1,0:T(8,128)S(1)} %second_merge.3), channel_id=1, source_target_pairs={{0,1},{1,0},{2,4},{4,2},{3,5},{5,3},{6,7},{7,6},{8,9},{9,8},{10,12... | collective-permute-start | bytes 786440 | tf_op jit(solution)/shard_map/ppermute | solution.py:837
  21.5 4.9 %collective-permute-start.7 = (f32[528,128]{1,0:T(8,128)S(1)}, f32[528,128]{1,0:T(8,128)S(1)}, u32[]{:S(2)}, u32[]{:S(2)}) collective-permute-start(f32[528,128]{1,0:T(8,128)S(1)} %collective-permute-done.1.first.chip_total), channel_id=1, source_target_pairs={{0,1},{1,0},{2,3},{3,2},{4,5},{5,4},{6,7},{7,6},{8,9},{9,8},{10,11... | collective-permute-start | bytes 811016 | tf_op jit(solution)/shard_map/ppermute | solution.py:837
  21.6 10.5 %collective-permute-start.13 = (f32[512,128]{1,0:T(8,128)S(1)}, f32[512,128]{1,0:T(8,128)S(1)}, u32[]{:S(2)}, u32[]{:S(2)}) collective-permute-start(f32[512,128]{1,0:T(8,128)S(1)} %collective-permute-done.6.second), channel_id=1, source_target_pairs={{0,2},{1,3},{2,0},{3,1},{4,6},{5,7},{6,4},{7,5},{8,10},{9,11},{10,... | collective-permute-start | bytes 786440 | tf_op jit(solution)/shard_map/ppermute | solution.py:837
  24.9 1.5 %collective-permute-start.8 = (f32[512,128]{1,0:T(8,128)S(1)}, f32[512,128]{1,0:T(8,128)S(1)}, u32[]{:S(2)}, u32[]{:S(2)}) collective-permute-start(f32[512,128]{1,0:T(8,128)S(1)} %collective-permute-done.6.second), channel_id=1, source_target_pairs={{0,1},{1,0},{2,3},{3,2},{4,5},{5,4},{6,7},{7,6},{8,9},{9,8},{10,11... | collective-permute-start | bytes 786440 | tf_op jit(solution)/shard_map/ppermute | solution.py:837
  27.6 9.6 %collective-permute-start.11 = (f32[512,128]{1,0:T(8,128)S(1)}, f32[512,128]{1,0:T(8,128)S(1)}, u32[]{:S(2)}, u32[]{:S(2)}) collective-permute-start(f32[512,128]{1,0:T(8,128)S(1)} %collective-permute-done.5.second), channel_id=1, source_target_pairs={{0,2},{1,3},{2,0},{3,1},{4,6},{5,7},{6,4},{7,5},{8,10},{9,11},{10,... | collective-permute-start | bytes 786440 | tf_op jit(solution)/shard_map/ppermute | solution.py:837
  28.5 5.7 %collective-permute-start.10 = (f32[512,128]{1,0:T(8,128)S(1)}, f32[512,128]{1,0:T(8,128)S(1)}, u32[]{:S(2)}, u32[]{:S(2)}) collective-permute-start(f32[512,128]{1,0:T(8,128)S(1)} %collective-permute-done.5.second), channel_id=1, source_target_pairs={{0,1},{1,0},{2,3},{3,2},{4,5},{5,4},{6,7},{7,6},{8,9},{9,8},{10,11... | collective-permute-start | bytes 786440 | tf_op jit(solution)/shard_map/ppermute | solution.py:837
  32.1 3.2 %collective-permute-start.14 = (f32[512,128]{1,0:T(8,128)S(1)}, f32[512,128]{1,0:T(8,128)S(1)}, u32[]{:S(2)}, u32[]{:S(2)}) collective-permute-start(f32[512,128]{1,0:T(8,128)S(1)} %collective-permute-done.13.third), channel_id=1, source_target_pairs={{0,1},{1,0},{2,3},{3,2},{4,5},{5,4},{6,7},{7,6},{8,9},{9,8},{10,11... | collective-permute-start | bytes 786440 | tf_op jit(solution)/shard_map/ppermute | solution.py:837
  32.4 1.8 %collective-permute-start.12 = (f32[512,128]{1,0:T(8,128)S(1)}, f32[512,128]{1,0:T(8,128)S(1)}, u32[]{:S(2)}, u32[]{:S(2)}) collective-permute-start(f32[512,128]{1,0:T(8,128)S(1)} %collective-permute-done.3.first), channel_id=1, source_target_pairs={{0,1},{1,0},{2,3},{3,2},{4,5},{5,4},{6,7},{7,6},{8,9},{9,8},{10,11... | collective-permute-start | bytes 786440 | tf_op jit(solution)/shard_map/ppermute | solution.py:837
  37.2 2.1 %collective-permute-start.15 = (f32[512,128]{1,0:T(8,128)S(1)}, f32[512,128]{1,0:T(8,128)S(1)}, u32[]{:S(2)}, u32[]{:S(2)}) collective-permute-start(f32[512,128]{1,0:T(8,128)S(1)} %collective-permute-done.11.third), channel_id=1, source_target_pairs={{0,1},{1,0},{2,3},{3,2},{4,5},{5,4},{6,7},{7,6},{8,9},{9,8},{10,11... | collective-permute-start | bytes 786440 | tf_op jit(solution)/shard_map/ppermute | solution.py:837

commit v5 on v4

--- a/solution.py
+++ b/solution.py
@@ -266,65 +266,126 @@
     return mxu(twice_lanes(turned), split_rows(right.astype(F32) * weight_column), NN)
 
 
+def first_export_half(state, core, weight, query, key, value, cotangent, out, ready):
+    heads, tok = weight.shape
+    dim = query.shape[1] // heads
+    half = heads // 2
+    spread = columns(half_first(weight, core))
+
+    def products(left, right):
+        for index in range(half):
+            head = core * half + index
+            out[pl.ds(index * dim, dim), :] = outer_products(
+                lane_block(left, head, dim),
+                lane_block(right, head, dim),
+                spread[:, index : index + 1],
+            )
+
+    @pl.when(state)
+    def _():
+        ready(key, value)
+        products(key, value)
+
+    @pl.when(jnp.logical_not(state))
+    def _():
+        ready(query, cotangent)
+        products(query, cotangent)
+
+
+def first_weights(position, gain, decay):
+    chip = position // 2
+    cross = gain.shape[0] - 3
+    running = running_decay(decay[...])
+    total = last_lane(running)
+    weight = jnp.where(
+        chip % 2 == 0,
+        jnp.exp(total - running),
+        jnp.where(chip == 1, gain[cross + 1], gain[cross + 2]) * jnp.exp(running),
+    )
+    return weight, total
+
+
 def first_export_kernel(
-    place, query, key, value, cotangent, gain, decay, send, keep, *rest
+    place, query, key, value, cotangent, gain, decay, send, *rest
 ):
-    kept, (lefts, rights, sems) = rest[:6], rest[6:]
+    kept, sems = rest[:6], rest[6]
     position = place[0]
     core = position % 2
-    chip = position // 2
     heads, tok = decay.shape
-    width = query.shape[1]
-    dim = width // heads
     half = heads // 2
-    cross = gain.shape[0] - 3
-    wide = half * dim
-    state = chip % 2 == 0
-    copies = []
-    for side in range(2):
-        lanes = pl.ds(pl.multiple_of((1 - core if side == 0 else core) * wide, wide), wide)
-        for slot, (chosen, plain, into) in enumerate(((key, query, lefts), (value, cotangent, rights))):
-            sem = sems.at[2 * side + slot]
-            target = into.at[:, pl.ds(side * wide, wide)]
-
-            @pl.when(state)
-            def _(chosen=chosen, target=target, sem=sem, lanes=lanes):
-                pltpu.make_async_copy(chosen.at[:, lanes], target, sem).start()
-
-            @pl.when(jnp.logical_not(state))
-            def _(plain=plain, target=target, sem=sem, lanes=lanes):
-                pltpu.make_async_copy(plain.at[:, lanes], target, sem).start()
-
-            copies.append(pltpu.make_async_copy(plain.at[:, lanes], target, sem))
-    sources = (query, key, value, cotangent, gain, decay)
-    moves = [
-        pltpu.make_async_copy(source, target, sems.at[4 + number])
-        for number, (source, target) in enumerate(zip(sources, kept))
+    wide = query.shape[1] // 2
+    state = position // 2 % 2 == 0
+    sources = (query, key, value, cotangent)
+    names = ("query", "key", "value", "cotangent")
+    moves = {}
+    for number, (name, source, target) in enumerate(zip(names, sources, kept)):
+        for side in range(2):
+            lanes = pl.ds(pl.multiple_of((1 - core if side == 0 else core) * wide, wide), wide)
+            moves[name, side] = pltpu.make_async_copy(
+                source.at[:, lanes], target.at[:, lanes], sems.at[2 * number + side]
+            )
+    small = [
+        pltpu.make_async_copy(source, target, sems.at[8 + number])
+        for number, (source, target) in enumerate(zip((gain, decay), kept[4:]))
     ]
-    for move in reversed(moves):
+    for move in small:
         move.start()
-    for move in moves[4:]:
+
+    def start(*order):
+        for side in range(2):
+            for name in order:
+                moves[name, side].start()
+
+    @pl.when(state)
+    def _():
+        start("key", "value")
+        start("query", "cotangent")
+
+    @pl.when(jnp.logical_not(state))
+    def _():
+        start("query", "cotangent")
+        start("key", "value")
+
+    for move in small:
         move.wait()
-    gains, decays = kept[4:]
-    running = running_decay(decays[...])
-    total = last_lane(running)
-    lift = jnp.exp(running)
-    weight = jnp.where(
-        state, jnp.exp(total - running), jnp.where(chip == 1, gains[cross + 1], gains[cross + 2]) * lift
-    )
-    spread = columns(half_first(weight, 1 - core))
-    send[pl.ds(half * dim, heads), :] = total
-    for index in range(heads):
-        if index % half == 0:
-            for copy in copies[2 * (index // half) : 2 * (index // half) + 2]:
-                copy.wait()
-        lanes = slice(index * dim, (index + 1) * dim)
-        rows = pl.ds(index % half * dim, dim)
-        (send if index < half else keep)[rows, :] = outer_products(
-            lefts[:, lanes], rights[:, lanes], spread[:, index : index + 1]
-        )
-    for move in moves[:4]:
-        move.wait()
+    weight, total = first_weights(position, *kept[4:])
+    send[pl.ds(send.shape[0] - heads, heads), :] = total
+
+    def ready(left, right):
+        for name, target in zip(names, kept):
+            if target is left or target is right:
+                moves[name, 0].wait()
+
+    first_export_half(state, 1 - core, weight, *kept[:4], send, ready)
+
+    @pl.when(state)
+    def _():
+        for name in ("query", "cotangent"):
+            moves[name, 0].wait()
+
+    @pl.when(jnp.logical_not(state))
+    def _():
+        for name in ("key", "value"):
+            moves[name, 0].wait()
+
+    for name in names:
+        moves[name, 1].wait()
+
+
+def own_export_kernel(place, query, key, value, cotangent, gain, decay, after, keep):
+    position = place[0]
+    weight, _ = first_weights(position, gain, decay)
+    first_export_half(
+        position // 2 % 2 == 0,
+        position % 2,
+        weight,
+        query,
+        key,
+        value,
+        cotangent,
+        keep,
+        lambda left, right: None,
+    )
 
 
 def second_core(position):
@@ -385,7 +446,7 @@
     )
 
 
-def first_merge_kernel(place, decay, keep, got, after, *outs):
+def first_merge_kernel(place, decay, keep, got, *outs):
     position = place[0]
     chip = position // 2
     heads, tok = decay.shape
@@ -777,11 +838,11 @@
     later = natural(of_kind(counts, first_rows, 1), core) + last(1)
     upper = lax.broadcasted_iota(jnp.int32, (tok, tok), 0)
     lower = lax.broadcasted_iota(jnp.int32, (tok, tok), 1)
-    from_here = (upper >= lower).astype(F32)
-    every = jnp.ones((tok, tok), F32)
-    grad_decay[...] = jnp.dot(
-        own, from_here, precision=TOP_ACCURACY, preferred_element_type=F32
-    ) + jnp.dot(later, every, precision=TOP_ACCURACY, preferred_element_type=F32)
+    from_here = (upper >= lower).astype(BF16)
+    sums = jnp.concatenate([twice_rows(from_here), jnp.ones((2 * tok, tok), BF16)], axis=0)
+    grad_decay[...] = mxu(
+        jnp.concatenate([split_lanes(own), split_lanes(later)], axis=1), sums, NN
+    )
 
 
 def after(value, *others):
@@ -847,23 +908,36 @@
             **options,
         )(*operands, *unread)
 
-    send1, keep1, *kept = pl.pallas_call(
+    send1, *kept = pl.pallas_call(
         first_export_kernel,
-        out_shape=(pltpu.VMEM((half * dim + heads, dim), F32), pltpu.VMEM((half * dim, dim), F32))
+        out_shape=(pltpu.VMEM((half * dim + heads, dim), F32),)
         + tuple(pltpu.VMEM(array.shape, array.dtype) for array in inputs[1:]),
         in_specs=[SCALAR] + [IN_HBM] * 6,
-        scratch_shapes=[
-            pltpu.VMEM((tok, heads * dim), BF16),
-            pltpu.VMEM((tok, heads * dim), BF16),
-            pltpu.SemaphoreType.DMA((10,)),
-        ],
-        compiler_params=params(FIRST_LIMIT),
-        cost_estimate=cost(3.3),
+        scratch_shapes=[pltpu.SemaphoreType.DMA((10,))],
+        compiler_params=params(),
+        cost_estimate=cost(2),
         name="first_exports",
     )(place, *(pltpu.with_memory_space_constraint(array, pltpu.HBM) for array in inputs[1:]))
     inputs = (place, *kept)
     decay_log = kept[-1]
     got1 = swap(send1, core_swap)
+    keep1 = call(
+        own_export_kernel,
+        sds(half * dim, dim),
+        inputs,
+        (send1,),
+        cost(0.8, RATE_FIRST),
+        "own_exports",
+    )
+    first_sent = call(
+        first_merge_kernel,
+        tuple(sds(count * dim + (0 if part else heads), dim) for part, count in enumerate(counts)),
+        (place, decay_log, keep1, got1),
+        spent=cost(0.3),
+        name="first_merge",
+    )
+    first = [swap(first_sent[0], side_swap)]
+
     local_done = {}
 
     def local(part, mine, *unread):
@@ -878,17 +952,6 @@
         )
         return local_done[part, mine][-1]
 
-    done = local(0, True)
-    first_sent = call(
-        first_merge_kernel,
-        tuple(sds(count * dim + (0 if part else heads), dim) for part, count in enumerate(counts)),
-        (place, decay_log, keep1, got1),
-        (done,),
-        spent=cost(0.3),
-        name="first_merge",
-    )
-    first = [swap(block, side_swap) for block in first_sent]
-
     done = first_sent[-1]
     *send2, keep2, bundle = call(
         second_export_kernel,
@@ -910,15 +973,18 @@
             "second_merge",
         )
 
-    done = local(0, False, keep2)
-    done = local(1, True, done)
+    done = local(0, True, keep2)
+    first.append(swap(after(first_sent[1], done), side_swap))
+    done = local(0, False, done)
     sent = [second_merge(0, done, *got2[1:])]
-    done = local(1, False, sent[0])
+    done = local(1, True, sent[0])
     sent.append(second_merge(1, done))
     front = swap(bundle, core_swap)
     second = [swap(block, middle_swap) for block in sent]
     third = [swap(second[0], side_swap)]
     second_over = [swap(second[0], core_swap)]
+    done = local(1, False, second[0])
+
     used = {}
 
     def first_use(part, mine, *unread):
@@ -992,7 +1058,7 @@
         results = found[:4]
         last_rows.extend(found[4:])
 
-    done = first_use(0, True)
+    done = first_use(0, True, done)
     first_over = [swap(after(first[0], second[0]), core_swap)]
     done = first_use(0, False, done)
     second[1] = after(second[1], done)

time: 41.5 us -> 40.5 us (0.976)
  starting transfers between devices: 14.2 us -> 12.6 us
  waiting for transfers between devices: 3.8 us -> 4.52 us
    ppermute x16, starting transfers between devices: 14.2 us -> 12.6 us  [swap(): return lax.ppermute(block, 'ctx', route)]
    pallas_call x12 -> x13, Pallas kernels: 13.3 us -> 14.2 us  [call(): pl.pallas_call(kernel, out_shape=out_shape, in_specs=[SCALAR] + [pl.Block...]
    pallas_call x1, Pallas kernels: 2.64 us -> 1.81 us  [line_device(): pl.pallas_call(first_export_kernel, out_shape=(pltpu.VMEM((half * dim + h...]
    ppermute x16, waiting for transfers between devices: 3.8 us -> 4.52 us  [swap(): return lax.ppermute(block, 'ctx', route)]
  transfers between devices with their start and end apart: 16 -> 16, of which waited for: 5 -> 3; matrix products, arithmetic and copies ran while one was open for 0% -> 0% of each run, Pallas kernels for 43% -> 46%
where the time goes in v5:
time: 40.5 us; the launch traced here: 40.4 us
  Pallas kernels  22.3 us (55%)
  starting transfers between devices  12.6 us (31%)
  waiting for transfers between devices  4.52 us (11%)
  between operations  1 us (2%)
    pallas_call x13, Pallas kernels, call(): pl.pallas_call(kernel, out_shape=out_shape, in_specs=[SCALAR] + [pl.Block...  14.2 us
    ppermute x16, starting transfers between devices, swap(): return lax.ppermute(block, 'ctx', route)  12.6 us
    pallas_call x4, Pallas kernels, last_use(): pl.pallas_call(functools.partial(last_use_kernel, lows[part], mine, count...  6.28 us
    ppermute x16, waiting for transfers between devices, swap(): return lax.ppermute(block, 'ctx', route)  4.52 us
    pallas_call x1, Pallas kernels, line_device(): pl.pallas_call(first_export_kernel, out_shape=(pltpu.VMEM((half * dim + h...  1.81 us
  transfers between devices with their start and end apart: 16, of which 3 were waited for; matrix products, arithmetic and copies ran while one was open for 0% of the time, Pallas kernels for 46%

profile of v5, /device:TPU:1, one launch (start us, length us, event | category | flops | bytes accessed | tf_op | source)
XLA Modules:
  0.0 40.4 jit_solution(15436461786180728873)
XLA Ops:
  0.6 1.8 %first_exports.1 = (f32[1040,128]{1,0:T(8,128)S(1)}, bf16[128,2048]{1,0:T(8,128)(2,1)S(1)}, bf16[128,2048]{1,0:T(8,128)(2,1)S(1)}, bf16[128,2048]{1,0:T(8,128)(2...) custom-call(s32[1]{0:T(128)} %bitcast.place, bf16[128,2048]{1,0:T(8,128)(2,1)} %query.1, ...), custom_call_target="tpu_custom_call" | custom-call | flops 32000000000 | bytes 1 | tf_op jit(solution)/shard_map/first_exports/pallas_call | solution.py:911
  2.5 0.1 collective-permute-start
  2.6 0.8 %own_exports.1.keep.keep1 = f32[1024,128]{1,0:T(8,128)S(1)} custom-call(s32[1]{0:T(128)} %bitcast.place, bf16[128,2048]{1,0:T(8,128)(2,1)S(1)} %get-tuple-element.84.query, bf16[128,2048]{1,0:T(8,128)(2,1)S(1)} %get-tuple-element.85.key, bf16[128,2048]{1,0:T(8,128)(2,1)S(1)} %get-tuple-element.86.value, bf16[128,2048]{1,0:T(8,128)(2,1)S(1)} %get-tuple-element.87.cotangent, ...), custom_call_target="tpu_custom_call" | custom-call | flops 12800000000 | bytes 1 | tf_op jit(solution)/shard_map/own_exports/pallas_call | solution.py:901
  3.4 1.0 %collective-permute-done.got.first_got = f32[1040,128]{1,0:T(8,128)S(1)} collective-permute-done((f32[1040,128]{1,0:T(8,128)S(1)}, f32[1040,128]{1,0:T(8,128)S(1)}, u32[]{:S(2)}, u32[]{:S(2)}) %collective-permute-start) | collective-permute-done | bytes 532512 | tf_op jit(solution)/shard_map/ppermute | solution.py:898
  4.4 0.3 first_merge.1
  4.8 2.5 %collective-permute-start.1 = (f32[528,128]{1,0:T(8,128)S(1)}, f32[528,128]{1,0:T(8,128)S(1)}, u32[]{:S(2)}, u32[]{:S(2)}) collective-permute-start(f32[528,128]{1,0:T(8,128)S(1)} %get-tuple-element.91), channel_id=1, source_target_pairs={{0,2},{1,3},{2,0},{3,1},{4,6},{5,7},{6,4},{7,5},{8,10},{9,11},{10,... | collective-permute-start | bytes 811016 | tf_op jit(solution)/shard_map/ppermute | solution.py:898
  7.2 1.6 %second_exports.1 = (f32[512,128]{1,0:T(8,128)S(1)}, f32[512,128]{1,0:T(8,128)S(1)}, f32[1024,128]{1,0:T(8,128)S(1)}, f32[4096,128]{1,0:T(8,128)S(1)}) custom-call(s32[1]{0:T(128)} %bitcast.place, bf16[128,2048]{1,0:T(8,128)(2,1)S(1)} %get-tuple-element.84.query, bf16[128,2048]{1,0:T(8,128)(2,1)S(1)} %get-tuple-element.85.key, ...), custom_call_target="tpu_custom_call" | custom-call | flops 1600000 | bytes 1 | tf_op jit(solution)/shard_map/second_exports/pallas_call | solution.py:901
  8.9 0.7 %collective-permute-start.2 = (f32[512,128]{1,0:T(8,128)S(1)}, f32[512,128]{1,0:T(8,128)S(1)}, u32[]{:S(2)}, u32[]{:S(2)}) collective-permute-start(f32[512,128]{1,0:T(8,128)S(1)} %get-tuple-element.94), channel_id=1, source_target_pairs={{0,1},{1,0},{2,3},{3,2},{4,5},{5,4},{6,7},{7,6},{8,9},{9,8},{10,11... | collective-permute-start | bytes 786440 | tf_op jit(solution)/shard_map/ppermute | solution.py:898
  9.6 0.1 collective-permute-start.4
  9.7 0.4 %collective-permute-start.9 = (f32[4096,128]{1,0:T(8,128)S(1)}, f32[4096,128]{1,0:T(8,128)S(1)}, u32[]{:S(2)}, u32[]{:S(2)}) collective-permute-start(f32[4096,128]{1,0:T(8,128)S(1)} %get-tuple-element.101), channel_id=1, source_target_pairs={{0,1},{1,0},{2,3},{3,2},{4,5},{5,4},{6,7},{7,6},{8,9},{9,8},{10,11... | collective-permute-start | bytes 6291464 | tf_op jit(solution)/shard_map/ppermute | solution.py:898
  10.1 1.6 %local.4 = (f32[128,512]{1,0:T(8,128)S(1)}, f32[128,512]{1,0:T(8,128)S(1)}, f32[128,512]{1,0:T(8,128)S(1)}, f32[128,512]{1,0:T(8,128)S(1)}, f32[8,4,128]{2,1,0:T(4,128)S(1)}, /*index=5*/f32[4,128]{1,0:T(4,128)S(1)}) custom-call(s32[1]{0:T(128)} %bitcast.place, bf16[128,2048]{1,0:T(8,128)(2,1)S(1)} %get-tuple-element.84.query, ...), custom_call_target="tpu_custom_call" | custom-call | flops 16000000 | bytes 1 | tf_op jit(solution)/shard_map/local/pallas_call | solution.py:901
  11.7 0.1 collective-permute-start.3
  11.7 1.6 %local.5 = (f32[128,512]{1,0:T(8,128)S(1)}, f32[128,512]{1,0:T(8,128)S(1)}, f32[128,512]{1,0:T(8,128)S(1)}, f32[128,512]{1,0:T(8,128)S(1)}, f32[8,4,128]{2,1,0:T(4,128)S(1)}, /*index=5*/f32[4,128]{1,0:T(4,128)S(1)}) custom-call(s32[1]{0:T(128)} %bitcast.place, bf16[128,2048]{1,0:T(8,128)(2,1)S(1)} %get-tuple-element.84.query, ...), custom_call_target="tpu_custom_call" | custom-call | flops 16000000 | bytes 1 | tf_op jit(solution)/shard_map/local/pallas_call | solution.py:901
  13.3 0.0 collective-permute-done.2.rest_1_.got.second_got
  13.3 0.0 collective-permute-done.4.got.second_got
  13.3 0.5 %collective-permute-done.1.first.chip_total = f32[528,128]{1,0:T(8,128)S(1)} collective-permute-done((f32[528,128]{1,0:T(8,128)S(1)}, f32[528,128]{1,0:T(8,128)S(1)}, u32[]{:S(2)}, u32[]{:S(2)}) %collective-permute-start.1) | collective-permute-done | bytes 270368 | tf_op jit(solution)/shard_map/ppermute | solution.py:898
  13.8 0.3 second_merge.2.rest_0_
  14.1 1.0 %collective-permute-start.6 = (f32[512,128]{1,0:T(8,128)S(1)}, f32[512,128]{1,0:T(8,128)S(1)}, u32[]{:S(2)}, u32[]{:S(2)}) collective-permute-start(f32[512,128]{1,0:T(8,128)S(1)} %second_merge.2.rest_0_), channel_id=1, source_target_pairs={{0,1},{1,0},{2,4},{4,2},{3,5},{5,3},{6,7},{7,6},{8,9},{9,8},{10,12... | collective-permute-start | bytes 786440 | tf_op jit(solution)/shard_map/ppermute | solution.py:898
  15.1 1.6 %local.6 = (f32[128,512]{1,0:T(8,128)S(1)}, f32[128,512]{1,0:T(8,128)S(1)}, f32[128,512]{1,0:T(8,128)S(1)}, f32[128,512]{1,0:T(8,128)S(1)}, f32[8,4,128]{2,1,0:T(4,128)S(1)}, /*index=5*/f32[4,128]{1,0:T(4,128)S(1)}) custom-call(s32[1]{0:T(128)} %bitcast.place, bf16[128,2048]{1,0:T(8,128)(2,1)S(1)} %get-tuple-element.84.query, ...), custom_call_target="tpu_custom_call" | custom-call | flops 1600000000 | bytes 1 | tf_op jit(solution)/shard_map/local/pallas_call | solution.py:901
  16.7 3.0 %collective-permute-done.3.first = f32[512,128]{1,0:T(8,128)S(1)} collective-permute-done((f32[512,128]{1,0:T(8,128)S(1)}, f32[512,128]{1,0:T(8,128)S(1)}, u32[]{:S(2)}, u32[]{:S(2)}) %collective-permute-start.3) | collective-permute-done | bytes 262176 | tf_op jit(solution)/shard_map/ppermute | solution.py:898
  19.6 0.3 second_merge.3
  19.9 0.9 %collective-permute-start.5 = (f32[512,128]{1,0:T(8,128)S(1)}, f32[512,128]{1,0:T(8,128)S(1)}, u32[]{:S(2)}, u32[]{:S(2)}) collective-permute-start(f32[512,128]{1,0:T(8,128)S(1)} %second_merge.3), channel_id=1, source_target_pairs={{0,1},{1,0},{2,4},{4,2},{3,5},{5,3},{6,7},{7,6},{8,9},{9,8},{10,12... | collective-permute-start | bytes 786440 | tf_op jit(solution)/shard_map/ppermute | solution.py:898
  20.8 0.0 collective-permute-done.6.rest_0_.second
  20.8 0.1 collective-permute-start.7
  20.9 3.1 %collective-permute-start.13 = (f32[512,128]{1,0:T(8,128)S(1)}, f32[512,128]{1,0:T(8,128)S(1)}, u32[]{:S(2)}, u32[]{:S(2)}) collective-permute-start(f32[512,128]{1,0:T(8,128)S(1)} %collective-permute-done.6.rest_0_.second), channel_id=1, source_target_pairs={{0,2},{1,3},{2,0},{3,1},{4,6},{5,7},{6,4},{7,5},{8,10},{9,11},{10,... | collective-permute-start | bytes 786440 | tf_op jit(solution)/shard_map/ppermute | solution.py:898
  24.0 0.3 collective-permute-start.8
  24.3 1.6 %local.7 = (f32[128,512]{1,0:T(8,128)S(1)}, f32[128,512]{1,0:T(8,128)S(1)}, f32[128,512]{1,0:T(8,128)S(1)}, f32[128,512]{1,0:T(8,128)S(1)}, f32[8,4,128]{2,1,0:T(4,128)S(1)}, /*index=5*/f32[4,128]{1,0:T(4,128)S(1)}) custom-call(s32[1]{0:T(128)} %bitcast.place, bf16[128,2048]{1,0:T(8,128)(2,1)S(1)} %get-tuple-element.84.query, ...), custom_call_target="tpu_custom_call" | custom-call | flops 25600000000 | bytes 1 | tf_op jit(solution)/shard_map/local/pallas_call | solution.py:901
  25.9 0.0 collective-permute-done.9.front
  25.9 1.1 %first_use.4 = (f32[128,512]{1,0:T(8,128)S(1)}, f32[128,512]{1,0:T(8,128)S(1)}, f32[128,512]{1,0:T(8,128)S(1)}, f32[128,512]{1,0:T(8,128)S(1)}, f32[16,128]{1,0:T(8,128)S(1)}) custom-call(s32[1]{0:T(128)} %bitcast.place, bf16[128,2048]{1,0:T(8,128)(2,1)S(1)} %get-tuple-element.84.query, bf16[128,2048]{1,0:T(8,128)(2,1)S(1)} %get-tuple-element.85.key, ...), custom_call_target="tpu_custom_call" | custom-call | flops 4800000000 | bytes 1 | tf_op jit(solution)/shard_map/first_use/pallas_call | solution.py:901
  27.0 0.0 collective-permute-done.8.second
  27.0 0.0 collective-permute-done.7.first
  27.0 1.1 %first_use.5 = (f32[128,512]{1,0:T(8,128)S(1)}, f32[128,512]{1,0:T(8,128)S(1)}, f32[128,512]{1,0:T(8,128)S(1)}, f32[128,512]{1,0:T(8,128)S(1)}, f32[16,128]{1,0:T(8,128)S(1)}) custom-call(s32[1]{0:T(128)} %bitcast.place, bf16[128,2048]{1,0:T(8,128)(2,1)S(1)} %get-tuple-element.84.query, bf16[128,2048]{1,0:T(8,128)(2,1)S(1)} %get-tuple-element.85.key, ...), custom_call_target="tpu_custom_call" | custom-call | flops 4800000000 | bytes 1 | tf_op jit(solution)/shard_map/first_use/pallas_call | solution.py:901
  28.2 0.0 collective-permute-done.5.second
  28.2 0.1 collective-permute-start.11
  28.3 1.9 %collective-permute-start.10 = (f32[512,128]{1,0:T(8,128)S(1)}, f32[512,128]{1,0:T(8,128)S(1)}, u32[]{:S(2)}, u32[]{:S(2)}) collective-permute-start(f32[512,128]{1,0:T(8,128)S(1)} %collective-permute-done.5.second), channel_id=1, source_target_pairs={{0,1},{1,0},{2,3},{3,2},{4,5},{5,4},{6,7},{7,6},{8,9},{9,8},{10,11... | collective-permute-start | bytes 786440 | tf_op jit(solution)/shard_map/ppermute | solution.py:898
  30.1 1.1 %first_use.6 = (f32[128,512]{1,0:T(8,128)S(1)}, f32[128,512]{1,0:T(8,128)S(1)}, f32[128,512]{1,0:T(8,128)S(1)}, f32[128,512]{1,0:T(8,128)S(1)}, f32[16,128]{1,0:T(8,128)S(1)}) custom-call(s32[1]{0:T(128)} %bitcast.place, bf16[128,2048]{1,0:T(8,128)(2,1)S(1)} %get-tuple-element.84.query, bf16[128,2048]{1,0:T(8,128)(2,1)S(1)} %get-tuple-element.85.key, ...), custom_call_target="tpu_custom_call" | custom-call | flops 4800000000 | bytes 1 | tf_op jit(solution)/shard_map/first_use/pallas_call | solution.py:901
  31.2 0.0 collective-permute-done.13.third
  31.2 0.1 collective-permute-start.14
  31.3 0.5 %collective-permute-start.12 = (f32[512,128]{1,0:T(8,128)S(1)}, f32[512,128]{1,0:T(8,128)S(1)}, u32[]{:S(2)}, u32[]{:S(2)}) collective-permute-start(f32[512,128]{1,0:T(8,128)S(1)} %collective-permute-done.3.first), channel_id=1, source_target_pairs={{0,1},{1,0},{2,3},{3,2},{4,5},{5,4},{6,7},{7,6},{8,9},{9,8},{10,11... | collective-permute-start | bytes 786440 | tf_op jit(solution)/shard_map/ppermute | solution.py:898
  31.8 1.5 %last_use.4 = (bf16[128,2048]{1,0:T(8,128)(2,1)}, bf16[128,2048]{1,0:T(8,128)(2,1)}, bf16[128,2048]{1,0:T(8,128)(2,1)}, bf16[128,2048]{1,0:T(8,128)(2,1)}, f32[12,128]{1,0:T(8,128)S(1)}) custom-call(s32[1]{0:T(128)} %bitcast.place, bf16[128,2048]{1,0:T(8,128)(2,1)S(1)} %get-tuple-element.84.query, bf16[128,2048]{1,0:T(8,128)(2,1)S(1)} %get-tuple-element.85.key, ...), custom_call_target="tpu_custom_call" | custom-call | flops 4000000000 | bytes 1 | tf_op jit(solution)/shard_map/last_use/pallas_call | solution.py:1041
  33.3 0.0 collective-permute-done.12.first
  33.3 0.0 collective-permute-done.10.second
  33.3 1.3 %first_use.7 = (f32[128,512]{1,0:T(8,128)S(1)}, f32[128,512]{1,0:T(8,128)S(1)}, f32[128,512]{1,0:T(8,128)S(1)}, f32[128,512]{1,0:T(8,128)S(1)}, f32[16,128]{1,0:T(8,128)S(1)}) custom-call(s32[1]{0:T(128)} %bitcast.place, bf16[128,2048]{1,0:T(8,128)(2,1)S(1)} %get-tuple-element.84.query, bf16[128,2048]{1,0:T(8,128)(2,1)S(1)} %get-tuple-element.85.key, ...), custom_call_target="tpu_custom_call" | custom-call | flops 4800000000 | bytes 1 | tf_op jit(solution)/shard_map/first_use/pallas_call | solution.py:901
  34.6 0.0 collective-permute-done.14.third
  34.6 1.5 %last_use.5 = (bf16[128,2048]{1,0:T(8,128)(2,1)}, bf16[128,2048]{1,0:T(8,128)(2,1)}, bf16[128,2048]{1,0:T(8,128)(2,1)}, bf16[128,2048]{1,0:T(8,128)(2,1)}, f32[12,128]{1,0:T(8,128)S(1)}) custom-call(s32[1]{0:T(128)} %bitcast.place, ...), custom_call_target="tpu_custom_call", output_to_operand_aliasing={{0}: (16, {}), {1}: (17, {}), {2}: (18, {}), {3}: (19, {})} | custom-call | flops 4000000000 | bytes 1 | tf_op jit(solution)/shard_map/last_use/pallas_call | solution.py:1041
  36.2 0.0 collective-permute-done.11.third
  36.2 0.8 %collective-permute-start.15 = (f32[512,128]{1,0:T(8,128)S(1)}, f32[512,128]{1,0:T(8,128)S(1)}, u32[]{:S(2)}, u32[]{:S(2)}) collective-permute-start(f32[512,128]{1,0:T(8,128)S(1)} %collective-permute-done.11.third), channel_id=1, source_target_pairs={{0,1},{1,0},{2,3},{3,2},{4,5},{5,4},{6,7},{7,6},{8,9},{9,8},{10,11... | collective-permute-start | bytes 786440 | tf_op jit(solution)/shard_map/ppermute | solution.py:898
  37.0 1.5 %last_use.6 = (bf16[128,2048]{1,0:T(8,128)(2,1)}, bf16[128,2048]{1,0:T(8,128)(2,1)}, bf16[128,2048]{1,0:T(8,128)(2,1)}, bf16[128,2048]{1,0:T(8,128)(2,1)}, f32[12,128]{1,0:T(8,128)S(1)}) custom-call(s32[1]{0:T(128)} %bitcast.place, ...), custom_call_target="tpu_custom_call", output_to_operand_aliasing={{0}: (16, {}), {1}: (17, {}), {2}: (18, {}), {3}: (19, {})} | custom-call | flops 4000000000 | bytes 1 | tf_op jit(solution)/shard_map/last_use/pallas_call | solution.py:1041
  38.5 0.0 collective-permute-done.15.third
  38.5 1.7 %last_use.7 = (bf16[128,2048]{1,0:T(8,128)(2,1)}, bf16[128,2048]{1,0:T(8,128)(2,1)}, bf16[128,2048]{1,0:T(8,128)(2,1)}, bf16[128,2048]{1,0:T(8,128)(2,1)}, f32[11,16,128]{2,1,0:T(8,128)}, /*index=5*/f32[16,128]{1,0:T(8,128)}) custom-call(s32[1]{0:T(128)} %bitcast.place, ...), custom_call_target="tpu_custom_call", output_to_operand_aliasing={{0}: (31, {}), {1}: (32, {}), {2}: (33, {}), {3}: (34, {})} | custom-call | flops 4000000000 | bytes 1 | tf_op jit(solution)/shard_map/last_use/pallas_call | solution.py:1041
Async XLA Ops:
  2.5 2.0 %collective-permute-start = (f32[1040,128]{1,0:T(8,128)S(1)}, f32[1040,128]{1,0:T(8,128)S(1)}, u32[]{:S(2)}, u32[]{:S(2)}) collective-permute-start(f32[1040,128]{1,0:T(8,128)S(1)} %get-tuple-element.90.after), channel_id=1, source_target_pairs={{0,1},{1,0},{2,3},{3,2},{4,5},{5,4},{6,7},{7,6},{8,9},{9,8},{10,11... | collective-permute-start | bytes 1597448 | tf_op jit(solution)/shard_map/ppermute | solution.py:898
  4.8 9.0 %collective-permute-start.1 = (f32[528,128]{1,0:T(8,128)S(1)}, f32[528,128]{1,0:T(8,128)S(1)}, u32[]{:S(2)}, u32[]{:S(2)}) collective-permute-start(f32[528,128]{1,0:T(8,128)S(1)} %get-tuple-element.91), channel_id=1, source_target_pairs={{0,2},{1,3},{2,0},{3,1},{4,6},{5,7},{6,4},{7,5},{8,10},{9,11},{10,... | collective-permute-start | bytes 811016 | tf_op jit(solution)/shard_map/ppermute | solution.py:898
  8.9 4.4 %collective-permute-start.2 = (f32[512,128]{1,0:T(8,128)S(1)}, f32[512,128]{1,0:T(8,128)S(1)}, u32[]{:S(2)}, u32[]{:S(2)}) collective-permute-start(f32[512,128]{1,0:T(8,128)S(1)} %get-tuple-element.94), channel_id=1, source_target_pairs={{0,1},{1,0},{2,3},{3,2},{4,5},{5,4},{6,7},{7,6},{8,9},{9,8},{10,11... | collective-permute-start | bytes 786440 | tf_op jit(solution)/shard_map/ppermute | solution.py:898
  9.6 3.7 %collective-permute-start.4 = (f32[512,128]{1,0:T(8,128)S(1)}, f32[512,128]{1,0:T(8,128)S(1)}, u32[]{:S(2)}, u32[]{:S(2)}) collective-permute-start(f32[512,128]{1,0:T(8,128)S(1)} %get-tuple-element.97), channel_id=1, source_target_pairs={{0,1},{1,0},{2,3},{3,2},{4,5},{5,4},{6,7},{7,6},{8,9},{9,8},{10,11... | collective-permute-start | bytes 786440 | tf_op jit(solution)/shard_map/ppermute | solution.py:898
  9.7 16.2 %collective-permute-start.9 = (f32[4096,128]{1,0:T(8,128)S(1)}, f32[4096,128]{1,0:T(8,128)S(1)}, u32[]{:S(2)}, u32[]{:S(2)}) collective-permute-start(f32[4096,128]{1,0:T(8,128)S(1)} %get-tuple-element.101), channel_id=1, source_target_pairs={{0,1},{1,0},{2,3},{3,2},{4,5},{5,4},{6,7},{7,6},{8,9},{9,8},{10,11... | collective-permute-start | bytes 6291464 | tf_op jit(solution)/shard_map/ppermute | solution.py:898
  11.7 8.0 %collective-permute-start.3 = (f32[512,128]{1,0:T(8,128)S(1)}, f32[512,128]{1,0:T(8,128)S(1)}, u32[]{:S(2)}, u32[]{:S(2)}) collective-permute-start(f32[512,128]{1,0:T(8,128)S(1)} %get-tuple-element.96.after), channel_id=1, source_target_pairs={{0,2},{1,3},{2,0},{3,1},{4,6},{5,7},{6,4},{7,5},{8,10},{9,11},{10,... | collective-permute-start | bytes 786440 | tf_op jit(solution)/shard_map/ppermute | solution.py:898
  14.1 6.7 %collective-permute-start.6 = (f32[512,128]{1,0:T(8,128)S(1)}, f32[512,128]{1,0:T(8,128)S(1)}, u32[]{:S(2)}, u32[]{:S(2)}) collective-permute-start(f32[512,128]{1,0:T(8,128)S(1)} %second_merge.2.rest_0_), channel_id=1, source_target_pairs={{0,1},{1,0},{2,4},{4,2},{3,5},{5,3},{6,7},{7,6},{8,9},{9,8},{10,12... | collective-permute-start | bytes 786440 | tf_op jit(solution)/shard_map/ppermute | solution.py:898
  19.9 8.3 %collective-permute-start.5 = (f32[512,128]{1,0:T(8,128)S(1)}, f32[512,128]{1,0:T(8,128)S(1)}, u32[]{:S(2)}, u32[]{:S(2)}) collective-permute-start(f32[512,128]{1,0:T(8,128)S(1)} %second_merge.3), channel_id=1, source_target_pairs={{0,1},{1,0},{2,4},{4,2},{3,5},{5,3},{6,7},{7,6},{8,9},{9,8},{10,12... | collective-permute-start | bytes 786440 | tf_op jit(solution)/shard_map/ppermute | solution.py:898
  20.8 6.2 %collective-permute-start.7 = (f32[528,128]{1,0:T(8,128)S(1)}, f32[528,128]{1,0:T(8,128)S(1)}, u32[]{:S(2)}, u32[]{:S(2)}) collective-permute-start(f32[528,128]{1,0:T(8,128)S(1)} %collective-permute-done.1.first.chip_total), channel_id=1, source_target_pairs={{0,1},{1,0},{2,3},{3,2},{4,5},{5,4},{6,7},{7,6},{8,9},{9,8},{10,11... | collective-permute-start | bytes 811016 | tf_op jit(solution)/shard_map/ppermute | solution.py:898
  20.9 10.3 %collective-permute-start.13 = (f32[512,128]{1,0:T(8,128)S(1)}, f32[512,128]{1,0:T(8,128)S(1)}, u32[]{:S(2)}, u32[]{:S(2)}) collective-permute-start(f32[512,128]{1,0:T(8,128)S(1)} %collective-permute-done.6.rest_0_.second), channel_id=1, source_target_pairs={{0,2},{1,3},{2,0},{3,1},{4,6},{5,7},{6,4},{7,5},{8,10},{9,11},{10,... | collective-permute-start | bytes 786440 | tf_op jit(solution)/shard_map/ppermute | solution.py:898
  24.0 3.0 %collective-permute-start.8 = (f32[512,128]{1,0:T(8,128)S(1)}, f32[512,128]{1,0:T(8,128)S(1)}, u32[]{:S(2)}, u32[]{:S(2)}) collective-permute-start(f32[512,128]{1,0:T(8,128)S(1)} %collective-permute-done.6.rest_0_.second), channel_id=1, source_target_pairs={{0,1},{1,0},{2,3},{3,2},{4,5},{5,4},{6,7},{7,6},{8,9},{9,8},{10,11... | collective-permute-start | bytes 786440 | tf_op jit(solution)/shard_map/ppermute | solution.py:898
  28.2 8.0 %collective-permute-start.11 = (f32[512,128]{1,0:T(8,128)S(1)}, f32[512,128]{1,0:T(8,128)S(1)}, u32[]{:S(2)}, u32[]{:S(2)}) collective-permute-start(f32[512,128]{1,0:T(8,128)S(1)} %collective-permute-done.5.second), channel_id=1, source_target_pairs={{0,2},{1,3},{2,0},{3,1},{4,6},{5,7},{6,4},{7,5},{8,10},{9,11},{10,... | collective-permute-start | bytes 786440 | tf_op jit(solution)/shard_map/ppermute | solution.py:898
  28.3 5.1 %collective-permute-start.10 = (f32[512,128]{1,0:T(8,128)S(1)}, f32[512,128]{1,0:T(8,128)S(1)}, u32[]{:S(2)}, u32[]{:S(2)}) collective-permute-start(f32[512,128]{1,0:T(8,128)S(1)} %collective-permute-done.5.second), channel_id=1, source_target_pairs={{0,1},{1,0},{2,3},{3,2},{4,5},{5,4},{6,7},{7,6},{8,9},{9,8},{10,11... | collective-permute-start | bytes 786440 | tf_op jit(solution)/shard_map/ppermute | solution.py:898
  31.2 3.4 %collective-permute-start.14 = (f32[512,128]{1,0:T(8,128)S(1)}, f32[512,128]{1,0:T(8,128)S(1)}, u32[]{:S(2)}, u32[]{:S(2)}) collective-permute-start(f32[512,128]{1,0:T(8,128)S(1)} %collective-permute-done.13.third), channel_id=1, source_target_pairs={{0,1},{1,0},{2,3},{3,2},{4,5},{5,4},{6,7},{7,6},{8,9},{9,8},{10,11... | collective-permute-start | bytes 786440 | tf_op jit(solution)/shard_map/ppermute | solution.py:898
  31.3 2.0 %collective-permute-start.12 = (f32[512,128]{1,0:T(8,128)S(1)}, f32[512,128]{1,0:T(8,128)S(1)}, u32[]{:S(2)}, u32[]{:S(2)}) collective-permute-start(f32[512,128]{1,0:T(8,128)S(1)} %collective-permute-done.3.first), channel_id=1, source_target_pairs={{0,1},{1,0},{2,3},{3,2},{4,5},{5,4},{6,7},{7,6},{8,9},{9,8},{10,11... | collective-permute-start | bytes 786440 | tf_op jit(solution)/shard_map/ppermute | solution.py:898
  36.2 2.3 %collective-permute-start.15 = (f32[512,128]{1,0:T(8,128)S(1)}, f32[512,128]{1,0:T(8,128)S(1)}, u32[]{:S(2)}, u32[]{:S(2)}) collective-permute-start(f32[512,128]{1,0:T(8,128)S(1)} %collective-permute-done.11.third), channel_id=1, source_target_pairs={{0,1},{1,0},{2,3},{3,2},{4,5},{5,4},{6,7},{7,6},{8,9},{9,8},{10,11... | collective-permute-start | bytes 786440 | tf_op jit(solution)/shard_map/ppermute | solution.py:898

commit v6 on v5

--- a/solution.py
+++ b/solution.py
@@ -266,16 +266,18 @@
     return mxu(twice_lanes(turned), split_rows(right.astype(F32) * weight_column), NN)
 
 
-def first_export_half(state, core, weight, query, key, value, cotangent, out, ready):
+def first_export_half(state, core, weight, query, key, value, cotangent, outs, ready):
     heads, tok = weight.shape
     dim = query.shape[1] // heads
     half = heads // 2
     spread = columns(half_first(weight, core))
+    targets = [(out, row) for out in outs for row in range(out.shape[0] // dim)]
 
     def products(left, right):
         for index in range(half):
             head = core * half + index
-            out[pl.ds(index * dim, dim), :] = outer_products(
+            out, row = targets[index]
+            out[pl.ds(row * dim, dim), :] = outer_products(
                 lane_block(left, head, dim),
                 lane_block(right, head, dim),
                 spread[:, index : index + 1],
@@ -306,9 +308,9 @@
 
 
 def first_export_kernel(
-    place, query, key, value, cotangent, gain, decay, send, *rest
+    place, query, key, value, cotangent, gain, decay, *rest
 ):
-    kept, sems = rest[:6], rest[6]
+    sends, kept, sems = rest[:-7], rest[-7:-1], rest[-1]
     position = place[0]
     core = position % 2
     heads, tok = decay.shape
@@ -349,14 +351,14 @@
     for move in small:
         move.wait()
     weight, total = first_weights(position, *kept[4:])
-    send[pl.ds(send.shape[0] - heads, heads), :] = total
+    sends[0][pl.ds(sends[0].shape[0] - heads, heads), :] = total
 
     def ready(left, right):
         for name, target in zip(names, kept):
             if target is left or target is right:
                 moves[name, 0].wait()
 
-    first_export_half(state, 1 - core, weight, *kept[:4], send, ready)
+    first_export_half(state, 1 - core, weight, *kept[:4], sends, ready)
 
     @pl.when(state)
     def _():
@@ -372,9 +374,10 @@
         moves[name, 1].wait()
 
 
-def own_export_kernel(place, query, key, value, cotangent, gain, decay, after, keep):
+def own_export_kernel(place, query, key, value, cotangent, gain, decay, after, keep, totals):
     position = place[0]
-    weight, _ = first_weights(position, gain, decay)
+    weight, total = first_weights(position, gain, decay)
+    totals[...] = total
     first_export_half(
         position // 2 % 2 == 0,
         position % 2,
@@ -383,7 +386,7 @@
         key,
         value,
         cotangent,
-        keep,
+        [keep],
         lambda left, right: None,
     )
 
@@ -393,9 +396,9 @@
 
 
 def second_export_kernel(
-    place, query, key, value, cotangent, gain, decay, keep1, after, *outs
+    place, query, key, value, cotangent, gain, decay, keep1, first_got, after, *outs
 ):
-    *sends, keep, bundle = outs
+    *sends, keep, bundle, factors = outs
     position = place[0]
     core = second_core(position)
     chip = position // 2
@@ -412,6 +415,15 @@
     weight2 = jnp.where(chip == 0, 0.0, weight2)
     weight0 = jnp.where(state0, fall, gain[cross] * lift)
     spread = columns(jnp.concatenate([half_first(weight2, 1 - core), weight0], axis=0))
+    own_total = last_lane(running)
+    other_total = first_got[pl.ds(first_got.shape[0] - heads, heads), :]
+    inner = (chip == 1) | (chip == 2)
+    merged = (
+        *pair_factors(position, own_total, other_total, chip == 1),
+        jnp.where(inner, jnp.exp(own_total + other_total), 0.0),
+    )
+    for kind, rows in enumerate(merged):
+        factors[kind * half : (kind + 1) * half, :] = half_first(rows, core)[:half]
     bundle[pl.ds(heads * dim, half * dim), :] = keep1[...]
     place_of = [(part, row) for part, send in enumerate(sends) for row in range(send.shape[0] // dim)]
     for index in range(heads):
@@ -446,51 +458,40 @@
     )
 
 
-def first_merge_kernel(place, decay, keep, got, *outs):
-    position = place[0]
-    chip = position // 2
-    heads, tok = decay.shape
-    half = heads // 2
-    dim = keep.shape[0] // half
-    own_total = last_lane(running_decay(decay[...]))
-    other_total = got[pl.ds(half * dim, heads), :]
-    own_factor, other_factor = pair_factors(position, own_total, other_total, chip % 2 == 0)
-    own_factor = half_first(own_factor, position % 2)[:half]
-    other_factor = half_first(other_factor, position % 2)[:half]
-    head = 0
-    for part, out in enumerate(outs):
-        for index in range(out.shape[0] // dim):
-            rows = pl.ds(head * dim, dim)
-            out[pl.ds(index * dim, dim), :] = (
-                own_factor[head : head + 1] * keep[rows, :]
-                + other_factor[head : head + 1] * got[rows, :]
-            )
-            head += 1
-    outs[0][pl.ds(outs[0].shape[0] - heads, heads), :] = own_total + other_total
-
-
-def second_merge_kernel(low, place, decay, first_got, keep, got, first, *rest):
+def first_merge_kernel(low, place, totals, first_got, keep, got, *rest):
     out = rest[-1]
     position = place[0]
     chip = position // 2
-    heads, tok = decay.shape
-    half = heads // 2
-    dim = keep.shape[0] // half
-    own_total = last_lane(running_decay(decay[...]))
-    other_total = first_got[pl.ds(half * dim, heads), :]
-    own_factor, other_factor = pair_factors(position, own_total, other_total, chip == 1)
-    inner = (chip == 1) | (chip == 2)
-    first_factor = jnp.where(inner, jnp.exp(own_total + other_total), 0.0)
-    own_factor, other_factor, first_factor = (
-        half_first(factor, second_core(position)) for factor in (own_factor, other_factor, first_factor)
-    )
-    for index in range(out.shape[0] // dim):
+    heads, dim = totals.shape[0], keep.shape[1]
+    own_total = totals[...]
+    other_total = first_got[pl.ds(first_got.shape[0] - heads, heads), :]
+    count = out.shape[0] // dim
+    factors = pair_factors(position, own_total, other_total, chip % 2 == 0)
+    own_factor, other_factor = (take_half(rows, position % 2, low, count) for rows in factors)
+    for index in range(count):
         rows = pl.ds(index * dim, dim)
-        one = slice(low + index, low + index + 1)
+        one = slice(index, index + 1)
         out[rows, :] = (
             own_factor[one] * keep[pl.ds((low + index) * dim, dim), :]
             + other_factor[one] * got[rows, :]
-            + first_factor[one] * first[rows, :]
+        )
+    if low == 0:
+        out[pl.ds(count * dim, heads), :] = own_total + other_total
+
+
+def second_merge_kernel(low, factors, keep, got, first, *rest):
+    out = rest[-1]
+    dim = keep.shape[1]
+    half = keep.shape[0] // dim
+    for index in range(out.shape[0] // dim):
+        rows = pl.ds(index * dim, dim)
+        own, other, earlier = (
+            factors[kind * half + low + index : kind * half + low + index + 1, :] for kind in range(3)
+        )
+        out[rows, :] = (
+            own * keep[pl.ds((low + index) * dim, dim), :]
+            + other * got[rows, :]
+            + earlier * first[rows, :]
         )
 
 
@@ -586,6 +587,7 @@
     gain,
     decay,
     first_got,
+    pair_got,
     first,
     second,
     second_got,
@@ -608,7 +610,7 @@
     cross = gain.shape[0] - 3
     running = running_decay(decay[...])
     total = last_lane(running)
-    other = first_got[pl.ds(half * dim, heads), :]
+    other = first_got[pl.ds(first_got.shape[0] - heads, heads), :]
     odd = core == 1
     forward = chip != 0
     offset = jnp.where(forward == odd, other, 0.0)
@@ -634,12 +636,11 @@
     for index in range(count):
         lanes = slice(index * dim, (index + 1) * dim)
         rows = pl.ds(index * dim, dim)
-        kept = pl.ds((low + index) * dim, dim)
         one = slice(index, index + 1)
         head = side * half + low + index
         q, k, v, o = (lane_block(ref, head, dim) for ref in (query, key, value, cotangent))
         level0 = front[pl.ds(pl.multiple_of(head * dim, dim), dim), :]
-        pair1 = first_got[kept, :] if mine else front[pl.ds((heads + low + index) * dim, dim), :]
+        pair1 = pair_got[rows, :] if mine else front[pl.ds((heads + low + index) * dim, dim), :]
         pair2_kept = front[pl.ds((heads + half + low + index) * dim, dim), :]
         pair2 = jnp.where((chip == 3) == mine, pair2_kept, second_got[rows, :])
         state = jnp.where(chip == 2, second[rows, :], first[rows, :])
@@ -691,6 +692,7 @@
     gain,
     decay,
     first_got,
+    pair_got,
     chip_total,
     second,
     third,
@@ -704,9 +706,13 @@
     ending = parts is not None
     if ending:
         *rest, grad_gain, grad_decay, staged, sems, gain_stage, decay_stage, end_sems = rest
+    elif mine:
+        *rest, rows_out = rest
     else:
         *rest, rows_out, staged, sems = rest
-    outs = rest[-4:]
+    outs, before = rest[-4:], rest[:4]
+    if not mine:
+        rest = rest[4:]
     position = place[0]
     core = position % 2
     side = core if mine else 1 - core
@@ -718,7 +724,7 @@
     cross = gain.shape[0] - 3
     running = running_decay(decay[...])
     total = last_lane(running)
-    other = first_got[pl.ds(half * dim, heads), :]
+    other = first_got[pl.ds(first_got.shape[0] - heads, heads), :]
     chip_rows = chip_total[pl.ds(chip_total.shape[0] - heads, heads), :]
     odd = core == 1
     forward = chip == 3
@@ -735,6 +741,15 @@
     gathered = jnp.zeros((tok, tok), F32)
     flows = []
     copies = []
+    if not mine:
+        wide = before[0].shape[1]
+        start = pl.multiple_of(core * half * dim + low * dim, dim)
+        for number in range(4):
+            copy = pltpu.make_async_copy(
+                before[number], outs[number].at[:, pl.ds(start, wide)], sems.at[4 * count + number]
+            )
+            copy.start()
+            copies.append(copy)
     if ending:
         early = gain.shape[0] - 2
         copies.append(
@@ -743,7 +758,7 @@
             )
         )
         early_gains(parts, rest[:-4], core, gain_stage)
-        copies[0].start()
+        copies[-1].start()
     for index in range(count):
         lanes = slice(index * dim, (index + 1) * dim)
         rows = pl.ds(index * dim, dim)
@@ -753,7 +768,7 @@
         state = jnp.where(chip == 1, second[rows, :], third[rows, :])
         level0 = front[pl.ds(pl.multiple_of(head * dim, dim), dim), :]
         if mine:
-            pair1 = first_got[pl.ds((low + index) * dim, dim), :]
+            pair1 = pair_got[rows, :]
         else:
             pair1 = front[pl.ds((heads + low + index) * dim, dim), :]
         partner = jnp.where(odd, level0, pair1)
@@ -769,6 +784,9 @@
             acc_value[:, lanes] + jnp.where(forward, 0.0, left),
         )
         for number, result in enumerate(results):
+            if mine:
+                outs[number][:, lanes] = result.astype(BF16)
+                continue
             staged[number, :, lanes] = result.astype(BF16)
             copy = pltpu.make_async_copy(
                 staged.at[number, :, pl.ds(index * dim, dim)],
@@ -867,7 +885,7 @@
 RATE_SECOND = 0.001
 RATE_LOCAL = ((.01,.01),(1,16))
 RATE_USE = ((4,4),(4,4))
-RATE_LAST = ((4,4),(4,4))
+RATE_LAST = ((16,4),(4,4))
 RATE_MERGE = (4,4)
 
 
@@ -908,9 +926,12 @@
             **options,
         )(*operands, *unread)
 
-    send1, *kept = pl.pallas_call(
+    found = pl.pallas_call(
         first_export_kernel,
-        out_shape=(pltpu.VMEM((half * dim + heads, dim), F32),)
+        out_shape=tuple(
+            pltpu.VMEM((count * dim + (0 if part else heads), dim), F32)
+            for part, count in enumerate(counts)
+        )
         + tuple(pltpu.VMEM(array.shape, array.dtype) for array in inputs[1:]),
         in_specs=[SCALAR] + [IN_HBM] * 6,
         scratch_shapes=[pltpu.SemaphoreType.DMA((10,))],
@@ -918,24 +939,30 @@
         cost_estimate=cost(2),
         name="first_exports",
     )(place, *(pltpu.with_memory_space_constraint(array, pltpu.HBM) for array in inputs[1:]))
+    send1, kept = found[: len(counts)], found[len(counts) :]
     inputs = (place, *kept)
     decay_log = kept[-1]
-    got1 = swap(send1, core_swap)
-    keep1 = call(
+    got1 = [swap(block, core_swap) for block in send1]
+    keep1, totals = call(
         own_export_kernel,
-        sds(half * dim, dim),
+        (sds(half * dim, dim), sds(heads, tok)),
         inputs,
-        (send1,),
+        (send1[0],),
         cost(0.8, RATE_FIRST),
         "own_exports",
     )
-    first_sent = call(
-        first_merge_kernel,
-        tuple(sds(count * dim + (0 if part else heads), dim) for part, count in enumerate(counts)),
-        (place, decay_log, keep1, got1),
-        spent=cost(0.3),
-        name="first_merge",
-    )
+
+    def first_merge(part, *unread):
+        return call(
+            functools.partial(first_merge_kernel, lows[part]),
+            sds(counts[part] * dim + (0 if part else heads), dim),
+            (place, totals, got1[0], keep1, got1[part]),
+            unread,
+            cost(0.2, RATE_FIRST),
+            "first_merge",
+        )
+
+    first_sent = [first_merge(0)]
     first = [swap(first_sent[0], side_swap)]
 
     local_done = {}
@@ -953,10 +980,11 @@
         return local_done[part, mine][-1]
 
     done = first_sent[-1]
-    *send2, keep2, bundle = call(
+    *send2, keep2, bundle, factors = call(
         second_export_kernel,
-        tuple(sds(count * dim, dim) for count in counts) + (sds(half * dim, dim), sds(4 * half * dim, dim)),
-        (*inputs, keep1),
+        tuple(sds(count * dim, dim) for count in counts)
+        + (sds(half * dim, dim), sds(4 * half * dim, dim), sds(3 * half, tok)),
+        (*inputs, keep1, got1[0]),
         (done,),
         cost(1.6, RATE_SECOND),
         "second_exports",
@@ -964,17 +992,18 @@
     got2 = [swap(block, core_swap) for block in send2]
 
     def second_merge(part, *unread):
-        return call(
+        return pl.pallas_call(
             functools.partial(second_merge_kernel, lows[part]),
-            sds(counts[part] * dim, dim),
-            (place, decay_log, got1, keep2, got2[part], first[part]),
-            unread,
-            cost(0.3, RATE_MERGE[part]),
-            "second_merge",
-        )
+            out_shape=sds(counts[part] * dim, dim),
+            in_specs=[pl.BlockSpec()] * 4 + [ANYWHERE] * len(unread),
+            compiler_params=params(),
+            cost_estimate=cost(0.3, RATE_MERGE[part]),
+            name="second_merge",
+        )(factors, keep2, got2[part], first[part], *unread)
 
     done = local(0, True, keep2)
-    first.append(swap(after(first_sent[1], done), side_swap))
+    first_sent.append(first_merge(1, done))
+    first.append(swap(first_sent[1], side_swap))
     done = local(0, False, done)
     sent = [second_merge(0, done, *got2[1:])]
     done = local(1, True, sent[0])
@@ -994,7 +1023,8 @@
             (sds(tok, count * dim),) * 4 + (sds(4 * count, tok),),
             (
                 *inputs,
-                got1,
+                got1[0],
+                got1[part],
                 (first if mine else first_over)[part],
                 (second if mine else second_over)[part],
                 got2[part],
@@ -1008,14 +1038,15 @@
         return used[part, mine][-1]
 
     results = ()
-    last_rows = []
+    last_rows, held = [], {}
 
     def last_use(part, mine, ending=False):
         nonlocal results
         count = counts[part]
         operands = (
             *inputs,
-            got1,
+            got1[0],
+            got1[part],
             first[0],
             (second if mine else second_over)[part],
             (third if mine else third_over)[part],
@@ -1031,6 +1062,18 @@
                 *(used[key][4] for key in order),
                 *last_rows,
             )
+        if mine:
+            *found, last = call(
+                functools.partial(last_use_kernel, lows[part], mine, None),
+                (sds(tok, count * dim, dtype=BF16),) * 4 + (sds(3 * count, tok),),
+                operands,
+                spent=cost(0.15 * count, RATE_LAST[part][0]),
+                name="last_use",
+            )
+            held[part] = found
+            last_rows.append(last)
+            return
+        operands = (*operands, *held[part])
         before = len(operands) + len(rows)
         tail = (sds(*level_gain.shape), sds(heads, tok)) if ending else (sds(3 * count, tok),)
         ending_scratch = [
@@ -1041,18 +1084,16 @@
         found = pl.pallas_call(
             functools.partial(last_use_kernel, lows[part], mine, counts if ending else None),
             out_shape=(sds(tok, heads * dim, dtype=BF16),) * 4 + tail,
-            in_specs=[SCALAR]
-            + [pl.BlockSpec()] * (before - 1)
-            + [ANYWHERE] * len(results),
+            in_specs=[SCALAR] + [pl.BlockSpec()] * (before - 1) + [ANYWHERE] * len(results),
             out_specs=(ANYWHERE,) * 4 + (ANYWHERE if ending else pl.BlockSpec(),) * len(tail),
             input_output_aliases={before + at: at for at in range(len(results))},
             scratch_shapes=[
                 pltpu.VMEM((4, tok, count * dim), BF16),
-                pltpu.SemaphoreType.DMA((4 * count,)),
+                pltpu.SemaphoreType.DMA((4 * count + 4,)),
             ]
             + ending_scratch * ending,
             compiler_params=params(),
-            cost_estimate=cost(0.25 * count, RATE_LAST[part][not mine]),
+            cost_estimate=cost(0.25 * count, RATE_LAST[part][1]),
             name="last_use",
         )(*operands, *rows, *results)
         results = found[:4]

time: 40.5 us -> 39.6 us (0.978)
  Pallas kernels: 22.3 us -> 20 us
  waiting for transfers between devices: 4.52 us -> 5.13 us
  starting transfers between devices: 12.6 us -> 13.1 us
    pallas_call x4 -> x2, Pallas kernels: 6.28 us -> 3.41 us  [last_use(): pl.pallas_call(functools.partial(last_use_kernel, lows[part], mine, count...]
    ppermute x16 -> x17, waiting for transfers between devices: 4.52 us -> 5.13 us  [swap(): return lax.ppermute(block, 'ctx', route)]
    pallas_call x13 -> x14, Pallas kernels: 14.2 us -> 14.7 us  [call(): pl.pallas_call(kernel, out_shape=out_shape, in_specs=[SCALAR] + [pl.Block...]
    ppermute x16 -> x17, starting transfers between devices: 12.6 us -> 13.1 us  [swap(): return lax.ppermute(block, 'ctx', route)]
    pallas_call x1 -> x3, Pallas kernels: 1.81 us -> 1.93 us  [the longest x1 1.81 us: line_device(): pl.pallas_call(first_export_kernel, out_shape=tuple((pltpu.VMEM((count *...]
  transfers between devices with their start and end apart: 16 -> 17, of which waited for: 3 -> 5; matrix products, arithmetic and copies ran while one was open for 0% -> 0% of each run, Pallas kernels for 46% -> 42%
where the time goes in v6:
time: 39.6 us; the launch traced here: 39.2 us
  Pallas kernels  20 us (51%)
  starting transfers between devices  13.1 us (33%)
  waiting for transfers between devices  5.13 us (13%)
  between operations  0.95 us (2%)
    pallas_call x14, Pallas kernels, call(): pl.pallas_call(kernel, out_shape=out_shape, in_specs=[SCALAR] + [pl.Block...  14.7 us
    ppermute x17, starting transfers between devices, swap(): return lax.ppermute(block, 'ctx', route)  13.1 us
    ppermute x17, waiting for transfers between devices, swap(): return lax.ppermute(block, 'ctx', route)  5.13 us
    pallas_call x2, Pallas kernels, last_use(): pl.pallas_call(functools.partial(last_use_kernel, lows[part], mine, count...  3.41 us
    pallas_call x1, Pallas kernels, line_device(): pl.pallas_call(first_export_kernel, out_shape=tuple((pltpu.VMEM((count *...  1.81 us
  transfers between devices with their start and end apart: 17, of which 5 were waited for; matrix products, arithmetic and copies ran while one was open for 0% of the time, Pallas kernels for 42%

profile of v6, /device:TPU:1, one launch (start us, length us, event | category | flops | bytes accessed | tf_op | source)
XLA Modules:
  0.0 39.2 jit_solution(9086352519252049502)
XLA Ops:
  0.6 1.8 %first_exports.1 = (f32[528,128]{1,0:T(8,128)S(1)}, f32[512,128]{1,0:T(8,128)S(1)}, bf16[128,2048]{1,0:T(8,128)(2,1)S(1)}, bf16[128,2048]{1,0:T(8,128)(2,1)S(1)}...) custom-call(s32[1]{0:T(128)} %bitcast.place, ...), custom_call_target="tpu_custom_call" | custom-call | flops 32000000000 | bytes 1 | tf_op jit(solution)/shard_map/first_exports/pallas_call | solution.py:929
  2.5 0.1 collective-permute-start
  2.6 0.5 %collective-permute-start.1 = (f32[512,128]{1,0:T(8,128)S(1)}, f32[512,128]{1,0:T(8,128)S(1)}, u32[]{:S(2)}, u32[]{:S(2)}) collective-permute-start(f32[512,128]{1,0:T(8,128)S(1)} %get-tuple-element.92), channel_id=1, source_target_pairs={{0,1},{1,0},{2,3},{3,2},{4,5},{5,4},{6,7},{7,6},{8,9},{9,8},{10,11... | collective-permute-start | bytes 786440 | tf_op jit(solution)/shard_map/ppermute | solution.py:916
  3.0 0.8 %own_exports.1 = (f32[1024,128]{1,0:T(8,128)S(1)}, f32[16,128]{1,0:T(8,128)S(1)}) custom-call(s32[1]{0:T(128)} %bitcast.place, bf16[128,2048]{1,0:T(8,128)(2,1)S(1)} %get-tuple-element.85.query, bf16[128,2048]{1,0:T(8,128)(2,1)S(1)} %get-tuple-element.86.key, bf16[128,2048]{1,0:T(8,128)(2,1)S(1)} %get-tuple-element.87.value, ...), custom_call_target="tpu_custom_call" | custom-call | flops 12800000000 | bytes 1 | tf_op jit(solution)/shard_map/own_exports/pallas_call | solution.py:919
  3.8 0.2 collective-permute-done.first_got.got.pair_got
  4.1 2.5 %collective-permute-start.2 = (f32[528,128]{1,0:T(8,128)S(1)}, f32[528,128]{1,0:T(8,128)S(1)}, u32[]{:S(2)}, u32[]{:S(2)}) collective-permute-start(f32[528,128]{1,0:T(8,128)S(1)} %first_merge.2.after), channel_id=1, source_target_pairs={{0,2},{1,3},{2,0},{3,1},{4,6},{5,7},{6,4},{7,5},{8,10},{9,11},{10,... | collective-permute-start | bytes 811016 | tf_op jit(solution)/shard_map/ppermute | solution.py:916
  6.6 1.6 %second_exports.1 = (f32[512,128]{1,0:T(8,128)S(1)}, f32[512,128]{1,0:T(8,128)S(1)}, f32[1024,128]{1,0:T(8,128)S(1)}, f32[4096,128]{1,0:T(8,128)S(1)}, f32[24,128]{1,0:T(8,128)S(1)}) custom-call(s32[1]{0:T(128)} %bitcast.place, bf16[128,2048]{1,0:T(8,128)(2,1)S(1)} %get-tuple-element.85.query, bf16[128,2048]{1,0:T(8,128)(2,1)S(1)} %get-tuple-element.86.key, ...), custom_call_target="tpu_custom_call" | custom-call | flops 1600000 | bytes 1 | tf_op jit(solution)/shard_map/second_exports/pallas_call | solution.py:919
  8.2 0.7 %collective-permute-start.3 = (f32[512,128]{1,0:T(8,128)S(1)}, f32[512,128]{1,0:T(8,128)S(1)}, u32[]{:S(2)}, u32[]{:S(2)}) collective-permute-start(f32[512,128]{1,0:T(8,128)S(1)} %get-tuple-element.97), channel_id=1, source_target_pairs={{0,1},{1,0},{2,3},{3,2},{4,5},{5,4},{6,7},{7,6},{8,9},{9,8},{10,11... | collective-permute-start | bytes 786440 | tf_op jit(solution)/shard_map/ppermute | solution.py:916
  9.0 0.1 collective-permute-start.5
  9.0 0.4 %collective-permute-start.10 = (f32[4096,128]{1,0:T(8,128)S(1)}, f32[4096,128]{1,0:T(8,128)S(1)}, u32[]{:S(2)}, u32[]{:S(2)}) collective-permute-start(f32[4096,128]{1,0:T(8,128)S(1)} %get-tuple-element.103), channel_id=1, source_target_pairs={{0,1},{1,0},{2,3},{3,2},{4,5},{5,4},{6,7},{7,6},{8,9},{9,8},{10,11... | collective-permute-start | bytes 6291464 | tf_op jit(solution)/shard_map/ppermute | solution.py:916
  9.5 1.6 %local.4 = (f32[128,512]{1,0:T(8,128)S(1)}, f32[128,512]{1,0:T(8,128)S(1)}, f32[128,512]{1,0:T(8,128)S(1)}, f32[128,512]{1,0:T(8,128)S(1)}, f32[8,4,128]{2,1,0:T(4,128)S(1)}, /*index=5*/f32[4,128]{1,0:T(4,128)S(1)}) custom-call(s32[1]{0:T(128)} %bitcast.place, bf16[128,2048]{1,0:T(8,128)(2,1)S(1)} %get-tuple-element.85.query, ...), custom_call_target="tpu_custom_call" | custom-call | flops 16000000 | bytes 1 | tf_op jit(solution)/shard_map/local/pallas_call | solution.py:919
  11.0 0.0 collective-permute-done.1.got.pair_got
  11.0 0.1 first_merge.3
  11.1 0.1 collective-permute-start.4
  11.2 1.6 %local.5 = (f32[128,512]{1,0:T(8,128)S(1)}, f32[128,512]{1,0:T(8,128)S(1)}, f32[128,512]{1,0:T(8,128)S(1)}, f32[128,512]{1,0:T(8,128)S(1)}, f32[8,4,128]{2,1,0:T(4,128)S(1)}, /*index=5*/f32[4,128]{1,0:T(4,128)S(1)}) custom-call(s32[1]{0:T(128)} %bitcast.place, bf16[128,2048]{1,0:T(8,128)(2,1)S(1)} %get-tuple-element.85.query, ...), custom_call_target="tpu_custom_call" | custom-call | flops 16000000 | bytes 1 | tf_op jit(solution)/shard_map/local/pallas_call | solution.py:919
  12.7 0.0 collective-permute-done.3.rest_1_.got.second_got
  12.7 0.0 collective-permute-done.5.got.second_got
  12.8 0.4 %collective-permute-done.2.first.chip_total = f32[528,128]{1,0:T(8,128)S(1)} collective-permute-done((f32[528,128]{1,0:T(8,128)S(1)}, f32[528,128]{1,0:T(8,128)S(1)}, u32[]{:S(2)}, u32[]{:S(2)}) %collective-permute-start.2) | collective-permute-done | bytes 270368 | tf_op jit(solution)/shard_map/ppermute | solution.py:916
  13.2 0.1 second_merge.2.rest_0_
  13.2 1.0 %collective-permute-start.7 = (f32[512,128]{1,0:T(8,128)S(1)}, f32[512,128]{1,0:T(8,128)S(1)}, u32[]{:S(2)}, u32[]{:S(2)}) collective-permute-start(f32[512,128]{1,0:T(8,128)S(1)} %second_merge.2.rest_0_), channel_id=1, source_target_pairs={{0,1},{1,0},{2,4},{4,2},{3,5},{5,3},{6,7},{7,6},{8,9},{9,8},{10,12... | collective-permute-start | bytes 786440 | tf_op jit(solution)/shard_map/ppermute | solution.py:916
  14.2 1.6 %local.6 = (f32[128,512]{1,0:T(8,128)S(1)}, f32[128,512]{1,0:T(8,128)S(1)}, f32[128,512]{1,0:T(8,128)S(1)}, f32[128,512]{1,0:T(8,128)S(1)}, f32[8,4,128]{2,1,0:T(4,128)S(1)}, /*index=5*/f32[4,128]{1,0:T(4,128)S(1)}) custom-call(s32[1]{0:T(128)} %bitcast.place, bf16[128,2048]{1,0:T(8,128)(2,1)S(1)} %get-tuple-element.85.query, ...), custom_call_target="tpu_custom_call" | custom-call | flops 1600000000 | bytes 1 | tf_op jit(solution)/shard_map/local/pallas_call | solution.py:919
  15.8 3.2 %collective-permute-done.4.first = f32[512,128]{1,0:T(8,128)S(1)} collective-permute-done((f32[512,128]{1,0:T(8,128)S(1)}, f32[512,128]{1,0:T(8,128)S(1)}, u32[]{:S(2)}, u32[]{:S(2)}) %collective-permute-start.4) | collective-permute-done | bytes 262176 | tf_op jit(solution)/shard_map/ppermute | solution.py:916
  19.0 0.1 second_merge.3
  19.1 0.9 %collective-permute-start.6 = (f32[512,128]{1,0:T(8,128)S(1)}, f32[512,128]{1,0:T(8,128)S(1)}, u32[]{:S(2)}, u32[]{:S(2)}) collective-permute-start(f32[512,128]{1,0:T(8,128)S(1)} %second_merge.3), channel_id=1, source_target_pairs={{0,1},{1,0},{2,4},{4,2},{3,5},{5,3},{6,7},{7,6},{8,9},{9,8},{10,12... | collective-permute-start | bytes 786440 | tf_op jit(solution)/shard_map/ppermute | solution.py:916
  20.0 0.0 collective-permute-done.7.rest_0_.second
  20.0 0.1 collective-permute-start.8
  20.1 0.4 %collective-permute-start.9 = (f32[512,128]{1,0:T(8,128)S(1)}, f32[512,128]{1,0:T(8,128)S(1)}, u32[]{:S(2)}, u32[]{:S(2)}) collective-permute-start(f32[512,128]{1,0:T(8,128)S(1)} %collective-permute-done.7.rest_0_.second), channel_id=1, source_target_pairs={{0,1},{1,0},{2,3},{3,2},{4,5},{5,4},{6,7},{7,6},{8,9},{9,8},{10,11... | collective-permute-start | bytes 786440 | tf_op jit(solution)/shard_map/ppermute | solution.py:916
  20.5 2.6 %collective-permute-start.14 = (f32[512,128]{1,0:T(8,128)S(1)}, f32[512,128]{1,0:T(8,128)S(1)}, u32[]{:S(2)}, u32[]{:S(2)}) collective-permute-start(f32[512,128]{1,0:T(8,128)S(1)} %collective-permute-done.7.rest_0_.second), channel_id=1, source_target_pairs={{0,2},{1,3},{2,0},{3,1},{4,6},{5,7},{6,4},{7,5},{8,10},{9,11},{10,... | collective-permute-start | bytes 786440 | tf_op jit(solution)/shard_map/ppermute | solution.py:916
  23.2 1.6 %local.7 = (f32[128,512]{1,0:T(8,128)S(1)}, f32[128,512]{1,0:T(8,128)S(1)}, f32[128,512]{1,0:T(8,128)S(1)}, f32[128,512]{1,0:T(8,128)S(1)}, f32[8,4,128]{2,1,0:T(4,128)S(1)}, /*index=5*/f32[4,128]{1,0:T(4,128)S(1)}) custom-call(s32[1]{0:T(128)} %bitcast.place, bf16[128,2048]{1,0:T(8,128)(2,1)S(1)} %get-tuple-element.85.query, ...), custom_call_target="tpu_custom_call" | custom-call | flops 25600000000 | bytes 1 | tf_op jit(solution)/shard_map/local/pallas_call | solution.py:919
  24.7 0.0 collective-permute-done.10.front
  24.7 1.1 %first_use.4 = (f32[128,512]{1,0:T(8,128)S(1)}, f32[128,512]{1,0:T(8,128)S(1)}, f32[128,512]{1,0:T(8,128)S(1)}, f32[128,512]{1,0:T(8,128)S(1)}, f32[16,128]{1,0:T(8,128)S(1)}) custom-call(s32[1]{0:T(128)} %bitcast.place, bf16[128,2048]{1,0:T(8,128)(2,1)S(1)} %get-tuple-element.85.query, bf16[128,2048]{1,0:T(8,128)(2,1)S(1)} %get-tuple-element.86.key, ...), custom_call_target="tpu_custom_call" | custom-call | flops 4800000000 | bytes 1 | tf_op jit(solution)/shard_map/first_use/pallas_call | solution.py:919
  25.8 0.0 collective-permute-done.9.second
  25.8 0.0 collective-permute-done.8.first
  25.9 1.1 %first_use.5 = (f32[128,512]{1,0:T(8,128)S(1)}, f32[128,512]{1,0:T(8,128)S(1)}, f32[128,512]{1,0:T(8,128)S(1)}, f32[128,512]{1,0:T(8,128)S(1)}, f32[16,128]{1,0:T(8,128)S(1)}) custom-call(s32[1]{0:T(128)} %bitcast.place, bf16[128,2048]{1,0:T(8,128)(2,1)S(1)} %get-tuple-element.85.query, bf16[128,2048]{1,0:T(8,128)(2,1)S(1)} %get-tuple-element.86.key, ...), custom_call_target="tpu_custom_call" | custom-call | flops 4800000000 | bytes 1 | tf_op jit(solution)/shard_map/first_use/pallas_call | solution.py:919
  27.0 0.0 collective-permute-done.6.second
  27.0 0.2 collective-permute-start.12
  27.2 2.1 %collective-permute-start.11 = (f32[512,128]{1,0:T(8,128)S(1)}, f32[512,128]{1,0:T(8,128)S(1)}, u32[]{:S(2)}, u32[]{:S(2)}) collective-permute-start(f32[512,128]{1,0:T(8,128)S(1)} %collective-permute-done.6.second), channel_id=1, source_target_pairs={{0,1},{1,0},{2,3},{3,2},{4,5},{5,4},{6,7},{7,6},{8,9},{9,8},{10,11... | collective-permute-start | bytes 786440 | tf_op jit(solution)/shard_map/ppermute | solution.py:916
  29.3 1.1 %first_use.6 = (f32[128,512]{1,0:T(8,128)S(1)}, f32[128,512]{1,0:T(8,128)S(1)}, f32[128,512]{1,0:T(8,128)S(1)}, f32[128,512]{1,0:T(8,128)S(1)}, f32[16,128]{1,0:T(8,128)S(1)}) custom-call(s32[1]{0:T(128)} %bitcast.place, bf16[128,2048]{1,0:T(8,128)(2,1)S(1)} %get-tuple-element.85.query, bf16[128,2048]{1,0:T(8,128)(2,1)S(1)} %get-tuple-element.86.key, ...), custom_call_target="tpu_custom_call" | custom-call | flops 4800000000 | bytes 1 | tf_op jit(solution)/shard_map/first_use/pallas_call | solution.py:919
  30.4 0.0 collective-permute-done.14.third
  30.4 0.2 collective-permute-start.15
  30.6 0.4 collective-permute-start.13
  31.0 0.7 %last_use.4 = (bf16[128,512]{1,0:T(8,128)(2,1)S(1)}, bf16[128,512]{1,0:T(8,128)(2,1)S(1)}, bf16[128,512]{1,0:T(8,128)(2,1)S(1)}, bf16[128,512]{1,0:T(8,128)(2,1)S(1)}, f32[12,128]{1,0:T(8,128)S(1)}) custom-call(s32[1]{0:T(128)} %bitcast.place, bf16[128,2048]{1,0:T(8,128)(2,1)S(1)} %get-tuple-element.85.query, bf16[128,2048]{1,0:T(8,128)(2,1)S(1)} %get-tuple-element.86.key, ...), custom_call_target="tpu_custom_call" | custom-call | flops 9600000000 | bytes 1 | tf_op jit(solution)/shard_map/last_use/pallas_call | solution.py:919
  31.7 0.7 %collective-permute-done.13.first = f32[512,128]{1,0:T(8,128)S(1)} collective-permute-done((f32[512,128]{1,0:T(8,128)S(1)}, f32[512,128]{1,0:T(8,128)S(1)}, u32[]{:S(2)}, u32[]{:S(2)}) %collective-permute-start.13) | collective-permute-done | bytes 262176 | tf_op jit(solution)/shard_map/ppermute | solution.py:916
  32.4 0.0 collective-permute-done.11.second
  32.4 1.3 %first_use.7 = (f32[128,512]{1,0:T(8,128)S(1)}, f32[128,512]{1,0:T(8,128)S(1)}, f32[128,512]{1,0:T(8,128)S(1)}, f32[128,512]{1,0:T(8,128)S(1)}, f32[16,128]{1,0:T(8,128)S(1)}) custom-call(s32[1]{0:T(128)} %bitcast.place, bf16[128,2048]{1,0:T(8,128)(2,1)S(1)} %get-tuple-element.85.query, bf16[128,2048]{1,0:T(8,128)(2,1)S(1)} %get-tuple-element.86.key, ...), custom_call_target="tpu_custom_call" | custom-call | flops 4800000000 | bytes 1 | tf_op jit(solution)/shard_map/first_use/pallas_call | solution.py:919
  33.7 0.0 collective-permute-done.15.third
  33.7 1.6 %last_use.5 = (bf16[128,2048]{1,0:T(8,128)(2,1)}, bf16[128,2048]{1,0:T(8,128)(2,1)}, bf16[128,2048]{1,0:T(8,128)(2,1)}, bf16[128,2048]{1,0:T(8,128)(2,1)}, f32[12,128]{1,0:T(8,128)S(1)}) custom-call(s32[1]{0:T(128)} %bitcast.place, bf16[128,2048]{1,0:T(8,128)(2,1)S(1)} %get-tuple-element.85.query, bf16[128,2048]{1,0:T(8,128)(2,1)S(1)} %get-tuple-element.86.key, ...), custom_call_target="tpu_custom_call" | custom-call | flops 4000000000 | bytes 1 | tf_op jit(solution)/shard_map/last_use/pallas_call | solution.py:1084
  35.3 0.0 collective-permute-done.12.third
  35.3 0.7 %collective-permute-start.16 = (f32[512,128]{1,0:T(8,128)S(1)}, f32[512,128]{1,0:T(8,128)S(1)}, u32[]{:S(2)}, u32[]{:S(2)}) collective-permute-start(f32[512,128]{1,0:T(8,128)S(1)} %collective-permute-done.12.third), channel_id=1, source_target_pairs={{0,1},{1,0},{2,3},{3,2},{4,5},{5,4},{6,7},{7,6},{8,9},{9,8},{10,11... | collective-permute-start | bytes 786440 | tf_op jit(solution)/shard_map/ppermute | solution.py:916
  36.0 0.7 %last_use.6 = (bf16[128,512]{1,0:T(8,128)(2,1)S(1)}, bf16[128,512]{1,0:T(8,128)(2,1)S(1)}, bf16[128,512]{1,0:T(8,128)(2,1)S(1)}, bf16[128,512]{1,0:T(8,128)(2,1)S(1)}, f32[12,128]{1,0:T(8,128)S(1)}) custom-call(s32[1]{0:T(128)} %bitcast.place, bf16[128,2048]{1,0:T(8,128)(2,1)S(1)} %get-tuple-element.85.query, bf16[128,2048]{1,0:T(8,128)(2,1)S(1)} %get-tuple-element.86.key, ...), custom_call_target="tpu_custom_call" | custom-call | flops 2400000000 | bytes 1 | tf_op jit(solution)/shard_map/last_use/pallas_call | solution.py:919
  36.7 0.5 %collective-permute-done.16.third = f32[512,128]{1,0:T(8,128)S(1)} collective-permute-done((f32[512,128]{1,0:T(8,128)S(1)}, f32[512,128]{1,0:T(8,128)S(1)}, u32[]{:S(2)}, u32[]{:S(2)}) %collective-permute-start.16) | collective-permute-done | bytes 262176 | tf_op jit(solution)/shard_map/ppermute | solution.py:916
  37.2 1.8 %last_use.7 = (bf16[128,2048]{1,0:T(8,128)(2,1)}, bf16[128,2048]{1,0:T(8,128)(2,1)}, bf16[128,2048]{1,0:T(8,128)(2,1)}, bf16[128,2048]{1,0:T(8,128)(2,1)}, f32[11,16,128]{2,1,0:T(8,128)}, /*index=5*/f32[16,128]{1,0:T(8,128)}) custom-call(s32[1]{0:T(128)} %bitcast.place, ...), custom_call_target="tpu_custom_call", output_to_operand_aliasing={{0}: (36, {}), {1}: (37, {}), {2}: (38, {}), {3}: (39, {})} | custom-call | flops 4000000000 | bytes 1 | tf_op jit(solution)/shard_map/last_use/pallas_call | solution.py:1084
  (1 shorter events, 0.0 us)
Async XLA Ops:
  2.5 1.6 %collective-permute-start = (f32[528,128]{1,0:T(8,128)S(1)}, f32[528,128]{1,0:T(8,128)S(1)}, u32[]{:S(2)}, u32[]{:S(2)}) collective-permute-start(f32[528,128]{1,0:T(8,128)S(1)} %get-tuple-element.91.after), channel_id=1, source_target_pairs={{0,1},{1,0},{2,3},{3,2},{4,5},{5,4},{6,7},{7,6},{8,9},{9,8},{10,11... | collective-permute-start | bytes 811016 | tf_op jit(solution)/shard_map/ppermute | solution.py:916
  2.6 8.5 %collective-permute-start.1 = (f32[512,128]{1,0:T(8,128)S(1)}, f32[512,128]{1,0:T(8,128)S(1)}, u32[]{:S(2)}, u32[]{:S(2)}) collective-permute-start(f32[512,128]{1,0:T(8,128)S(1)} %get-tuple-element.92), channel_id=1, source_target_pairs={{0,1},{1,0},{2,3},{3,2},{4,5},{5,4},{6,7},{7,6},{8,9},{9,8},{10,11... | collective-permute-start | bytes 786440 | tf_op jit(solution)/shard_map/ppermute | solution.py:916
  4.1 9.0 %collective-permute-start.2 = (f32[528,128]{1,0:T(8,128)S(1)}, f32[528,128]{1,0:T(8,128)S(1)}, u32[]{:S(2)}, u32[]{:S(2)}) collective-permute-start(f32[528,128]{1,0:T(8,128)S(1)} %first_merge.2.after), channel_id=1, source_target_pairs={{0,2},{1,3},{2,0},{3,1},{4,6},{5,7},{6,4},{7,5},{8,10},{9,11},{10,... | collective-permute-start | bytes 811016 | tf_op jit(solution)/shard_map/ppermute | solution.py:916
  8.2 4.5 %collective-permute-start.3 = (f32[512,128]{1,0:T(8,128)S(1)}, f32[512,128]{1,0:T(8,128)S(1)}, u32[]{:S(2)}, u32[]{:S(2)}) collective-permute-start(f32[512,128]{1,0:T(8,128)S(1)} %get-tuple-element.97), channel_id=1, source_target_pairs={{0,1},{1,0},{2,3},{3,2},{4,5},{5,4},{6,7},{7,6},{8,9},{9,8},{10,11... | collective-permute-start | bytes 786440 | tf_op jit(solution)/shard_map/ppermute | solution.py:916
  9.0 3.8 %collective-permute-start.5 = (f32[512,128]{1,0:T(8,128)S(1)}, f32[512,128]{1,0:T(8,128)S(1)}, u32[]{:S(2)}, u32[]{:S(2)}) collective-permute-start(f32[512,128]{1,0:T(8,128)S(1)} %get-tuple-element.99), channel_id=1, source_target_pairs={{0,1},{1,0},{2,3},{3,2},{4,5},{5,4},{6,7},{7,6},{8,9},{9,8},{10,11... | collective-permute-start | bytes 786440 | tf_op jit(solution)/shard_map/ppermute | solution.py:916
  9.0 15.7 %collective-permute-start.10 = (f32[4096,128]{1,0:T(8,128)S(1)}, f32[4096,128]{1,0:T(8,128)S(1)}, u32[]{:S(2)}, u32[]{:S(2)}) collective-permute-start(f32[4096,128]{1,0:T(8,128)S(1)} %get-tuple-element.103), channel_id=1, source_target_pairs={{0,1},{1,0},{2,3},{3,2},{4,5},{5,4},{6,7},{7,6},{8,9},{9,8},{10,11... | collective-permute-start | bytes 6291464 | tf_op jit(solution)/shard_map/ppermute | solution.py:916
  11.1 8.0 %collective-permute-start.4 = (f32[512,128]{1,0:T(8,128)S(1)}, f32[512,128]{1,0:T(8,128)S(1)}, u32[]{:S(2)}, u32[]{:S(2)}) collective-permute-start(f32[512,128]{1,0:T(8,128)S(1)} %first_merge.3), channel_id=1, source_target_pairs={{0,2},{1,3},{2,0},{3,1},{4,6},{5,7},{6,4},{7,5},{8,10},{9,11},{10,... | collective-permute-start | bytes 786440 | tf_op jit(solution)/shard_map/ppermute | solution.py:916
  13.2 6.8 %collective-permute-start.7 = (f32[512,128]{1,0:T(8,128)S(1)}, f32[512,128]{1,0:T(8,128)S(1)}, u32[]{:S(2)}, u32[]{:S(2)}) collective-permute-start(f32[512,128]{1,0:T(8,128)S(1)} %second_merge.2.rest_0_), channel_id=1, source_target_pairs={{0,1},{1,0},{2,4},{4,2},{3,5},{5,3},{6,7},{7,6},{8,9},{9,8},{10,12... | collective-permute-start | bytes 786440 | tf_op jit(solution)/shard_map/ppermute | solution.py:916
  19.1 7.9 %collective-permute-start.6 = (f32[512,128]{1,0:T(8,128)S(1)}, f32[512,128]{1,0:T(8,128)S(1)}, u32[]{:S(2)}, u32[]{:S(2)}) collective-permute-start(f32[512,128]{1,0:T(8,128)S(1)} %second_merge.3), channel_id=1, source_target_pairs={{0,1},{1,0},{2,4},{4,2},{3,5},{5,3},{6,7},{7,6},{8,9},{9,8},{10,12... | collective-permute-start | bytes 786440 | tf_op jit(solution)/shard_map/ppermute | solution.py:916
  20.0 5.8 %collective-permute-start.8 = (f32[528,128]{1,0:T(8,128)S(1)}, f32[528,128]{1,0:T(8,128)S(1)}, u32[]{:S(2)}, u32[]{:S(2)}) collective-permute-start(f32[528,128]{1,0:T(8,128)S(1)} %collective-permute-done.2.first.chip_total), channel_id=1, source_target_pairs={{0,1},{1,0},{2,3},{3,2},{4,5},{5,4},{6,7},{7,6},{8,9},{9,8},{10,11... | collective-permute-start | bytes 811016 | tf_op jit(solution)/shard_map/ppermute | solution.py:916
  20.1 5.7 %collective-permute-start.9 = (f32[512,128]{1,0:T(8,128)S(1)}, f32[512,128]{1,0:T(8,128)S(1)}, u32[]{:S(2)}, u32[]{:S(2)}) collective-permute-start(f32[512,128]{1,0:T(8,128)S(1)} %collective-permute-done.7.rest_0_.second), channel_id=1, source_target_pairs={{0,1},{1,0},{2,3},{3,2},{4,5},{5,4},{6,7},{7,6},{8,9},{9,8},{10,11... | collective-permute-start | bytes 786440 | tf_op jit(solution)/shard_map/ppermute | solution.py:916
  20.5 9.9 %collective-permute-start.14 = (f32[512,128]{1,0:T(8,128)S(1)}, f32[512,128]{1,0:T(8,128)S(1)}, u32[]{:S(2)}, u32[]{:S(2)}) collective-permute-start(f32[512,128]{1,0:T(8,128)S(1)} %collective-permute-done.7.rest_0_.second), channel_id=1, source_target_pairs={{0,2},{1,3},{2,0},{3,1},{4,6},{5,7},{6,4},{7,5},{8,10},{9,11},{10,... | collective-permute-start | bytes 786440 | tf_op jit(solution)/shard_map/ppermute | solution.py:916
  27.0 8.3 %collective-permute-start.12 = (f32[512,128]{1,0:T(8,128)S(1)}, f32[512,128]{1,0:T(8,128)S(1)}, u32[]{:S(2)}, u32[]{:S(2)}) collective-permute-start(f32[512,128]{1,0:T(8,128)S(1)} %collective-permute-done.6.second), channel_id=1, source_target_pairs={{0,2},{1,3},{2,0},{3,1},{4,6},{5,7},{6,4},{7,5},{8,10},{9,11},{10,... | collective-permute-start | bytes 786440 | tf_op jit(solution)/shard_map/ppermute | solution.py:916
  27.2 5.2 %collective-permute-start.11 = (f32[512,128]{1,0:T(8,128)S(1)}, f32[512,128]{1,0:T(8,128)S(1)}, u32[]{:S(2)}, u32[]{:S(2)}) collective-permute-start(f32[512,128]{1,0:T(8,128)S(1)} %collective-permute-done.6.second), channel_id=1, source_target_pairs={{0,1},{1,0},{2,3},{3,2},{4,5},{5,4},{6,7},{7,6},{8,9},{9,8},{10,11... | collective-permute-start | bytes 786440 | tf_op jit(solution)/shard_map/ppermute | solution.py:916
  30.4 3.3 %collective-permute-start.15 = (f32[512,128]{1,0:T(8,128)S(1)}, f32[512,128]{1,0:T(8,128)S(1)}, u32[]{:S(2)}, u32[]{:S(2)}) collective-permute-start(f32[512,128]{1,0:T(8,128)S(1)} %collective-permute-done.14.third), channel_id=1, source_target_pairs={{0,1},{1,0},{2,3},{3,2},{4,5},{5,4},{6,7},{7,6},{8,9},{9,8},{10,11... | collective-permute-start | bytes 786440 | tf_op jit(solution)/shard_map/ppermute | solution.py:916
  30.6 1.8 %collective-permute-start.13 = (f32[512,128]{1,0:T(8,128)S(1)}, f32[512,128]{1,0:T(8,128)S(1)}, u32[]{:S(2)}, u32[]{:S(2)}) collective-permute-start(f32[512,128]{1,0:T(8,128)S(1)} %collective-permute-done.4.first), channel_id=1, source_target_pairs={{0,1},{1,0},{2,3},{3,2},{4,5},{5,4},{6,7},{7,6},{8,9},{9,8},{10,11... | collective-permute-start | bytes 786440 | tf_op jit(solution)/shard_map/ppermute | solution.py:916
  35.3 1.9 %collective-permute-start.16 = (f32[512,128]{1,0:T(8,128)S(1)}, f32[512,128]{1,0:T(8,128)S(1)}, u32[]{:S(2)}, u32[]{:S(2)}) collective-permute-start(f32[512,128]{1,0:T(8,128)S(1)} %collective-permute-done.12.third), channel_id=1, source_target_pairs={{0,1},{1,0},{2,3},{3,2},{4,5},{5,4},{6,7},{7,6},{8,9},{9,8},{10,11... | collective-permute-start | bytes 786440 | tf_op jit(solution)/shard_map/ppermute | solution.py:916

commit v7 on v6

--- a/solution.py
+++ b/solution.py
@@ -231,8 +231,14 @@
     tok = decay.shape[1]
     earlier = lax.broadcasted_iota(jnp.int32, (tok, tok), 0)
     later = lax.broadcasted_iota(jnp.int32, (tok, tok), 1)
-    upto = (earlier <= later).astype(F32)
-    return jnp.dot(decay, upto, precision=TOP_ACCURACY, preferred_element_type=F32)
+    upto = (earlier <= later).astype(BF16)
+    high, _ = halves(decay)
+    middle, low = halves(decay - high.astype(F32))
+    return mxu(
+        jnp.concatenate([high, middle, low], axis=1),
+        jnp.concatenate([upto, upto, upto], axis=0),
+        NN,
+    )
 
 
 def last_lane(running):
@@ -297,7 +303,7 @@
 def first_weights(position, gain, decay):
     chip = position // 2
     cross = gain.shape[0] - 3
-    running = running_decay(decay[...])
+    running = decay[...]
     total = last_lane(running)
     weight = jnp.where(
         chip % 2 == 0,
@@ -310,7 +316,7 @@
 def first_export_kernel(
     place, query, key, value, cotangent, gain, decay, *rest
 ):
-    sends, kept, sems = rest[:-7], rest[-7:-1], rest[-1]
+    sends, kept, raw, sems = rest[:-8], rest[-8:-2], rest[-2], rest[-1]
     position = place[0]
     core = position % 2
     heads, tok = decay.shape
@@ -328,7 +334,7 @@
             )
     small = [
         pltpu.make_async_copy(source, target, sems.at[8 + number])
-        for number, (source, target) in enumerate(zip((gain, decay), kept[4:]))
+        for number, (source, target) in enumerate(zip((gain, decay), (kept[4], raw)))
     ]
     for move in small:
         move.start()
@@ -350,6 +356,7 @@
 
     for move in small:
         move.wait()
+    kept[5][...] = running_decay(raw[...])
     weight, total = first_weights(position, *kept[4:])
     sends[0][pl.ds(sends[0].shape[0] - heads, heads), :] = total
 
@@ -406,7 +413,7 @@
     dim = query.shape[1] // heads
     half = heads // 2
     cross = gain.shape[0] - 3
-    running = running_decay(decay[...])
+    running = decay[...]
     lift = jnp.exp(running)
     fall = jnp.exp(last_lane(running) - running)
     state2 = chip == 1
@@ -500,11 +507,16 @@
     return mxu(split_lanes(value), ones, NN)
 
 
-def apply_state(left, right, state, weight):
+def row_sums(value):
+    ones = jnp.ones((16, 2 * value.shape[1]), BF16)
+    return mxu(ones, split_lanes(value), NT)[:1]
+
+
+def apply_state(left, right, state, weight, summed=lane_sums):
     high, low = halves(state)
     first = mxu(twice_lanes(left), jnp.concatenate([high, low], axis=0), NN)
     second = mxu(twice_lanes(right), jnp.concatenate([high, low], axis=1), NT)
-    sums = lane_sums(first * right.astype(F32))
+    sums = summed(first * right.astype(F32))
     return weight * first, weight * second, sums
 
 
@@ -516,7 +528,7 @@
     count = decay_rows.shape[0]
     dim = query.shape[1] // heads
     inner_levels = tok.bit_length()
-    running = take_half(running_decay(decay[...]), side, low, count)
+    running = take_half(decay[...], side, low, count)
     gains = [take_half(gain[place_in], side, low, count) for place_in in range(inner_levels)]
     spread = columns(running)
     source = lax.broadcasted_iota(jnp.int32, (tok, tok), 0)
@@ -608,7 +620,7 @@
     dim = query.shape[1] // heads
     count = acc_out.shape[1] // dim
     cross = gain.shape[0] - 3
-    running = running_decay(decay[...])
+    running = decay[...]
     total = last_lane(running)
     other = first_got[pl.ds(first_got.shape[0] - heads, heads), :]
     odd = core == 1
@@ -722,7 +734,7 @@
     dim = query.shape[1] // heads
     count = acc_out.shape[1] // dim
     cross = gain.shape[0] - 3
-    running = running_decay(decay[...])
+    running = decay[...]
     total = last_lane(running)
     other = first_got[pl.ds(first_got.shape[0] - heads, heads), :]
     chip_rows = chip_total[pl.ds(chip_total.shape[0] - heads, heads), :]
@@ -739,7 +751,7 @@
     spread = columns(weight)
     lane = lax.broadcasted_iota(jnp.int32, (tok, tok), 1)
     gathered = jnp.zeros((tok, tok), F32)
-    flows = []
+    flows, summed = [], []
     copies = []
     if not mine:
         wide = before[0].shape[1]
@@ -774,9 +786,16 @@
         partner = jnp.where(odd, level0, pair1)
         flows.append(pair_flow[one] * jnp.sum(state * partner, axis=0, keepdims=True))
         left, right, sums = apply_state(
-            jnp.where(forward, q, k), jnp.where(forward, o, v), state, spread[:, one]
-        )
-        gathered = jnp.where(lane == index, sums, gathered)
+            jnp.where(forward, q, k),
+            jnp.where(forward, o, v),
+            state,
+            spread[:, one],
+            row_sums if ending else lane_sums,
+        )
+        if ending:
+            summed.append(sums)
+        else:
+            gathered = jnp.where(lane == index, sums, gathered)
         results = (
             acc_out[:, lanes] + jnp.where(forward, left, 0.0),
             acc_query[:, lanes] + jnp.where(forward, right, 0.0),
@@ -799,7 +818,7 @@
     if not ending:
         use_rows(rows_out, ((forward, weight, lift),), gathered, extra)
     else:
-        sums = gathered.T[:count]
+        sums = jnp.concatenate(summed, axis=0)
         weighted = weight * sums
         own_rows = (
             jnp.where(forward, weighted, -weighted),
@@ -883,7 +902,7 @@
 IN_HBM = pl.BlockSpec(memory_space=pltpu.HBM)
 RATE_FIRST = 16
 RATE_SECOND = 0.001
-RATE_LOCAL = ((.01,.01),(1,16))
+RATE_LOCAL = ((.01,.01),(16,1))
 RATE_USE = ((4,4),(4,4))
 RATE_LAST = ((16,4),(4,4))
 RATE_MERGE = (4,4)
@@ -934,14 +953,13 @@
         )
         + tuple(pltpu.VMEM(array.shape, array.dtype) for array in inputs[1:]),
         in_specs=[SCALAR] + [IN_HBM] * 6,
-        scratch_shapes=[pltpu.SemaphoreType.DMA((10,))],
+        scratch_shapes=[pltpu.VMEM((heads, tok), F32), pltpu.SemaphoreType.DMA((10,))],
         compiler_params=params(),
         cost_estimate=cost(2),
         name="first_exports",
     )(place, *(pltpu.with_memory_space_constraint(array, pltpu.HBM) for array in inputs[1:]))
     send1, kept = found[: len(counts)], found[len(counts) :]
     inputs = (place, *kept)
-    decay_log = kept[-1]
     got1 = [swap(block, core_swap) for block in send1]
     keep1, totals = call(
         own_export_kernel,
@@ -1007,12 +1025,13 @@
     done = local(0, False, done)
     sent = [second_merge(0, done, *got2[1:])]
     done = local(1, True, sent[0])
+    done = local(1, False, done)
     sent.append(second_merge(1, done))
     front = swap(bundle, core_swap)
     second = [swap(block, middle_swap) for block in sent]
     third = [swap(second[0], side_swap)]
     second_over = [swap(second[0], core_swap)]
-    done = local(1, False, second[0])
+    done = second[0]
 
     used = {}
 
@@ -1099,16 +1118,16 @@
         results = found[:4]
         last_rows.extend(found[4:])
 
-    done = first_use(0, True, done)
-    first_over = [swap(after(first[0], second[0]), core_swap)]
+    first_over = [swap(after(first[0], sent[0]), core_swap)]
+    done = first_use(0, True, done, first_over[0])
     done = first_use(0, False, done)
     second[1] = after(second[1], done)
     third.append(swap(second[1], side_swap))
     second_over.append(swap(second[1], core_swap))
     first_over.append(swap(after(first[1], second[1]), core_swap))
     done = first_use(1, True, done)
+    done = first_use(1, False, done)
     third_over = [swap(after(third[0], done), core_swap)]
-    done = first_use(1, False, done)
     last_use(0, True)
     last_use(0, False)
     third_over.append(swap(after(third[1], done, last_rows[-1]), core_swap))

time: 39.6 us -> 39.2 us (0.990)
  starting transfers between devices: 13.1 us -> 15 us
  Pallas kernels: 20 us -> 18.5 us
  waiting for transfers between devices: 5.13 us -> 4.45 us
    ppermute x17, starting transfers between devices: 13.1 us -> 15 us  [swap(): return lax.ppermute(block, 'ctx', route)]
    pallas_call x14, Pallas kernels: 14.7 us -> 13.6 us  [call(): pl.pallas_call(kernel, out_shape=out_shape, in_specs=[SCALAR] + [pl.Block...]
    ppermute x17, waiting for transfers between devices: 5.13 us -> 4.45 us  [swap(): return lax.ppermute(block, 'ctx', route)]
  transfers between devices with their start and end apart: 17 -> 17, of which waited for: 5 -> 7; matrix products, arithmetic and copies ran while one was open for 0% -> 0% of each run, Pallas kernels for 42% -> 39%
where the time goes in v7:
time: 39.2 us; the launch traced here: 38.8 us
  Pallas kernels  18.5 us (47%)
  starting transfers between devices  15 us (38%)
  waiting for transfers between devices  4.45 us (11%)
  between operations  0.75 us (2%)
    ppermute x17, starting transfers between devices, swap(): return lax.ppermute(block, 'ctx', route)  15 us
    pallas_call x14, Pallas kernels, call(): pl.pallas_call(kernel, out_shape=out_shape, in_specs=[SCALAR] + [pl.Block...  13.6 us
    ppermute x17, waiting for transfers between devices, swap(): return lax.ppermute(block, 'ctx', route)  4.45 us
    pallas_call x2, Pallas kernels, last_use(): pl.pallas_call(functools.partial(last_use_kernel, lows[part], mine, count...  3.03 us
    pallas_call x1, Pallas kernels, line_device(): pl.pallas_call(first_export_kernel, out_shape=tuple((pltpu.VMEM((count *...  1.78 us
  transfers between devices with their start and end apart: 17, of which 7 were waited for; matrix products, arithmetic and copies ran while one was open for 0% of the time, Pallas kernels for 39%

profile of v7, /device:TPU:1, one launch (start us, length us, event | category | flops | bytes accessed | tf_op | source)
XLA Modules:
  0.0 38.8 jit_solution(10351106648856228377)
XLA Ops:
  0.6 1.8 %first_exports.1 = (f32[528,128]{1,0:T(8,128)S(1)}, f32[512,128]{1,0:T(8,128)S(1)}, bf16[128,2048]{1,0:T(8,128)(2,1)S(1)}, bf16[128,2048]{1,0:T(8,128)(2,1)S(1)}...) custom-call(s32[1]{0:T(128)} %bitcast.place, ...), custom_call_target="tpu_custom_call" | custom-call | flops 32000000000 | bytes 1 | tf_op jit(solution)/shard_map/first_exports/pallas_call | solution.py:948
  2.4 0.1 collective-permute-start
  2.5 0.5 %collective-permute-start.1 = (f32[512,128]{1,0:T(8,128)S(1)}, f32[512,128]{1,0:T(8,128)S(1)}, u32[]{:S(2)}, u32[]{:S(2)}) collective-permute-start(f32[512,128]{1,0:T(8,128)S(1)} %get-tuple-element.92), channel_id=1, source_target_pairs={{0,1},{1,0},{2,3},{3,2},{4,5},{5,4},{6,7},{7,6},{8,9},{9,8},{10,11... | collective-permute-start | bytes 786440 | tf_op jit(solution)/shard_map/ppermute | solution.py:935
  3.0 0.6 %own_exports.1 = (f32[1024,128]{1,0:T(8,128)S(1)}, f32[16,128]{1,0:T(8,128)S(1)}) custom-call(s32[1]{0:T(128)} %bitcast.place, bf16[128,2048]{1,0:T(8,128)(2,1)S(1)} %get-tuple-element.85.query, bf16[128,2048]{1,0:T(8,128)(2,1)S(1)} %get-tuple-element.86.key, bf16[128,2048]{1,0:T(8,128)(2,1)S(1)} %get-tuple-element.87.value, ...), custom_call_target="tpu_custom_call" | custom-call | flops 12800000000 | bytes 1 | tf_op jit(solution)/shard_map/own_exports/pallas_call | solution.py:938
  3.6 0.4 %collective-permute-done.first_got.got.pair_got = f32[528,128]{1,0:T(8,128)S(1)} collective-permute-done((f32[528,128]{1,0:T(8,128)S(1)}, f32[528,128]{1,0:T(8,128)S(1)}, u32[]{:S(2)}, u32[]{:S(2)}) %collective-permute-start) | collective-permute-done | bytes 270368 | tf_op jit(solution)/shard_map/ppermute | solution.py:935
  4.1 2.5 %collective-permute-start.2 = (f32[528,128]{1,0:T(8,128)S(1)}, f32[528,128]{1,0:T(8,128)S(1)}, u32[]{:S(2)}, u32[]{:S(2)}) collective-permute-start(f32[528,128]{1,0:T(8,128)S(1)} %first_merge.2.after), channel_id=1, source_target_pairs={{0,2},{1,3},{2,0},{3,1},{4,6},{5,7},{6,4},{7,5},{8,10},{9,11},{10,... | collective-permute-start | bytes 811016 | tf_op jit(solution)/shard_map/ppermute | solution.py:935
  6.6 1.6 %second_exports.1 = (f32[512,128]{1,0:T(8,128)S(1)}, f32[512,128]{1,0:T(8,128)S(1)}, f32[1024,128]{1,0:T(8,128)S(1)}, f32[4096,128]{1,0:T(8,128)S(1)}, f32[24,128]{1,0:T(8,128)S(1)}) custom-call(s32[1]{0:T(128)} %bitcast.place, bf16[128,2048]{1,0:T(8,128)(2,1)S(1)} %get-tuple-element.85.query, bf16[128,2048]{1,0:T(8,128)(2,1)S(1)} %get-tuple-element.86.key, ...), custom_call_target="tpu_custom_call" | custom-call | flops 1600000 | bytes 1 | tf_op jit(solution)/shard_map/second_exports/pallas_call | solution.py:938
  8.2 0.7 %collective-permute-start.3 = (f32[512,128]{1,0:T(8,128)S(1)}, f32[512,128]{1,0:T(8,128)S(1)}, u32[]{:S(2)}, u32[]{:S(2)}) collective-permute-start(f32[512,128]{1,0:T(8,128)S(1)} %get-tuple-element.97), channel_id=1, source_target_pairs={{0,1},{1,0},{2,3},{3,2},{4,5},{5,4},{6,7},{7,6},{8,9},{9,8},{10,11... | collective-permute-start | bytes 786440 | tf_op jit(solution)/shard_map/ppermute | solution.py:935
  8.9 0.1 collective-permute-start.5
  9.0 0.4 %collective-permute-start.10 = (f32[4096,128]{1,0:T(8,128)S(1)}, f32[4096,128]{1,0:T(8,128)S(1)}, u32[]{:S(2)}, u32[]{:S(2)}) collective-permute-start(f32[4096,128]{1,0:T(8,128)S(1)} %get-tuple-element.104), channel_id=1, source_target_pairs={{0,1},{1,0},{2,3},{3,2},{4,5},{5,4},{6,7},{7,6},{8,9},{9,8},{10,11... | collective-permute-start | bytes 6291464 | tf_op jit(solution)/shard_map/ppermute | solution.py:935
  9.4 1.4 %local.4 = (f32[128,512]{1,0:T(8,128)S(1)}, f32[128,512]{1,0:T(8,128)S(1)}, f32[128,512]{1,0:T(8,128)S(1)}, f32[128,512]{1,0:T(8,128)S(1)}, f32[8,4,128]{2,1,0:T(4,128)S(1)}, /*index=5*/f32[4,128]{1,0:T(4,128)S(1)}) custom-call(s32[1]{0:T(128)} %bitcast.place, bf16[128,2048]{1,0:T(8,128)(2,1)S(1)} %get-tuple-element.85.query, ...), custom_call_target="tpu_custom_call" | custom-call | flops 16000000 | bytes 1 | tf_op jit(solution)/shard_map/local/pallas_call | solution.py:938
  10.8 0.0 collective-permute-done.1.got.pair_got
  10.8 0.1 first_merge.3
  10.9 0.1 collective-permute-start.4
  11.0 1.4 %local.5 = (f32[128,512]{1,0:T(8,128)S(1)}, f32[128,512]{1,0:T(8,128)S(1)}, f32[128,512]{1,0:T(8,128)S(1)}, f32[128,512]{1,0:T(8,128)S(1)}, f32[8,4,128]{2,1,0:T(4,128)S(1)}, /*index=5*/f32[4,128]{1,0:T(4,128)S(1)}) custom-call(s32[1]{0:T(128)} %bitcast.place, bf16[128,2048]{1,0:T(8,128)(2,1)S(1)} %get-tuple-element.85.query, ...), custom_call_target="tpu_custom_call" | custom-call | flops 16000000 | bytes 1 | tf_op jit(solution)/shard_map/local/pallas_call | solution.py:938
  12.4 0.0 collective-permute-done.3.rest_1_.got.second_got
  12.4 0.0 collective-permute-done.5.got.second_got
  12.4 0.7 %collective-permute-done.2.first.chip_total = f32[528,128]{1,0:T(8,128)S(1)} collective-permute-done((f32[528,128]{1,0:T(8,128)S(1)}, f32[528,128]{1,0:T(8,128)S(1)}, u32[]{:S(2)}, u32[]{:S(2)}) %collective-permute-start.2) | collective-permute-done | bytes 270368 | tf_op jit(solution)/shard_map/ppermute | solution.py:935
  13.1 0.1 second_merge.2.rest_0_
  13.2 1.0 %collective-permute-start.8 = (f32[512,128]{1,0:T(8,128)S(1)}, f32[512,128]{1,0:T(8,128)S(1)}, u32[]{:S(2)}, u32[]{:S(2)}) collective-permute-start(f32[512,128]{1,0:T(8,128)S(1)} %second_merge.2.rest_0_), channel_id=1, source_target_pairs={{0,1},{1,0},{2,4},{4,2},{3,5},{5,3},{6,7},{7,6},{8,9},{9,8},{10,12... | collective-permute-start | bytes 786440 | tf_op jit(solution)/shard_map/ppermute | solution.py:935
  14.2 0.1 collective-permute-start.7
  14.3 1.4 %local.6 = (f32[128,512]{1,0:T(8,128)S(1)}, f32[128,512]{1,0:T(8,128)S(1)}, f32[128,512]{1,0:T(8,128)S(1)}, f32[128,512]{1,0:T(8,128)S(1)}, f32[8,4,128]{2,1,0:T(4,128)S(1)}, /*index=5*/f32[4,128]{1,0:T(4,128)S(1)}) custom-call(s32[1]{0:T(128)} %bitcast.place, bf16[128,2048]{1,0:T(8,128)(2,1)S(1)} %get-tuple-element.85.query, ...), custom_call_target="tpu_custom_call" | custom-call | flops 25600000000 | bytes 1 | tf_op jit(solution)/shard_map/local/pallas_call | solution.py:938
  15.7 1.4 %local.7 = (f32[128,512]{1,0:T(8,128)S(1)}, f32[128,512]{1,0:T(8,128)S(1)}, f32[128,512]{1,0:T(8,128)S(1)}, f32[128,512]{1,0:T(8,128)S(1)}, f32[8,4,128]{2,1,0:T(4,128)S(1)}, /*index=5*/f32[4,128]{1,0:T(4,128)S(1)}) custom-call(s32[1]{0:T(128)} %bitcast.place, bf16[128,2048]{1,0:T(8,128)(2,1)S(1)} %get-tuple-element.85.query, ...), custom_call_target="tpu_custom_call" | custom-call | flops 1600000000 | bytes 1 | tf_op jit(solution)/shard_map/local/pallas_call | solution.py:938
  17.1 1.7 %collective-permute-done.4.first = f32[512,128]{1,0:T(8,128)S(1)} collective-permute-done((f32[512,128]{1,0:T(8,128)S(1)}, f32[512,128]{1,0:T(8,128)S(1)}, u32[]{:S(2)}, u32[]{:S(2)}) %collective-permute-start.4) | collective-permute-done | bytes 262176 | tf_op jit(solution)/shard_map/ppermute | solution.py:935
  18.8 0.1 second_merge.3
  18.9 0.9 %collective-permute-start.6 = (f32[512,128]{1,0:T(8,128)S(1)}, f32[512,128]{1,0:T(8,128)S(1)}, u32[]{:S(2)}, u32[]{:S(2)}) collective-permute-start(f32[512,128]{1,0:T(8,128)S(1)} %second_merge.3), channel_id=1, source_target_pairs={{0,1},{1,0},{2,4},{4,2},{3,5},{5,3},{6,7},{7,6},{8,9},{9,8},{10,12... | collective-permute-start | bytes 786440 | tf_op jit(solution)/shard_map/ppermute | solution.py:935
  19.8 0.0 collective-permute-done.8.second.rest_0_
  19.8 0.1 collective-permute-start.9
  19.9 3.2 %collective-permute-start.14 = (f32[512,128]{1,0:T(8,128)S(1)}, f32[512,128]{1,0:T(8,128)S(1)}, u32[]{:S(2)}, u32[]{:S(2)}) collective-permute-start(f32[512,128]{1,0:T(8,128)S(1)} %collective-permute-done.8.second.rest_0_), channel_id=1, source_target_pairs={{0,2},{1,3},{2,0},{3,1},{4,6},{5,7},{6,4},{7,5},{8,10},{9,11},{10,... | collective-permute-start | bytes 786440 | tf_op jit(solution)/shard_map/ppermute | solution.py:935
  23.1 0.0 collective-permute-done.7.rest_1_.first
  23.1 0.0 collective-permute-done.10.front
  23.1 1.1 %first_use.4 = (f32[128,512]{1,0:T(8,128)S(1)}, f32[128,512]{1,0:T(8,128)S(1)}, f32[128,512]{1,0:T(8,128)S(1)}, f32[128,512]{1,0:T(8,128)S(1)}, f32[16,128]{1,0:T(8,128)S(1)}) custom-call(s32[1]{0:T(128)} %bitcast.place, bf16[128,2048]{1,0:T(8,128)(2,1)S(1)} %get-tuple-element.85.query, bf16[128,2048]{1,0:T(8,128)(2,1)S(1)} %get-tuple-element.86.key, ...), custom_call_target="tpu_custom_call" | custom-call | flops 4800000000 | bytes 1 | tf_op jit(solution)/shard_map/first_use/pallas_call | solution.py:938
  24.2 0.0 collective-permute-done.9.second
  24.2 1.1 %first_use.5 = (f32[128,512]{1,0:T(8,128)S(1)}, f32[128,512]{1,0:T(8,128)S(1)}, f32[128,512]{1,0:T(8,128)S(1)}, f32[128,512]{1,0:T(8,128)S(1)}, f32[16,128]{1,0:T(8,128)S(1)}) custom-call(s32[1]{0:T(128)} %bitcast.place, bf16[128,2048]{1,0:T(8,128)(2,1)S(1)} %get-tuple-element.85.query, bf16[128,2048]{1,0:T(8,128)(2,1)S(1)} %get-tuple-element.86.key, ...), custom_call_target="tpu_custom_call" | custom-call | flops 4800000000 | bytes 1 | tf_op jit(solution)/shard_map/first_use/pallas_call | solution.py:938
  25.3 0.0 collective-permute-done.6.second
  25.3 1.9 %collective-permute-start.12 = (f32[512,128]{1,0:T(8,128)S(1)}, f32[512,128]{1,0:T(8,128)S(1)}, u32[]{:S(2)}, u32[]{:S(2)}) collective-permute-start(f32[512,128]{1,0:T(8,128)S(1)} %collective-permute-done.6.second), channel_id=1, source_target_pairs={{0,2},{1,3},{2,0},{3,1},{4,6},{5,7},{6,4},{7,5},{8,10},{9,11},{10,... | collective-permute-start | bytes 786440 | tf_op jit(solution)/shard_map/ppermute | solution.py:935
  27.2 2.1 %collective-permute-start.11 = (f32[512,128]{1,0:T(8,128)S(1)}, f32[512,128]{1,0:T(8,128)S(1)}, u32[]{:S(2)}, u32[]{:S(2)}) collective-permute-start(f32[512,128]{1,0:T(8,128)S(1)} %collective-permute-done.6.second), channel_id=1, source_target_pairs={{0,1},{1,0},{2,3},{3,2},{4,5},{5,4},{6,7},{7,6},{8,9},{9,8},{10,11... | collective-permute-start | bytes 786440 | tf_op jit(solution)/shard_map/ppermute | solution.py:935
  29.3 0.0 collective-permute-start.13
  29.3 1.1 %first_use.6 = (f32[128,512]{1,0:T(8,128)S(1)}, f32[128,512]{1,0:T(8,128)S(1)}, f32[128,512]{1,0:T(8,128)S(1)}, f32[128,512]{1,0:T(8,128)S(1)}, f32[16,128]{1,0:T(8,128)S(1)}) custom-call(s32[1]{0:T(128)} %bitcast.place, bf16[128,2048]{1,0:T(8,128)(2,1)S(1)} %get-tuple-element.85.query, bf16[128,2048]{1,0:T(8,128)(2,1)S(1)} %get-tuple-element.86.key, ...), custom_call_target="tpu_custom_call" | custom-call | flops 4800000000 | bytes 1 | tf_op jit(solution)/shard_map/first_use/pallas_call | solution.py:938
  30.4 0.4 %collective-permute-done.13.first = f32[512,128]{1,0:T(8,128)S(1)} collective-permute-done((f32[512,128]{1,0:T(8,128)S(1)}, f32[512,128]{1,0:T(8,128)S(1)}, u32[]{:S(2)}, u32[]{:S(2)}) %collective-permute-start.13) | collective-permute-done | bytes 262176 | tf_op jit(solution)/shard_map/ppermute | solution.py:935
  30.8 0.0 collective-permute-done.11.second
  30.9 1.1 %first_use.7 = (f32[128,512]{1,0:T(8,128)S(1)}, f32[128,512]{1,0:T(8,128)S(1)}, f32[128,512]{1,0:T(8,128)S(1)}, f32[128,512]{1,0:T(8,128)S(1)}, f32[16,128]{1,0:T(8,128)S(1)}) custom-call(s32[1]{0:T(128)} %bitcast.place, bf16[128,2048]{1,0:T(8,128)(2,1)S(1)} %get-tuple-element.85.query, bf16[128,2048]{1,0:T(8,128)(2,1)S(1)} %get-tuple-element.86.key, ...), custom_call_target="tpu_custom_call" | custom-call | flops 4800000000 | bytes 1 | tf_op jit(solution)/shard_map/first_use/pallas_call | solution.py:938
  31.9 0.0 collective-permute-done.14.third
  31.9 0.4 %collective-permute-start.15 = (f32[512,128]{1,0:T(8,128)S(1)}, f32[512,128]{1,0:T(8,128)S(1)}, u32[]{:S(2)}, u32[]{:S(2)}) collective-permute-start(f32[512,128]{1,0:T(8,128)S(1)} %collective-permute-done.14.third), channel_id=1, source_target_pairs={{0,1},{1,0},{2,3},{3,2},{4,5},{5,4},{6,7},{7,6},{8,9},{9,8},{10,11... | collective-permute-start | bytes 786440 | tf_op jit(solution)/shard_map/ppermute | solution.py:935
  32.4 0.6 %last_use.4 = (bf16[128,512]{1,0:T(8,128)(2,1)S(1)}, bf16[128,512]{1,0:T(8,128)(2,1)S(1)}, bf16[128,512]{1,0:T(8,128)(2,1)S(1)}, bf16[128,512]{1,0:T(8,128)(2,1)S(1)}, f32[12,128]{1,0:T(8,128)S(1)}) custom-call(s32[1]{0:T(128)} %bitcast.place, bf16[128,2048]{1,0:T(8,128)(2,1)S(1)} %get-tuple-element.85.query, bf16[128,2048]{1,0:T(8,128)(2,1)S(1)} %get-tuple-element.86.key, ...), custom_call_target="tpu_custom_call" | custom-call | flops 9600000000 | bytes 1 | tf_op jit(solution)/shard_map/last_use/pallas_call | solution.py:938
  33.0 0.5 %collective-permute-done.15.third = f32[512,128]{1,0:T(8,128)S(1)} collective-permute-done((f32[512,128]{1,0:T(8,128)S(1)}, f32[512,128]{1,0:T(8,128)S(1)}, u32[]{:S(2)}, u32[]{:S(2)}) %collective-permute-start.15) | collective-permute-done | bytes 262176 | tf_op jit(solution)/shard_map/ppermute | solution.py:935
  33.5 1.4 %last_use.5 = (bf16[128,2048]{1,0:T(8,128)(2,1)}, bf16[128,2048]{1,0:T(8,128)(2,1)}, bf16[128,2048]{1,0:T(8,128)(2,1)}, bf16[128,2048]{1,0:T(8,128)(2,1)}, f32[12,128]{1,0:T(8,128)S(1)}) custom-call(s32[1]{0:T(128)} %bitcast.place, bf16[128,2048]{1,0:T(8,128)(2,1)S(1)} %get-tuple-element.85.query, bf16[128,2048]{1,0:T(8,128)(2,1)S(1)} %get-tuple-element.86.key, ...), custom_call_target="tpu_custom_call" | custom-call | flops 4000000000 | bytes 1 | tf_op jit(solution)/shard_map/last_use/pallas_call | solution.py:1103
  35.0 0.1 collective-permute-done.12.third
  35.1 0.9 %collective-permute-start.16 = (f32[512,128]{1,0:T(8,128)S(1)}, f32[512,128]{1,0:T(8,128)S(1)}, u32[]{:S(2)}, u32[]{:S(2)}) collective-permute-start(f32[512,128]{1,0:T(8,128)S(1)} %collective-permute-done.12.third), channel_id=1, source_target_pairs={{0,1},{1,0},{2,3},{3,2},{4,5},{5,4},{6,7},{7,6},{8,9},{9,8},{10,11... | collective-permute-start | bytes 786440 | tf_op jit(solution)/shard_map/ppermute | solution.py:935
  36.0 0.6 %last_use.6 = (bf16[128,512]{1,0:T(8,128)(2,1)S(1)}, bf16[128,512]{1,0:T(8,128)(2,1)S(1)}, bf16[128,512]{1,0:T(8,128)(2,1)S(1)}, bf16[128,512]{1,0:T(8,128)(2,1)S(1)}, f32[12,128]{1,0:T(8,128)S(1)}) custom-call(s32[1]{0:T(128)} %bitcast.place, bf16[128,2048]{1,0:T(8,128)(2,1)S(1)} %get-tuple-element.85.query, bf16[128,2048]{1,0:T(8,128)(2,1)S(1)} %get-tuple-element.86.key, ...), custom_call_target="tpu_custom_call" | custom-call | flops 2400000000 | bytes 1 | tf_op jit(solution)/shard_map/last_use/pallas_call | solution.py:938
  36.6 0.5 %collective-permute-done.16.third = f32[512,128]{1,0:T(8,128)S(1)} collective-permute-done((f32[512,128]{1,0:T(8,128)S(1)}, f32[512,128]{1,0:T(8,128)S(1)}, u32[]{:S(2)}, u32[]{:S(2)}) %collective-permute-start.16) | collective-permute-done | bytes 262176 | tf_op jit(solution)/shard_map/ppermute | solution.py:935
  37.2 1.6 %last_use.7 = (bf16[128,2048]{1,0:T(8,128)(2,1)}, bf16[128,2048]{1,0:T(8,128)(2,1)}, bf16[128,2048]{1,0:T(8,128)(2,1)}, bf16[128,2048]{1,0:T(8,128)(2,1)}, f32[11,16,128]{2,1,0:T(8,128)}, /*index=5*/f32[16,128]{1,0:T(8,128)}) custom-call(s32[1]{0:T(128)} %bitcast.place, ...), custom_call_target="tpu_custom_call", output_to_operand_aliasing={{0}: (36, {}), {1}: (37, {}), {2}: (38, {}), {3}: (39, {})} | custom-call | flops 4000000000 | bytes 1 | tf_op jit(solution)/shard_map/last_use/pallas_call | solution.py:1103
  (1 shorter events, 0.0 us)
Async XLA Ops:
  2.4 1.6 %collective-permute-start = (f32[528,128]{1,0:T(8,128)S(1)}, f32[528,128]{1,0:T(8,128)S(1)}, u32[]{:S(2)}, u32[]{:S(2)}) collective-permute-start(f32[528,128]{1,0:T(8,128)S(1)} %get-tuple-element.91.after), channel_id=1, source_target_pairs={{0,1},{1,0},{2,3},{3,2},{4,5},{5,4},{6,7},{7,6},{8,9},{9,8},{10,11... | collective-permute-start | bytes 811016 | tf_op jit(solution)/shard_map/ppermute | solution.py:935
  2.5 8.3 %collective-permute-start.1 = (f32[512,128]{1,0:T(8,128)S(1)}, f32[512,128]{1,0:T(8,128)S(1)}, u32[]{:S(2)}, u32[]{:S(2)}) collective-permute-start(f32[512,128]{1,0:T(8,128)S(1)} %get-tuple-element.92), channel_id=1, source_target_pairs={{0,1},{1,0},{2,3},{3,2},{4,5},{5,4},{6,7},{7,6},{8,9},{9,8},{10,11... | collective-permute-start | bytes 786440 | tf_op jit(solution)/shard_map/ppermute | solution.py:935
  4.1 9.0 %collective-permute-start.2 = (f32[528,128]{1,0:T(8,128)S(1)}, f32[528,128]{1,0:T(8,128)S(1)}, u32[]{:S(2)}, u32[]{:S(2)}) collective-permute-start(f32[528,128]{1,0:T(8,128)S(1)} %first_merge.2.after), channel_id=1, source_target_pairs={{0,2},{1,3},{2,0},{3,1},{4,6},{5,7},{6,4},{7,5},{8,10},{9,11},{10,... | collective-permute-start | bytes 811016 | tf_op jit(solution)/shard_map/ppermute | solution.py:935
  8.2 4.2 %collective-permute-start.3 = (f32[512,128]{1,0:T(8,128)S(1)}, f32[512,128]{1,0:T(8,128)S(1)}, u32[]{:S(2)}, u32[]{:S(2)}) collective-permute-start(f32[512,128]{1,0:T(8,128)S(1)} %get-tuple-element.97), channel_id=1, source_target_pairs={{0,1},{1,0},{2,3},{3,2},{4,5},{5,4},{6,7},{7,6},{8,9},{9,8},{10,11... | collective-permute-start | bytes 786440 | tf_op jit(solution)/shard_map/ppermute | solution.py:935
  8.9 3.5 %collective-permute-start.5 = (f32[512,128]{1,0:T(8,128)S(1)}, f32[512,128]{1,0:T(8,128)S(1)}, u32[]{:S(2)}, u32[]{:S(2)}) collective-permute-start(f32[512,128]{1,0:T(8,128)S(1)} %get-tuple-element.99), channel_id=1, source_target_pairs={{0,1},{1,0},{2,3},{3,2},{4,5},{5,4},{6,7},{7,6},{8,9},{9,8},{10,11... | collective-permute-start | bytes 786440 | tf_op jit(solution)/shard_map/ppermute | solution.py:935
  9.0 14.1 %collective-permute-start.10 = (f32[4096,128]{1,0:T(8,128)S(1)}, f32[4096,128]{1,0:T(8,128)S(1)}, u32[]{:S(2)}, u32[]{:S(2)}) collective-permute-start(f32[4096,128]{1,0:T(8,128)S(1)} %get-tuple-element.104), channel_id=1, source_target_pairs={{0,1},{1,0},{2,3},{3,2},{4,5},{5,4},{6,7},{7,6},{8,9},{9,8},{10,11... | collective-permute-start | bytes 6291464 | tf_op jit(solution)/shard_map/ppermute | solution.py:935
  10.9 8.0 %collective-permute-start.4 = (f32[512,128]{1,0:T(8,128)S(1)}, f32[512,128]{1,0:T(8,128)S(1)}, u32[]{:S(2)}, u32[]{:S(2)}) collective-permute-start(f32[512,128]{1,0:T(8,128)S(1)} %first_merge.3), channel_id=1, source_target_pairs={{0,2},{1,3},{2,0},{3,1},{4,6},{5,7},{6,4},{7,5},{8,10},{9,11},{10,... | collective-permute-start | bytes 786440 | tf_op jit(solution)/shard_map/ppermute | solution.py:935
  13.2 6.6 %collective-permute-start.8 = (f32[512,128]{1,0:T(8,128)S(1)}, f32[512,128]{1,0:T(8,128)S(1)}, u32[]{:S(2)}, u32[]{:S(2)}) collective-permute-start(f32[512,128]{1,0:T(8,128)S(1)} %second_merge.2.rest_0_), channel_id=1, source_target_pairs={{0,1},{1,0},{2,4},{4,2},{3,5},{5,3},{6,7},{7,6},{8,9},{9,8},{10,12... | collective-permute-start | bytes 786440 | tf_op jit(solution)/shard_map/ppermute | solution.py:935
  14.2 8.9 %collective-permute-start.7 = (f32[528,128]{1,0:T(8,128)S(1)}, f32[528,128]{1,0:T(8,128)S(1)}, u32[]{:S(2)}, u32[]{:S(2)}) collective-permute-start(f32[528,128]{1,0:T(8,128)S(1)} %collective-permute-done.2.first.chip_total), channel_id=1, source_target_pairs={{0,1},{1,0},{2,3},{3,2},{4,5},{5,4},{6,7},{7,6},{8,9},{9,8},{10,11... | collective-permute-start | bytes 811016 | tf_op jit(solution)/shard_map/ppermute | solution.py:935
  18.9 6.4 %collective-permute-start.6 = (f32[512,128]{1,0:T(8,128)S(1)}, f32[512,128]{1,0:T(8,128)S(1)}, u32[]{:S(2)}, u32[]{:S(2)}) collective-permute-start(f32[512,128]{1,0:T(8,128)S(1)} %second_merge.3), channel_id=1, source_target_pairs={{0,1},{1,0},{2,4},{4,2},{3,5},{5,3},{6,7},{7,6},{8,9},{9,8},{10,12... | collective-permute-start | bytes 786440 | tf_op jit(solution)/shard_map/ppermute | solution.py:935
  19.8 4.4 %collective-permute-start.9 = (f32[512,128]{1,0:T(8,128)S(1)}, f32[512,128]{1,0:T(8,128)S(1)}, u32[]{:S(2)}, u32[]{:S(2)}) collective-permute-start(f32[512,128]{1,0:T(8,128)S(1)} %collective-permute-done.8.second.rest_0_), channel_id=1, source_target_pairs={{0,1},{1,0},{2,3},{3,2},{4,5},{5,4},{6,7},{7,6},{8,9},{9,8},{10,11... | collective-permute-start | bytes 786440 | tf_op jit(solution)/shard_map/ppermute | solution.py:935
  19.9 12.0 %collective-permute-start.14 = (f32[512,128]{1,0:T(8,128)S(1)}, f32[512,128]{1,0:T(8,128)S(1)}, u32[]{:S(2)}, u32[]{:S(2)}) collective-permute-start(f32[512,128]{1,0:T(8,128)S(1)} %collective-permute-done.8.second.rest_0_), channel_id=1, source_target_pairs={{0,2},{1,3},{2,0},{3,1},{4,6},{5,7},{6,4},{7,5},{8,10},{9,11},{10,... | collective-permute-start | bytes 786440 | tf_op jit(solution)/shard_map/ppermute | solution.py:935
  25.3 9.7 %collective-permute-start.12 = (f32[512,128]{1,0:T(8,128)S(1)}, f32[512,128]{1,0:T(8,128)S(1)}, u32[]{:S(2)}, u32[]{:S(2)}) collective-permute-start(f32[512,128]{1,0:T(8,128)S(1)} %collective-permute-done.6.second), channel_id=1, source_target_pairs={{0,2},{1,3},{2,0},{3,1},{4,6},{5,7},{6,4},{7,5},{8,10},{9,11},{10,... | collective-permute-start | bytes 786440 | tf_op jit(solution)/shard_map/ppermute | solution.py:935
  27.2 3.6 %collective-permute-start.11 = (f32[512,128]{1,0:T(8,128)S(1)}, f32[512,128]{1,0:T(8,128)S(1)}, u32[]{:S(2)}, u32[]{:S(2)}) collective-permute-start(f32[512,128]{1,0:T(8,128)S(1)} %collective-permute-done.6.second), channel_id=1, source_target_pairs={{0,1},{1,0},{2,3},{3,2},{4,5},{5,4},{6,7},{7,6},{8,9},{9,8},{10,11... | collective-permute-start | bytes 786440 | tf_op jit(solution)/shard_map/ppermute | solution.py:935
  29.3 1.5 %collective-permute-start.13 = (f32[512,128]{1,0:T(8,128)S(1)}, f32[512,128]{1,0:T(8,128)S(1)}, u32[]{:S(2)}, u32[]{:S(2)}) collective-permute-start(f32[512,128]{1,0:T(8,128)S(1)} %collective-permute-done.4.first), channel_id=1, source_target_pairs={{0,1},{1,0},{2,3},{3,2},{4,5},{5,4},{6,7},{7,6},{8,9},{9,8},{10,11... | collective-permute-start | bytes 786440 | tf_op jit(solution)/shard_map/ppermute | solution.py:935
  31.9 1.6 %collective-permute-start.15 = (f32[512,128]{1,0:T(8,128)S(1)}, f32[512,128]{1,0:T(8,128)S(1)}, u32[]{:S(2)}, u32[]{:S(2)}) collective-permute-start(f32[512,128]{1,0:T(8,128)S(1)} %collective-permute-done.14.third), channel_id=1, source_target_pairs={{0,1},{1,0},{2,3},{3,2},{4,5},{5,4},{6,7},{7,6},{8,9},{9,8},{10,11... | collective-permute-start | bytes 786440 | tf_op jit(solution)/shard_map/ppermute | solution.py:935
  35.1 2.1 %collective-permute-start.16 = (f32[512,128]{1,0:T(8,128)S(1)}, f32[512,128]{1,0:T(8,128)S(1)}, u32[]{:S(2)}, u32[]{:S(2)}) collective-permute-start(f32[512,128]{1,0:T(8,128)S(1)} %collective-permute-done.12.third), channel_id=1, source_target_pairs={{0,1},{1,0},{2,3},{3,2},{4,5},{5,4},{6,7},{7,6},{8,9},{9,8},{10,11... | collective-permute-start | bytes 786440 | tf_op jit(solution)/shard_map/ppermute | solution.py:935

commit v8 on v7

--- a/solution.py
+++ b/solution.py
@@ -465,14 +465,14 @@
     )
 
 
-def first_merge_kernel(low, place, totals, first_got, keep, got, *rest):
+def first_merge_kernel(low, last, place, totals, first_got, keep, got, *rest):
     out = rest[-1]
     position = place[0]
     chip = position // 2
     heads, dim = totals.shape[0], keep.shape[1]
     own_total = totals[...]
     other_total = first_got[pl.ds(first_got.shape[0] - heads, heads), :]
-    count = out.shape[0] // dim
+    count = got.shape[0] // dim
     factors = pair_factors(position, own_total, other_total, chip % 2 == 0)
     own_factor, other_factor = (take_half(rows, position % 2, low, count) for rows in factors)
     for index in range(count):
@@ -482,7 +482,7 @@
             own_factor[one] * keep[pl.ds((low + index) * dim, dim), :]
             + other_factor[one] * got[rows, :]
         )
-    if low == 0:
+    if last:
         out[pl.ds(count * dim, heads), :] = own_total + other_total
 
 
@@ -972,8 +972,8 @@
 
     def first_merge(part, *unread):
         return call(
-            functools.partial(first_merge_kernel, lows[part]),
-            sds(counts[part] * dim + (0 if part else heads), dim),
+            functools.partial(first_merge_kernel, lows[part], part == parts[-1]),
+            sds(counts[part] * dim + (heads if part == parts[-1] else 0), dim),
             (place, totals, got1[0], keep1, got1[part]),
             unread,
             cost(0.2, RATE_FIRST),
@@ -1066,7 +1066,7 @@
             *inputs,
             got1[0],
             got1[part],
-            first[0],
+            first[-1],
             (second if mine else second_over)[part],
             (third if mine else third_over)[part],
             front,

time: 39.2 us -> 39 us (level)
  no operation moved by 1% of the time
where the time goes in v8:
time: 39 us; the launch traced here: 38.6 us
  Pallas kernels  18.5 us (47%)
  starting transfers between devices  14.7 us (38%)
  waiting for transfers between devices  4.55 us (12%)
  between operations  0.77 us (2%)
    ppermute x17, starting transfers between devices, swap(): return lax.ppermute(block, 'ctx', route)  14.7 us
    pallas_call x14, Pallas kernels, call(): pl.pallas_call(kernel, out_shape=out_shape, in_specs=[SCALAR] + [pl.Block...  13.6 us
    ppermute x17, waiting for transfers between devices, swap(): return lax.ppermute(block, 'ctx', route)  4.55 us
    pallas_call x2, Pallas kernels, last_use(): pl.pallas_call(functools.partial(last_use_kernel, lows[part], mine, count...  3.03 us
    pallas_call x1, Pallas kernels, line_device(): pl.pallas_call(first_export_kernel, out_shape=tuple((pltpu.VMEM((count *...  1.78 us
  transfers between devices with their start and end apart: 17, of which 7 were waited for; matrix products, arithmetic and copies ran while one was open for 0% of the time, Pallas kernels for 39%

profile of v8, /device:TPU:1, one launch (start us, length us, event | category | flops | bytes accessed | tf_op | source)
XLA Modules:
  0.0 38.6 jit_solution(11096441012133348471)
XLA Ops:
  0.6 1.8 %first_exports.1 = (f32[528,128]{1,0:T(8,128)S(1)}, f32[512,128]{1,0:T(8,128)S(1)}, bf16[128,2048]{1,0:T(8,128)(2,1)S(1)}, bf16[128,2048]{1,0:T(8,128)(2,1)S(1)}...) custom-call(s32[1]{0:T(128)} %bitcast.place, ...), custom_call_target="tpu_custom_call" | custom-call | flops 32000000000 | bytes 1 | tf_op jit(solution)/shard_map/first_exports/pallas_call | solution.py:948
  2.4 0.1 collective-permute-start
  2.5 0.5 %collective-permute-start.1 = (f32[512,128]{1,0:T(8,128)S(1)}, f32[512,128]{1,0:T(8,128)S(1)}, u32[]{:S(2)}, u32[]{:S(2)}) collective-permute-start(f32[512,128]{1,0:T(8,128)S(1)} %get-tuple-element.92), channel_id=1, source_target_pairs={{0,1},{1,0},{2,3},{3,2},{4,5},{5,4},{6,7},{7,6},{8,9},{9,8},{10,11... | collective-permute-start | bytes 786440 | tf_op jit(solution)/shard_map/ppermute | solution.py:935
  3.0 0.6 %own_exports.1 = (f32[1024,128]{1,0:T(8,128)S(1)}, f32[16,128]{1,0:T(8,128)S(1)}) custom-call(s32[1]{0:T(128)} %bitcast.place, bf16[128,2048]{1,0:T(8,128)(2,1)S(1)} %get-tuple-element.85.query, bf16[128,2048]{1,0:T(8,128)(2,1)S(1)} %get-tuple-element.86.key, bf16[128,2048]{1,0:T(8,128)(2,1)S(1)} %get-tuple-element.87.value, ...), custom_call_target="tpu_custom_call" | custom-call | flops 12800000000 | bytes 1 | tf_op jit(solution)/shard_map/own_exports/pallas_call | solution.py:938
  3.6 0.4 %collective-permute-done.first_got.got.pair_got = f32[528,128]{1,0:T(8,128)S(1)} collective-permute-done((f32[528,128]{1,0:T(8,128)S(1)}, f32[528,128]{1,0:T(8,128)S(1)}, u32[]{:S(2)}, u32[]{:S(2)}) %collective-permute-start) | collective-permute-done | bytes 270368 | tf_op jit(solution)/shard_map/ppermute | solution.py:935
  4.1 2.5 %collective-permute-start.5 = (f32[512,128]{1,0:T(8,128)S(1)}, f32[512,128]{1,0:T(8,128)S(1)}, u32[]{:S(2)}, u32[]{:S(2)}) collective-permute-start(f32[512,128]{1,0:T(8,128)S(1)} %first_merge.2.after), channel_id=1, source_target_pairs={{0,2},{1,3},{2,0},{3,1},{4,6},{5,7},{6,4},{7,5},{8,10},{9,11},{10,... | collective-permute-start | bytes 786440 | tf_op jit(solution)/shard_map/ppermute | solution.py:935
  6.6 1.6 %second_exports.1 = (f32[512,128]{1,0:T(8,128)S(1)}, f32[512,128]{1,0:T(8,128)S(1)}, f32[1024,128]{1,0:T(8,128)S(1)}, f32[4096,128]{1,0:T(8,128)S(1)}, f32[24,128]{1,0:T(8,128)S(1)}) custom-call(s32[1]{0:T(128)} %bitcast.place, bf16[128,2048]{1,0:T(8,128)(2,1)S(1)} %get-tuple-element.85.query, bf16[128,2048]{1,0:T(8,128)(2,1)S(1)} %get-tuple-element.86.key, ...), custom_call_target="tpu_custom_call" | custom-call | flops 1600000 | bytes 1 | tf_op jit(solution)/shard_map/second_exports/pallas_call | solution.py:938
  8.2 0.7 %collective-permute-start.3 = (f32[512,128]{1,0:T(8,128)S(1)}, f32[512,128]{1,0:T(8,128)S(1)}, u32[]{:S(2)}, u32[]{:S(2)}) collective-permute-start(f32[512,128]{1,0:T(8,128)S(1)} %get-tuple-element.98), channel_id=1, source_target_pairs={{0,1},{1,0},{2,3},{3,2},{4,5},{5,4},{6,7},{7,6},{8,9},{9,8},{10,11... | collective-permute-start | bytes 786440 | tf_op jit(solution)/shard_map/ppermute | solution.py:935
  8.9 0.1 collective-permute-start.4
  9.0 0.4 %collective-permute-start.10 = (f32[4096,128]{1,0:T(8,128)S(1)}, f32[4096,128]{1,0:T(8,128)S(1)}, u32[]{:S(2)}, u32[]{:S(2)}) collective-permute-start(f32[4096,128]{1,0:T(8,128)S(1)} %get-tuple-element.104), channel_id=1, source_target_pairs={{0,1},{1,0},{2,3},{3,2},{4,5},{5,4},{6,7},{7,6},{8,9},{9,8},{10,11... | collective-permute-start | bytes 6291464 | tf_op jit(solution)/shard_map/ppermute | solution.py:935
  9.4 1.4 %local.4 = (f32[128,512]{1,0:T(8,128)S(1)}, f32[128,512]{1,0:T(8,128)S(1)}, f32[128,512]{1,0:T(8,128)S(1)}, f32[128,512]{1,0:T(8,128)S(1)}, f32[8,4,128]{2,1,0:T(4,128)S(1)}, /*index=5*/f32[4,128]{1,0:T(4,128)S(1)}) custom-call(s32[1]{0:T(128)} %bitcast.place, bf16[128,2048]{1,0:T(8,128)(2,1)S(1)} %get-tuple-element.85.query, ...), custom_call_target="tpu_custom_call" | custom-call | flops 16000000 | bytes 1 | tf_op jit(solution)/shard_map/local/pallas_call | solution.py:938
  10.8 0.0 collective-permute-done.1.got.pair_got
  10.8 0.1 first_merge.3
  10.9 0.1 collective-permute-start.2
  11.0 1.4 %local.5 = (f32[128,512]{1,0:T(8,128)S(1)}, f32[128,512]{1,0:T(8,128)S(1)}, f32[128,512]{1,0:T(8,128)S(1)}, f32[128,512]{1,0:T(8,128)S(1)}, f32[8,4,128]{2,1,0:T(4,128)S(1)}, /*index=5*/f32[4,128]{1,0:T(4,128)S(1)}) custom-call(s32[1]{0:T(128)} %bitcast.place, bf16[128,2048]{1,0:T(8,128)(2,1)S(1)} %get-tuple-element.85.query, ...), custom_call_target="tpu_custom_call" | custom-call | flops 16000000 | bytes 1 | tf_op jit(solution)/shard_map/local/pallas_call | solution.py:938
  12.4 0.0 collective-permute-done.3.rest_1_.got.second_got
  12.4 0.0 collective-permute-done.4.got.second_got
  12.4 0.5 %collective-permute-done.5.first = f32[512,128]{1,0:T(8,128)S(1)} collective-permute-done((f32[512,128]{1,0:T(8,128)S(1)}, f32[512,128]{1,0:T(8,128)S(1)}, u32[]{:S(2)}, u32[]{:S(2)}) %collective-permute-start.5) | collective-permute-done | bytes 262176 | tf_op jit(solution)/shard_map/ppermute | solution.py:935
  12.9 0.1 second_merge.2.rest_0_
  13.0 1.0 %collective-permute-start.8 = (f32[512,128]{1,0:T(8,128)S(1)}, f32[512,128]{1,0:T(8,128)S(1)}, u32[]{:S(2)}, u32[]{:S(2)}) collective-permute-start(f32[512,128]{1,0:T(8,128)S(1)} %second_merge.2.rest_0_), channel_id=1, source_target_pairs={{0,1},{1,0},{2,4},{4,2},{3,5},{5,3},{6,7},{7,6},{8,9},{9,8},{10,12... | collective-permute-start | bytes 786440 | tf_op jit(solution)/shard_map/ppermute | solution.py:935
  14.0 1.4 %local.6 = (f32[128,512]{1,0:T(8,128)S(1)}, f32[128,512]{1,0:T(8,128)S(1)}, f32[128,512]{1,0:T(8,128)S(1)}, f32[128,512]{1,0:T(8,128)S(1)}, f32[8,4,128]{2,1,0:T(4,128)S(1)}, /*index=5*/f32[4,128]{1,0:T(4,128)S(1)}) custom-call(s32[1]{0:T(128)} %bitcast.place, bf16[128,2048]{1,0:T(8,128)(2,1)S(1)} %get-tuple-element.85.query, ...), custom_call_target="tpu_custom_call" | custom-call | flops 25600000000 | bytes 1 | tf_op jit(solution)/shard_map/local/pallas_call | solution.py:938
  15.4 0.1 collective-permute-start.7
  15.5 1.4 %local.7 = (f32[128,512]{1,0:T(8,128)S(1)}, f32[128,512]{1,0:T(8,128)S(1)}, f32[128,512]{1,0:T(8,128)S(1)}, f32[128,512]{1,0:T(8,128)S(1)}, f32[8,4,128]{2,1,0:T(4,128)S(1)}, /*index=5*/f32[4,128]{1,0:T(4,128)S(1)}) custom-call(s32[1]{0:T(128)} %bitcast.place, bf16[128,2048]{1,0:T(8,128)(2,1)S(1)} %get-tuple-element.85.query, ...), custom_call_target="tpu_custom_call" | custom-call | flops 1600000000 | bytes 1 | tf_op jit(solution)/shard_map/local/pallas_call | solution.py:938
  16.9 2.1 %collective-permute-done.2.first.chip_total = f32[528,128]{1,0:T(8,128)S(1)} collective-permute-done((f32[528,128]{1,0:T(8,128)S(1)}, f32[528,128]{1,0:T(8,128)S(1)}, u32[]{:S(2)}, u32[]{:S(2)}) %collective-permute-start.2) | collective-permute-done | bytes 270368 | tf_op jit(solution)/shard_map/ppermute | solution.py:935
  19.0 0.1 second_merge.3
  19.1 0.9 %collective-permute-start.6 = (f32[512,128]{1,0:T(8,128)S(1)}, f32[512,128]{1,0:T(8,128)S(1)}, u32[]{:S(2)}, u32[]{:S(2)}) collective-permute-start(f32[512,128]{1,0:T(8,128)S(1)} %second_merge.3), channel_id=1, source_target_pairs={{0,1},{1,0},{2,4},{4,2},{3,5},{5,3},{6,7},{7,6},{8,9},{9,8},{10,12... | collective-permute-start | bytes 786440 | tf_op jit(solution)/shard_map/ppermute | solution.py:935
  20.0 0.0 collective-permute-done.8.second.rest_0_
  20.0 0.1 collective-permute-start.9
  20.1 2.9 %collective-permute-start.14 = (f32[512,128]{1,0:T(8,128)S(1)}, f32[512,128]{1,0:T(8,128)S(1)}, u32[]{:S(2)}, u32[]{:S(2)}) collective-permute-start(f32[512,128]{1,0:T(8,128)S(1)} %collective-permute-done.8.second.rest_0_), channel_id=1, source_target_pairs={{0,2},{1,3},{2,0},{3,1},{4,6},{5,7},{6,4},{7,5},{8,10},{9,11},{10,... | collective-permute-start | bytes 786440 | tf_op jit(solution)/shard_map/ppermute | solution.py:935
  22.9 0.0 collective-permute-done.7.rest_1_.first
  22.9 0.0 collective-permute-done.10.front
  23.0 1.1 %first_use.4 = (f32[128,512]{1,0:T(8,128)S(1)}, f32[128,512]{1,0:T(8,128)S(1)}, f32[128,512]{1,0:T(8,128)S(1)}, f32[128,512]{1,0:T(8,128)S(1)}, f32[16,128]{1,0:T(8,128)S(1)}) custom-call(s32[1]{0:T(128)} %bitcast.place, bf16[128,2048]{1,0:T(8,128)(2,1)S(1)} %get-tuple-element.85.query, bf16[128,2048]{1,0:T(8,128)(2,1)S(1)} %get-tuple-element.86.key, ...), custom_call_target="tpu_custom_call" | custom-call | flops 4800000000 | bytes 1 | tf_op jit(solution)/shard_map/first_use/pallas_call | solution.py:938
  24.0 0.0 collective-permute-done.9.second
  24.1 1.1 %first_use.5 = (f32[128,512]{1,0:T(8,128)S(1)}, f32[128,512]{1,0:T(8,128)S(1)}, f32[128,512]{1,0:T(8,128)S(1)}, f32[128,512]{1,0:T(8,128)S(1)}, f32[16,128]{1,0:T(8,128)S(1)}) custom-call(s32[1]{0:T(128)} %bitcast.place, bf16[128,2048]{1,0:T(8,128)(2,1)S(1)} %get-tuple-element.85.query, bf16[128,2048]{1,0:T(8,128)(2,1)S(1)} %get-tuple-element.86.key, ...), custom_call_target="tpu_custom_call" | custom-call | flops 4800000000 | bytes 1 | tf_op jit(solution)/shard_map/first_use/pallas_call | solution.py:938
  25.2 0.0 collective-permute-done.6.second
  25.2 2.0 %collective-permute-start.12 = (f32[512,128]{1,0:T(8,128)S(1)}, f32[512,128]{1,0:T(8,128)S(1)}, u32[]{:S(2)}, u32[]{:S(2)}) collective-permute-start(f32[512,128]{1,0:T(8,128)S(1)} %collective-permute-done.6.second), channel_id=1, source_target_pairs={{0,2},{1,3},{2,0},{3,1},{4,6},{5,7},{6,4},{7,5},{8,10},{9,11},{10,... | collective-permute-start | bytes 786440 | tf_op jit(solution)/shard_map/ppermute | solution.py:935
  27.1 2.1 %collective-permute-start.11 = (f32[512,128]{1,0:T(8,128)S(1)}, f32[512,128]{1,0:T(8,128)S(1)}, u32[]{:S(2)}, u32[]{:S(2)}) collective-permute-start(f32[512,128]{1,0:T(8,128)S(1)} %collective-permute-done.6.second), channel_id=1, source_target_pairs={{0,1},{1,0},{2,3},{3,2},{4,5},{5,4},{6,7},{7,6},{8,9},{9,8},{10,11... | collective-permute-start | bytes 786440 | tf_op jit(solution)/shard_map/ppermute | solution.py:935
  29.3 0.0 collective-permute-start.13
  29.3 1.1 %first_use.6 = (f32[128,512]{1,0:T(8,128)S(1)}, f32[128,512]{1,0:T(8,128)S(1)}, f32[128,512]{1,0:T(8,128)S(1)}, f32[128,512]{1,0:T(8,128)S(1)}, f32[16,128]{1,0:T(8,128)S(1)}) custom-call(s32[1]{0:T(128)} %bitcast.place, bf16[128,2048]{1,0:T(8,128)(2,1)S(1)} %get-tuple-element.85.query, bf16[128,2048]{1,0:T(8,128)(2,1)S(1)} %get-tuple-element.86.key, ...), custom_call_target="tpu_custom_call" | custom-call | flops 4800000000 | bytes 1 | tf_op jit(solution)/shard_map/first_use/pallas_call | solution.py:938
  30.4 0.1 collective-permute-done.11.second
  30.4 0.4 collective-permute-done.13.first
  30.8 1.1 %first_use.7 = (f32[128,512]{1,0:T(8,128)S(1)}, f32[128,512]{1,0:T(8,128)S(1)}, f32[128,512]{1,0:T(8,128)S(1)}, f32[128,512]{1,0:T(8,128)S(1)}, f32[16,128]{1,0:T(8,128)S(1)}) custom-call(s32[1]{0:T(128)} %bitcast.place, bf16[128,2048]{1,0:T(8,128)(2,1)S(1)} %get-tuple-element.85.query, bf16[128,2048]{1,0:T(8,128)(2,1)S(1)} %get-tuple-element.86.key, ...), custom_call_target="tpu_custom_call" | custom-call | flops 4800000000 | bytes 1 | tf_op jit(solution)/shard_map/first_use/pallas_call | solution.py:938
  31.9 0.0 collective-permute-done.14.third
  31.9 0.4 %collective-permute-start.15 = (f32[512,128]{1,0:T(8,128)S(1)}, f32[512,128]{1,0:T(8,128)S(1)}, u32[]{:S(2)}, u32[]{:S(2)}) collective-permute-start(f32[512,128]{1,0:T(8,128)S(1)} %collective-permute-done.14.third), channel_id=1, source_target_pairs={{0,1},{1,0},{2,3},{3,2},{4,5},{5,4},{6,7},{7,6},{8,9},{9,8},{10,11... | collective-permute-start | bytes 786440 | tf_op jit(solution)/shard_map/ppermute | solution.py:935
  32.3 0.6 %last_use.4 = (bf16[128,512]{1,0:T(8,128)(2,1)S(1)}, bf16[128,512]{1,0:T(8,128)(2,1)S(1)}, bf16[128,512]{1,0:T(8,128)(2,1)S(1)}, bf16[128,512]{1,0:T(8,128)(2,1)S(1)}, f32[12,128]{1,0:T(8,128)S(1)}) custom-call(s32[1]{0:T(128)} %bitcast.place, bf16[128,2048]{1,0:T(8,128)(2,1)S(1)} %get-tuple-element.85.query, bf16[128,2048]{1,0:T(8,128)(2,1)S(1)} %get-tuple-element.86.key, ...), custom_call_target="tpu_custom_call" | custom-call | flops 9600000000 | bytes 1 | tf_op jit(solution)/shard_map/last_use/pallas_call | solution.py:938
  33.0 0.5 %collective-permute-done.15.third = f32[512,128]{1,0:T(8,128)S(1)} collective-permute-done((f32[512,128]{1,0:T(8,128)S(1)}, f32[512,128]{1,0:T(8,128)S(1)}, u32[]{:S(2)}, u32[]{:S(2)}) %collective-permute-start.15) | collective-permute-done | bytes 262176 | tf_op jit(solution)/shard_map/ppermute | solution.py:935
  33.5 1.4 %last_use.5 = (bf16[128,2048]{1,0:T(8,128)(2,1)}, bf16[128,2048]{1,0:T(8,128)(2,1)}, bf16[128,2048]{1,0:T(8,128)(2,1)}, bf16[128,2048]{1,0:T(8,128)(2,1)}, f32[12,128]{1,0:T(8,128)S(1)}) custom-call(s32[1]{0:T(128)} %bitcast.place, bf16[128,2048]{1,0:T(8,128)(2,1)S(1)} %get-tuple-element.85.query, bf16[128,2048]{1,0:T(8,128)(2,1)S(1)} %get-tuple-element.86.key, ...), custom_call_target="tpu_custom_call" | custom-call | flops 4000000000 | bytes 1 | tf_op jit(solution)/shard_map/last_use/pallas_call | solution.py:1103
  34.9 0.0 collective-permute-done.12.third
  35.0 0.9 %collective-permute-start.16 = (f32[512,128]{1,0:T(8,128)S(1)}, f32[512,128]{1,0:T(8,128)S(1)}, u32[]{:S(2)}, u32[]{:S(2)}) collective-permute-start(f32[512,128]{1,0:T(8,128)S(1)} %collective-permute-done.12.third), channel_id=1, source_target_pairs={{0,1},{1,0},{2,3},{3,2},{4,5},{5,4},{6,7},{7,6},{8,9},{9,8},{10,11... | collective-permute-start | bytes 786440 | tf_op jit(solution)/shard_map/ppermute | solution.py:935
  35.8 0.6 %last_use.6 = (bf16[128,512]{1,0:T(8,128)(2,1)S(1)}, bf16[128,512]{1,0:T(8,128)(2,1)S(1)}, bf16[128,512]{1,0:T(8,128)(2,1)S(1)}, bf16[128,512]{1,0:T(8,128)(2,1)S(1)}, f32[12,128]{1,0:T(8,128)S(1)}) custom-call(s32[1]{0:T(128)} %bitcast.place, bf16[128,2048]{1,0:T(8,128)(2,1)S(1)} %get-tuple-element.85.query, bf16[128,2048]{1,0:T(8,128)(2,1)S(1)} %get-tuple-element.86.key, ...), custom_call_target="tpu_custom_call" | custom-call | flops 2400000000 | bytes 1 | tf_op jit(solution)/shard_map/last_use/pallas_call | solution.py:938
  36.5 0.5 %collective-permute-done.16.third = f32[512,128]{1,0:T(8,128)S(1)} collective-permute-done((f32[512,128]{1,0:T(8,128)S(1)}, f32[512,128]{1,0:T(8,128)S(1)}, u32[]{:S(2)}, u32[]{:S(2)}) %collective-permute-start.16) | collective-permute-done | bytes 262176 | tf_op jit(solution)/shard_map/ppermute | solution.py:935
  37.0 1.6 %last_use.7 = (bf16[128,2048]{1,0:T(8,128)(2,1)}, bf16[128,2048]{1,0:T(8,128)(2,1)}, bf16[128,2048]{1,0:T(8,128)(2,1)}, bf16[128,2048]{1,0:T(8,128)(2,1)}, f32[11,16,128]{2,1,0:T(8,128)}, /*index=5*/f32[16,128]{1,0:T(8,128)}) custom-call(s32[1]{0:T(128)} %bitcast.place, ...), custom_call_target="tpu_custom_call", output_to_operand_aliasing={{0}: (36, {}), {1}: (37, {}), {2}: (38, {}), {3}: (39, {})} | custom-call | flops 4000000000 | bytes 1 | tf_op jit(solution)/shard_map/last_use/pallas_call | solution.py:1103
  (1 shorter events, 0.0 us)
Async XLA Ops:
  2.4 1.6 %collective-permute-start = (f32[528,128]{1,0:T(8,128)S(1)}, f32[528,128]{1,0:T(8,128)S(1)}, u32[]{:S(2)}, u32[]{:S(2)}) collective-permute-start(f32[528,128]{1,0:T(8,128)S(1)} %get-tuple-element.91.after), channel_id=1, source_target_pairs={{0,1},{1,0},{2,3},{3,2},{4,5},{5,4},{6,7},{7,6},{8,9},{9,8},{10,11... | collective-permute-start | bytes 811016 | tf_op jit(solution)/shard_map/ppermute | solution.py:935
  2.5 8.3 %collective-permute-start.1 = (f32[512,128]{1,0:T(8,128)S(1)}, f32[512,128]{1,0:T(8,128)S(1)}, u32[]{:S(2)}, u32[]{:S(2)}) collective-permute-start(f32[512,128]{1,0:T(8,128)S(1)} %get-tuple-element.92), channel_id=1, source_target_pairs={{0,1},{1,0},{2,3},{3,2},{4,5},{5,4},{6,7},{7,6},{8,9},{9,8},{10,11... | collective-permute-start | bytes 786440 | tf_op jit(solution)/shard_map/ppermute | solution.py:935
  4.1 8.9 %collective-permute-start.5 = (f32[512,128]{1,0:T(8,128)S(1)}, f32[512,128]{1,0:T(8,128)S(1)}, u32[]{:S(2)}, u32[]{:S(2)}) collective-permute-start(f32[512,128]{1,0:T(8,128)S(1)} %first_merge.2.after), channel_id=1, source_target_pairs={{0,2},{1,3},{2,0},{3,1},{4,6},{5,7},{6,4},{7,5},{8,10},{9,11},{10,... | collective-permute-start | bytes 786440 | tf_op jit(solution)/shard_map/ppermute | solution.py:935
  8.2 4.2 %collective-permute-start.3 = (f32[512,128]{1,0:T(8,128)S(1)}, f32[512,128]{1,0:T(8,128)S(1)}, u32[]{:S(2)}, u32[]{:S(2)}) collective-permute-start(f32[512,128]{1,0:T(8,128)S(1)} %get-tuple-element.98), channel_id=1, source_target_pairs={{0,1},{1,0},{2,3},{3,2},{4,5},{5,4},{6,7},{7,6},{8,9},{9,8},{10,11... | collective-permute-start | bytes 786440 | tf_op jit(solution)/shard_map/ppermute | solution.py:935
  8.9 3.5 %collective-permute-start.4 = (f32[512,128]{1,0:T(8,128)S(1)}, f32[512,128]{1,0:T(8,128)S(1)}, u32[]{:S(2)}, u32[]{:S(2)}) collective-permute-start(f32[512,128]{1,0:T(8,128)S(1)} %get-tuple-element.99), channel_id=1, source_target_pairs={{0,1},{1,0},{2,3},{3,2},{4,5},{5,4},{6,7},{7,6},{8,9},{9,8},{10,11... | collective-permute-start | bytes 786440 | tf_op jit(solution)/shard_map/ppermute | solution.py:935
  9.0 14.0 %collective-permute-start.10 = (f32[4096,128]{1,0:T(8,128)S(1)}, f32[4096,128]{1,0:T(8,128)S(1)}, u32[]{:S(2)}, u32[]{:S(2)}) collective-permute-start(f32[4096,128]{1,0:T(8,128)S(1)} %get-tuple-element.104), channel_id=1, source_target_pairs={{0,1},{1,0},{2,3},{3,2},{4,5},{5,4},{6,7},{7,6},{8,9},{9,8},{10,11... | collective-permute-start | bytes 6291464 | tf_op jit(solution)/shard_map/ppermute | solution.py:935
  10.9 8.1 %collective-permute-start.2 = (f32[528,128]{1,0:T(8,128)S(1)}, f32[528,128]{1,0:T(8,128)S(1)}, u32[]{:S(2)}, u32[]{:S(2)}) collective-permute-start(f32[528,128]{1,0:T(8,128)S(1)} %first_merge.3), channel_id=1, source_target_pairs={{0,2},{1,3},{2,0},{3,1},{4,6},{5,7},{6,4},{7,5},{8,10},{9,11},{10,... | collective-permute-start | bytes 811016 | tf_op jit(solution)/shard_map/ppermute | solution.py:935
  13.0 7.0 %collective-permute-start.8 = (f32[512,128]{1,0:T(8,128)S(1)}, f32[512,128]{1,0:T(8,128)S(1)}, u32[]{:S(2)}, u32[]{:S(2)}) collective-permute-start(f32[512,128]{1,0:T(8,128)S(1)} %second_merge.2.rest_0_), channel_id=1, source_target_pairs={{0,1},{1,0},{2,4},{4,2},{3,5},{5,3},{6,7},{7,6},{8,9},{9,8},{10,12... | collective-permute-start | bytes 786440 | tf_op jit(solution)/shard_map/ppermute | solution.py:935
  15.4 7.5 %collective-permute-start.7 = (f32[512,128]{1,0:T(8,128)S(1)}, f32[512,128]{1,0:T(8,128)S(1)}, u32[]{:S(2)}, u32[]{:S(2)}) collective-permute-start(f32[512,128]{1,0:T(8,128)S(1)} %collective-permute-done.5.first), channel_id=1, source_target_pairs={{0,1},{1,0},{2,3},{3,2},{4,5},{5,4},{6,7},{7,6},{8,9},{9,8},{10,11... | collective-permute-start | bytes 786440 | tf_op jit(solution)/shard_map/ppermute | solution.py:935
  19.1 6.1 %collective-permute-start.6 = (f32[512,128]{1,0:T(8,128)S(1)}, f32[512,128]{1,0:T(8,128)S(1)}, u32[]{:S(2)}, u32[]{:S(2)}) collective-permute-start(f32[512,128]{1,0:T(8,128)S(1)} %second_merge.3), channel_id=1, source_target_pairs={{0,1},{1,0},{2,4},{4,2},{3,5},{5,3},{6,7},{7,6},{8,9},{9,8},{10,12... | collective-permute-start | bytes 786440 | tf_op jit(solution)/shard_map/ppermute | solution.py:935
  20.0 4.1 %collective-permute-start.9 = (f32[512,128]{1,0:T(8,128)S(1)}, f32[512,128]{1,0:T(8,128)S(1)}, u32[]{:S(2)}, u32[]{:S(2)}) collective-permute-start(f32[512,128]{1,0:T(8,128)S(1)} %collective-permute-done.8.second.rest_0_), channel_id=1, source_target_pairs={{0,1},{1,0},{2,3},{3,2},{4,5},{5,4},{6,7},{7,6},{8,9},{9,8},{10,11... | collective-permute-start | bytes 786440 | tf_op jit(solution)/shard_map/ppermute | solution.py:935
  20.1 11.8 %collective-permute-start.14 = (f32[512,128]{1,0:T(8,128)S(1)}, f32[512,128]{1,0:T(8,128)S(1)}, u32[]{:S(2)}, u32[]{:S(2)}) collective-permute-start(f32[512,128]{1,0:T(8,128)S(1)} %collective-permute-done.8.second.rest_0_), channel_id=1, source_target_pairs={{0,2},{1,3},{2,0},{3,1},{4,6},{5,7},{6,4},{7,5},{8,10},{9,11},{10,... | collective-permute-start | bytes 786440 | tf_op jit(solution)/shard_map/ppermute | solution.py:935
  25.2 9.8 %collective-permute-start.12 = (f32[512,128]{1,0:T(8,128)S(1)}, f32[512,128]{1,0:T(8,128)S(1)}, u32[]{:S(2)}, u32[]{:S(2)}) collective-permute-start(f32[512,128]{1,0:T(8,128)S(1)} %collective-permute-done.6.second), channel_id=1, source_target_pairs={{0,2},{1,3},{2,0},{3,1},{4,6},{5,7},{6,4},{7,5},{8,10},{9,11},{10,... | collective-permute-start | bytes 786440 | tf_op jit(solution)/shard_map/ppermute | solution.py:935
  27.1 3.3 %collective-permute-start.11 = (f32[512,128]{1,0:T(8,128)S(1)}, f32[512,128]{1,0:T(8,128)S(1)}, u32[]{:S(2)}, u32[]{:S(2)}) collective-permute-start(f32[512,128]{1,0:T(8,128)S(1)} %collective-permute-done.6.second), channel_id=1, source_target_pairs={{0,1},{1,0},{2,3},{3,2},{4,5},{5,4},{6,7},{7,6},{8,9},{9,8},{10,11... | collective-permute-start | bytes 786440 | tf_op jit(solution)/shard_map/ppermute | solution.py:935
  29.3 1.5 %collective-permute-start.13 = (f32[528,128]{1,0:T(8,128)S(1)}, f32[528,128]{1,0:T(8,128)S(1)}, u32[]{:S(2)}, u32[]{:S(2)}) collective-permute-start(f32[528,128]{1,0:T(8,128)S(1)} %collective-permute-done.2.first.chip_total), channel_id=1, source_target_pairs={{0,1},{1,0},{2,3},{3,2},{4,5},{5,4},{6,7},{7,6},{8,9},{9,8},{10,11... | collective-permute-start | bytes 811016 | tf_op jit(solution)/shard_map/ppermute | solution.py:935
  31.9 1.6 %collective-permute-start.15 = (f32[512,128]{1,0:T(8,128)S(1)}, f32[512,128]{1,0:T(8,128)S(1)}, u32[]{:S(2)}, u32[]{:S(2)}) collective-permute-start(f32[512,128]{1,0:T(8,128)S(1)} %collective-permute-done.14.third), channel_id=1, source_target_pairs={{0,1},{1,0},{2,3},{3,2},{4,5},{5,4},{6,7},{7,6},{8,9},{9,8},{10,11... | collective-permute-start | bytes 786440 | tf_op jit(solution)/shard_map/ppermute | solution.py:935
  35.0 2.0 %collective-permute-start.16 = (f32[512,128]{1,0:T(8,128)S(1)}, f32[512,128]{1,0:T(8,128)S(1)}, u32[]{:S(2)}, u32[]{:S(2)}) collective-permute-start(f32[512,128]{1,0:T(8,128)S(1)} %collective-permute-done.12.third), channel_id=1, source_target_pairs={{0,1},{1,0},{2,3},{3,2},{4,5},{5,4},{6,7},{7,6},{8,9},{9,8},{10,11... | collective-permute-start | bytes 786440 | tf_op jit(solution)/shard_map/ppermute | solution.py:935

commit v9 on v8

--- a/solution.py
+++ b/solution.py
@@ -1030,7 +1030,6 @@
     front = swap(bundle, core_swap)
     second = [swap(block, middle_swap) for block in sent]
     third = [swap(second[0], side_swap)]
-    second_over = [swap(second[0], core_swap)]
     done = second[0]
 
     used = {}
@@ -1119,6 +1118,7 @@
         last_rows.extend(found[4:])
 
     first_over = [swap(after(first[0], sent[0]), core_swap)]
+    second_over = [swap(after(second[0], first_over[0]), core_swap)]
     done = first_use(0, True, done, first_over[0])
     done = first_use(0, False, done)
     second[1] = after(second[1], done)

time: 39 us -> 39 us (level)
  no operation moved by 1% of the time
where the time goes in v9:
time: 39 us; the launch traced here: 38.6 us
  Pallas kernels  18.5 us (47%)
  starting transfers between devices  14.8 us (38%)
  waiting for transfers between devices  4.55 us (12%)
  between operations  0.77 us (2%)
    ppermute x17, starting transfers between devices, swap(): return lax.ppermute(block, 'ctx', route)  14.8 us
    pallas_call x14, Pallas kernels, call(): pl.pallas_call(kernel, out_shape=out_shape, in_specs=[SCALAR] + [pl.Block...  13.6 us
    ppermute x17, waiting for transfers between devices, swap(): return lax.ppermute(block, 'ctx', route)  4.55 us
    pallas_call x2, Pallas kernels, last_use(): pl.pallas_call(functools.partial(last_use_kernel, lows[part], mine, count...  3.03 us
    pallas_call x1, Pallas kernels, line_device(): pl.pallas_call(first_export_kernel, out_shape=tuple((pltpu.VMEM((count *...  1.78 us
  transfers between devices with their start and end apart: 17, of which 7 were waited for; matrix products, arithmetic and copies ran while one was open for 0% of the time, Pallas kernels for 39%

profile of v9, /device:TPU:1, one launch (start us, length us, event | category | flops | bytes accessed | tf_op | source)
XLA Modules:
  0.0 38.6 jit_solution(13901151665372731163)
XLA Ops:
  0.6 1.8 %first_exports.1 = (f32[528,128]{1,0:T(8,128)S(1)}, f32[512,128]{1,0:T(8,128)S(1)}, bf16[128,2048]{1,0:T(8,128)(2,1)S(1)}, bf16[128,2048]{1,0:T(8,128)(2,1)S(1)}...) custom-call(s32[1]{0:T(128)} %bitcast.place, ...), custom_call_target="tpu_custom_call" | custom-call | flops 32000000000 | bytes 1 | tf_op jit(solution)/shard_map/first_exports/pallas_call | solution.py:948
  2.4 0.1 collective-permute-start
  2.5 0.5 %collective-permute-start.1 = (f32[512,128]{1,0:T(8,128)S(1)}, f32[512,128]{1,0:T(8,128)S(1)}, u32[]{:S(2)}, u32[]{:S(2)}) collective-permute-start(f32[512,128]{1,0:T(8,128)S(1)} %get-tuple-element.93), channel_id=1, source_target_pairs={{0,1},{1,0},{2,3},{3,2},{4,5},{5,4},{6,7},{7,6},{8,9},{9,8},{10,11... | collective-permute-start | bytes 786440 | tf_op jit(solution)/shard_map/ppermute | solution.py:935
  3.0 0.6 %own_exports.1 = (f32[1024,128]{1,0:T(8,128)S(1)}, f32[16,128]{1,0:T(8,128)S(1)}) custom-call(s32[1]{0:T(128)} %bitcast.place, bf16[128,2048]{1,0:T(8,128)(2,1)S(1)} %get-tuple-element.86.query, bf16[128,2048]{1,0:T(8,128)(2,1)S(1)} %get-tuple-element.87.key, bf16[128,2048]{1,0:T(8,128)(2,1)S(1)} %get-tuple-element.88.value, ...), custom_call_target="tpu_custom_call" | custom-call | flops 12800000000 | bytes 1 | tf_op jit(solution)/shard_map/own_exports/pallas_call | solution.py:938
  3.6 0.4 %collective-permute-done.first_got.got.pair_got = f32[528,128]{1,0:T(8,128)S(1)} collective-permute-done((f32[528,128]{1,0:T(8,128)S(1)}, f32[528,128]{1,0:T(8,128)S(1)}, u32[]{:S(2)}, u32[]{:S(2)}) %collective-permute-start) | collective-permute-done | bytes 270368 | tf_op jit(solution)/shard_map/ppermute | solution.py:935
  4.1 2.5 %collective-permute-start.5 = (f32[512,128]{1,0:T(8,128)S(1)}, f32[512,128]{1,0:T(8,128)S(1)}, u32[]{:S(2)}, u32[]{:S(2)}) collective-permute-start(f32[512,128]{1,0:T(8,128)S(1)} %first_merge.2.after), channel_id=1, source_target_pairs={{0,2},{1,3},{2,0},{3,1},{4,6},{5,7},{6,4},{7,5},{8,10},{9,11},{10,... | collective-permute-start | bytes 786440 | tf_op jit(solution)/shard_map/ppermute | solution.py:935
  6.6 1.6 %second_exports.1 = (f32[512,128]{1,0:T(8,128)S(1)}, f32[512,128]{1,0:T(8,128)S(1)}, f32[1024,128]{1,0:T(8,128)S(1)}, f32[4096,128]{1,0:T(8,128)S(1)}, f32[24,128]{1,0:T(8,128)S(1)}) custom-call(s32[1]{0:T(128)} %bitcast.place, bf16[128,2048]{1,0:T(8,128)(2,1)S(1)} %get-tuple-element.86.query, bf16[128,2048]{1,0:T(8,128)(2,1)S(1)} %get-tuple-element.87.key, ...), custom_call_target="tpu_custom_call" | custom-call | flops 1600000 | bytes 1 | tf_op jit(solution)/shard_map/second_exports/pallas_call | solution.py:938
  8.2 0.7 %collective-permute-start.3 = (f32[512,128]{1,0:T(8,128)S(1)}, f32[512,128]{1,0:T(8,128)S(1)}, u32[]{:S(2)}, u32[]{:S(2)}) collective-permute-start(f32[512,128]{1,0:T(8,128)S(1)} %get-tuple-element.99), channel_id=1, source_target_pairs={{0,1},{1,0},{2,3},{3,2},{4,5},{5,4},{6,7},{7,6},{8,9},{9,8},{10,11... | collective-permute-start | bytes 786440 | tf_op jit(solution)/shard_map/ppermute | solution.py:935
  8.9 0.1 collective-permute-start.4
  9.0 0.4 %collective-permute-start.10 = (f32[4096,128]{1,0:T(8,128)S(1)}, f32[4096,128]{1,0:T(8,128)S(1)}, u32[]{:S(2)}, u32[]{:S(2)}) collective-permute-start(f32[4096,128]{1,0:T(8,128)S(1)} %get-tuple-element.106), channel_id=1, source_target_pairs={{0,1},{1,0},{2,3},{3,2},{4,5},{5,4},{6,7},{7,6},{8,9},{9,8},{10,11... | collective-permute-start | bytes 6291464 | tf_op jit(solution)/shard_map/ppermute | solution.py:935
  9.4 1.4 %local.4 = (f32[128,512]{1,0:T(8,128)S(1)}, f32[128,512]{1,0:T(8,128)S(1)}, f32[128,512]{1,0:T(8,128)S(1)}, f32[128,512]{1,0:T(8,128)S(1)}, f32[8,4,128]{2,1,0:T(4,128)S(1)}, /*index=5*/f32[4,128]{1,0:T(4,128)S(1)}) custom-call(s32[1]{0:T(128)} %bitcast.place, bf16[128,2048]{1,0:T(8,128)(2,1)S(1)} %get-tuple-element.86.query, ...), custom_call_target="tpu_custom_call" | custom-call | flops 16000000 | bytes 1 | tf_op jit(solution)/shard_map/local/pallas_call | solution.py:938
  10.8 0.0 collective-permute-done.1.got.pair_got
  10.8 0.1 first_merge.3
  10.9 0.1 collective-permute-start.2
  11.0 1.4 %local.5 = (f32[128,512]{1,0:T(8,128)S(1)}, f32[128,512]{1,0:T(8,128)S(1)}, f32[128,512]{1,0:T(8,128)S(1)}, f32[128,512]{1,0:T(8,128)S(1)}, f32[8,4,128]{2,1,0:T(4,128)S(1)}, /*index=5*/f32[4,128]{1,0:T(4,128)S(1)}) custom-call(s32[1]{0:T(128)} %bitcast.place, bf16[128,2048]{1,0:T(8,128)(2,1)S(1)} %get-tuple-element.86.query, ...), custom_call_target="tpu_custom_call" | custom-call | flops 16000000 | bytes 1 | tf_op jit(solution)/shard_map/local/pallas_call | solution.py:938
  12.4 0.0 collective-permute-done.3.rest_1_.got.second_got
  12.4 0.0 collective-permute-done.4.got.second_got
  12.4 0.5 %collective-permute-done.5.first = f32[512,128]{1,0:T(8,128)S(1)} collective-permute-done((f32[512,128]{1,0:T(8,128)S(1)}, f32[512,128]{1,0:T(8,128)S(1)}, u32[]{:S(2)}, u32[]{:S(2)}) %collective-permute-start.5) | collective-permute-done | bytes 262176 | tf_op jit(solution)/shard_map/ppermute | solution.py:935
  12.9 0.1 second_merge.2.rest_0_
  13.0 1.0 %collective-permute-start.8 = (f32[512,128]{1,0:T(8,128)S(1)}, f32[512,128]{1,0:T(8,128)S(1)}, u32[]{:S(2)}, u32[]{:S(2)}) collective-permute-start(f32[512,128]{1,0:T(8,128)S(1)} %second_merge.2.rest_0_), channel_id=1, source_target_pairs={{0,1},{1,0},{2,4},{4,2},{3,5},{5,3},{6,7},{7,6},{8,9},{9,8},{10,12... | collective-permute-start | bytes 786440 | tf_op jit(solution)/shard_map/ppermute | solution.py:935
  14.0 1.4 %local.6 = (f32[128,512]{1,0:T(8,128)S(1)}, f32[128,512]{1,0:T(8,128)S(1)}, f32[128,512]{1,0:T(8,128)S(1)}, f32[128,512]{1,0:T(8,128)S(1)}, f32[8,4,128]{2,1,0:T(4,128)S(1)}, /*index=5*/f32[4,128]{1,0:T(4,128)S(1)}) custom-call(s32[1]{0:T(128)} %bitcast.place, bf16[128,2048]{1,0:T(8,128)(2,1)S(1)} %get-tuple-element.86.query, ...), custom_call_target="tpu_custom_call" | custom-call | flops 25600000000 | bytes 1 | tf_op jit(solution)/shard_map/local/pallas_call | solution.py:938
  15.4 0.1 collective-permute-start.7
  15.5 1.4 %local.7 = (f32[128,512]{1,0:T(8,128)S(1)}, f32[128,512]{1,0:T(8,128)S(1)}, f32[128,512]{1,0:T(8,128)S(1)}, f32[128,512]{1,0:T(8,128)S(1)}, f32[8,4,128]{2,1,0:T(4,128)S(1)}, /*index=5*/f32[4,128]{1,0:T(4,128)S(1)}) custom-call(s32[1]{0:T(128)} %bitcast.place, bf16[128,2048]{1,0:T(8,128)(2,1)S(1)} %get-tuple-element.86.query, ...), custom_call_target="tpu_custom_call" | custom-call | flops 1600000000 | bytes 1 | tf_op jit(solution)/shard_map/local/pallas_call | solution.py:938
  16.9 2.1 %collective-permute-done.2.first.chip_total = f32[528,128]{1,0:T(8,128)S(1)} collective-permute-done((f32[528,128]{1,0:T(8,128)S(1)}, f32[528,128]{1,0:T(8,128)S(1)}, u32[]{:S(2)}, u32[]{:S(2)}) %collective-permute-start.2) | collective-permute-done | bytes 270368 | tf_op jit(solution)/shard_map/ppermute | solution.py:935
  19.0 0.1 second_merge.3
  19.1 0.9 %collective-permute-start.6 = (f32[512,128]{1,0:T(8,128)S(1)}, f32[512,128]{1,0:T(8,128)S(1)}, u32[]{:S(2)}, u32[]{:S(2)}) collective-permute-start(f32[512,128]{1,0:T(8,128)S(1)} %second_merge.3), channel_id=1, source_target_pairs={{0,1},{1,0},{2,4},{4,2},{3,5},{5,3},{6,7},{7,6},{8,9},{9,8},{10,12... | collective-permute-start | bytes 786440 | tf_op jit(solution)/shard_map/ppermute | solution.py:935
  20.0 0.0 collective-permute-done.7.rest_1_.first
  20.0 0.0 collective-permute-done.8.second.rest_0_
  20.0 0.1 collective-permute-start.9
  20.1 2.9 %collective-permute-start.14 = (f32[512,128]{1,0:T(8,128)S(1)}, f32[512,128]{1,0:T(8,128)S(1)}, u32[]{:S(2)}, u32[]{:S(2)}) collective-permute-start(f32[512,128]{1,0:T(8,128)S(1)} %collective-permute-done.8.second.rest_0_), channel_id=1, source_target_pairs={{0,2},{1,3},{2,0},{3,1},{4,6},{5,7},{6,4},{7,5},{8,10},{9,11},{10,... | collective-permute-start | bytes 786440 | tf_op jit(solution)/shard_map/ppermute | solution.py:935
  22.9 0.0 collective-permute-done.10.front
  22.9 1.1 %first_use.4 = (f32[128,512]{1,0:T(8,128)S(1)}, f32[128,512]{1,0:T(8,128)S(1)}, f32[128,512]{1,0:T(8,128)S(1)}, f32[128,512]{1,0:T(8,128)S(1)}, f32[16,128]{1,0:T(8,128)S(1)}) custom-call(s32[1]{0:T(128)} %bitcast.place, bf16[128,2048]{1,0:T(8,128)(2,1)S(1)} %get-tuple-element.86.query, bf16[128,2048]{1,0:T(8,128)(2,1)S(1)} %get-tuple-element.87.key, ...), custom_call_target="tpu_custom_call" | custom-call | flops 4800000000 | bytes 1 | tf_op jit(solution)/shard_map/first_use/pallas_call | solution.py:938
  24.0 0.0 collective-permute-done.9.second
  24.0 1.1 %first_use.5 = (f32[128,512]{1,0:T(8,128)S(1)}, f32[128,512]{1,0:T(8,128)S(1)}, f32[128,512]{1,0:T(8,128)S(1)}, f32[128,512]{1,0:T(8,128)S(1)}, f32[16,128]{1,0:T(8,128)S(1)}) custom-call(s32[1]{0:T(128)} %bitcast.place, bf16[128,2048]{1,0:T(8,128)(2,1)S(1)} %get-tuple-element.86.query, bf16[128,2048]{1,0:T(8,128)(2,1)S(1)} %get-tuple-element.87.key, ...), custom_call_target="tpu_custom_call" | custom-call | flops 4800000000 | bytes 1 | tf_op jit(solution)/shard_map/first_use/pallas_call | solution.py:938
  25.2 0.0 collective-permute-done.6.second
  25.2 2.0 %collective-permute-start.12 = (f32[512,128]{1,0:T(8,128)S(1)}, f32[512,128]{1,0:T(8,128)S(1)}, u32[]{:S(2)}, u32[]{:S(2)}) collective-permute-start(f32[512,128]{1,0:T(8,128)S(1)} %collective-permute-done.6.second), channel_id=1, source_target_pairs={{0,2},{1,3},{2,0},{3,1},{4,6},{5,7},{6,4},{7,5},{8,10},{9,11},{10,... | collective-permute-start | bytes 786440 | tf_op jit(solution)/shard_map/ppermute | solution.py:935
  27.1 2.1 %collective-permute-start.11 = (f32[512,128]{1,0:T(8,128)S(1)}, f32[512,128]{1,0:T(8,128)S(1)}, u32[]{:S(2)}, u32[]{:S(2)}) collective-permute-start(f32[512,128]{1,0:T(8,128)S(1)} %collective-permute-done.6.second), channel_id=1, source_target_pairs={{0,1},{1,0},{2,3},{3,2},{4,5},{5,4},{6,7},{7,6},{8,9},{9,8},{10,11... | collective-permute-start | bytes 786440 | tf_op jit(solution)/shard_map/ppermute | solution.py:935
  29.3 0.0 collective-permute-start.13
  29.3 1.1 %first_use.6 = (f32[128,512]{1,0:T(8,128)S(1)}, f32[128,512]{1,0:T(8,128)S(1)}, f32[128,512]{1,0:T(8,128)S(1)}, f32[128,512]{1,0:T(8,128)S(1)}, f32[16,128]{1,0:T(8,128)S(1)}) custom-call(s32[1]{0:T(128)} %bitcast.place, bf16[128,2048]{1,0:T(8,128)(2,1)S(1)} %get-tuple-element.86.query, bf16[128,2048]{1,0:T(8,128)(2,1)S(1)} %get-tuple-element.87.key, ...), custom_call_target="tpu_custom_call" | custom-call | flops 4800000000 | bytes 1 | tf_op jit(solution)/shard_map/first_use/pallas_call | solution.py:938
  30.4 0.1 collective-permute-done.11.second
  30.4 0.4 collective-permute-done.13.first
  30.8 1.1 %first_use.7 = (f32[128,512]{1,0:T(8,128)S(1)}, f32[128,512]{1,0:T(8,128)S(1)}, f32[128,512]{1,0:T(8,128)S(1)}, f32[128,512]{1,0:T(8,128)S(1)}, f32[16,128]{1,0:T(8,128)S(1)}) custom-call(s32[1]{0:T(128)} %bitcast.place, bf16[128,2048]{1,0:T(8,128)(2,1)S(1)} %get-tuple-element.86.query, bf16[128,2048]{1,0:T(8,128)(2,1)S(1)} %get-tuple-element.87.key, ...), custom_call_target="tpu_custom_call" | custom-call | flops 4800000000 | bytes 1 | tf_op jit(solution)/shard_map/first_use/pallas_call | solution.py:938
  31.9 0.0 collective-permute-done.14.third
  31.9 0.4 %collective-permute-start.15 = (f32[512,128]{1,0:T(8,128)S(1)}, f32[512,128]{1,0:T(8,128)S(1)}, u32[]{:S(2)}, u32[]{:S(2)}) collective-permute-start(f32[512,128]{1,0:T(8,128)S(1)} %collective-permute-done.14.third), channel_id=1, source_target_pairs={{0,1},{1,0},{2,3},{3,2},{4,5},{5,4},{6,7},{7,6},{8,9},{9,8},{10,11... | collective-permute-start | bytes 786440 | tf_op jit(solution)/shard_map/ppermute | solution.py:935
  32.3 0.6 %last_use.4 = (bf16[128,512]{1,0:T(8,128)(2,1)S(1)}, bf16[128,512]{1,0:T(8,128)(2,1)S(1)}, bf16[128,512]{1,0:T(8,128)(2,1)S(1)}, bf16[128,512]{1,0:T(8,128)(2,1)S(1)}, f32[12,128]{1,0:T(8,128)S(1)}) custom-call(s32[1]{0:T(128)} %bitcast.place, bf16[128,2048]{1,0:T(8,128)(2,1)S(1)} %get-tuple-element.86.query, bf16[128,2048]{1,0:T(8,128)(2,1)S(1)} %get-tuple-element.87.key, ...), custom_call_target="tpu_custom_call" | custom-call | flops 9600000000 | bytes 1 | tf_op jit(solution)/shard_map/last_use/pallas_call | solution.py:938
  33.0 0.5 %collective-permute-done.15.third = f32[512,128]{1,0:T(8,128)S(1)} collective-permute-done((f32[512,128]{1,0:T(8,128)S(1)}, f32[512,128]{1,0:T(8,128)S(1)}, u32[]{:S(2)}, u32[]{:S(2)}) %collective-permute-start.15) | collective-permute-done | bytes 262176 | tf_op jit(solution)/shard_map/ppermute | solution.py:935
  33.5 1.4 %last_use.5 = (bf16[128,2048]{1,0:T(8,128)(2,1)}, bf16[128,2048]{1,0:T(8,128)(2,1)}, bf16[128,2048]{1,0:T(8,128)(2,1)}, bf16[128,2048]{1,0:T(8,128)(2,1)}, f32[12,128]{1,0:T(8,128)S(1)}) custom-call(s32[1]{0:T(128)} %bitcast.place, bf16[128,2048]{1,0:T(8,128)(2,1)S(1)} %get-tuple-element.86.query, bf16[128,2048]{1,0:T(8,128)(2,1)S(1)} %get-tuple-element.87.key, ...), custom_call_target="tpu_custom_call" | custom-call | flops 4000000000 | bytes 1 | tf_op jit(solution)/shard_map/last_use/pallas_call | solution.py:1102
  34.9 0.0 collective-permute-done.12.third
  35.0 0.9 %collective-permute-start.16 = (f32[512,128]{1,0:T(8,128)S(1)}, f32[512,128]{1,0:T(8,128)S(1)}, u32[]{:S(2)}, u32[]{:S(2)}) collective-permute-start(f32[512,128]{1,0:T(8,128)S(1)} %collective-permute-done.12.third), channel_id=1, source_target_pairs={{0,1},{1,0},{2,3},{3,2},{4,5},{5,4},{6,7},{7,6},{8,9},{9,8},{10,11... | collective-permute-start | bytes 786440 | tf_op jit(solution)/shard_map/ppermute | solution.py:935
  35.8 0.6 %last_use.6 = (bf16[128,512]{1,0:T(8,128)(2,1)S(1)}, bf16[128,512]{1,0:T(8,128)(2,1)S(1)}, bf16[128,512]{1,0:T(8,128)(2,1)S(1)}, bf16[128,512]{1,0:T(8,128)(2,1)S(1)}, f32[12,128]{1,0:T(8,128)S(1)}) custom-call(s32[1]{0:T(128)} %bitcast.place, bf16[128,2048]{1,0:T(8,128)(2,1)S(1)} %get-tuple-element.86.query, bf16[128,2048]{1,0:T(8,128)(2,1)S(1)} %get-tuple-element.87.key, ...), custom_call_target="tpu_custom_call" | custom-call | flops 2400000000 | bytes 1 | tf_op jit(solution)/shard_map/last_use/pallas_call | solution.py:938
  36.5 0.5 %collective-permute-done.16.third = f32[512,128]{1,0:T(8,128)S(1)} collective-permute-done((f32[512,128]{1,0:T(8,128)S(1)}, f32[512,128]{1,0:T(8,128)S(1)}, u32[]{:S(2)}, u32[]{:S(2)}) %collective-permute-start.16) | collective-permute-done | bytes 262176 | tf_op jit(solution)/shard_map/ppermute | solution.py:935
  37.0 1.6 %last_use.7 = (bf16[128,2048]{1,0:T(8,128)(2,1)}, bf16[128,2048]{1,0:T(8,128)(2,1)}, bf16[128,2048]{1,0:T(8,128)(2,1)}, bf16[128,2048]{1,0:T(8,128)(2,1)}, f32[11,16,128]{2,1,0:T(8,128)}, /*index=5*/f32[16,128]{1,0:T(8,128)}) custom-call(s32[1]{0:T(128)} %bitcast.place, ...), custom_call_target="tpu_custom_call", output_to_operand_aliasing={{0}: (36, {}), {1}: (37, {}), {2}: (38, {}), {3}: (39, {})} | custom-call | flops 4000000000 | bytes 1 | tf_op jit(solution)/shard_map/last_use/pallas_call | solution.py:1102
  (1 shorter events, 0.0 us)
Async XLA Ops:
  2.4 1.6 %collective-permute-start = (f32[528,128]{1,0:T(8,128)S(1)}, f32[528,128]{1,0:T(8,128)S(1)}, u32[]{:S(2)}, u32[]{:S(2)}) collective-permute-start(f32[528,128]{1,0:T(8,128)S(1)} %get-tuple-element.92.after), channel_id=1, source_target_pairs={{0,1},{1,0},{2,3},{3,2},{4,5},{5,4},{6,7},{7,6},{8,9},{9,8},{10,11... | collective-permute-start | bytes 811016 | tf_op jit(solution)/shard_map/ppermute | solution.py:935
  2.5 8.3 %collective-permute-start.1 = (f32[512,128]{1,0:T(8,128)S(1)}, f32[512,128]{1,0:T(8,128)S(1)}, u32[]{:S(2)}, u32[]{:S(2)}) collective-permute-start(f32[512,128]{1,0:T(8,128)S(1)} %get-tuple-element.93), channel_id=1, source_target_pairs={{0,1},{1,0},{2,3},{3,2},{4,5},{5,4},{6,7},{7,6},{8,9},{9,8},{10,11... | collective-permute-start | bytes 786440 | tf_op jit(solution)/shard_map/ppermute | solution.py:935
  4.1 8.9 %collective-permute-start.5 = (f32[512,128]{1,0:T(8,128)S(1)}, f32[512,128]{1,0:T(8,128)S(1)}, u32[]{:S(2)}, u32[]{:S(2)}) collective-permute-start(f32[512,128]{1,0:T(8,128)S(1)} %first_merge.2.after), channel_id=1, source_target_pairs={{0,2},{1,3},{2,0},{3,1},{4,6},{5,7},{6,4},{7,5},{8,10},{9,11},{10,... | collective-permute-start | bytes 786440 | tf_op jit(solution)/shard_map/ppermute | solution.py:935
  8.2 4.2 %collective-permute-start.3 = (f32[512,128]{1,0:T(8,128)S(1)}, f32[512,128]{1,0:T(8,128)S(1)}, u32[]{:S(2)}, u32[]{:S(2)}) collective-permute-start(f32[512,128]{1,0:T(8,128)S(1)} %get-tuple-element.99), channel_id=1, source_target_pairs={{0,1},{1,0},{2,3},{3,2},{4,5},{5,4},{6,7},{7,6},{8,9},{9,8},{10,11... | collective-permute-start | bytes 786440 | tf_op jit(solution)/shard_map/ppermute | solution.py:935
  8.9 3.5 %collective-permute-start.4 = (f32[512,128]{1,0:T(8,128)S(1)}, f32[512,128]{1,0:T(8,128)S(1)}, u32[]{:S(2)}, u32[]{:S(2)}) collective-permute-start(f32[512,128]{1,0:T(8,128)S(1)} %get-tuple-element.100), channel_id=1, source_target_pairs={{0,1},{1,0},{2,3},{3,2},{4,5},{5,4},{6,7},{7,6},{8,9},{9,8},{10,11... | collective-permute-start | bytes 786440 | tf_op jit(solution)/shard_map/ppermute | solution.py:935
  9.0 14.0 %collective-permute-start.10 = (f32[4096,128]{1,0:T(8,128)S(1)}, f32[4096,128]{1,0:T(8,128)S(1)}, u32[]{:S(2)}, u32[]{:S(2)}) collective-permute-start(f32[4096,128]{1,0:T(8,128)S(1)} %get-tuple-element.106), channel_id=1, source_target_pairs={{0,1},{1,0},{2,3},{3,2},{4,5},{5,4},{6,7},{7,6},{8,9},{9,8},{10,11... | collective-permute-start | bytes 6291464 | tf_op jit(solution)/shard_map/ppermute | solution.py:935
  10.9 8.1 %collective-permute-start.2 = (f32[528,128]{1,0:T(8,128)S(1)}, f32[528,128]{1,0:T(8,128)S(1)}, u32[]{:S(2)}, u32[]{:S(2)}) collective-permute-start(f32[528,128]{1,0:T(8,128)S(1)} %first_merge.3), channel_id=1, source_target_pairs={{0,2},{1,3},{2,0},{3,1},{4,6},{5,7},{6,4},{7,5},{8,10},{9,11},{10,... | collective-permute-start | bytes 811016 | tf_op jit(solution)/shard_map/ppermute | solution.py:935
  13.0 7.0 %collective-permute-start.8 = (f32[512,128]{1,0:T(8,128)S(1)}, f32[512,128]{1,0:T(8,128)S(1)}, u32[]{:S(2)}, u32[]{:S(2)}) collective-permute-start(f32[512,128]{1,0:T(8,128)S(1)} %second_merge.2.rest_0_), channel_id=1, source_target_pairs={{0,1},{1,0},{2,4},{4,2},{3,5},{5,3},{6,7},{7,6},{8,9},{9,8},{10,12... | collective-permute-start | bytes 786440 | tf_op jit(solution)/shard_map/ppermute | solution.py:935
  15.4 4.6 %collective-permute-start.7 = (f32[512,128]{1,0:T(8,128)S(1)}, f32[512,128]{1,0:T(8,128)S(1)}, u32[]{:S(2)}, u32[]{:S(2)}) collective-permute-start(f32[512,128]{1,0:T(8,128)S(1)} %collective-permute-done.5.first), channel_id=1, source_target_pairs={{0,1},{1,0},{2,3},{3,2},{4,5},{5,4},{6,7},{7,6},{8,9},{9,8},{10,11... | collective-permute-start | bytes 786440 | tf_op jit(solution)/shard_map/ppermute | solution.py:935
  19.1 6.1 %collective-permute-start.6 = (f32[512,128]{1,0:T(8,128)S(1)}, f32[512,128]{1,0:T(8,128)S(1)}, u32[]{:S(2)}, u32[]{:S(2)}) collective-permute-start(f32[512,128]{1,0:T(8,128)S(1)} %second_merge.3), channel_id=1, source_target_pairs={{0,1},{1,0},{2,4},{4,2},{3,5},{5,3},{6,7},{7,6},{8,9},{9,8},{10,12... | collective-permute-start | bytes 786440 | tf_op jit(solution)/shard_map/ppermute | solution.py:935
  20.0 4.1 %collective-permute-start.9 = (f32[512,128]{1,0:T(8,128)S(1)}, f32[512,128]{1,0:T(8,128)S(1)}, u32[]{:S(2)}, u32[]{:S(2)}) collective-permute-start(f32[512,128]{1,0:T(8,128)S(1)} %collective-permute-done.8.second.rest_0_), channel_id=1, source_target_pairs={{0,1},{1,0},{2,3},{3,2},{4,5},{5,4},{6,7},{7,6},{8,9},{9,8},{10,11... | collective-permute-start | bytes 786440 | tf_op jit(solution)/shard_map/ppermute | solution.py:935
  20.1 11.8 %collective-permute-start.14 = (f32[512,128]{1,0:T(8,128)S(1)}, f32[512,128]{1,0:T(8,128)S(1)}, u32[]{:S(2)}, u32[]{:S(2)}) collective-permute-start(f32[512,128]{1,0:T(8,128)S(1)} %collective-permute-done.8.second.rest_0_), channel_id=1, source_target_pairs={{0,2},{1,3},{2,0},{3,1},{4,6},{5,7},{6,4},{7,5},{8,10},{9,11},{10,... | collective-permute-start | bytes 786440 | tf_op jit(solution)/shard_map/ppermute | solution.py:935
  25.2 9.8 %collective-permute-start.12 = (f32[512,128]{1,0:T(8,128)S(1)}, f32[512,128]{1,0:T(8,128)S(1)}, u32[]{:S(2)}, u32[]{:S(2)}) collective-permute-start(f32[512,128]{1,0:T(8,128)S(1)} %collective-permute-done.6.second), channel_id=1, source_target_pairs={{0,2},{1,3},{2,0},{3,1},{4,6},{5,7},{6,4},{7,5},{8,10},{9,11},{10,... | collective-permute-start | bytes 786440 | tf_op jit(solution)/shard_map/ppermute | solution.py:935
  27.1 3.3 %collective-permute-start.11 = (f32[512,128]{1,0:T(8,128)S(1)}, f32[512,128]{1,0:T(8,128)S(1)}, u32[]{:S(2)}, u32[]{:S(2)}) collective-permute-start(f32[512,128]{1,0:T(8,128)S(1)} %collective-permute-done.6.second), channel_id=1, source_target_pairs={{0,1},{1,0},{2,3},{3,2},{4,5},{5,4},{6,7},{7,6},{8,9},{9,8},{10,11... | collective-permute-start | bytes 786440 | tf_op jit(solution)/shard_map/ppermute | solution.py:935
  29.3 1.5 %collective-permute-start.13 = (f32[528,128]{1,0:T(8,128)S(1)}, f32[528,128]{1,0:T(8,128)S(1)}, u32[]{:S(2)}, u32[]{:S(2)}) collective-permute-start(f32[528,128]{1,0:T(8,128)S(1)} %collective-permute-done.2.first.chip_total), channel_id=1, source_target_pairs={{0,1},{1,0},{2,3},{3,2},{4,5},{5,4},{6,7},{7,6},{8,9},{9,8},{10,11... | collective-permute-start | bytes 811016 | tf_op jit(solution)/shard_map/ppermute | solution.py:935
  31.9 1.6 %collective-permute-start.15 = (f32[512,128]{1,0:T(8,128)S(1)}, f32[512,128]{1,0:T(8,128)S(1)}, u32[]{:S(2)}, u32[]{:S(2)}) collective-permute-start(f32[512,128]{1,0:T(8,128)S(1)} %collective-permute-done.14.third), channel_id=1, source_target_pairs={{0,1},{1,0},{2,3},{3,2},{4,5},{5,4},{6,7},{7,6},{8,9},{9,8},{10,11... | collective-permute-start | bytes 786440 | tf_op jit(solution)/shard_map/ppermute | solution.py:935
  35.0 2.0 %collective-permute-start.16 = (f32[512,128]{1,0:T(8,128)S(1)}, f32[512,128]{1,0:T(8,128)S(1)}, u32[]{:S(2)}, u32[]{:S(2)}) collective-permute-start(f32[512,128]{1,0:T(8,128)S(1)} %collective-permute-done.12.third), channel_id=1, source_target_pairs={{0,1},{1,0},{2,3},{3,2},{4,5},{5,4},{6,7},{7,6},{8,9},{9,8},{10,11... | collective-permute-start | bytes 786440 | tf_op jit(solution)/shard_map/ppermute | solution.py:935
